TPU v7x, 32 devices: a whole 2x2x4 slice. The times are simulated.
32 devices in a mesh: section: 2 (over x), dp: 4 (over y, core), tensor: 4 (over z).
Axes of the slice: x: 2, y: 2, z: 4, core: 2. Of those that a mesh axis runs over, the one named last changes fastest.
Arguments:
- block_eight_input: bfloat16 [192, 16, 1152], P('tensor', 'dp'), may hold values from -6 to 6
- cond: bfloat16 [16, 3, 1152], P('dp'), may hold values from -6 to 6
- image_slot_index: int32 [16, 192], P('dp'), may hold values from 0 to 2, never falling along the last dimension, each value on 1 to 96 neighbouring positions
- targets: bfloat16 [192, 16, 768], P(None, 'dp', 'tensor'), may hold values from -6 to 6
- cot: bfloat16 [192, 16, 1152], P('tensor', 'dp'), may hold values from -6 to 6
- ada_w: bfloat16 [2, 1152, 6912], P('section', None, 'tensor'), may hold values from -0.1875 to 0.1875
- ada_b: bfloat16 [2, 6912], P('section', 'tensor'), may hold values from -3 to 3
- query_key_value_weight: bfloat16 [2, 1152, 3, 1152], P('section', None, None, 'tensor'), may hold values from -0.1875 to 0.1875
- query_value_bias: bfloat16 [2, 2, 1152], P('section', None, 'tensor'), may hold values from -2 to 2
- attention_output_weight: bfloat16 [2, 1152, 1152], P('section', 'tensor'), may hold values from -1.5 to 1.5
- attention_output_bias: bfloat16 [2, 1152], P('section'), may hold values from -2 to 2
- hidden_weight: bfloat16 [2, 1152, 4608], P('section', None, 'tensor'), may hold values from -0.1875 to 0.1875
- hidden_bias: bfloat16 [2, 4608], P('section', 'tensor'), may hold values from -2 to 2
- output_weight_mlp: bfloat16 [2, 4608, 1152], P('section', 'tensor'), may hold values from -0.09375 to 0.09375
- output_bias_mlp: bfloat16 [2, 1152], P('section'), may hold values from -2 to 2
- p1_w: bfloat16 [1152, 2048], P(None, 'tensor'), may hold values from -0.1875 to 0.1875
- p1_b: bfloat16 [2048], P('tensor'), may hold values from -2 to 2
- p2_w: bfloat16 [2048, 2048], P('tensor'), may hold values from -0.125 to 0.125
- p2_b: bfloat16 [2048], replicated, may hold values from -2 to 2
- p3_w: bfloat16 [2048, 768], P(None, 'tensor'), may hold values from -0.125 to 0.125
- p3_b: bfloat16 [768], P('tensor'), may hold values from -2 to 2
Outputs:
- section_out: bfloat16 [2, 192, 16, 1152], P('section', 'tensor', 'dp')
- section_grad: float32 [2, 192, 16, 1152], P('section', 'tensor', 'dp')
- align_loss: float32 [], replicated
- g_ada_w: float32 [2, 1152, 6912], P('section', 'dp', 'tensor')
- g_ada_b: float32 [2, 6912], P('section', 'tensor')
- g_qkv_w: float32 [2, 1152, 3, 1152], P('section', 'dp', None, 'tensor')
- g_qv_b: float32 [2, 2, 1152], P('section', None, 'tensor')
- g_out_w: float32 [2, 1152, 1152], P('section', 'tensor', 'dp')
- g_out_b: float32 [2, 1152], P('section')
- g_fc1_w: float32 [2, 1152, 4608], P('section', 'dp', 'tensor')
- g_fc1_b: float32 [2, 4608], P('section', 'tensor')
- g_fc2_w: float32 [2, 4608, 1152], P('section', 'tensor', 'dp')
- g_fc2_b: float32 [2, 1152], P('section')
- g_p1_w: float32 [1152, 2048], P(('section', 'dp'), 'tensor')
- g_p1_b: float32 [2048], P('tensor')
- g_p2_w: float32 [2048, 2048], P('tensor', ('section', 'dp'))
- g_p2_b: float32 [2048], replicated
- g_p3_w: float32 [2048, 768], P(('section', 'dp'), 'tensor')
- g_p3_b: float32 [768], P('tensor')
Inputs may be any that keep to these rules, and one draw needn't show every extreme that they name: `image_slot_index`: within a row the slot numbers never fall; each slot covers 1 to 96 positions and one covers exactly 96.
All inputs are finite; a program needn't handle non-finite values.
Results may differ from a plain program's by a relative error of at most 0.035.
The roundings to bfloat16 on the way count: a program that leaves them out, or rounds other values in their place, can miss the bound.
Values may be sent and summed in bfloat16 or wider, within the bound.
A program may use at most 192 MiB of HBM per device.

v0:
```python
import jax
import jax.numpy as jnp
from jax import lax
from jax.sharding import PartitionSpec as P

HEAD_WIDTH = 72
ROW_LENGTH = 192
IMAGES_PER_ROW = 3
MICRO = 2


norm_eps = 1e-06
cosine_eps = 1e-06
masked_score = -1e30
highest = lax.Precision.HIGHEST


def from_behind(block, axis, distance):
    devices = range(lax.axis_size(axis))
    route = [(i - distance, i) for i in devices if i - distance in devices]
    return lax.ppermute(block, axis, route)


def layer_norm(source_rows):
    centred = source_rows - jnp.mean(source_rows, axis=-1, keepdims=True)
    inverse = lax.rsqrt(jnp.mean(centred * centred, axis=-1, keepdims=True) + norm_eps)
    return (centred * inverse, inverse)


def norm_back(grad_normed, normed, inverse):
    mean_grad = jnp.mean(grad_normed, axis=-1, keepdims=True)
    mean_cross = jnp.mean(grad_normed * normed, axis=-1, keepdims=True)
    return inverse * (grad_normed - mean_grad - normed * mean_cross)


def gelu_tanh(source_rows):
    return jax.nn.gelu(source_rows, approximate=True)


def act_grad(function, source_rows, upstream):
    unused_value, pullback = jax.vjp(function, source_rows)
    return pullback(upstream)[0]


def contract_rows(left_rows, right_rows):
    return lax.dot_general(
        left_rows, right_rows, (((0,), (0,)), ((), ())), preferred_element_type=jnp.float32
    )


def gather_rows(source_rows):
    return lax.all_gather(source_rows, "tensor", axis=0, tiled=True)


def gather_grads(source_rows):
    return lax.all_gather(source_rows, "tensor", axis=0, tiled=True)


def scatter_forward(left_rows, weight, local_rows):

    def partial_term(start, count):
        return jnp.dot(left_rows, weight, preferred_element_type=jnp.float32)

    return lax.psum_scatter(
        partial_term(jnp.int32(0), local_rows * lax.axis_size("tensor")),
        "tensor",
        scatter_dimension=0,
        tiled=True,
    )


def scatter_backward(left_rows, weight, local_rows):

    def partial_term(start, count):
        return lax.dot_general(
            left_rows, weight, (((1,), (1,)), ((), ())), preferred_element_type=jnp.float32
        )

    return lax.psum_scatter(
        partial_term(jnp.int32(0), local_rows * lax.axis_size("tensor")),
        "tensor",
        scatter_dimension=0,
        tiled=True,
    )


def split_heads(source_rows, rows_micro):
    return source_rows.reshape(-1, rows_micro, source_rows.shape[-1] // HEAD_WIDTH, HEAD_WIDTH)


def masked_scores(query_heads, key_heads, same_image_mask):
    scores = jnp.einsum(
        "prhd,qrhd->rhpq", query_heads, key_heads, preferred_element_type=jnp.float32
    ) * HEAD_WIDTH ** (-0.5)
    return jnp.where(same_image_mask[:, None], scores, masked_score)


def take_rows(source_rows, micro_index, rows_micro):
    picked = lax.dynamic_slice_in_dim(source_rows, micro_index * rows_micro, rows_micro, 1)
    return picked.reshape(-1, source_rows.shape[-1])


def same_of(image_slot_index, micro_index, rows_micro):
    seg_micro = lax.dynamic_slice_in_dim(image_slot_index, micro_index * rows_micro, rows_micro, 0)
    return seg_micro[:, :, None] == seg_micro[:, None, :]


def forward_block(block_input, apply_modulation, same_image_mask, weights):
    (
        query_key_value_weight,
        query_value_bias,
        attention_output_weight,
        attention_output_bias,
        hidden_weight,
        hidden_bias,
        output_weight_mlp,
        output_bias_mlp,
    ) = weights
    rows_micro = same_image_mask.shape[0]
    local_rows = block_input.shape[0]
    shift_one, scale_one, gate_one, shift_two, scale_two, gate_two = jnp.split(
        apply_modulation, 6, axis=1
    )
    normed, inverse = layer_norm(block_input)
    attn_in = (normed * (1.0 + scale_one) + shift_one).astype(jnp.bfloat16)
    attn_full = gather_rows(attn_in)
    projected = jnp.einsum(
        "td,dkc->tkc", attn_full, query_key_value_weight, preferred_element_type=jnp.float32
    )
    query_rows = (projected[:, 0] + query_value_bias[0].astype(jnp.float32)).astype(jnp.bfloat16)
    key_rows = projected[:, 1].astype(jnp.bfloat16)
    value_rows = (projected[:, 2] + query_value_bias[1].astype(jnp.float32)).astype(jnp.bfloat16)
    scores = masked_scores(
        split_heads(query_rows, rows_micro), split_heads(key_rows, rows_micro), same_image_mask
    )
    top_score = jnp.max(scores, axis=-1, keepdims=True)
    log_total = top_score + jnp.log(jnp.sum(jnp.exp(scores - top_score), axis=-1, keepdims=True))
    soft_rows = jnp.exp(scores - log_total).astype(jnp.bfloat16)
    mixed_tokens = jnp.einsum(
        "rhpq,qrhd->prhd",
        soft_rows,
        split_heads(value_rows, rows_micro),
        preferred_element_type=jnp.float32,
    )
    mixed_tokens = mixed_tokens.reshape(query_rows.shape).astype(jnp.bfloat16)
    branch_one = scatter_forward(
        mixed_tokens, attention_output_weight, local_rows
    ) + attention_output_bias.astype(jnp.float32)
    middle = block_input + gate_one * branch_one
    normed_two, inverse_two = layer_norm(middle)
    mlp_in = (normed_two * (1.0 + scale_two) + shift_two).astype(jnp.bfloat16)
    mlp_full = gather_rows(mlp_in)
    hidden_pre = jnp.dot(
        mlp_full, hidden_weight, preferred_element_type=jnp.float32
    ) + hidden_bias.astype(jnp.float32)
    hidden_act = gelu_tanh(hidden_pre).astype(jnp.bfloat16)
    branch_two = scatter_forward(
        hidden_act, output_weight_mlp, local_rows
    ) + output_bias_mlp.astype(jnp.float32)
    block_out = middle + gate_two * branch_two
    kept = (
        normed,
        inverse,
        branch_one,
        normed_two,
        inverse_two,
        branch_two,
        attn_full,
        query_rows,
        key_rows,
        value_rows,
        log_total,
        mixed_tokens,
        mlp_full,
        hidden_pre,
        hidden_act,
    )
    return (block_out, kept)


def backward_block(grad_out, apply_modulation, same_image_mask, weights, kept):
    (
        query_key_value_weight,
        query_value_bias,
        attention_output_weight,
        attention_output_bias,
        hidden_weight,
        hidden_bias,
        output_weight_mlp,
        output_bias_mlp,
    ) = weights
    (
        normed,
        inverse,
        branch_one,
        normed_two,
        inverse_two,
        branch_two,
        attn_full,
        query_rows,
        key_rows,
        value_rows,
        log_total,
        mixed_tokens,
        mlp_full,
        hidden_pre,
        hidden_act,
    ) = kept
    rows_micro = same_image_mask.shape[0]
    local_rows = grad_out.shape[0]
    shift_one, scale_one, gate_one, shift_two, scale_two, gate_two = jnp.split(
        apply_modulation, 6, axis=1
    )
    grad_gate_two = grad_out * branch_two
    grad_branch_two = gather_grads((grad_out * gate_two).astype(jnp.bfloat16))
    grad_fc2_b = jnp.sum(grad_branch_two.astype(jnp.float32), axis=0)
    grad_fc2_w = contract_rows(hidden_act, grad_branch_two)
    grad_act = lax.dot_general(
        grad_branch_two,
        output_weight_mlp,
        (((1,), (1,)), ((), ())),
        preferred_element_type=jnp.float32,
    )
    grad_pre = act_grad(gelu_tanh, hidden_pre, grad_act).astype(jnp.bfloat16)
    grad_fc1_b = jnp.sum(grad_pre.astype(jnp.float32), axis=0)
    grad_fc1_w = contract_rows(mlp_full, grad_pre)
    grad_mlp_in = scatter_backward(grad_pre, hidden_weight, local_rows)
    grad_scale_two = grad_mlp_in * normed_two
    grad_middle = grad_out + norm_back(grad_mlp_in * (1.0 + scale_two), normed_two, inverse_two)
    grad_gate_one = grad_middle * branch_one
    grad_branch_one = gather_grads((grad_middle * gate_one).astype(jnp.bfloat16))
    grad_out_b = jnp.sum(grad_branch_one.astype(jnp.float32), axis=0)
    grad_out_w = contract_rows(mixed_tokens, grad_branch_one)
    grad_mixed = lax.dot_general(
        grad_branch_one,
        attention_output_weight,
        (((1,), (1,)), ((), ())),
        preferred_element_type=jnp.float32,
    ).astype(jnp.bfloat16)
    query_heads = split_heads(query_rows, rows_micro)
    key_heads = split_heads(key_rows, rows_micro)
    value_heads = split_heads(value_rows, rows_micro)
    grad_heads = split_heads(grad_mixed, rows_micro)
    probs = jnp.exp(masked_scores(query_heads, key_heads, same_image_mask) - log_total)
    grad_probs = jnp.einsum(
        "prhd,qrhd->rhpq", grad_heads, value_heads, preferred_element_type=jnp.float32
    )
    grad_scores = (
        probs * (grad_probs - jnp.sum(grad_probs * probs, axis=-1, keepdims=True))
    ).astype(jnp.bfloat16)
    grad_query = jnp.einsum(
        "rhpq,qrhd->prhd", grad_scores, key_heads, preferred_element_type=jnp.float32
    ) * HEAD_WIDTH ** (-0.5)
    grad_key = jnp.einsum(
        "rhpq,prhd->qrhd", grad_scores, query_heads, preferred_element_type=jnp.float32
    ) * HEAD_WIDTH ** (-0.5)
    grad_value = jnp.einsum(
        "rhpq,prhd->qrhd",
        probs.astype(jnp.bfloat16),
        grad_heads,
        preferred_element_type=jnp.float32,
    )
    token_count = query_rows.shape[0]
    width_local = query_rows.shape[1]
    grad_qkv = jnp.stack(
        [
            grad_query.reshape(token_count, width_local),
            grad_key.reshape(token_count, width_local),
            grad_value.reshape(token_count, width_local),
        ],
        axis=1,
    ).astype(jnp.bfloat16)
    grad_qv_b = jnp.stack(
        [
            jnp.sum(grad_qkv[:, 0].astype(jnp.float32), axis=0),
            jnp.sum(grad_qkv[:, 2].astype(jnp.float32), axis=0),
        ]
    )
    grad_qkv_w = jnp.einsum("td,tkc->dkc", attn_full, grad_qkv, preferred_element_type=jnp.float32)
    grad_attn_in = scatter_backward(
        grad_qkv.reshape(token_count, 3 * width_local),
        query_key_value_weight.reshape(query_key_value_weight.shape[0], 3 * width_local),
        local_rows,
    )
    grad_scale_one = grad_attn_in * normed
    grad_in = grad_middle + norm_back(grad_attn_in * (1.0 + scale_one), normed, inverse)
    grad_modulate = jnp.concatenate(
        [grad_attn_in, grad_scale_one, grad_gate_one, grad_mlp_in, grad_scale_two, grad_gate_two],
        axis=1,
    )
    grads = (
        grad_qkv_w,
        grad_qv_b,
        grad_out_w,
        grad_out_b,
        grad_fc1_w,
        grad_fc1_b,
        grad_fc2_w,
        grad_fc2_b,
    )
    return (grad_in, grads, grad_modulate)


def align_pass(forwarded_rows, target_cols, proj_weights, total_token_count):
    p1_w, p1_b, p2_w, p2_b, p3_w, p3_b = proj_weights
    local_rows = forwarded_rows.shape[0]
    input_full = gather_rows(forwarded_rows)
    first_pre = jnp.dot(input_full, p1_w, preferred_element_type=jnp.float32) + p1_b.astype(
        jnp.float32
    )
    first_act = jax.nn.silu(first_pre).astype(jnp.bfloat16)
    second_pre = scatter_forward(first_act, p2_w, local_rows) + p2_b.astype(jnp.float32)
    second_act = jax.nn.silu(second_pre).astype(jnp.bfloat16)
    second_full = gather_rows(second_act)
    predicted = jnp.dot(second_full, p3_w, preferred_element_type=jnp.float32) + p3_b.astype(
        jnp.float32
    )
    pred_sq, cross, target_sq = lax.psum(
        (
            jnp.sum(predicted * predicted, axis=1),
            jnp.sum(predicted * target_cols, axis=1),
            jnp.sum(target_cols * target_cols, axis=1),
        ),
        "tensor",
    )
    inv_pred = lax.rsqrt(pred_sq + cosine_eps)
    inv_target = lax.rsqrt(target_sq + cosine_eps)
    cosine = cross * inv_pred * inv_target
    loss_local = jnp.sum(cosine)
    factor = -0.5 / total_token_count
    grad_pred = (
        (factor * inv_pred * inv_target)[:, None] * target_cols
        - (factor * cosine * inv_pred * inv_pred)[:, None] * predicted
    ).astype(jnp.bfloat16)
    grad_p3_b = jnp.sum(grad_pred.astype(jnp.float32), axis=0)
    grad_p3_w = contract_rows(second_full, grad_pred)
    grad_second_act = scatter_backward(grad_pred, p3_w, local_rows)
    grad_second_pre = act_grad(jax.nn.silu, second_pre, grad_second_act).astype(jnp.bfloat16)
    grad_second_full = gather_grads(grad_second_pre)
    grad_p2_b = jnp.sum(grad_second_full.astype(jnp.float32), axis=0)
    grad_p2_w = contract_rows(first_act, grad_second_full)
    grad_first_act = lax.dot_general(
        grad_second_full, p2_w, (((1,), (1,)), ((), ())), preferred_element_type=jnp.float32
    )
    grad_first_pre = act_grad(jax.nn.silu, first_pre, grad_first_act).astype(jnp.bfloat16)
    grad_p1_b = jnp.sum(grad_first_pre.astype(jnp.float32), axis=0)
    grad_p1_w = contract_rows(input_full, grad_first_pre)
    grad_sent = scatter_backward(grad_first_pre, p1_w, local_rows)
    return (
        loss_local,
        grad_sent,
        (grad_p1_w, grad_p1_b, grad_p2_w, grad_p2_b, grad_p3_w, grad_p3_b),
    )


def per_device(
    block_eight_input,
    cond,
    image_slot_index,
    targets,
    cot,
    ada_w,
    ada_b,
    query_key_value_weight,
    query_value_bias,
    attention_output_weight,
    attention_output_bias,
    hidden_weight,
    hidden_bias,
    output_weight_mlp,
    output_bias_mlp,
    p1_w,
    p1_b,
    p2_w,
    p2_b,
    p3_w,
    p3_b,
):
    section_index = lax.axis_index("section")
    is_first = section_index == 0
    tensor_index = lax.axis_index("tensor")
    local_pos = block_eight_input.shape[0]
    replica_rows = block_eight_input.shape[1]
    width = block_eight_input.shape[2]
    rows_micro = replica_rows // MICRO
    local_rows = local_pos * rows_micro
    total_token_count = ROW_LENGTH * replica_rows * lax.axis_size("dp")
    weights = (
        query_key_value_weight[0],
        query_value_bias[0],
        attention_output_weight[0],
        attention_output_bias[0],
        hidden_weight[0],
        hidden_bias[0],
        output_weight_mlp[0],
        output_bias_mlp[0],
    )
    cond_act = jax.nn.silu(cond.astype(jnp.float32)).astype(jnp.bfloat16)
    mod_local = jnp.einsum(
        "rsd,dc->rsc", cond_act, ada_w[0], preferred_element_type=jnp.float32
    ) + ada_b[0].astype(jnp.float32)
    mod_full = lax.all_gather(mod_local, "tensor", axis=2, tiled=True)
    slot_ids = jnp.arange(IMAGES_PER_ROW, dtype=jnp.int32)
    seg_local = lax.dynamic_slice_in_dim(image_slot_index, tensor_index * local_pos, local_pos, 1)
    onehot_local = (seg_local[:, :, None] == slot_ids).astype(jnp.float32)
    tok_mod = jnp.einsum("rps,rsc->prc", onehot_local, mod_full, precision=highest)
    incoming = jnp.zeros((local_rows, width), jnp.float32)
    inputs_seen = []
    outputs_seen = []
    kept_seen = []
    for step_index in range(MICRO + 1):
        micro_index = jnp.clip(step_index - section_index, 0, MICRO - 1)
        block_input = jnp.where(
            is_first,
            take_rows(block_eight_input, micro_index, rows_micro).astype(jnp.float32),
            incoming,
        )
        block_out, kept = forward_block(
            block_input,
            take_rows(tok_mod, micro_index, rows_micro),
            same_of(image_slot_index, micro_index, rows_micro),
            weights,
        )
        inputs_seen.append(block_input)
        outputs_seen.append(block_out)
        kept_seen.append(kept)
        if step_index < MICRO:
            incoming = from_behind(block_out.astype(jnp.bfloat16), "section", 1).astype(jnp.float32)
    forwarded_rows = jnp.where(is_first, outputs_seen[0], inputs_seen[MICRO]).astype(jnp.bfloat16)
    target_cols = (
        lax.dynamic_slice_in_dim(targets, section_index * rows_micro, rows_micro, 1)
        .astype(jnp.float32)
        .reshape(-1, targets.shape[2])
    )
    loss_local, grad_sent, proj_grads = align_pass(
        forwarded_rows, target_cols, (p1_w, p1_b, p2_w, p2_b, p3_w, p3_b), total_token_count
    )
    incoming_grad = jnp.zeros((local_rows, width), jnp.float32)
    mod_grad = jnp.zeros((replica_rows, IMAGES_PER_ROW, mod_full.shape[2]), jnp.float32)
    grads_sum = None
    recorded = []
    for step_index in range(MICRO + 1):
        raw_index = step_index - 1 + section_index
        is_valid = (raw_index >= 0) & (raw_index < MICRO)
        micro_index = jnp.clip(raw_index, 0, MICRO - 1)
        before = max(step_index - 1, 0)
        after = min(step_index + 1, MICRO)
        apply_modulation = take_rows(tok_mod, micro_index, rows_micro)
        same_image_mask = same_of(image_slot_index, micro_index, rows_micro)
        block_input = jnp.where(is_first, inputs_seen[before], inputs_seen[after])
        unused_out, kept = forward_block(block_input, apply_modulation, same_image_mask, weights)
        added = grad_sent if step_index == 1 else jnp.zeros_like(grad_sent)
        grad_out = jnp.where(
            is_first,
            incoming_grad + added,
            take_rows(cot, micro_index, rows_micro).astype(jnp.float32),
        )
        grad_in, grads, grad_modulate = backward_block(
            grad_out, apply_modulation, same_image_mask, weights, kept
        )
        recorded.append(grad_in)
        if step_index < MICRO:
            incoming_grad = from_behind(
                jnp.where(is_first, grad_in, grad_in + added), "section", -1
            )
        masked_grads = jax.tree.map(lambda term: jnp.where(is_valid, term, 0.0), grads)
        if grads_sum is None:
            grads_sum = masked_grads
        else:
            grads_sum = jax.tree.map(lambda total, term: total + term, grads_sum, masked_grads)
        onehot_micro = lax.dynamic_slice_in_dim(
            onehot_local, micro_index * rows_micro, rows_micro, 0
        )
        contrib = jnp.einsum(
            "rps,prc->rsc",
            onehot_micro,
            grad_modulate.reshape(local_pos, rows_micro, -1),
            precision=highest,
        )
        current = lax.dynamic_slice_in_dim(mod_grad, micro_index * rows_micro, rows_micro, 0)
        mod_grad = lax.dynamic_update_slice_in_dim(
            mod_grad, current + jnp.where(is_valid, contrib, 0.0), micro_index * rows_micro, 0
        )
    mod_grad_local = lax.psum_scatter(mod_grad, "tensor", scatter_dimension=2, tiled=True)
    grad_ada_w = jnp.einsum(
        "rsd,rsc->dc", cond_act.astype(jnp.float32), mod_grad_local, precision=highest
    )
    grad_ada_b = jnp.sum(mod_grad_local, axis=(0, 1))
    (
        grad_qkv_w,
        grad_qv_b,
        grad_out_w,
        grad_out_b,
        grad_fc1_w,
        grad_fc1_b,
        grad_fc2_w,
        grad_fc2_b,
    ) = grads_sum
    red_qkv_w, red_out_w, red_fc1_w, red_fc2_w, red_ada_w = (
        lax.psum_scatter(grad_qkv_w, "dp", scatter_dimension=0, tiled=True),
        lax.psum_scatter(grad_out_w, "dp", scatter_dimension=1, tiled=True),
        lax.psum_scatter(grad_fc1_w, "dp", scatter_dimension=0, tiled=True),
        lax.psum_scatter(grad_fc2_w, "dp", scatter_dimension=1, tiled=True),
        lax.psum_scatter(grad_ada_w, "dp", scatter_dimension=0, tiled=True),
    )
    red_qv_b, red_out_b, red_fc1_b, red_fc2_b, red_ada_b = lax.psum(
        (grad_qv_b, grad_out_b, grad_fc1_b, grad_fc2_b, grad_ada_b), "dp"
    )
    grad_p1_w, grad_p1_b, grad_p2_w, grad_p2_b, grad_p3_w, grad_p3_b = proj_grads
    red_p1_w, red_p2_w, red_p3_w = (
        lax.psum_scatter(grad_p1_w, ("section", "dp"), scatter_dimension=0, tiled=True),
        lax.psum_scatter(grad_p2_w, ("section", "dp"), scatter_dimension=1, tiled=True),
        lax.psum_scatter(grad_p3_w, ("section", "dp"), scatter_dimension=0, tiled=True),
    )
    loss_total, red_p1_b, red_p2_b, red_p3_b = lax.psum(
        (loss_local, grad_p1_b, grad_p2_b, grad_p3_b), ("section", "dp")
    )
    align_loss = -0.5 * loss_total / total_token_count
    out_parts = []
    grad_parts = []
    for micro_number in range(MICRO):
        out_parts.append(
            jnp.where(is_first, outputs_seen[micro_number], outputs_seen[micro_number + 1]).reshape(
                local_pos, rows_micro, width
            )
        )
        grad_parts.append(
            jnp.where(is_first, recorded[micro_number + 1], recorded[micro_number]).reshape(
                local_pos, rows_micro, width
            )
        )
    section_out = jnp.concatenate(out_parts, axis=1).astype(jnp.bfloat16)[None]
    section_grad = jnp.concatenate(grad_parts, axis=1)[None]
    return (
        section_out,
        section_grad,
        align_loss,
        red_ada_w[None],
        red_ada_b[None],
        red_qkv_w[None],
        red_qv_b[None],
        red_out_w[None],
        red_out_b[None],
        red_fc1_w[None],
        red_fc1_b[None],
        red_fc2_w[None],
        red_fc2_b[None],
        red_p1_w,
        red_p1_b,
        red_p2_w,
        red_p2_b,
        red_p3_w,
        red_p3_b,
    )


def solution(mesh):
    in_specs = (
        P("tensor", "dp", None),
        P("dp", None, None),
        P("dp", None),
        P(None, "dp", "tensor"),
        P("tensor", "dp", None),
        P("section", None, "tensor"),
        P("section", "tensor"),
        P("section", None, None, "tensor"),
        P("section", None, "tensor"),
        P("section", "tensor", None),
        P("section", None),
        P("section", None, "tensor"),
        P("section", "tensor"),
        P("section", "tensor", None),
        P("section", None),
        P(None, "tensor"),
        P("tensor"),
        P("tensor", None),
        P(),
        P(None, "tensor"),
        P("tensor"),
    )
    out_specs = (
        P("section", "tensor", "dp", None),
        P("section", "tensor", "dp", None),
        P(),
        P("section", "dp", "tensor"),
        P("section", "tensor"),
        P("section", "dp", None, "tensor"),
        P("section", None, "tensor"),
        P("section", "tensor", "dp"),
        P("section", None),
        P("section", "dp", "tensor"),
        P("section", "tensor"),
        P("section", "tensor", "dp"),
        P("section", None),
        P(("section", "dp"), "tensor"),
        P("tensor"),
        P("tensor", ("section", "dp")),
        P(),
        P(("section", "dp"), "tensor"),
        P("tensor"),
    )
    return jax.shard_map(
        per_device, mesh=mesh, in_specs=in_specs, out_specs=out_specs, check_vma=False
    )
```

profile of v0, /device:TPU:0, one launch (start us, length us, event | category | flops | bytes accessed | tf_op | source)
XLA Modules:
  0.0 2473.7 jit_solution(11387928378538062027)
XLA Ops:
  19.7 259.6 %all_gather.66 = f32[4,3,6912]{1,0,2:T(4,128)} all-gather(f32[4,3,1728]{1,0,2:T(4,128)} %copy.201), channel_id=1, replica_groups=mesh['section'=2,'dp'=4,'tensor'=4] {'tensor'}, dimensions={2}, use_global_device_ids=true | all-gather | bytes 414720 | tf_op jit(solution)/shard_map/all_gather | solution.py:402
  279.3 12.1 fusion
  306.3 20.3 all_gather.67
  349.0 38.1 %reduce-scatter.37.cloned.1.call-done = f32[96,1152]{1,0:T(8,128)} async-done(((f32[384,1152]{1,0:T(8,128)}), f32[96,1152]{1,0:T(8,128)}) %reduce-scatter.37.cloned.1.call-update) | async-done | bytes 442384 | tf_op jit(solution)/shard_map/reduce_scatter | solution.py:64
  390.6 19.4 all_gather.68
  440.6 13.4 reduce-scatter.39.cloned.1.call-done
  466.4 18.9 all_gather.73
  493.4 18.3 all_gather.69
  562.4 35.6 %reduce-scatter.49.cloned.1.call-done = f32[96,1152]{1,0:T(8,128)} async-done(((f32[384,1152]{1,0:T(8,128)}), f32[96,1152]{1,0:T(8,128)}) %reduce-scatter.49.cloned.1.call-update) | async-done | bytes 442384 | tf_op jit(solution)/shard_map/reduce_scatter | solution.py:64
  601.4 19.0 all_gather.74
  620.4 19.8 all_gather.75
  648.8 37.6 %reduce-scatter.51.cloned.1.call-done = f32[96,1152]{1,0:T(8,128)} async-done(((f32[384,1152]{1,0:T(8,128)}), f32[96,1152]{1,0:T(8,128)}) %reduce-scatter.51.cloned.1.call-update) | async-done | bytes 442384 | tf_op jit(solution)/shard_map/reduce_scatter | solution.py:79
  690.5 18.9 all_gather.76
  761.7 22.4 reduce-scatter.53.cloned.1.call-done
  788.8 35.7 %reduce-scatter.41.cloned.1.call-done = f32[96,1152]{1,0:T(8,128)} async-done(((f32[384,1152]{1,0:T(8,128)}), f32[96,1152]{1,0:T(8,128)}) %reduce-scatter.41.cloned.1.call-update) | async-done | bytes 442384 | tf_op jit(solution)/shard_map/reduce_scatter | solution.py:64
  829.1 19.4 all_gather.70
  854.4 38.0 %reduce-scatter.43.cloned.1.call-done = f32[96,1152]{1,0:T(8,128)} async-done(((f32[384,1152]{1,0:T(8,128)}), f32[96,1152]{1,0:T(8,128)}) %reduce-scatter.43.cloned.1.call-update) | async-done | bytes 442384 | tf_op jit(solution)/shard_map/reduce_scatter | solution.py:64
  906.3 18.8 all_gather.77
  931.0 59.9 %reduce-scatter.55.cloned.1.call-done = f32[96,2048]{1,0:T(8,128)} async-done(((f32[384,2048]{1,0:T(8,128)}), f32[96,2048]{1,0:T(8,128)}) %reduce-scatter.55.cloned.1.call-update) | async-done | bytes 786448 | tf_op jit(solution)/shard_map/reduce_scatter | solution.py:64
  1000.4 29.8 %all-gather.3.cloned.1.call-done = bf16[384,2048]{1,0:T(8,128)(2,1)} async-done(((bf16[96,2048]{1,0:T(8,128)(2,1)}), bf16[384,2048]{1,0:T(8,128)(2,1)}) %all-gather.3.cloned.1.call-update) | async-done | bytes 1572880 | tf_op jit(solution)/shard_map/all_gather | solution.py:52
  1085.4 33.1 %all_gather.71 = bf16[384,1152]{1,0:T(8,128)(2,1)S(1)} all-gather(bf16[96,1152]{1,0:T(8,128)(2,1)S(1)} %get-tuple-element.174), channel_id=1, replica_groups=mesh['section'=2,'dp'=4,'tensor'=4] {'tensor'}, dimensions={0}, use_global_device_ids=true | all-gather | bytes 1105920 | tf_op jit(solution)/shard_map/all_gather | solution.py:52
  1133.5 18.7 all_gather.80
  1166.5 18.7 all_gather.84
  1266.4 39.8 %reduce-scatter.61.cloned.1.call-done = f32[96,1152]{1,0:T(8,128)} async-done(((f32[384,1152]{1,0:T(8,128)}), f32[96,1152]{1,0:T(8,128)}) %reduce-scatter.61.cloned.1.call-update) | async-done | bytes 442384 | tf_op jit(solution)/shard_map/reduce_scatter | solution.py:64
  1310.4 36.2 %reduce-scatter.59.cloned.1.call-done = f32[96,1152]{1,0:T(8,128)} async-done(((f32[384,1152]{1,0:T(8,128)}), f32[96,1152]{1,0:T(8,128)}) %reduce-scatter.59.cloned.1.call-update) | async-done | bytes 442384 | tf_op jit(solution)/shard_map/reduce_scatter | solution.py:79
  1349.5 19.1 all_gather.81
  1368.6 19.3 all_gather.82
  1396.5 37.7 %reduce-scatter.63.cloned.1.call-done = f32[96,1152]{1,0:T(8,128)} async-done(((f32[384,1152]{1,0:T(8,128)}), f32[96,1152]{1,0:T(8,128)}) %reduce-scatter.63.cloned.1.call-update) | async-done | bytes 442384 | tf_op jit(solution)/shard_map/reduce_scatter | solution.py:79
  1438.4 19.2 all_gather.83
  1494.0 35.9 %reduce-scatter.65.cloned.1.call-done = f32[96,1152]{1,0:T(8,128)} async-done(((f32[384,1152]{1,0:T(8,128)}), f32[96,1152]{1,0:T(8,128)}) %reduce-scatter.65.cloned.1.call-update) | async-done | bytes 442384 | tf_op jit(solution)/shard_map/reduce_scatter | solution.py:79
  1535.7 12.1 collective-permute-done.3
  1548.8 19.6 all_gather.85
  1568.4 18.1 all_gather.86
  1595.1 37.2 %reduce-scatter.69.cloned.1.call-done = f32[96,1152]{1,0:T(8,128)} async-done(((f32[384,1152]{1,0:T(8,128)}), f32[96,1152]{1,0:T(8,128)}) %reduce-scatter.69.cloned.1.call-update) | async-done | bytes 442384 | tf_op jit(solution)/shard_map/reduce_scatter | solution.py:79
  1636.5 19.4 all_gather.87
  1732.8 35.9 %reduce-scatter.45.cloned.1.call-done = f32[96,1152]{1,0:T(8,128)} async-done(((f32[384,1152]{1,0:T(8,128)}), f32[96,1152]{1,0:T(8,128)}) %reduce-scatter.45.cloned.1.call-update) | async-done | bytes 442384 | tf_op jit(solution)/shard_map/reduce_scatter | solution.py:64
  1775.7 32.7 %reduce-scatter.73.cloned.1.call-done = f32[96,1152]{1,0:T(8,128)} async-done(((f32[384,1152]{1,0:T(8,128)}), f32[96,1152]{1,0:T(8,128)}) %reduce-scatter.73.cloned.1.call-update) | async-done | bytes 442384 | tf_op jit(solution)/shard_map/reduce_scatter | solution.py:64
  1808.4 39.9 %reduce-scatter.75.cloned.1.call-done = f32[96,1152]{1,0:T(8,128)} async-done(((f32[384,1152]{1,0:T(8,128)}), f32[96,1152]{1,0:T(8,128)}) %reduce-scatter.75.cloned.1.call-update) | async-done | bytes 442384 | tf_op jit(solution)/shard_map/reduce_scatter | solution.py:64
  1848.3 40.0 %reduce-scatter.77.cloned.1.call-done = f32[96,1152]{1,0:T(8,128)} async-done(((f32[384,1152]{1,0:T(8,128)}), f32[96,1152]{1,0:T(8,128)}) %reduce-scatter.77.cloned.1.call-update) | async-done | bytes 442384 | tf_op jit(solution)/shard_map/reduce_scatter | solution.py:64
  1959.5 34.0 %all_gather.72 = bf16[384,1152]{1,0:T(8,128)(2,1)} all-gather(bf16[96,1152]{1,0:T(8,128)(2,1)S(1)} %fusion.200), channel_id=1, replica_groups=mesh['section'=2,'dp'=4,'tensor'=4] {'tensor'}, dimensions={0}, use_global_device_ids=true | all-gather | bytes 1105920 | tf_op jit(solution)/shard_map/all_gather | solution.py:52
  2054.7 22.9 all-reduce
  2097.0 14.4 bitcast_reduce_fusion
  2140.4 39.0 %reduce-scatter.89.cloned.1.call-done = f32[256,192]{0,1:T(8,128)} async-done(((f32[2048,192]{0,1:T(8,128)}), f32[256,192]{0,1:T(8,128)}) %reduce-scatter.89.cloned.1.call-update) | async-done | bytes 196624 | tf_op jit(solution)/shard_map/reduce_scatter | solution.py:513
  2179.4 46.8 %reduce-scatter.85.cloned.1.call-done = f32[144,512]{1,0:T(8,128)} async-done(((f32[1152,512]{1,0:T(8,128)}), f32[144,512]{1,0:T(8,128)}) %reduce-scatter.85.cloned.1.call-update) | async-done | bytes 294928 | tf_op jit(solution)/shard_map/reduce_scatter | solution.py:511
  2226.2 55.3 %reduce-scatter.87.cloned.1.call-done = f32[512,256]{1,0:T(8,128)} async-done(((f32[512,2048]{1,0:T(8,128)}), f32[512,256]{1,0:T(8,128)}) %reduce-scatter.87.cloned.1.call-update) | async-done | bytes 524304 | tf_op jit(solution)/shard_map/reduce_scatter | solution.py:512
  2281.5 55.0 %reduce-scatter.83.cloned.1.call-done = f32[288,1152]{1,0:T(8,128)} async-done(((f32[1152,1152]{1,0:T(8,128)}), f32[288,1152]{1,0:T(8,128)}) %reduce-scatter.83.cloned.1.call-update) | async-done | bytes 1327120 | tf_op jit(solution)/shard_map/reduce_scatter | solution.py:502
  2336.5 55.0 %reduce-scatter.81.cloned.1.call-done = f32[288,3,288]{2,0,1:T(8,128)} async-done(((f32[1152,3,288]{2,0,1:T(8,128)}), f32[288,3,288]{2,0,1:T(8,128)}) %reduce-scatter.81.cloned.1.call-update) | async-done | bytes 995344 | tf_op jit(solution)/shard_map/reduce_scatter | solution.py:500
  2391.5 74.3 %reduce-scatter.79.cloned.1.call-done = f32[288,1728]{1,0:T(8,128)} async-done(((f32[1152,1728]{1,0:T(8,128)}), f32[288,1728]{1,0:T(8,128)}) %reduce-scatter.79.cloned.1.call-update) | async-done | bytes 1990672 | tf_op jit(solution)/shard_map/reduce_scatter | solution.py:504
  (874 shorter events, 771.1 us)
Async XLA Ops:
  7.2 402.8 %copy-start = (bf16[1,1152,1152]{2,1,0:T(8,128)(2,1)S(1)}, bf16[1,1152,1152]{2,1,0:T(8,128)(2,1)}, u32[]{:S(2)}) copy-start(bf16[1,1152,1152]{2,1,0:T(8,128)(2,1)} %param.34) | copy-start | bytes 7962628
  7.2 379.9 %reduce-scatter.37.cloned.1.call-start = ((), (), s32[]{:S(2)}) async-start(), calls=%async_computation.30 | async-start | bytes 2211840 | tf_op jit(solution)/shard_map/reduce_scatter | solution.py:64
  13.1 291.8 %copy-start.26 = (f32[96,1152]{1,0:T(8,128)}, f32[96,1152]{1,0:T(8,128)S(1)}, u32[]{:S(2)}) copy-start(f32[96,1152]{1,0:T(8,128)S(1)} %select_n.302) | copy-start | bytes 1327108
  19.7 259.6 %copy-start.136 = (s32[4,192]{1,0:T(4,128)S(1)}, s32[4,192]{1,0:T(4,128)}, u32[]{:S(2)}) copy-start(s32[4,192]{1,0:T(4,128)} %param.23) | copy-start | bytes 9220
  348.9 105.1 %reduce-scatter.39.cloned.1.call-start = ((), (), s32[]{:S(2)}) async-start(), calls=%async_computation.31 | async-start | bytes 2211840 | tf_op jit(solution)/shard_map/reduce_scatter | solution.py:64
  349.0 61.1 %copy-start.159 = (f32[1152]{0:T(1024)}, f32[1152]{0:T(1024)S(1)}, u32[]{:S(2)}) copy-start(f32[1152]{0:T(1024)S(1)} %convert_reduce_fusion.20) | copy-start | bytes 13828
  416.0 182.0 %reduce-scatter.49.cloned.1.call-start = ((), (), s32[]{:S(2)}) async-start(), calls=%async_computation.36 | async-start | bytes 2211840 | tf_op jit(solution)/shard_map/reduce_scatter | solution.py:64
  455.4 7.9 collective-permute-start
  558.2 128.2 %reduce-scatter.51.cloned.1.call-start = ((), (), s32[]{:S(2)}) async-start(), calls=%async_computation.37 | async-start | bytes 2211840 | tf_op jit(solution)/shard_map/reduce_scatter | solution.py:79
  648.7 135.4 %reduce-scatter.53.cloned.1.call-start = ((), (), s32[]{:S(2)}) async-start(), calls=%async_computation.38 | async-start | bytes 2211840 | tf_op jit(solution)/shard_map/reduce_scatter | solution.py:79
  746.1 78.4 %reduce-scatter.41.cloned.1.call-start = ((), (), s32[]{:S(2)}) async-start(), calls=%async_computation.32 | async-start | bytes 2211840 | tf_op jit(solution)/shard_map/reduce_scatter | solution.py:64
  761.6 130.8 %reduce-scatter.43.cloned.1.call-start = ((), (), s32[]{:S(2)}) async-start(), calls=%async_computation.33 | async-start | bytes 2211840 | tf_op jit(solution)/shard_map/reduce_scatter | solution.py:64
  854.4 136.5 %reduce-scatter.55.cloned.1.call-start = ((), (), s32[]{:S(2)}) async-start(), calls=%async_computation.39 | async-start | bytes 3932160 | tf_op jit(solution)/shard_map/reduce_scatter | solution.py:64
  894.6 8.2 collective-permute-start.1
  930.3 62.7 %copy-start.193 = (bf16[192]{0:T(256)(128)(2,1)S(1)}, bf16[192]{0:T(256)(128)(2,1)}, u32[]{:S(2)}) copy-start(bf16[192]{0:T(256)(128)(2,1)} %param.41) | copy-start | bytes 1156
  930.3 99.9 %all-gather.3.cloned.1.call-start = ((), (), s32[]{:S(2)}) async-start(), calls=%async_computation.40 | async-start | bytes 1966080 | tf_op jit(solution)/shard_map/all_gather | solution.py:52
  993.0 192.3 %reduce-scatter.57.cloned.1.call-start = ((), (), s32[]{:S(2)}) async-start(), calls=%async_computation.41 | async-start | bytes 3932160 | tf_op jit(solution)/shard_map/reduce_scatter | solution.py:79
  1049.5 199.6 %all-gather.5.cloned.1.call-start = ((), (), s32[]{:S(2)}) async-start(), calls=%async_computation.42 | async-start | bytes 1966080 | tf_op jit(solution)/shard_map/all_gather | solution.py:56
  1187.7 78.7 %reduce-scatter.67.cloned.1.call-start = ((), (), s32[]{:S(2)}) async-start(), calls=%async_computation.47 | async-start | bytes 2211840 | tf_op jit(solution)/shard_map/reduce_scatter | solution.py:64
  1228.3 77.9 %reduce-scatter.61.cloned.1.call-start = ((), (), s32[]{:S(2)}) async-start(), calls=%async_computation.44 | async-start | bytes 2211840 | tf_op jit(solution)/shard_map/reduce_scatter | solution.py:64
  1249.0 97.6 %reduce-scatter.59.cloned.1.call-start = ((), (), s32[]{:S(2)}) async-start(), calls=%async_computation.43 | async-start | bytes 2211840 | tf_op jit(solution)/shard_map/reduce_scatter | solution.py:79
  1255.9 178.3 %reduce-scatter.63.cloned.1.call-start = ((), (), s32[]{:S(2)}) async-start(), calls=%async_computation.45 | async-start | bytes 2211840 | tf_op jit(solution)/shard_map/reduce_scatter | solution.py:79
  1260.5 49.9 %collective-permute-start.2 = (f32[96,1152]{1,0:T(8,128)}, f32[96,1152]{1,0:T(8,128)}, u32[]{:S(2)}, u32[]{:S(2)}) collective-permute-start(f32[96,1152]{1,0:T(8,128)} %get-tuple-element.168), channel_id=1, source_target_pairs={{16,0},{17,1},{18,2},{19,3},{20,4},{21,5},{22,6},{23,7},{24,8},{25... | collective-permute-start | bytes 1327112 | tf_op jit(solution)/shard_map/ppermute | solution.py:21
  1309.4 126.4 %copy-start.148 = (f32[96]{0:T(128)}, f32[96]{0:T(128)S(1)}, u32[]{:S(2)}) copy-start(f32[96]{0:T(128)S(1)} %broadcast_multiply_fusion.11) | copy-start | bytes 1156
  1310.4 125.4 %copy-start.155 = (f32[96]{0:T(128)}, f32[96]{0:T(128)S(1)}, u32[]{:S(2)}) copy-start(f32[96]{0:T(128)S(1)} %add_rsqrt_fusion.5) | copy-start | bytes 1156
  1346.6 42.2 %copy-start.190 = (bf16[1,1152,1152]{2,1,0:T(8,128)(2,1)S(1)}, bf16[1,1152,1152]{2,1,0:T(8,128)(2,1)}, u32[]{:S(2)}) copy-start(bf16[1,1152,1152]{2,1,0:T(8,128)(2,1)} %param.32) | copy-start | bytes 7962628
  1396.5 133.4 %reduce-scatter.65.cloned.1.call-start = ((), (), s32[]{:S(2)}) async-start(), calls=%async_computation.46 | async-start | bytes 2211840 | tf_op jit(solution)/shard_map/reduce_scatter | solution.py:79
  1491.9 140.4 %reduce-scatter.69.cloned.1.call-start = ((), (), s32[]{:S(2)}) async-start(), calls=%async_computation.48 | async-start | bytes 2211840 | tf_op jit(solution)/shard_map/reduce_scatter | solution.py:79
  1534.0 13.8 collective-permute-start.3
  1535.4 98.4 %copy-start.150 = (f32[96]{0:T(128)}, f32[96]{0:T(128)S(1)}, u32[]{:S(2)}) copy-start(f32[96]{0:T(128)S(1)} %broadcast_multiply_fusion.5) | copy-start | bytes 1156
  1535.7 98.2 %copy-start.157 = (f32[96]{0:T(128)}, f32[96]{0:T(128)S(1)}, u32[]{:S(2)}) copy-start(f32[96]{0:T(128)S(1)} %add_rsqrt_fusion.3) | copy-start | bytes 1156
  1595.1 133.1 %reduce-scatter.71.cloned.1.call-start = ((), (), s32[]{:S(2)}) async-start(), calls=%async_computation.49 | async-start | bytes 2211840 | tf_op jit(solution)/shard_map/reduce_scatter | solution.py:79
  1690.2 78.5 %reduce-scatter.45.cloned.1.call-start = ((), (), s32[]{:S(2)}) async-start(), calls=%async_computation.34 | async-start | bytes 2211840 | tf_op jit(solution)/shard_map/reduce_scatter | solution.py:64
  1704.0 104.5 %reduce-scatter.73.cloned.1.call-start = ((), (), s32[]{:S(2)}) async-start(), calls=%async_computation.50 | async-start | bytes 2211840 | tf_op jit(solution)/shard_map/reduce_scatter | solution.py:64
  1708.5 139.8 %reduce-scatter.75.cloned.1.call-start = ((), (), s32[]{:S(2)}) async-start(), calls=%async_computation.51 | async-start | bytes 2211840 | tf_op jit(solution)/shard_map/reduce_scatter | solution.py:64
  1712.9 175.3 %reduce-scatter.77.cloned.1.call-start = ((), (), s32[]{:S(2)}) async-start(), calls=%async_computation.52 | async-start | bytes 2211840 | tf_op jit(solution)/shard_map/reduce_scatter | solution.py:64
  1719.4 311.3 %reduce-scatter.91.cloned.1.call-start = ((), (), s32[]{:S(2)}) async-start(), calls=%async_computation.59 | async-start | bytes 4423680
  1773.0 115.2 %copy-start.48 = (f32[96,1152]{1,0:T(8,128)S(1)}, f32[96,1152]{1,0:T(8,128)}, u32[]{:S(2)}) copy-start(f32[96,1152]{1,0:T(8,128)} %select_n.315) | copy-start | bytes 1327108
  1773.0 115.2 %copy-start.52 = (f32[96,1152]{1,0:T(8,128)S(1)}, f32[96,1152]{1,0:T(8,128)}, u32[]{:S(2)}) copy-start(f32[96,1152]{1,0:T(8,128)} %get-tuple-element.122) | copy-start | bytes 1327108
  1930.4 162.0 %reduce-scatter.93.cloned.1.call-start = ((), (), s32[]{:S(2)}) async-start(), calls=%async_computation.60 | async-start | bytes 2211840
  1939.2 183.9 %reduce-scatter.95.cloned.1.call-start = ((), (), s32[]{:S(2)}) async-start(), calls=%async_computation.61 | async-start | bytes 6635520
  1956.1 181.7 %reduce-scatter.47.cloned.1.call-start = ((), (), s32[]{:S(2)}) async-start(), calls=%async_computation.35 | async-start | bytes 2211840 | tf_op jit(solution)/shard_map/reduce_scatter | solution.py:64
  1999.5 179.9 %reduce-scatter.89.cloned.1.call-start = ((), (), s32[]{:S(2)}) async-start(), calls=%async_computation.58 | async-start | bytes 1769472 | tf_op jit(solution)/shard_map/reduce_scatter | solution.py:513
  2002.9 223.4 %reduce-scatter.85.cloned.1.call-start = ((), (), s32[]{:S(2)}) async-start(), calls=%async_computation.56 | async-start | bytes 2654208 | tf_op jit(solution)/shard_map/reduce_scatter | solution.py:511
  2006.4 275.1 %reduce-scatter.87.cloned.1.call-start = ((), (), s32[]{:S(2)}) async-start(), calls=%async_computation.57 | async-start | bytes 4718592 | tf_op jit(solution)/shard_map/reduce_scatter | solution.py:512
  2012.0 324.5 %reduce-scatter.83.cloned.1.call-start = ((), (), s32[]{:S(2)}) async-start(), calls=%async_computation.55 | async-start | bytes 6635520 | tf_op jit(solution)/shard_map/reduce_scatter | solution.py:502
  2021.2 370.3 %reduce-scatter.81.cloned.1.call-start = ((), (), s32[]{:S(2)}) async-start(), calls=%async_computation.54 | async-start | bytes 6635520 | tf_op jit(solution)/shard_map/reduce_scatter | solution.py:500
  2030.5 435.4 %reduce-scatter.79.cloned.1.call-start = ((), (), s32[]{:S(2)}) async-start(), calls=%async_computation.53 | async-start | bytes 10321920 | tf_op jit(solution)/shard_map/reduce_scatter | solution.py:504
  (183 other events, 1338.5 us)
Sparse Core Ops, SparseCore 0:
  349.0 38.0 reduce-scatter.36
  416.1 37.8 reduce-scatter.38
  558.4 39.5 reduce-scatter.48
  648.9 37.5 reduce-scatter.50
  746.2 37.8 reduce-scatter.52
  787.0 37.4 reduce-scatter.40
  854.5 37.8 reduce-scatter.42
  930.4 60.3 reduce-scatter.54
  993.1 37.1 all-gather.2
  1049.6 72.6 reduce-scatter.56
  1187.8 36.5 all-gather.4
  1228.4 37.8 reduce-scatter.66
  1268.7 37.4 reduce-scatter.60
  1309.1 37.4 reduce-scatter.58
  1396.6 37.5 reduce-scatter.62
  1492.0 37.8 reduce-scatter.64
  1595.2 37.0 reduce-scatter.68
  1690.3 37.8 reduce-scatter.70
  1731.1 37.4 reduce-scatter.44
  1770.9 37.4 reduce-scatter.72
  1810.8 37.4 reduce-scatter.74
  1850.7 37.4 reduce-scatter.76
  1930.6 79.5 reduce-scatter.90
  2012.6 29.6 reduce-scatter.92
  2045.0 52.0 reduce-scatter.94
  2099.4 38.3 reduce-scatter.46
  2141.8 37.5 reduce-scatter.88
  2183.7 42.4 reduce-scatter.84
  2230.2 51.3 reduce-scatter.86
  2284.7 51.8 reduce-scatter.82
  2339.7 51.8 reduce-scatter.80
  2394.9 70.8 reduce-scatter.78
where the time goes:
time: 2490 us; the launch traced here: 2470 us
  waiting for transfers between devices  1010 us (41%)
  blocking collectives  696 us (28%)
  local copies, waits for them, and re-layouts  369 us (15%)
  matrix products  210 us (8%)
  other arithmetic  160 us (6%)
    reduce_scatter x13, waiting for transfers between devices, scatter_forward(): lax.psum_scatter(partial_term(jnp.int32(0), local_rows * lax.axis_size('t...  422 us
    all_gather x13, blocking collectives, gather_rows(): return lax.all_gather(source_rows, 'tensor', axis=0, tiled=True)  277 us
    all_gather x1, blocking collectives, per_device(): mod_full = lax.all_gather(mod_local, 'tensor', axis=2, tiled=True)  260 us
    reduce_scatter x8, waiting for transfers between devices, scatter_backward(): lax.psum_scatter(partial_term(jnp.int32(0), local_rows * lax.axis_size('t...  213 us
    all_gather x6, blocking collectives, gather_grads(): return lax.all_gather(source_rows, 'tensor', axis=0, tiled=True)  115 us
    reduce_scatter x1, waiting for transfers between devices, per_device(): lax.psum_scatter(grad_ada_w, 'dp', scatter_dimension=0, tiled=True)  74.3 us
    unnamed x401, local copies, waits for them, and re-layouts  73 us
    reduce_scatter x1, waiting for transfers between devices, per_device(): lax.psum_scatter(grad_p2_w, ('section', 'dp'), scatter_dimension=1, tiled...  55.3 us
  transfers between devices with their start and end apart: 36, of which 30 were waited for; matrix products, arithmetic and copies ran while one was open for 15% of the time, Pallas kernels for 0%

commit v1 on v0

v1 whole, which is shorter than its diff:
```python
import functools
import math

import jax
import jax.numpy as jnp
from jax import lax
from jax.experimental import pallas as pl
from jax.experimental.pallas import tpu as pltpu
from jax.sharding import PartitionSpec as P

HEAD_WIDTH = 72
HEAD_LANES = 128
IMAGES_PER_ROW = 3
NORM_EPS = 1e-06
COSINE_EPS = 1e-06
MASKED_SCORE = -1e30
HIGHEST = lax.Precision.HIGHEST
MESH = pl.DeviceIdType.MESH
F32 = jnp.float32
BF16 = jnp.bfloat16
NN = (((1,), (0,)), ((), ()))
NT = (((1,), (1,)), ((), ()))
TN = (((0,), (0,)), ((), ()))


def dot(left, right, form=NN):
    return lax.dot_general(left, right, form, preferred_element_type=F32)


def greet(count):
    me = lax.axis_index("tensor")
    barrier = pltpu.get_barrier_semaphore()
    for step in range(1, count):
        pl.semaphore_signal(
            barrier, inc=1, device_id={"tensor": lax.rem(me + step, count)}, device_id_type=MESH
        )
    pl.semaphore_wait(barrier, count - 1)


def own_rows(me, length):
    return pl.ds(pl.multiple_of(me * length, 16), length)


def start_gather(full, length, count, send_sem, recv_sem):
    me = lax.axis_index("tensor")
    copies = []
    for step in range(1, count):
        mine = full.at[:, own_rows(me, length)]
        copy = pltpu.make_async_remote_copy(
            src_ref=mine,
            dst_ref=mine,
            send_sem=send_sem.at[step - 1],
            recv_sem=recv_sem.at[step - 1],
            device_id={"tensor": lax.rem(me + step, count)},
            device_id_type=MESH,
        )
        copy.start()
        copies.append(copy)
    return copies


def wait_all(copies):
    for copy in copies:
        copy.wait()


def scatter_sum(partial, length, count, send_buf, recv_buf, send_sem, recv_sem):
    me = lax.axis_index("tensor")
    copies = []
    for step in range(1, count):
        peer = lax.rem(me + step, count)
        term = partial(own_rows(peer, length))
        send_buf[step - 1] = term.astype(BF16).reshape(send_buf.shape[1:])
        copy = pltpu.make_async_remote_copy(
            src_ref=send_buf.at[step - 1],
            dst_ref=recv_buf.at[step - 1],
            send_sem=send_sem.at[step - 1],
            recv_sem=recv_sem.at[step - 1],
            device_id={"tensor": peer},
            device_id_type=MESH,
        )
        copy.start()
        copies.append(copy)
    total = partial(own_rows(me, length))
    return copies, total


def finish_sum(copies, total, recv_buf):
    wait_all(copies)
    for step in range(recv_buf.shape[0]):
        total = total + recv_buf[step].reshape(total.shape).astype(F32)
    return total


def fetch(block, own_ref, other_ref, target, sem):
    mine = lax.axis_index("section") == block

    @pl.when(mine)
    def own_start():
        pltpu.make_async_copy(own_ref, target, sem).start()

    @pl.when(jnp.logical_not(mine))
    def other_start():
        pltpu.make_async_copy(other_ref, target, sem).start()

    return pltpu.make_async_copy(own_ref, target, sem)


def layer_norm(rows):
    centred = rows - jnp.mean(rows, axis=-1, keepdims=True)
    inverse = lax.rsqrt(jnp.mean(centred * centred, axis=-1, keepdims=True) + NORM_EPS)
    return centred * inverse, inverse


def norm_back(grad, normed, inverse):
    mean_grad = jnp.mean(grad, axis=-1, keepdims=True)
    mean_cross = jnp.mean(grad * normed, axis=-1, keepdims=True)
    return inverse * (grad - mean_grad - normed * mean_cross)


def token_mod(mod_ref, seg_ref, which):
    parts = []
    for row in range(seg_ref.shape[0]):
        seg = seg_ref[row]
        value = mod_ref[which, row, IMAGES_PER_ROW - 1 : IMAGES_PER_ROW, :]
        for slot in range(IMAGES_PER_ROW - 2, -1, -1):
            value = jnp.where(seg == slot, mod_ref[which, row, slot : slot + 1, :], value)
        parts.append(value)
    return jnp.concatenate(parts, axis=0)


def slot_sums(value, seg_ref, out_ref, which):
    length = seg_ref.shape[1]
    for row in range(seg_ref.shape[0]):
        seg = seg_ref[row]
        piece = value[row * length : (row + 1) * length]
        for slot in range(IMAGES_PER_ROW):
            out_ref[which, row, slot : slot + 1, :] = jnp.sum(
                jnp.where(seg == slot, piece, 0.0), axis=0, keepdims=True
            )


def flat(ref):
    return ref[...].reshape(-1, ref.shape[-1])


def spread_matrix(width):
    lanes = width // HEAD_WIDTH * HEAD_LANES
    source = lax.broadcasted_iota(jnp.int32, (width, lanes), 0)
    target = lax.broadcasted_iota(jnp.int32, (width, lanes), 1)
    within = target & (HEAD_LANES - 1)
    head = target >> (HEAD_LANES.bit_length() - 1)
    hit = (within < HEAD_WIDTH) & (source == head * HEAD_WIDTH + within)
    return jnp.where(hit, 1.0, 0.0).astype(BF16)


def gelu_tanh(pre):
    inner = math.sqrt(2.0 / math.pi) * (pre + 0.044715 * (pre * pre * pre))
    return 0.5 * pre * (1.0 + jnp.tanh(inner))


def gelu_slope(pre):
    scale = math.sqrt(2.0 / math.pi)
    square = pre * pre
    tanh = jnp.tanh(scale * (pre + 0.044715 * (pre * square)))
    return 0.5 * (1.0 + tanh) + 0.5 * pre * (1.0 - tanh * tanh) * scale * (
        1.0 + 3 * 0.044715 * square
    )


def attend_kernel(
    count, block,
    u_ref, mod_ref, seg_own, seg_col, seg_row, bias_ref, out_bias_ref, wqkv_own, wqkv_other, wo_own, wo_other,
    middle_ref, branch_ref, full_ref, q_ref, k_ref, v_ref, probs_ref, mixed_ref,
    full, wqkv, wo, mixed_wide, send_buf, recv_buf, w_sem, ag_send, ag_recv, rs_send, rs_recv,
):
    me = lax.axis_index("tensor")
    rows, length, width = u_ref.shape
    heads_width = wo.shape[0]
    heads = heads_width // HEAD_WIDTH
    load_qkv = fetch(block, wqkv_own, wqkv_other, wqkv, w_sem.at[0])
    load_out = fetch(block, wo_own, wo_other, wo, w_sem.at[1])
    u = flat(u_ref).astype(F32)
    normed, unused = layer_norm(u)
    attn_in = normed * (1.0 + token_mod(mod_ref, seg_own, 1)) + token_mod(mod_ref, seg_own, 0)
    full[:, own_rows(me, length), :] = attn_in.astype(BF16).reshape(rows, length, width)
    greet(count)
    gather = start_gather(full, length, count, ag_send, ag_recv)
    spread = spread_matrix(heads_width)
    load_qkv.wait()
    wait_all(gather)
    full_ref[...] = full[...]
    tokens = flat(full)
    for which, target in ((0, q_ref), (1, k_ref), (2, v_ref)):
        projected = dot(tokens, wqkv[which])
        if which != 1:
            projected = projected + bias_ref[which // 2 : which // 2 + 1, :]
        target[...] = dot(projected.astype(BF16), spread).astype(BF16).reshape(target.shape)

    def one_head(index, carry):
        row = index // heads
        head = lax.rem(index, heads)
        lanes = pl.ds(pl.multiple_of(head * HEAD_LANES, HEAD_LANES), HEAD_LANES)
        scores = dot(q_ref[row, :, lanes], k_ref[row, :, lanes], NT) * HEAD_WIDTH ** (-0.5)
        scores = jnp.where(seg_col[row] == seg_row[row], scores, MASKED_SCORE)
        raised = jnp.exp(scores - jnp.max(scores, axis=-1, keepdims=True))
        probs = raised / jnp.sum(raised, axis=-1, keepdims=True)
        probs_ref[index] = probs
        mixed_wide[row, :, lanes] = dot(probs.astype(BF16), v_ref[row, :, lanes]).astype(BF16)
        return carry

    lax.fori_loop(0, rows * heads, one_head, 0)
    mixed_ref[...] = dot(flat(mixed_wide), spread, NT).astype(BF16).reshape(mixed_ref.shape)
    load_out.wait()

    def partial(which_rows):
        return dot(mixed_ref[:, which_rows, :].reshape(rows * length, heads_width), wo[...])

    copies, total = scatter_sum(partial, length, count, send_buf, recv_buf, rs_send, rs_recv)
    branch = finish_sum(copies, total, recv_buf) + out_bias_ref[...]
    branch_ref[...] = branch.reshape(branch_ref.shape)
    middle = flat(u_ref).astype(F32) + token_mod(mod_ref, seg_own, 2) * branch
    middle_ref[...] = middle.reshape(middle_ref.shape)


def mlp_kernel(
    count, block,
    middle_ref, mod_ref, seg_own, hidden_bias_ref, out_bias_ref, w1_own, w1_other, w2_own, w2_other,
    out_ref, branch_ref, full_ref, pre_ref, act_ref,
    full, w1, w2, send_buf, recv_buf, w_sem, ag_send, ag_recv, rs_send, rs_recv,
):
    me = lax.axis_index("tensor")
    rows, length, width = middle_ref.shape
    load_one = fetch(block, w1_own, w1_other, w1, w_sem.at[0])
    load_two = fetch(block, w2_own, w2_other, w2, w_sem.at[1])
    normed, unused = layer_norm(flat(middle_ref))
    mlp_in = normed * (1.0 + token_mod(mod_ref, seg_own, 4)) + token_mod(mod_ref, seg_own, 3)
    full[:, own_rows(me, length), :] = mlp_in.astype(BF16).reshape(rows, length, width)
    greet(count)
    gather = start_gather(full, length, count, ag_send, ag_recv)
    load_one.wait()
    wait_all(gather)
    full_ref[...] = full[...]
    pre = dot(flat(full), w1[...]) + hidden_bias_ref[...]
    pre_ref[...] = pre.reshape(pre_ref.shape)
    act_ref[...] = gelu_tanh(pre).astype(BF16).reshape(act_ref.shape)
    load_two.wait()

    def partial(which_rows):
        return dot(act_ref[:, which_rows, :].reshape(rows * length, -1), w2[...])

    copies, total = scatter_sum(partial, length, count, send_buf, recv_buf, rs_send, rs_recv)
    branch = finish_sum(copies, total, recv_buf) + out_bias_ref[...]
    branch_ref[...] = branch.reshape(branch_ref.shape)
    out = flat(middle_ref) + token_mod(mod_ref, seg_own, 5) * branch
    out_ref[...] = out.astype(BF16).reshape(out_ref.shape)


def mlp_back_kernel(
    count, block,
    g_ref, middle_ref, branch_ref, mod_ref, seg_own, full_ref, pre_ref, act_ref, w1_own, w1_other, w2_own, w2_other,
    d_middle_ref, d_mod_ref, d_w1_ref, d_w2_ref, d_b1_ref, d_b2_ref,
    full, d_pre, w1, w2, send_buf, recv_buf, w_sem, ag_send, ag_recv, rs_send, rs_recv,
):
    me = lax.axis_index("tensor")
    rows, length, width = middle_ref.shape
    load_one = fetch(block, w1_own, w1_other, w1, w_sem.at[0])
    load_two = fetch(block, w2_own, w2_other, w2, w_sem.at[1])
    g = flat(g_ref).astype(F32)
    d_branch = (g * token_mod(mod_ref, seg_own, 5)).astype(BF16)
    full[:, own_rows(me, length), :] = d_branch.reshape(rows, length, width)
    greet(count)
    gather = start_gather(full, length, count, ag_send, ag_recv)
    slot_sums(g * flat(branch_ref), seg_own, d_mod_ref, 2)
    load_two.wait()
    wait_all(gather)
    d_act = dot(flat(full), w2[...], NT)
    d_pre[...] = (d_act * gelu_slope(flat(pre_ref))).astype(BF16).reshape(d_pre.shape)
    load_one.wait()

    def partial(which_rows):
        return dot(d_pre[:, which_rows, :].reshape(rows * length, -1), w1[...], NT)

    copies, total = scatter_sum(partial, length, count, send_buf, recv_buf, rs_send, rs_recv)
    d_b2_ref[...] = jnp.sum(flat(full).astype(F32), axis=0, keepdims=True)
    d_b1_ref[...] = jnp.sum(flat(d_pre).astype(F32), axis=0, keepdims=True)
    d_w2_ref[...] = dot(flat(full), flat(act_ref), TN).astype(BF16)
    d_w1_ref[...] = dot(flat(full_ref), flat(d_pre), TN).astype(BF16)
    d_in = finish_sum(copies, total, recv_buf)
    normed, inverse = layer_norm(flat(middle_ref))
    d_middle = flat(g_ref).astype(F32) + norm_back(
        d_in * (1.0 + token_mod(mod_ref, seg_own, 4)), normed, inverse
    )
    d_middle_ref[...] = d_middle.reshape(d_middle_ref.shape)
    slot_sums(d_in, seg_own, d_mod_ref, 0)
    slot_sums(d_in * normed, seg_own, d_mod_ref, 1)


def attend_back_kernel(
    count, block,
    d_middle_ref, u_ref, branch_ref, mod_ref, seg_own, full_ref, q_ref, k_ref, v_ref, probs_ref, mixed_ref,
    wqkv_own, wqkv_other, wo_own, wo_other,
    d_in_ref, d_mod_ref, d_wqkv_ref, d_wo_ref, d_bqv_ref, d_bo_ref,
    full, wide, narrow, wqkv, wo, send_buf, recv_buf, w_sem, ag_send, ag_recv, rs_send, rs_recv,
):
    me = lax.axis_index("tensor")
    rows, length, width = u_ref.shape
    heads_width = wo.shape[0]
    heads = heads_width // HEAD_WIDTH
    load_qkv = fetch(block, wqkv_own, wqkv_other, wqkv, w_sem.at[0])
    load_out = fetch(block, wo_own, wo_other, wo, w_sem.at[1])
    d_middle = flat(d_middle_ref)
    d_branch = (d_middle * token_mod(mod_ref, seg_own, 2)).astype(BF16)
    full[:, own_rows(me, length), :] = d_branch.reshape(rows, length, width)
    greet(count)
    gather = start_gather(full, length, count, ag_send, ag_recv)
    slot_sums(d_middle * flat(branch_ref), seg_own, d_mod_ref, 2)
    spread = spread_matrix(heads_width)
    load_out.wait()
    wait_all(gather)
    d_mixed = dot(flat(full), wo[...], NT).astype(BF16)
    wide[3] = dot(d_mixed, spread).astype(BF16).reshape(wide.shape[1:])

    def one_head(index, carry):
        row = index // heads
        head = lax.rem(index, heads)
        lanes = pl.ds(pl.multiple_of(head * HEAD_LANES, HEAD_LANES), HEAD_LANES)
        grad = wide[3, row, :, lanes]
        probs = probs_ref[index]
        d_probs = dot(grad, v_ref[row, :, lanes], NT)
        d_scores = (
            probs * (d_probs - jnp.sum(d_probs * probs, axis=-1, keepdims=True))
        ).astype(BF16)
        scale = HEAD_WIDTH ** (-0.5)
        wide[0, row, :, lanes] = (dot(d_scores, k_ref[row, :, lanes]) * scale).astype(BF16)
        wide[1, row, :, lanes] = (dot(d_scores, q_ref[row, :, lanes], TN) * scale).astype(BF16)
        wide[2, row, :, lanes] = dot(probs.astype(BF16), grad, TN).astype(BF16)
        return carry

    lax.fori_loop(0, rows * heads, one_head, 0)
    for which in range(3):
        narrow[which] = (
            dot(flat(wide.at[which]), spread, NT).astype(BF16).reshape(narrow.shape[1:])
        )
    load_qkv.wait()

    def partial(which_rows):
        total = dot(narrow[0, :, which_rows, :].reshape(rows * length, heads_width), wqkv[0], NT)
        for which in (1, 2):
            total = total + dot(
                narrow[which, :, which_rows, :].reshape(rows * length, heads_width), wqkv[which], NT
            )
        return total

    copies, total = scatter_sum(partial, length, count, send_buf, recv_buf, rs_send, rs_recv)
    d_bo_ref[...] = jnp.sum(flat(full).astype(F32), axis=0, keepdims=True)
    d_bqv_ref[0:1, :] = jnp.sum(flat(narrow.at[0]).astype(F32), axis=0, keepdims=True)
    d_bqv_ref[1:2, :] = jnp.sum(flat(narrow.at[2]).astype(F32), axis=0, keepdims=True)
    d_wo_ref[...] = dot(flat(full), flat(mixed_ref), TN).astype(BF16)
    for which in range(3):
        d_wqkv_ref[which] = dot(flat(full_ref), flat(narrow.at[which]), TN).astype(BF16)
    d_attn_in = finish_sum(copies, total, recv_buf)
    normed, inverse = layer_norm(flat(u_ref).astype(F32))
    d_in = flat(d_middle_ref) + norm_back(
        d_attn_in * (1.0 + token_mod(mod_ref, seg_own, 1)), normed, inverse
    )
    d_in_ref[...] = d_in.reshape(d_in_ref.shape)
    slot_sums(d_attn_in, seg_own, d_mod_ref, 0)
    slot_sums(d_attn_in * normed, seg_own, d_mod_ref, 1)


VMEM = pl.BlockSpec(memory_space=pltpu.VMEM)
ANY = pl.BlockSpec(memory_space=pl.ANY)


def call(kernel, number, inputs, specs, outs, scratch, flops):
    moved = sum(math.prod(one.shape) * one.dtype.itemsize for one in inputs)
    return pl.pallas_call(
        kernel,
        out_shape=[jax.ShapeDtypeStruct(shape, dtype) for shape, dtype in outs],
        in_specs=specs,
        out_specs=[VMEM] * len(outs),
        scratch_shapes=scratch,
        compiler_params=pltpu.CompilerParams(
            collective_id=number, has_side_effects=True, vmem_limit_bytes=52 * 2**20
        ),
        cost_estimate=pl.CostEstimate(flops=flops, bytes_accessed=moved, transcendentals=0),
    )(*inputs)


def exchange_scratch(count, rows, length, width):
    return [
        pltpu.VMEM((count - 1, rows, length, width), BF16),
        pltpu.VMEM((count - 1, rows, length, width), BF16),
    ]


def semaphores(count):
    return [pltpu.SemaphoreType.DMA((2,))] + [pltpu.SemaphoreType.DMA((count - 1,))] * 4


class Block:
    def __init__(self, number, count, mod, segs, biases, own, other):
        self.number, self.count, self.mod = number, count, mod
        self.seg_own, self.seg_col, self.seg_row = segs
        self.bias_qv, self.bias_out, self.bias_one, self.bias_two = biases
        self.own, self.other = own, other

    def pair(self, which):
        return [self.own[which], self.other[which]]

    def forward(self, u):
        rows, length, width = u.shape
        count = self.count
        positions = length * count
        heads_width = self.own["out"].shape[0]
        hidden = self.own["one"].shape[1]
        heads = heads_width // HEAD_WIDTH
        wide = (rows, positions, heads * HEAD_LANES)
        local, full = (rows, length, width), (rows, positions, width)
        tokens = rows * positions
        self.u = u
        inputs = [u, self.mod, self.seg_own, self.seg_col, self.seg_row, self.bias_qv, self.bias_out]
        inputs += self.pair("qkv") + self.pair("out")
        (
            self.middle, self.branch_one, self.attn_full, self.q, self.k, self.v, self.probs, self.mixed
        ) = call(
            functools.partial(attend_kernel, count, self.number),
            self.number * 4,
            inputs,
            [VMEM] * 7 + [ANY] * 4,
            [
                (local, F32), (local, F32), (full, BF16), (wide, BF16), (wide, BF16), (wide, BF16),
                ((rows * heads, positions, positions), F32), ((rows, positions, heads_width), BF16),
            ],
            [
                pltpu.VMEM(full, BF16),
                pltpu.VMEM(self.own["qkv"].shape, BF16),
                pltpu.VMEM(self.own["out"].shape, BF16),
                pltpu.VMEM(wide, BF16),
            ] + exchange_scratch(count, *local) + semaphores(count),
            2 * tokens * width * heads_width * 4,
        )
        inputs = [self.middle, self.mod, self.seg_own, self.bias_one, self.bias_two]
        inputs += self.pair("one") + self.pair("two")
        out, self.branch_two, self.mlp_full, self.pre, self.act = call(
            functools.partial(mlp_kernel, count, self.number),
            self.number * 4 + 1,
            inputs,
            [VMEM] * 5 + [ANY] * 4,
            [
                (local, BF16), (local, F32), (full, BF16),
                ((rows, positions, hidden), F32), ((rows, positions, hidden), BF16),
            ],
            [
                pltpu.VMEM(full, BF16),
                pltpu.VMEM(self.own["one"].shape, BF16),
                pltpu.VMEM(self.own["two"].shape, BF16),
            ] + exchange_scratch(count, *local) + semaphores(count),
            2 * tokens * width * hidden * 2,
        )
        return out

    def backward_mlp(self, g):
        rows, length, width = g.shape
        count = self.count
        positions = length * count
        hidden = self.own["one"].shape[1]
        local, full = (rows, length, width), (rows, positions, width)
        inputs = [
            g, self.middle, self.branch_two, self.mod, self.seg_own, self.mlp_full, self.pre, self.act
        ] + self.pair("one") + self.pair("two")
        return call(
            functools.partial(mlp_back_kernel, count, self.number),
            self.number * 4 + 2,
            inputs,
            [VMEM] * 8 + [ANY] * 4,
            [
                (local, F32), ((3, rows, IMAGES_PER_ROW, width), F32),
                ((width, hidden), BF16), ((width, hidden), BF16),
                ((1, hidden), F32), ((1, width), F32),
            ],
            [
                pltpu.VMEM(full, BF16),
                pltpu.VMEM((rows, positions, hidden), BF16),
                pltpu.VMEM(self.own["one"].shape, BF16),
                pltpu.VMEM(self.own["two"].shape, BF16),
            ] + exchange_scratch(count, *local) + semaphores(count),
            2 * rows * positions * width * hidden * 4,
        )

    def backward_attend(self, d_middle):
        rows, length, width = d_middle.shape
        count = self.count
        positions = length * count
        heads_width = self.own["out"].shape[0]
        heads = heads_width // HEAD_WIDTH
        local, full = (rows, length, width), (rows, positions, width)
        inputs = [
            d_middle, self.u, self.branch_one, self.mod, self.seg_own, self.attn_full,
            self.q, self.k, self.v, self.probs, self.mixed,
        ] + self.pair("qkv") + self.pair("out")
        return call(
            functools.partial(attend_back_kernel, count, self.number),
            self.number * 4 + 3,
            inputs,
            [VMEM] * 11 + [ANY] * 4,
            [
                (local, F32), ((3, rows, IMAGES_PER_ROW, width), F32),
                ((3, width, heads_width), BF16), ((width, heads_width), BF16),
                ((2, heads_width), F32), ((1, width), F32),
            ],
            [
                pltpu.VMEM(full, BF16),
                pltpu.VMEM((4, rows, positions, heads * HEAD_LANES), BF16),
                pltpu.VMEM((3, rows, positions, heads_width), BF16),
                pltpu.VMEM(self.own["qkv"].shape, BF16),
                pltpu.VMEM(self.own["out"].shape, BF16),
            ] + exchange_scratch(count, *local) + semaphores(count),
            2 * rows * positions * width * heads_width * 8,
        )


def act_grad(function, source_rows, upstream):
    unused_value, pullback = jax.vjp(function, source_rows)
    return pullback(upstream)[0]


def gather_rows(source_rows):
    return lax.all_gather(source_rows, "tensor", axis=0, tiled=True)


def scatter_rows(terms):
    return lax.psum_scatter(
        terms.astype(BF16), "tensor", scatter_dimension=0, tiled=True
    ).astype(F32)


def align_pass(sent_rows, target_cols, proj_weights, total_token_count):
    p1_w, p1_b, p2_w, p2_b, p3_w, p3_b = proj_weights
    input_full = gather_rows(sent_rows)
    first_pre = dot(input_full, p1_w) + p1_b.astype(F32)
    first_act = jax.nn.silu(first_pre).astype(BF16)
    second_pre = scatter_rows(dot(first_act, p2_w)) + p2_b.astype(F32)
    second_act = jax.nn.silu(second_pre).astype(BF16)
    second_full = gather_rows(second_act)
    predicted = dot(second_full, p3_w) + p3_b.astype(F32)
    pred_sq, cross, target_sq = lax.psum(
        jnp.stack(
            [
                jnp.sum(predicted * predicted, axis=1),
                jnp.sum(predicted * target_cols, axis=1),
                jnp.sum(target_cols * target_cols, axis=1),
            ]
        ),
        "tensor",
    )
    inv_pred = lax.rsqrt(pred_sq + COSINE_EPS)
    inv_target = lax.rsqrt(target_sq + COSINE_EPS)
    cosine = cross * inv_pred * inv_target
    loss_local = jnp.sum(cosine)
    factor = -0.5 / total_token_count
    grad_pred = (
        (factor * inv_pred * inv_target)[:, None] * target_cols
        - (factor * cosine * inv_pred * inv_pred)[:, None] * predicted
    ).astype(BF16)
    grad_p3_b = jnp.sum(grad_pred.astype(F32), axis=0)
    grad_p3_w = dot(second_full, grad_pred, TN)
    grad_second_act = scatter_rows(dot(grad_pred, p3_w, NT))
    grad_second_pre = act_grad(jax.nn.silu, second_pre, grad_second_act).astype(BF16)
    grad_second_full = gather_rows(grad_second_pre)
    grad_p2_b = jnp.sum(grad_second_full.astype(F32), axis=0)
    grad_p2_w = dot(grad_second_full, first_act, TN)
    grad_first_act = dot(grad_second_full, p2_w, NT)
    grad_first_pre = act_grad(jax.nn.silu, first_pre, grad_first_act).astype(BF16)
    grad_p1_b = jnp.sum(grad_first_pre.astype(F32), axis=0)
    grad_p1_w = dot(input_full, grad_first_pre, TN)
    grad_sent = scatter_rows(dot(grad_first_pre, p1_w, NT))
    return (
        loss_local,
        grad_sent,
        (grad_p1_w, grad_p2_w, grad_p3_w),
        (grad_p1_b, grad_p2_b, grad_p3_b),
    )


def swap(value, axis, bit):
    size = lax.axis_size(axis)
    return lax.ppermute(value, axis, [(i, i ^ bit) for i in range(size)])


def halve(value, axis, bit, position):
    mine = (lax.axis_index(axis) & bit) // bit
    keep = lax.dynamic_index_in_dim(value, mine, position, keepdims=False)
    give = lax.dynamic_index_in_dim(value, 1 - mine, position, keepdims=False)
    got = swap(give, axis, bit)
    return (keep.astype(F32) + got.astype(F32)).astype(BF16)


def sum_over_dp(value):
    size = lax.axis_size("dp")
    bits = size.bit_length() - 1
    value = value.reshape((2,) * bits + (value.shape[0] // size, value.shape[1]))
    for bit in range(bits):
        value = halve(value, "dp", 1 << bit, bits - 1 - bit)
    return value


def send_to(value, owner):
    return lax.ppermute(value, "section", [(1 - owner, owner)])


def from_other(weight):
    share = weight.shape[0] // lax.axis_size("dp")
    part = lax.dynamic_slice_in_dim(weight, lax.axis_index("dp") * share, share, 0)
    return lax.all_gather(swap(part, "section", 1), "dp", axis=0, tiled=True)


def per_device(
    block_eight_input,
    cond,
    image_slot_index,
    targets,
    cot,
    ada_w,
    ada_b,
    query_key_value_weight,
    query_value_bias,
    attention_output_weight,
    attention_output_bias,
    hidden_weight,
    hidden_bias,
    output_weight_mlp,
    output_bias_mlp,
    p1_w,
    p1_b,
    p2_w,
    p2_b,
    p3_w,
    p3_b,
):
    section = lax.axis_index("section")
    tensor = lax.axis_index("tensor")
    is_first = section == 0
    count = lax.axis_size("tensor")
    sections = lax.axis_size("section")
    length, replica_rows, width = block_eight_input.shape
    positions = length * count
    rows = replica_rows // sections
    total_token_count = positions * replica_rows * lax.axis_size("dp")
    heads_width = attention_output_weight.shape[1]

    def my_rows(value, axis):
        return lax.dynamic_slice_in_dim(value, section * rows, rows, axis)

    def to_rows(value):
        return jnp.transpose(my_rows(value, 1), (1, 0, 2))

    own = {
        "qkv": jnp.transpose(query_key_value_weight[0], (1, 0, 2)),
        "out": attention_output_weight[0],
        "one": hidden_weight[0],
        "two": output_weight_mlp[0],
    }
    other = {}
    for name in ("qkv", "out", "one", "two"):
        shard = own[name]
        other[name] = from_other(shard.reshape(-1, shard.shape[-1])).reshape(shard.shape)

    cond_act = jax.nn.silu(cond.astype(F32)).astype(BF16)
    mod_local = jnp.einsum(
        "rsd,dc->rsc", cond_act, ada_w[0], preferred_element_type=F32
    ) + ada_b[0].astype(F32)
    mod_all = lax.all_gather(mod_local, ("section", "tensor"), axis=0, tiled=False)
    mod_all = mod_all.reshape(sections, count, replica_rows, IMAGES_PER_ROW, -1)
    mod_all = jnp.transpose(my_rows(mod_all, 2), (0, 2, 3, 1, 4))
    mod_all = mod_all.reshape(sections, rows, IMAGES_PER_ROW, 6, width)
    mod_all = jnp.transpose(mod_all, (0, 3, 1, 2, 4))
    biases = jnp.concatenate(
        [
            query_value_bias.reshape(-1),
            attention_output_bias.reshape(-1),
            hidden_bias.reshape(-1),
            output_bias_mlp.reshape(-1),
        ]
    ).astype(F32)
    other_biases = swap(biases, "section", 1)

    segs_full = my_rows(image_slot_index, 0)
    seg_own = lax.dynamic_slice_in_dim(segs_full, tensor * length, length, 1)
    segs = (seg_own[:, :, None], segs_full[:, :, None], segs_full[:, None, :])

    def make_block(number):
        values = jnp.where(section == number, biases, other_biases)
        cuts = [2 * heads_width, width, hidden_weight.shape[2], width]
        starts = [sum(cuts[:i]) for i in range(4)]
        pieces = [values[start : start + cut] for start, cut in zip(starts, cuts)]
        shaped = [pieces[0].reshape(2, heads_width)] + [piece[None] for piece in pieces[1:]]
        return Block(number, count, mod_all[number], segs, shaped, own, other)

    first, second = make_block(0), make_block(1)
    first_out = first.forward(to_rows(block_eight_input))
    second_out = second.forward(first_out)

    target_cols = my_rows(targets, 1).reshape(count, length, rows, -1)
    target_cols = jnp.transpose(target_cols, (0, 2, 1, 3)).reshape(rows * positions, -1)
    loss_local, grad_sent, proj_grads, proj_bias_grads = align_pass(
        first_out.reshape(rows * length, width),
        target_cols.astype(F32),
        (p1_w, p1_b, p2_w, p2_b, p3_w, p3_b),
        total_token_count,
    )

    sums = {}
    mods = {}
    bias_grads = {}

    def run_back(block, g):
        d_middle, mod_mlp, d_w1, d_w2, d_b1, d_b2 = block.backward_mlp(g)
        d_in, mod_attend, d_wqkv, d_wo, d_bqv, d_bo = block.backward_attend(d_middle)
        reduced = []
        for value in (d_w1, d_w2, d_wo):
            value = sum_over_dp(value)
            reduced.append((value, send_to(value, block.number)))
        parts = sum_over_dp(jnp.transpose(d_wqkv, (1, 0, 2)).reshape(width, 3 * heads_width))
        reduced.append((parts, send_to(parts, block.number)))
        sums[block.number] = [mine.astype(F32) + got.astype(F32) for mine, got in reduced]
        mods[block.number] = jnp.concatenate([mod_attend, mod_mlp], axis=0)
        bias_grads[block.number] = jnp.concatenate(
            [d_bqv.reshape(-1), d_bo[0], d_b1[0], d_b2[0]]
        )
        return d_in

    second_grad = run_back(second, to_rows(cot))
    first_grad = run_back(first, second_grad + grad_sent.reshape(rows, length, width))

    red_fc1, red_fc2, red_out, red_qkv = [
        jnp.where(is_first, one, two) for one, two in zip(sums[0], sums[1])
    ]

    mod_grad = jnp.stack([mods[0], mods[1]])
    mod_grad = jnp.transpose(mod_grad, (0, 2, 3, 1, 4)).reshape(
        sections, rows * IMAGES_PER_ROW, 6 * width
    )
    mod_grad = lax.psum_scatter(mod_grad, "tensor", scatter_dimension=2, tiled=True)
    mod_grad = lax.all_gather(mod_grad, ("dp", "section"), axis=0, tiled=False)
    mod_grad = lax.dynamic_index_in_dim(mod_grad, section, 1, keepdims=False)
    mod_grad = mod_grad.reshape(-1, mod_grad.shape[-1])
    cond_all = lax.all_gather(cond_act, "dp", axis=0, tiled=True).reshape(-1, width)
    share = width // lax.axis_size("dp")
    cond_cols = lax.dynamic_slice_in_dim(cond_all, lax.axis_index("dp") * share, share, 1)
    grad_ada_w = lax.dot_general(cond_cols.astype(F32), mod_grad, TN, precision=HIGHEST)
    grad_ada_b = jnp.sum(mod_grad, axis=0)

    small = jnp.stack([bias_grads[0], bias_grads[1]])
    small, loss_total, red_p1_b, red_p2_b, red_p3_b = lax.psum(
        (small, loss_local) + proj_bias_grads, ("section", "dp")
    )
    small = lax.dynamic_index_in_dim(small, section, 0, keepdims=False)
    align_loss = -0.5 * loss_total / total_token_count
    hidden = hidden_weight.shape[2]
    cut_one = 2 * heads_width
    red_qv_b = small[:cut_one].reshape(2, heads_width)
    red_out_b = small[cut_one : cut_one + width]
    red_fc1_b = small[cut_one + width : cut_one + width + hidden]
    red_fc2_b = small[cut_one + width + hidden :]

    grad_p1_w, grad_p2_w, grad_p3_w = proj_grads
    red_p1_w, red_p2_w, red_p3_w = [
        lax.psum_scatter(value.astype(BF16), ("section", "dp"), scatter_dimension=0, tiled=True)
        for value in (grad_p1_w, grad_p2_w, grad_p3_w)
    ]

    def place(one, two):
        got = swap(jnp.where(is_first, two, one), "section", 1).astype(one.dtype)
        keep = jnp.where(is_first, one, two)
        both = jnp.where(
            is_first, jnp.concatenate([keep, got], axis=0), jnp.concatenate([got, keep], axis=0)
        )
        return jnp.transpose(both, (1, 0, 2))[None]

    section_out = place(first_out, second_out)
    section_grad = place(first_grad.astype(BF16), second_grad.astype(BF16)).astype(F32)
    return (
        section_out,
        section_grad,
        align_loss,
        grad_ada_w[None],
        grad_ada_b[None],
        red_qkv.reshape(1, -1, 3, heads_width),
        red_qv_b[None],
        red_out.T[None],
        red_out_b[None],
        red_fc1[None],
        red_fc1_b[None],
        red_fc2.T[None],
        red_fc2_b[None],
        red_p1_w.astype(F32),
        red_p1_b,
        red_p2_w.T.astype(F32),
        red_p2_b,
        red_p3_w.astype(F32),
        red_p3_b,
    )


def solution(mesh):
    in_specs = (
        P("tensor", "dp", None),
        P("dp", None, None),
        P("dp", None),
        P(None, "dp", "tensor"),
        P("tensor", "dp", None),
        P("section", None, "tensor"),
        P("section", "tensor"),
        P("section", None, None, "tensor"),
        P("section", None, "tensor"),
        P("section", "tensor", None),
        P("section", None),
        P("section", None, "tensor"),
        P("section", "tensor"),
        P("section", "tensor", None),
        P("section", None),
        P(None, "tensor"),
        P("tensor"),
        P("tensor", None),
        P(),
        P(None, "tensor"),
        P("tensor"),
    )
    out_specs = (
        P("section", "tensor", "dp", None),
        P("section", "tensor", "dp", None),
        P(),
        P("section", "dp", "tensor"),
        P("section", "tensor"),
        P("section", "dp", None, "tensor"),
        P("section", None, "tensor"),
        P("section", "tensor", "dp"),
        P("section", None),
        P("section", "dp", "tensor"),
        P("section", "tensor"),
        P("section", "tensor", "dp"),
        P("section", None),
        P(("section", "dp"), "tensor"),
        P("tensor"),
        P("tensor", ("section", "dp")),
        P(),
        P(("section", "dp"), "tensor"),
        P("tensor"),
    )
    return jax.shard_map(
        per_device, mesh=mesh, in_specs=in_specs, out_specs=out_specs, check_vma=False
    )
```

time: 2490 us -> 1060 us (0.43)
  waiting for transfers between devices: 1010 us -> 170 us
  blocking collectives: 696 us -> 129 us
  Pallas kernels: 0 us -> 434 us
  local copies, waits for them, and re-layouts: 369 us -> 184 us
  matrix products: 210 us -> 27.2 us
  other arithmetic: 160 us -> 53.9 us
  starting transfers between devices: 13.3 us -> 40.7 us
    reduce_scatter x27 -> x6, waiting for transfers between devices: 960 us -> 33.3 us  [the longest x3 33.3 us: scatter_rows(): lax.psum_scatter(terms.astype(BF16), 'tensor', scatter_dimension=0, tiled...]
    pallas_call x0 -> x8, Pallas kernels: none -> 434 us  [call(): pl.pallas_call(kernel, out_shape=[jax.ShapeDtypeStruct(shape, dtype) for...]
    all_gather x7 -> x4, blocking collectives: 375 us -> 70.2 us  [the longest x1 34.5 us: per_device(): lax.all_gather(mod_local, ('section', 'tensor'), axis=0, tiled=False)]
    all_gather x13 -> x1, blocking collectives: 277 us -> 24.2 us  [gather_rows(): return lax.all_gather(source_rows, 'tensor', axis=0, tiled=True)]
    dot_general x84 -> x11, matrix products: 210 us -> 27.2 us  [the longest x9 20.7 us: dot(): return lax.dot_general(left, right, form, preferred_element_type=F32)]
    ppermute x4 -> x31, waiting for transfers between devices: 16.4 us -> 106 us  [the longest x23 83.6 us: swap(): return lax.ppermute(value, axis, [(i, i ^ bit) for i in range(size)])]
    reduce_sum x50 -> x3, other arithmetic: 73.6 us -> 1.98 us  [the longest x1 1.66 us: align_pass(): grad_p3_b = jnp.sum(grad_pred.astype(F32), axis=0)]
    convert_element_type x36 -> x3, local copies, waits for them, and re-layouts: 64.2 us -> 1.96 us  [the longest x2 1.94 us: per_device(): target_cols.astype(F32)]
  transfers between devices with their start and end apart: 36 -> 43, of which waited for: 30 -> 14; matrix products, arithmetic and copies ran while one was open for 15% -> 21% of each run, Pallas kernels for 0% -> 37%
where the time goes in v1:
time: 1060 us
  Pallas kernels  434 us (41%)
  local copies, waits for them, and re-layouts  184 us (17%)
  waiting for transfers between devices  170 us (16%)
  blocking collectives  129 us (12%)
  other arithmetic  53.9 us (5%)
  starting transfers between devices  40.7 us (4%)
  matrix products  27.2 us (3%)
  between operations  17.4 us (2%)
    pallas_call x8, Pallas kernels, call(): pl.pallas_call(kernel, out_shape=[jax.ShapeDtypeStruct(shape, dtype) for...  434 us
    unnamed x174, local copies, waits for them, and re-layouts  87.9 us
    ppermute x23, waiting for transfers between devices, swap(): return lax.ppermute(value, axis, [(i, i ^ bit) for i in range(size)])  83.6 us
    all_gather x1, blocking collectives, per_device(): lax.all_gather(mod_local, ('section', 'tensor'), axis=0, tiled=False)  34.5 us
    reduce_scatter x3, waiting for transfers between devices, scatter_rows(): lax.psum_scatter(terms.astype(BF16), 'tensor', scatter_dimension=0, tiled...  33.3 us
    all_gather x2, waiting for transfers between devices, gather_rows(): return lax.all_gather(source_rows, 'tensor', axis=0, tiled=True)  30.3 us
    psum x1, blocking collectives, per_device(): lax.psum((small, loss_local) + proj_bias_grads, ('section', 'dp'))  24.6 us
    all_gather x1, blocking collectives, gather_rows(): return lax.all_gather(source_rows, 'tensor', axis=0, tiled=True)  24.2 us
  transfers between devices with their start and end apart: 43, of which 14 were waited for; matrix products, arithmetic and copies ran while one was open for 21% of the time, Pallas kernels for 37%

profile of v1, /device:TPU:0, one launch (start us, length us, event | category | flops | bytes accessed | tf_op | source)
XLA Modules:
  0.0 1056.6 jit_solution(2429183907092435714)
XLA Ops:
  7.3 4.3 copy.192
  16.7 12.0 %collective-permute-done.1 = bf16[864,288]{0,1:T(8,128)(2,1)S(1)} collective-permute-done((bf16[864,288]{0,1:T(8,128)(2,1)}, bf16[864,288]{0,1:T(8,128)(2,1)S(1)}, u32[]{:S(2)}, u32[]{:S(2)}) %collective-permute-start.1) | collective-permute-done | bytes 497696 | tf_op jit(solution)/shard_map/ppermute | solution.py:589
  32.6 14.4 %collective-permute-done.4 = bf16[288,1152]{1,0:T(8,128)(2,1)S(1)} collective-permute-done((bf16[288,1152]{1,0:T(8,128)(2,1)S(1)}, bf16[288,1152]{1,0:T(8,128)(2,1)S(1)}, u32[]{:S(2)}, u32[]{:S(2)}) %collective-permute-start.4) | collective-permute-done | bytes 663584 | tf_op jit(solution)/shard_map/ppermute | solution.py:589
  50.5 13.9 %collective-permute-done.3 = bf16[288,1152]{1,0:T(8,128)(2,1)S(1)} collective-permute-done((bf16[288,1152]{1,0:T(8,128)(2,1)S(1)}, bf16[288,1152]{1,0:T(8,128)(2,1)S(1)}, u32[]{:S(2)}, u32[]{:S(2)}) %collective-permute-start.3) | collective-permute-done | bytes 663584 | tf_op jit(solution)/shard_map/ppermute | solution.py:589
  69.3 3.3 fusion.6
  72.7 34.5 %all-gather = f32[32,3,1728]{2,1,0:T(4,128)S(1)} all-gather(f32[4,3,1728]{2,1,0:T(4,128)S(1)} %copy.189), channel_id=2, replica_groups=mesh['section'=2,'dp'=4,'tensor'=4] {'section','tensor'}, dimensions={0}, use_global_device_ids=true | all-gather | bytes 746496 | tf_op jit(solution)/shard_map/all_gather | solution.py:674
  110.5 8.6 all_gather.39.wo_other
  119.0 4.3 copy.194
  123.3 48.7 %shard_map.348 = (f32[2,48,1152]{2,1,0:T(8,128)}, f32[2,48,1152]{2,1,0:T(8,128)}, bf16[2,192,1152]{2,1,0:T(8,128)(2,1)}, bf16[2,192,512]{2,1,0:T(8,128)(2,1)S(1)...) custom-call(bf16[2,48,1152]{2,1,0:T(8,128)(2,1)S(1)} %bitcast.208, ...), custom_call_target="tpu_custom_call" | custom-call | flops 1019215872 | bytes 5705856 | tf_op jit(solution)/shard_map/pallas_call | solution.py:378
  175.2 46.4 %shard_map.349 = (bf16[2,48,1152]{2,1,0:T(8,128)(2,1)S(1)}, f32[2,48,1152]{2,1,0:T(8,128)S(1)}, bf16[2,192,1152]{2,1,0:T(8,128)(2,1)}, f32[2,192,1152]{2,1,0:T(8,128)}, bf16[2,192,1152]{2,1,0:T(8,128)(2,1)}) custom-call(f32[2,48,1152]{2,1,0:T(8,128)S(1)} %copy-done.2, f32[6,2,3,1152]{3,2,1,0:T(4,128)S(1)} %get-tuple-element.243.mod_ref, ...), custom_call_target="tpu_custom_call" | custom-call | flops 2038431744 | bytes 11234688 | tf_op jit(solution)/shard_map/pallas_call | solution.py:378
  221.7 24.2 %all_gather.42 = bf16[384,1152]{1,0:T(8,128)(2,1)S(1)} all-gather(bf16[96,1152]{1,0:T(8,128)(2,1)S(1)} %bitcast.207), channel_id=1, replica_groups=mesh['section'=2,'dp'=4,'tensor'=4] {'tensor'}, dimensions={0}, use_global_device_ids=true | all-gather | bytes 1105920 | tf_op jit(solution)/shard_map/all_gather | solution.py:530
  250.6 33.3 %reduce-scatter.10.cloned.1.call-done = bf16[96,2048]{1,0:T(8,128)(2,1)} async-done(((bf16[384,2048]{1,0:T(8,128)(2,1)}), bf16[96,2048]{1,0:T(8,128)(2,1)}) %reduce-scatter.10.cloned.1.call-update) | async-done | bytes 393232 | tf_op jit(solution)/shard_map/reduce_scatter | solution.py:534
  291.8 30.3 %all-gather.13.cloned.1.call-done = bf16[384,2048]{1,0:T(8,128)(2,1)} async-done(((bf16[96,2048]{1,0:T(8,128)(2,1)}), bf16[384,2048]{1,0:T(8,128)(2,1)}) %all-gather.13.cloned.1.call-update) | async-done | bytes 1572880 | tf_op jit(solution)/shard_map/all_gather | solution.py:530
  325.8 10.5 psum.42
  343.2 5.5 all_gather.45
  352.2 67.4 %shard_map.350 = (f32[2,48,1152]{2,1,0:T(8,128)}, f32[2,48,1152]{2,1,0:T(8,128)}, bf16[2,192,1152]{2,1,0:T(8,128)(2,1)}, bf16[2,192,512]{2,1,0:T(8,128)(2,1)S(1)...) custom-call(bf16[2,48,1152]{2,1,0:T(8,128)(2,1)S(1)} %get-tuple-elem, ...), custom_call_target="tpu_custom_call" | custom-call | flops 1019215872 | bytes 5705856 | tf_op jit(solution)/shard_map/pallas_call | solution.py:378
  422.9 44.7 %shard_map.351 = (bf16[2,48,1152]{2,1,0:T(8,128)(2,1)S(1)}, f32[2,48,1152]{2,1,0:T(8,128)S(1)}, bf16[2,192,1152]{2,1,0:T(8,128)(2,1)}, f32[2,192,1152]{2,1,0:T(8,128)}, bf16[2,192,1152]{2,1,0:T(8,128)(2,1)}) custom-call(f32[2,48,1152]{2,1,0:T(8,128)S(1)} %copy-done.4, f32[6,2,3,1152]{3,2,1,0:T(4,128)S(1)} %get-tuple-element.242.mod_ref, ...), custom_call_target="tpu_custom_call" | custom-call | flops 2038431744 | bytes 11234688 | tf_op jit(solution)/shard_map/pallas_call | solution.py:378
  475.3 72.6 %shard_map.352 = (f32[2,48,1152]{2,1,0:T(8,128)S(1)}, f32[3,2,3,1152]{3,2,1,0:T(4,128)S(1)}, bf16[1152,1152]{1,0:T(8,128)(2,1)}, bf16[1152,1152]{1,0:T(8,128)(2,...) custom-call(bf16[2,48,1152]{2,1,0:T(8,128)(2,1)S(1)} %bitcast.210, f32[2,48,1152]{2,1,0:T(8,128)S(1)} %copy-done.5, ...), custom_call_target="tpu_custom_call" | custom-call | flops 4076863488 | bytes 15427968 | tf_op jit(solution)/shard_map/pallas_call | solution.py:378
  548.7 51.6 %shard_map.353 = (f32[2,48,1152]{2,1,0:T(8,128)}, f32[3,2,3,1152]{3,2,1,0:T(4,128)S(1)}, bf16[3,1152,288]{2,1,0:T(8,128)(2,1)}, bf16[1152,288]{1,0:T(8,128)(2,1)...) custom-call(f32[2,48,1152]{2,1,0:T(8,128)} %copy-done.11, bf16[2,48,1152]{2,1,0:T(8,128)(2,1)S(1)} %get-tuple-element.70.u_ref, ...), custom_call_target="tpu_custom_call" | custom-call | flops 2038431744 | bytes 10045824 | tf_op jit(solution)/shard_map/pallas_call | solution.py:378
  600.4 4.2 copy.218
  604.6 7.3 reshape_reshape.7
  619.8 7.8 constant_dynamic-slice_fusion.6
  627.6 8.1 copy.220
  638.2 8.1 copy.244
  657.3 3.4 collective-permute-start.18
  674.1 3.9 collective-permute-done.11
  684.4 7.9 collective-permute-done.29
  694.8 46.8 %shard_map.354 = (f32[2,48,1152]{2,1,0:T(8,128)S(1)}, f32[3,2,3,1152]{3,2,1,0:T(4,128)S(1)}, bf16[1152,1152]{1,0:T(8,128)(2,1)}, bf16[1152,1152]{1,0:T(8,128)(2,...) custom-call(f32[2,48,1152]{2,1,0:T(8,128)S(1)} %convert_add_fusion.17.g_ref, f32[2,48,1152]{2,1,0:T(8,128)S(1)} %copy-done.3, ...), custom_call_target="tpu_custom_call" | custom-call | flops 4076863488 | bytes 15649152 | tf_op jit(solution)/shard_map/pallas_call | solution.py:378
  742.4 55.6 %shard_map.355 = (f32[2,48,1152]{2,1,0:T(8,128)}, f32[3,2,3,1152]{3,2,1,0:T(4,128)S(1)}, bf16[3,1152,288]{2,1,0:T(8,128)(2,1)}, bf16[1152,288]{1,0:T(8,128)(2,1)...) custom-call(f32[2,48,1152]{2,1,0:T(8,128)} %copy-done.10, bf16[2,48,1152]{2,1,0:T(8,128)(2,1)S(1)} %bitcast.209, ...), custom_call_target="tpu_custom_call" | custom-call | flops 2038431744 | bytes 10045824 | tf_op jit(solution)/shard_map/pallas_call | solution.py:378
  798.5 13.7 %copy.235 = f32[2,6,6912]{0,1,2:T(8,128)} copy(f32[2,6,6912]{2,0,1:T(2,128)S(1)} %reshape.239) | data formatting | bytes 663552
  812.2 17.3 %reshape.279 = f32[6912,12]{1,0:T(8,128)} reshape(f32[6912,6,2]{2,1,0:T(8,128)} %bitcast.211) | data formatting | bytes 663552
  834.5 4.1 convolution_convert_fusion
  841.6 24.6 %all-reduce = (f32[]{:T(128)}, f32[2,4032]{1,0:T(2,128)S(1)}, f32[512]{0:T(512)}, f32[2048]{0:T(1024)}, f32[192]{0:T(256)}) all-reduce(f32[]{:T(128)} %get-tuple-element.255, f32[2,4032]{1,0:T(2,128)S(1)} %pad_maximum_fusion, f32[512]{0:T(512)S(1)} %get-tuple-element.228, ...), channel_id=1, replica_groups=mesh['section'=2,'dp'=4,'tensor'=4] {'section','dp'}, use_global_device_ids=true, to_apply=%region_8.9 | all-reduce | flops 10817 | bytes 86536 | tf_op jit(solution)/shard_map/psum | solution.py:756
  874.3 3.9 reshape_reshape.6
  878.2 10.4 constant_dynamic-slice_fusion.8
  889.3 8.0 copy.243
  897.3 8.1 copy.217
  915.1 4.3 collective-permute-done.14
  921.5 5.2 reshape.280
  926.6 4.8 copy.213
  931.5 21.7 %all-gather.1 = f32[16,6,1728]{2,1,0:T(8,128)S(1)} all-gather(f32[2,6,1728]{2,1,0:T(8,128)S(1)} %copy.213), channel_id=3, replica_groups=mesh['section'=2,'dp'=4,'tensor'=4] {'dp','section'}, dimensions={0}, use_global_device_ids=true | all-gather | bytes 746496 | tf_op jit(solution)/shard_map/all_gather | solution.py:746
  953.9 5.8 collective-permute-start.30
  962.1 3.2 convolution_bitcast_fusion
  981.0 4.0 collective-permute-done.8
  986.6 12.6 %collective-permute-done.26 = bf16[288,1152]{1,0:T(8,128)(2,1)} collective-permute-done((bf16[288,1152]{1,0:T(8,128)(2,1)}, bf16[288,1152]{1,0:T(8,128)(2,1)}, u32[]{:S(2)}, u32[]{:S(2)}) %collective-permute-start.26) | collective-permute-done | bytes 663584 | tf_op jit(solution)/shard_map/ppermute | solution.py:589
  1002.6 10.0 collective-permute-done.20
  1019.7 12.9 %collective-permute-done.27 = bf16[288,1152]{1,0:T(8,128)(2,1)} collective-permute-done((bf16[288,1152]{1,0:T(8,128)(2,1)}, bf16[288,1152]{1,0:T(8,128)(2,1)}, u32[]{:S(2)}, u32[]{:S(2)}) %collective-permute-start.27) | collective-permute-done | bytes 663584 | tf_op jit(solution)/shard_map/ppermute | solution.py:610
  1035.7 9.6 collective-permute-done.21
  (385 shorter events, 171.3 us)
Async XLA Ops:
  7.2 240.6 %copy-start = (bf16[512,2048]{1,0:T(8,128)(2,1)S(1)}, bf16[512,2048]{1,0:T(8,128)(2,1)}, u32[]{:S(2)}) copy-start(bf16[512,2048]{1,0:T(8,128)(2,1)} %param.38) | copy-start | bytes 6291460
  7.2 111.8 %all-gather.17.cloned.1.call-start = ((), (), s32[]{:S(2)}) async-start(), calls=%async_computation.17 | async-start | bytes 2580480 | tf_op jit(solution)/shard_map/all_gather | solution.py:616
  13.8 14.9 %collective-permute-start.1 = (bf16[864,288]{0,1:T(8,128)(2,1)}, bf16[864,288]{0,1:T(8,128)(2,1)S(1)}, u32[]{:S(2)}, u32[]{:S(2)}) collective-permute-start(bf16[864,288]{0,1:T(8,128)(2,1)} %copy.240), channel_id=1, source_target_pairs={{0,16},{16,0},{1,17},{17,1},{2,18},{18,2},{3,19},{19,3},{4,20},{20... | collective-permute-start | bytes 1493000 | tf_op jit(solution)/shard_map/ppermute | solution.py:589
  29.5 144.7 %all-gather.11.cloned.1.call-start = ((), (), s32[]{:S(2)}) async-start(), calls=%async_computation.8 | async-start | bytes 3317760 | tf_op jit(solution)/shard_map/all_gather | solution.py:616
  30.8 16.2 %collective-permute-start.4 = (bf16[288,1152]{1,0:T(8,128)(2,1)S(1)}, bf16[288,1152]{1,0:T(8,128)(2,1)S(1)}, u32[]{:S(2)}, u32[]{:S(2)}) collective-permute-start(bf16[288,1152]{1,0:T(8,128)(2,1)S(1)} %dynamic-slice_bitcast_fusion.8), channel_id=1, source_target_pairs={{0,16},{16,0},{1,17},{17,1},{2,18},{18,2},{3,19},{19,3},{4,20},{20... | collective-permute-start | bytes 1990664 | tf_op jit(solution)/shard_map/ppermute | solution.py:589
  47.8 126.4 %all-gather.9.cloned.1.call-start = ((), (), s32[]{:S(2)}) async-start(), calls=%async_computation.7 | async-start | bytes 3317760 | tf_op jit(solution)/shard_map/all_gather | solution.py:616
  49.0 15.3 %collective-permute-start.3 = (bf16[288,1152]{1,0:T(8,128)(2,1)S(1)}, bf16[288,1152]{1,0:T(8,128)(2,1)S(1)}, u32[]{:S(2)}, u32[]{:S(2)}) collective-permute-start(bf16[288,1152]{1,0:T(8,128)(2,1)S(1)} %dynamic-slice_bitcast_fusion.9), channel_id=1, source_target_pairs={{0,16},{16,0},{1,17},{17,1},{2,18},{18,2},{3,19},{19,3},{4,20},{20... | collective-permute-start | bytes 1990664 | tf_op jit(solution)/shard_map/ppermute | solution.py:589
  65.2 218.6 %reduce-scatter.10.cloned.1.call-start = ((), (), s32[]{:S(2)}) async-start(), calls=%async_computation.9 | async-start | bytes 1966080 | tf_op jit(solution)/shard_map/reduce_scatter | solution.py:534
  65.6 44.0 %collective-permute-start = (f32[4032]{0:T(1024)S(1)}, f32[4032]{0:T(1024)S(1)}, u32[]{:S(2)}, u32[]{:S(2)}) collective-permute-start(f32[4032]{0:T(1024)S(1)} %convert_element_type.366), channel_id=1, source_target_pairs={{0,16},{16,0},{1,17},{17,1},{2,18},{18,2},{3,19},{19,3},{4,20},{20... | collective-permute-start | bytes 48392 | tf_op jit(solution)/shard_map/ppermute | solution.py:589
  68.3 42.1 %collective-permute-start.2 = (bf16[72,1152]{1,0:T(8,128)(2,1)}, bf16[72,1152]{1,0:T(8,128)(2,1)}, u32[]{:S(2)}, u32[]{:S(2)}) collective-permute-start(bf16[72,1152]{1,0:T(8,128)(2,1)} %dynamic-slice_bitcast_fusion.15), channel_id=1, source_target_pairs={{0,16},{16,0},{1,17},{17,1},{2,18},{18,2},{3,19},{19,3},{4,20},{20... | collective-permute-start | bytes 497672 | tf_op jit(solution)/shard_map/ppermute | solution.py:589
  175.2 70.6 %copy-start.72 = (bf16[1152,512]{1,0:T(8,128)(2,1)S(1)}, bf16[1152,512]{1,0:T(8,128)(2,1)}, u32[]{:S(2)}) copy-start(bf16[1152,512]{1,0:T(8,128)(2,1)} %param.36) | copy-start | bytes 3538948
  249.9 72.1 %all-gather.13.cloned.1.call-start = ((), (), s32[]{:S(2)}) async-start(), calls=%async_computation.10 | async-start | bytes 1966080 | tf_op jit(solution)/shard_map/all_gather | solution.py:530
  285.9 184.8 %reduce-scatter.12.cloned.1.call-start = ((), (), s32[]{:S(2)}) async-start(), calls=%async_computation.11 | async-start | bytes 1966080 | tf_op jit(solution)/shard_map/reduce_scatter | solution.py:534
  342.9 308.3 %all-gather.15.cloned.1.call-start = ((), (), s32[]{:S(2)}) async-start(), calls=%async_computation.12 | async-start | bytes 1966080 | tf_op jit(solution)/shard_map/all_gather | solution.py:530
  469.2 177.2 %collective-permute-start.5 = (bf16[2,48,1152]{2,1,0:T(8,128)(2,1)}, bf16[2,48,1152]{2,1,0:T(8,128)(2,1)}, u32[]{:S(2)}, u32[]{:S(2)}) collective-permute-start(bf16[2,48,1152]{2,1,0:T(8,128)(2,1)} %get-tuple-element.241), channel_id=1, source_target_pairs={{0,16},{16,0},{1,17},{17,1},{2,18},{18,2},{3,19},{19,3},{4,20},{20... | collective-permute-start | bytes 663560 | tf_op jit(solution)/shard_map/ppermute | solution.py:589
  472.9 220.8 %reduce-scatter.14.cloned.1.call-start = ((), (), s32[]{:S(2)}) async-start(), calls=%async_computation.13 | async-start | bytes 1105920 | tf_op jit(solution)/shard_map/reduce_scatter | solution.py:534
  475.3 73.4 %copy-start.17 = (bf16[2,192,512]{2,1,0:T(8,128)(2,1)S(1)}, bf16[2,192,512]{2,1,0:T(8,128)(2,1)}, u32[]{:S(2)}) copy-start(bf16[2,192,512]{2,1,0:T(8,128)(2,1)} %copy-done.16) | copy-start | bytes 1179652
  475.3 73.4 %copy-start.19 = (bf16[2,192,512]{2,1,0:T(8,128)(2,1)S(1)}, bf16[2,192,512]{2,1,0:T(8,128)(2,1)}, u32[]{:S(2)}) copy-start(bf16[2,192,512]{2,1,0:T(8,128)(2,1)} %copy-done.18) | copy-start | bytes 1179652
  475.3 73.4 %copy-start.23 = (bf16[2,192,288]{2,1,0:T(8,128)(2,1)S(1)}, bf16[2,192,288]{2,1,0:T(8,128)(2,1)}, u32[]{:S(2)}) copy-start(bf16[2,192,288]{2,1,0:T(8,128)(2,1)} %copy-done.22) | copy-start | bytes 663556
  614.9 33.6 %collective-permute-start.16 = (bf16[2,288,288]{1,2,0:T(8,128)(2,1)}, bf16[2,288,288]{1,2,0:T(8,128)(2,1)}, u32[]{:S(2)}, u32[]{:S(2)}) collective-permute-start(bf16[2,288,288]{1,2,0:T(8,128)(2,1)} %bitcast.255), channel_id=1, source_target_pairs={{0,4},{4,0},{8,12},{12,8},{1,5},{5,1},{9,13},{13,9},{2,6},{6,2},{1... | collective-permute-start | bytes 995336 | tf_op jit(solution)/shard_map/ppermute | solution.py:589
  617.5 47.0 %collective-permute-start.28 = (bf16[2,288,1152]{2,1,0:T(8,128)(2,1)}, bf16[2,288,1152]{2,1,0:T(8,128)(2,1)}, u32[]{:S(2)}, u32[]{:S(2)}) collective-permute-start(bf16[2,288,1152]{2,1,0:T(8,128)(2,1)} %dynamic-slice_bitcast_fusion), channel_id=1, source_target_pairs={{0,4},{4,0},{8,12},{12,8},{1,5},{5,1},{9,13},{13,9},{2,6},{6,2},{1... | collective-permute-start | bytes 3981320 | tf_op jit(solution)/shard_map/ppermute | solution.py:589
  619.1 50.5 %collective-permute-start.22 = (bf16[2,288,1152]{2,1,0:T(8,128)(2,1)}, bf16[2,288,1152]{2,1,0:T(8,128)(2,1)}, u32[]{:S(2)}, u32[]{:S(2)}) collective-permute-start(bf16[2,288,1152]{2,1,0:T(8,128)(2,1)} %dynamic-slice_bitcast_fusion.2), channel_id=1, source_target_pairs={{0,4},{4,0},{8,12},{12,8},{1,5},{5,1},{9,13},{13,9},{2,6},{6,2},{1... | collective-permute-start | bytes 3981320 | tf_op jit(solution)/shard_map/ppermute | solution.py:589
  635.7 25.0 %collective-permute-start.10 = (bf16[2,288,864]{2,1,0:T(8,128)(2,1)}, bf16[2,288,864]{2,1,0:T(8,128)(2,1)}, u32[]{:S(2)}, u32[]{:S(2)}) collective-permute-start(bf16[2,288,864]{2,1,0:T(8,128)(2,1)} %bitcast.251), channel_id=1, source_target_pairs={{0,4},{4,0},{8,12},{12,8},{1,5},{5,1},{9,13},{13,9},{2,6},{6,2},{1... | collective-permute-start | bytes 2985992 | tf_op jit(solution)/shard_map/ppermute | solution.py:589
  649.6 7.6 collective-permute-start.17
  656.5 176.4 %reduce-scatter.20.cloned.1.call-start = ((), (), s32[]{:S(2)}) async-start(), calls=%async_computation.16 | async-start | bytes 884736 | tf_op jit(solution)/shard_map/reduce_scatter | solution.py:770
  657.3 296.7 %collective-permute-start.18 = (bf16[288,288]{0,1:T(8,128)(2,1)S(1)}, bf16[288,288]{0,1:T(8,128)(2,1)}, u32[]{:S(2)}, u32[]{:S(2)}) collective-permute-start(bf16[288,288]{0,1:T(8,128)(2,1)S(1)} %fusion.26), channel_id=1, source_target_pairs={{0,16},{1,17},{2,18},{3,19},{4,20},{5,21},{6,22},{7,23},{8,24},{9,... | collective-permute-start | bytes 497672 | tf_op jit(solution)/shard_map/ppermute | solution.py:610
  663.1 15.0 %collective-permute-start.11 = (bf16[288,864]{1,0:T(8,128)(2,1)}, bf16[288,864]{1,0:T(8,128)(2,1)}, u32[]{:S(2)}, u32[]{:S(2)}) collective-permute-start(bf16[288,864]{1,0:T(8,128)(2,1)} %dynamic-slice_bitcast_fusion.10), channel_id=1, source_target_pairs={{0,8},{4,12},{8,0},{12,4},{1,9},{5,13},{9,1},{13,5},{2,10},{6,14},... | collective-permute-start | bytes 1493000 | tf_op jit(solution)/shard_map/ppermute | solution.py:589
  667.5 24.8 %collective-permute-start.29 = (bf16[288,1152]{1,0:T(8,128)(2,1)S(1)}, bf16[288,1152]{1,0:T(8,128)(2,1)}, u32[]{:S(2)}, u32[]{:S(2)}) collective-permute-start(bf16[288,1152]{1,0:T(8,128)(2,1)S(1)} %dynamic-slice_bitcast_fusion.4), channel_id=1, source_target_pairs={{0,8},{4,12},{8,0},{12,4},{1,9},{5,13},{9,1},{13,5},{2,10},{6,14},... | collective-permute-start | bytes 1990664 | tf_op jit(solution)/shard_map/ppermute | solution.py:589
  669.6 236.5 %reduce-scatter.16.cloned.1.call-start = ((), (), s32[]{:S(2)}) async-start(), calls=%async_computation.14 | async-start | bytes 1327104 | tf_op jit(solution)/shard_map/reduce_scatter | solution.py:770
  672.6 157.0 %collective-permute-start.23 = (bf16[288,1152]{1,0:T(8,128)(2,1)}, bf16[288,1152]{1,0:T(8,128)(2,1)}, u32[]{:S(2)}, u32[]{:S(2)}) collective-permute-start(bf16[288,1152]{1,0:T(8,128)(2,1)} %dynamic-slice_bitcast_fusion.6), channel_id=1, source_target_pairs={{0,8},{4,12},{8,0},{12,4},{1,9},{5,13},{9,1},{13,5},{2,10},{6,14},... | collective-permute-start | bytes 1990664 | tf_op jit(solution)/shard_map/ppermute | solution.py:589
  680.0 335.0 %collective-permute-start.12 = (bf16[288,864]{1,0:T(8,128)(2,1)}, bf16[288,864]{1,0:T(8,128)(2,1)}, u32[]{:S(2)}, u32[]{:S(2)}) collective-permute-start(bf16[288,864]{1,0:T(8,128)(2,1)} %fusion.15), channel_id=1, source_target_pairs={{0,16},{1,17},{2,18},{3,19},{4,20},{5,21},{6,22},{7,23},{8,24},{9,... | collective-permute-start | bytes 1493000 | tf_op jit(solution)/shard_map/ppermute | solution.py:610
  684.4 237.1 %reduce-scatter.22.cloned.1.call-start = ((), (), s32[]{:S(2)}) async-start(), calls=%async_computation.18 | async-start | bytes 4423680
  829.5 147.6 %reduce-scatter.18.cloned.1.call-start = ((), (), s32[]{:S(2)}) async-start(), calls=%async_computation.15 | async-start | bytes 2359296 | tf_op jit(solution)/shard_map/reduce_scatter | solution.py:770
  866.9 44.7 %collective-permute-start.6 = (bf16[2,48,1152]{2,1,0:T(8,128)(2,1)}, bf16[2,48,1152]{2,1,0:T(8,128)(2,1)}, u32[]{:S(2)}, u32[]{:S(2)}) collective-permute-start(bf16[2,48,1152]{2,1,0:T(8,128)(2,1)} %get-tuple-element.239), channel_id=1, source_target_pairs={{0,16},{16,0},{1,17},{17,1},{2,18},{18,2},{3,19},{19,3},{4,20},{20... | collective-permute-start | bytes 663560 | tf_op jit(solution)/shard_map/ppermute | solution.py:589
  868.3 42.0 %collective-permute-start.13 = (bf16[2,288,288]{1,2,0:T(8,128)(2,1)}, bf16[2,288,288]{1,2,0:T(8,128)(2,1)}, u32[]{:S(2)}, u32[]{:S(2)}) collective-permute-start(bf16[2,288,288]{1,2,0:T(8,128)(2,1)} %bitcast.55), channel_id=1, source_target_pairs={{0,4},{4,0},{8,12},{12,8},{1,5},{5,1},{9,13},{13,9},{2,6},{6,2},{1... | collective-permute-start | bytes 995336 | tf_op jit(solution)/shard_map/ppermute | solution.py:589
  870.8 99.3 %collective-permute-start.25 = (bf16[2,288,1152]{2,1,0:T(8,128)(2,1)}, bf16[2,288,1152]{2,1,0:T(8,128)(2,1)}, u32[]{:S(2)}, u32[]{:S(2)}) collective-permute-start(bf16[2,288,1152]{2,1,0:T(8,128)(2,1)} %dynamic-slice_bitcast_fusion.1), channel_id=1, source_target_pairs={{0,4},{4,0},{8,12},{12,8},{1,5},{5,1},{9,13},{13,9},{2,6},{6,2},{1... | collective-permute-start | bytes 3981320 | tf_op jit(solution)/shard_map/ppermute | solution.py:589
  910.3 55.0 %collective-permute-start.7 = (bf16[2,288,864]{2,1,0:T(8,128)(2,1)}, bf16[2,288,864]{2,1,0:T(8,128)(2,1)}, u32[]{:S(2)}, u32[]{:S(2)}) collective-permute-start(bf16[2,288,864]{2,1,0:T(8,128)(2,1)} %bitcast.42), channel_id=1, source_target_pairs={{0,4},{4,0},{8,12},{12,8},{1,5},{5,1},{9,13},{13,9},{2,6},{6,2},{1... | collective-permute-start | bytes 2985992 | tf_op jit(solution)/shard_map/ppermute | solution.py:589
  911.5 7.8 collective-permute-start.14
  920.1 39.6 %collective-permute-start.15 = (bf16[288,288]{0,1:T(8,128)(2,1)}, bf16[288,288]{0,1:T(8,128)(2,1)}, u32[]{:S(2)}, u32[]{:S(2)}) collective-permute-start(bf16[288,288]{0,1:T(8,128)(2,1)} %fusion.27), channel_id=1, source_target_pairs={{16,0},{17,1},{18,2},{19,3},{20,4},{21,5},{22,6},{23,7},{24,8},{25... | collective-permute-start | bytes 497672 | tf_op jit(solution)/shard_map/ppermute | solution.py:610
  953.9 65.8 %collective-permute-start.30 = (bf16[288,1152]{1,0:T(8,128)(2,1)S(1)}, bf16[288,1152]{1,0:T(8,128)(2,1)}, u32[]{:S(2)}, u32[]{:S(2)}) collective-permute-start(bf16[288,1152]{1,0:T(8,128)(2,1)S(1)} %fusion.11), channel_id=1, source_target_pairs={{0,16},{1,17},{2,18},{3,19},{4,20},{5,21},{6,22},{7,23},{8,24},{9,... | collective-permute-start | bytes 1990664 | tf_op jit(solution)/shard_map/ppermute | solution.py:610
  959.8 13.5 %collective-permute-start.19 = (bf16[2,288,1152]{2,1,0:T(8,128)(2,1)}, bf16[2,288,1152]{2,1,0:T(8,128)(2,1)S(1)}, u32[]{:S(2)}, u32[]{:S(2)}) collective-permute-start(bf16[2,288,1152]{2,1,0:T(8,128)(2,1)} %dynamic-slice_bitcast_fusion.3), channel_id=1, source_target_pairs={{0,4},{4,0},{8,12},{12,8},{1,5},{5,1},{9,13},{13,9},{2,6},{6,2},{1... | collective-permute-start | bytes 3981320 | tf_op jit(solution)/shard_map/ppermute | solution.py:589
  965.3 70.4 %collective-permute-start.24 = (bf16[288,1152]{1,0:T(8,128)(2,1)}, bf16[288,1152]{1,0:T(8,128)(2,1)}, u32[]{:S(2)}, u32[]{:S(2)}) collective-permute-start(bf16[288,1152]{1,0:T(8,128)(2,1)} %fusion.13), channel_id=1, source_target_pairs={{0,16},{1,17},{2,18},{3,19},{4,20},{5,21},{6,22},{7,23},{8,24},{9,... | collective-permute-start | bytes 1990664 | tf_op jit(solution)/shard_map/ppermute | solution.py:610
  970.1 14.9 %collective-permute-start.8 = (bf16[288,864]{1,0:T(8,128)(2,1)}, bf16[288,864]{1,0:T(8,128)(2,1)}, u32[]{:S(2)}, u32[]{:S(2)}) collective-permute-start(bf16[288,864]{1,0:T(8,128)(2,1)} %dynamic-slice_bitcast_fusion.11), channel_id=1, source_target_pairs={{0,8},{4,12},{8,0},{12,4},{1,9},{5,13},{9,1},{13,5},{2,10},{6,14},... | collective-permute-start | bytes 1493000 | tf_op jit(solution)/shard_map/ppermute | solution.py:589
  973.2 26.0 %collective-permute-start.26 = (bf16[288,1152]{1,0:T(8,128)(2,1)}, bf16[288,1152]{1,0:T(8,128)(2,1)}, u32[]{:S(2)}, u32[]{:S(2)}) collective-permute-start(bf16[288,1152]{1,0:T(8,128)(2,1)} %dynamic-slice_bitcast_fusion.5), channel_id=1, source_target_pairs={{0,8},{4,12},{8,0},{12,4},{1,9},{5,13},{9,1},{13,5},{2,10},{6,14},... | collective-permute-start | bytes 1990664 | tf_op jit(solution)/shard_map/ppermute | solution.py:589
  985.0 27.7 %collective-permute-start.20 = (bf16[288,1152]{1,0:T(8,128)(2,1)}, bf16[288,1152]{1,0:T(8,128)(2,1)S(1)}, u32[]{:S(2)}, u32[]{:S(2)}) collective-permute-start(bf16[288,1152]{1,0:T(8,128)(2,1)} %dynamic-slice_bitcast_fusion.7), channel_id=1, source_target_pairs={{0,8},{4,12},{8,0},{12,4},{1,9},{5,13},{9,1},{13,5},{2,10},{6,14},... | collective-permute-start | bytes 1990664 | tf_op jit(solution)/shard_map/ppermute | solution.py:589
  999.2 17.1 %collective-permute-start.9 = (bf16[288,864]{1,0:T(8,128)(2,1)S(1)}, bf16[288,864]{1,0:T(8,128)(2,1)S(1)}, u32[]{:S(2)}, u32[]{:S(2)}) collective-permute-start(bf16[288,864]{1,0:T(8,128)(2,1)S(1)} %fusion.16), channel_id=1, source_target_pairs={{16,0},{17,1},{18,2},{19,3},{20,4},{21,5},{22,6},{23,7},{24,8},{25... | collective-permute-start | bytes 1493000 | tf_op jit(solution)/shard_map/ppermute | solution.py:610
  1012.6 20.0 %collective-permute-start.27 = (bf16[288,1152]{1,0:T(8,128)(2,1)}, bf16[288,1152]{1,0:T(8,128)(2,1)}, u32[]{:S(2)}, u32[]{:S(2)}) collective-permute-start(bf16[288,1152]{1,0:T(8,128)(2,1)} %fusion.12), channel_id=1, source_target_pairs={{16,0},{17,1},{18,2},{19,3},{20,4},{21,5},{22,6},{23,7},{24,8},{25... | collective-permute-start | bytes 1990664 | tf_op jit(solution)/shard_map/ppermute | solution.py:610
  1015.0 30.3 %collective-permute-start.21 = (bf16[288,1152]{1,0:T(8,128)(2,1)}, bf16[288,1152]{1,0:T(8,128)(2,1)}, u32[]{:S(2)}, u32[]{:S(2)}) collective-permute-start(bf16[288,1152]{1,0:T(8,128)(2,1)} %fusion.14), channel_id=1, source_target_pairs={{16,0},{17,1},{18,2},{19,3},{20,4},{21,5},{22,6},{23,7},{24,8},{25... | collective-permute-start | bytes 1990664 | tf_op jit(solution)/shard_map/ppermute | solution.py:610
  (74 other events, 880.9 us)
Sparse Core Ops, SparseCore 0:
  29.6 23.8 all-gather.16
  55.7 25.7 all-gather.10
  83.6 25.7 all-gather.8
  250.1 33.7 reduce-scatter.9
  286.0 36.0 all-gather.12
  343.0 47.8 reduce-scatter.11
  473.0 67.8 all-gather.14
  656.6 27.2 reduce-scatter.13
  687.7 34.0 reduce-scatter.19
  725.4 36.7 reduce-scatter.15
  829.6 69.2 reduce-scatter.21
  902.5 49.1 reduce-scatter.17

commit v2 on v1

v2 whole, which is shorter than its diff:
```python
import functools
import math

import jax
import jax.numpy as jnp
from jax import lax
from jax.experimental import pallas as pl
from jax.experimental.pallas import tpu as pltpu
from jax.sharding import PartitionSpec as P

HEAD_WIDTH = 72
HEAD_LANES = 128
IMAGES_PER_ROW = 3
NORM_EPS = 1e-06
COSINE_EPS = 1e-06
MASKED_SCORE = -1e30
HIGHEST = lax.Precision.HIGHEST
MESH = pl.DeviceIdType.MESH
F32 = jnp.float32
BF16 = jnp.bfloat16
NN = (((1,), (0,)), ((), ()))
NT = (((1,), (1,)), ((), ()))
TN = (((0,), (0,)), ((), ()))


def dot(left, right, form=NN):
    return lax.dot_general(left, right, form, preferred_element_type=F32)


def z_peers(count):
    me = lax.axis_index("tensor")
    return [{"tensor": lax.rem(me + step, count)} for step in range(1, count)]


def x_peer():
    return {"section": 1 - lax.axis_index("section")}


def core_bit():
    return lax.rem(lax.axis_index("dp"), 2)


def y_bit():
    return lax.rem(lax.axis_index("dp") // 2, 2)


def core_peer():
    return {"dp": lax.axis_index("dp") + 1 - 2 * core_bit()}


def y_peer():
    return {"dp": lax.axis_index("dp") + 2 - 4 * y_bit()}


def greet(peers):
    barrier = pltpu.get_barrier_semaphore()
    for peer in peers:
        pl.semaphore_signal(barrier, inc=1, device_id=peer, device_id_type=MESH)
    pl.semaphore_wait(barrier, len(peers))


def remote(source, target, send_sem, recv_sem, peer):
    copy = pltpu.make_async_remote_copy(
        src_ref=source,
        dst_ref=target,
        send_sem=send_sem,
        recv_sem=recv_sem,
        device_id=peer,
        device_id_type=MESH,
    )
    copy.start()
    return copy


def local(source, target, sem):
    copy = pltpu.make_async_copy(source, target, sem)
    copy.start()
    return copy


def own_rows(me, length):
    return pl.ds(pl.multiple_of(me * length, 16), length)


def start_gather(full, length, count, sems):
    mine = full.at[:, own_rows(lax.axis_index("tensor"), length)]
    return [
        remote(mine, mine, sems[0].at[step], sems[1].at[step], peer)
        for step, peer in enumerate(z_peers(count))
    ]


def wait_all(copies):
    for copy in copies:
        copy.wait()


def scatter_sum(partial, length, count, buffers, sems):
    send_buf, recv_buf = buffers
    copies = []
    for step, peer in enumerate(z_peers(count)):
        term = partial(own_rows(peer["tensor"], length))
        send_buf[step] = term.astype(BF16).reshape(send_buf.shape[1:])
        copies.append(
            remote(send_buf.at[step], recv_buf.at[step], sems[2].at[step], sems[3].at[step], peer)
        )
    return copies, partial(own_rows(lax.axis_index("tensor"), length))


def finish_sum(copies, total, buffers):
    wait_all(copies)
    recv_buf = buffers[1]
    for step in range(recv_buf.shape[0]):
        total = total + recv_buf[step].reshape(total.shape).astype(F32)
    return total


def fetch(block, own_ref, other_ref, target, sem):
    mine = lax.axis_index("section") == block

    @pl.when(mine)
    def own_start():
        pltpu.make_async_copy(own_ref, target, sem).start()

    @pl.when(jnp.logical_not(mine))
    def other_start():
        pltpu.make_async_copy(other_ref, target, sem).start()

    return pltpu.make_async_copy(own_ref, target, sem)


def layer_norm(rows):
    centred = rows - jnp.mean(rows, axis=-1, keepdims=True)
    inverse = lax.rsqrt(jnp.mean(centred * centred, axis=-1, keepdims=True) + NORM_EPS)
    return centred * inverse, inverse


def norm_back(grad, normed, inverse):
    mean_grad = jnp.mean(grad, axis=-1, keepdims=True)
    mean_cross = jnp.mean(grad * normed, axis=-1, keepdims=True)
    return inverse * (grad - mean_grad - normed * mean_cross)


def token_mod(mod_ref, seg_ref, which):
    parts = []
    for row in range(seg_ref.shape[0]):
        seg = seg_ref[row]
        line = [
            mod_ref[which, pl.ds(row * IMAGES_PER_ROW + slot, 1), :]
            for slot in range(IMAGES_PER_ROW)
        ]
        value = line[-1]
        for slot in range(IMAGES_PER_ROW - 2, -1, -1):
            value = jnp.where(seg == slot, line[slot], value)
        parts.append(value)
    return jnp.concatenate(parts, axis=0)


def slot_sums(value, seg_ref, out_ref, which):
    length = seg_ref.shape[1]
    lines = []
    for row in range(seg_ref.shape[0]):
        seg = seg_ref[row]
        piece = value[row * length : (row + 1) * length]
        for slot in range(IMAGES_PER_ROW):
            lines.append(jnp.sum(jnp.where(seg == slot, piece, 0.0), axis=0, keepdims=True))
    spare = out_ref.shape[1] - len(lines)
    lines.append(jnp.zeros((spare, value.shape[1]), F32))
    out_ref[which] = jnp.concatenate(lines, axis=0)


def flat(ref):
    return ref[...].reshape(-1, ref.shape[-1])


def spread_matrix(width):
    lanes = width // HEAD_WIDTH * HEAD_LANES
    source = lax.broadcasted_iota(jnp.int32, (width, lanes), 0)
    target = lax.broadcasted_iota(jnp.int32, (width, lanes), 1)
    within = target & (HEAD_LANES - 1)
    head = target >> (HEAD_LANES.bit_length() - 1)
    hit = (within < HEAD_WIDTH) & (source == head * HEAD_WIDTH + within)
    return jnp.where(hit, 1.0, 0.0).astype(BF16)


def gelu_tanh(pre):
    inner = math.sqrt(2.0 / math.pi) * (pre + 0.044715 * (pre * pre * pre))
    return 0.5 * pre * (1.0 + jnp.tanh(inner))


def gelu_slope(pre):
    scale = math.sqrt(2.0 / math.pi)
    square = pre * pre
    tanh = jnp.tanh(scale * (pre + 0.044715 * (pre * square)))
    return 0.5 * (1.0 + tanh) + 0.5 * pre * (1.0 - tanh * tanh) * scale * (
        1.0 + 3 * 0.044715 * square
    )


def silu(value):
    return value / (1.0 + jnp.exp(-value))


class Share:
    def __init__(self, own, other, parts, sems):
        self.own, self.other, self.parts = own, other, parts
        self.send, self.recv = sems
        self.size = own.shape[0] // parts
        self.copies = []

    def rows(self, core, y):
        part = core if self.parts == 2 else core + 2 * y
        return pl.ds(pl.multiple_of(part * self.size, 16), self.size)

    def begin(self):
        rows = self.rows(core_bit(), y_bit())
        self.first = remote(
            self.own.at[rows], self.other.at[rows], self.send.at[0], self.recv.at[0], x_peer()
        )

    def forward(self):
        self.first.wait()
        mine = self.other.at[self.rows(core_bit(), y_bit())]
        self.copies.append(remote(mine, mine, self.send.at[1], self.recv.at[1], core_peer()))
        if self.parts == 4:
            self.second = remote(mine, mine, self.send.at[2], self.recv.at[2], y_peer())

    def forward_again(self):
        if self.parts == 4:
            self.second.wait()
            got = self.other.at[self.rows(core_bit(), 1 - y_bit())]
            self.copies.append(remote(got, got, self.send.at[3], self.recv.at[3], core_peer()))

    def finish(self):
        wait_all(self.copies)


class Courier:
    def __init__(self, grad, out, scratch):
        self.grad, self.out = grad, out
        self.keep, self.from_core, self.from_y, self.part, self.from_x, self.sems = scratch
        self.size = grad.shape[-2] // 4

    def rows(self, core, y):
        part = pl.ds(pl.multiple_of((core + 2 * y) * self.size, 16), self.size)
        return self.grad.at[:, part] if len(self.grad.shape) == 3 else self.grad.at[part]

    def begin(self):
        core, self.copies = core_bit(), []
        for y in range(2):
            self.copies.append(
                remote(
                    self.rows(1 - core, y), self.from_core.at[y],
                    self.sems.at[0, y], self.sems.at[1, y], core_peer(),
                )
            )
            self.copies.append(local(self.rows(core, y), self.keep.at[y], self.sems.at[2, y]))

    def to_y(self):
        wait_all(self.copies)
        for y in range(2):
            self.keep[y] = (self.keep[y].astype(F32) + self.from_core[y].astype(F32)).astype(BF16)
        self.copies = [
            remote(
                self.keep.at[1 - y_bit()], self.from_y,
                self.sems.at[0, 2], self.sems.at[1, 2], y_peer(),
            )
        ]

    def to_x(self):
        wait_all(self.copies)
        mine = self.keep[y_bit()].astype(F32) + self.from_y[...].astype(F32)
        self.part[...] = mine.astype(BF16)
        self.copies = [
            remote(self.part, self.from_x, self.sems.at[0, 3], self.sems.at[1, 3], x_peer())
        ]

    def finish(self):
        wait_all(self.copies)
        self.out[...] = self.part[...].astype(F32) + self.from_x[...].astype(F32)


COURIER_REFS = 6


def quarter(shape):
    return shape[:-2] + (shape[-2] // 4, shape[-1])


def courier_scratch(shape):
    part = quarter(shape)
    return [
        pltpu.VMEM((2,) + part, BF16),
        pltpu.VMEM((2,) + part, BF16),
        pltpu.VMEM(part, BF16),
        pltpu.VMEM(part, BF16),
        pltpu.VMEM(part, BF16),
        pltpu.SemaphoreType.DMA((3, 4)),
    ]


def make_couriers(grads, outs, scratch):
    return [
        Courier(grad, out, scratch[COURIER_REFS * i : COURIER_REFS * (i + 1)])
        for i, (grad, out) in enumerate(zip(grads, outs))
    ]


def courier_peers(couriers):
    return [core_peer(), y_peer(), x_peer()] if couriers else []


def attend_body(
    count, peers, u_ref, mods, segs, biases, outs, scratch, sems, need_qkv, need_out, steps
):
    middle_ref, branch_ref, full_ref, q_ref, k_ref, v_ref, probs_ref, mixed_ref = outs
    full, wqkv, wo, mixed_wide = scratch[:4]
    buffers = scratch[4:6]
    seg_own, seg_col, seg_row = segs
    mod_ref = mods()
    me = lax.axis_index("tensor")
    rows, length, width = u_ref.shape
    heads_width = wo.shape[0]
    heads = heads_width // HEAD_WIDTH
    u = flat(u_ref).astype(F32)
    normed, unused = layer_norm(u)
    attn_in = normed * (1.0 + token_mod(mod_ref, seg_own, 1)) + token_mod(mod_ref, seg_own, 0)
    full[:, own_rows(me, length), :] = attn_in.astype(BF16).reshape(rows, length, width)
    if peers is not None:
        greet(peers)
    gather = start_gather(full, length, count, sems)
    steps[0]()
    spread = spread_matrix(heads_width)
    need_qkv()
    wait_all(gather)
    full_ref[...] = full[...]
    tokens = flat(full)
    bias = biases()
    for which, target in ((0, q_ref), (1, k_ref), (2, v_ref)):
        projected = dot(tokens, wqkv[pl.ds(which * width, width), :])
        if which != 1:
            projected = projected + bias[which // 2 : which // 2 + 1, :heads_width]
        target[...] = dot(projected.astype(BF16), spread).astype(BF16).reshape(target.shape)

    def one_head(index, carry):
        row = index // heads
        head = lax.rem(index, heads)
        lanes = pl.ds(pl.multiple_of(head * HEAD_LANES, HEAD_LANES), HEAD_LANES)
        scores = dot(q_ref[row, :, lanes], k_ref[row, :, lanes], NT) * HEAD_WIDTH ** (-0.5)
        scores = jnp.where(seg_col[row] == seg_row[row], scores, MASKED_SCORE)
        raised = jnp.exp(scores - jnp.max(scores, axis=-1, keepdims=True))
        probs = raised / jnp.sum(raised, axis=-1, keepdims=True)
        probs_ref[index] = probs
        mixed_wide[row, :, lanes] = dot(probs.astype(BF16), v_ref[row, :, lanes]).astype(BF16)
        return carry

    lax.fori_loop(0, rows * heads, one_head, 0)
    mixed_ref[...] = dot(flat(mixed_wide), spread, NT).astype(BF16).reshape(mixed_ref.shape)
    need_out()

    def partial(which_rows):
        return dot(mixed_ref[:, which_rows, :].reshape(rows * length, heads_width), wo[...])

    copies, total = scatter_sum(partial, length, count, buffers, sems)
    steps[1]()
    branch = finish_sum(copies, total, buffers) + bias[2:3, :]
    branch_ref[...] = branch.reshape(branch_ref.shape)
    middle = flat(u_ref).astype(F32) + token_mod(mod_ref, seg_own, 2) * branch
    middle_ref[...] = middle.reshape(middle_ref.shape)


def nothing():
    pass


def open_kernel(count, sections, *refs):
    u_ref, cond_ref, ada_b_ref, biases_ref, seg_own, seg_col, seg_row = refs[:7]
    ada_w, own_qkv, own_out, own_one, own_two = refs[7:12]
    mods_ref, bias_ref, other_qkv, other_out, other_one, other_two = refs[12:18]
    outs = refs[18:26]
    scratch = refs[26:32]
    ada, mod_src, mod_buf, bias_buf, w_sem, ag_send, ag_recv, rs_send, rs_recv = refs[32:41]
    mod_send, mod_recv, share_send, share_recv, ada_sem = refs[41:]
    wqkv, wo = scratch[1:3]
    section, tensor = lax.axis_index("section"), lax.axis_index("tensor")
    load_ada = local(ada_w, ada, ada_sem)
    shares = [
        Share(own, other, parts, (share_send.at[i], share_recv.at[i]))
        for i, (own, other, parts) in enumerate(
            (
                (own_qkv, other_qkv, 4), (own_out, other_out, 2),
                (own_one, other_one, 4), (own_two, other_two, 4),
            )
        )
    ]
    plane = [
        {"section": lax.rem(section + a, sections), "tensor": lax.rem(tensor + b, count)}
        for a in range(sections)
        for b in range(count)
        if a or b
    ]
    greet(plane + [core_peer(), y_peer()])
    for share in shares:
        share.begin()
    bias_buf[section] = biases_ref[...]
    bias_copy = remote(
        biases_ref, bias_buf.at[section],
        mod_send.at[len(plane)], mod_recv.at[len(plane)], x_peer(),
    )
    cond_act = silu(cond_ref[...].astype(F32)).astype(BF16)
    load_ada.wait()
    mod = dot(cond_act, ada[...]) + ada_b_ref[...].astype(F32)
    mod_src[...] = mod.reshape(mod_src.shape)
    mod_buf[section, tensor] = mod_src[section]
    copies = [
        remote(
            mod_src.at[peer["section"]], mod_buf.at[section, tensor],
            mod_send.at[i], mod_recv.at[i], peer,
        )
        for i, peer in enumerate(plane)
    ]

    def mods():
        wait_all(copies)
        width, piece = mods_ref.shape[-1], mod_buf.shape[-1]
        for block in range(sections):
            for which in range(6):
                parts, at = [], which * width
                while at < (which + 1) * width:
                    end = min((at // piece + 1) * piece, (which + 1) * width)
                    start = at - at // piece * piece
                    parts.append(mod_buf[block, at // piece][:, start : start + end - at])
                    at = end
                mods_ref[block, which] = (
                    jnp.concatenate(parts, axis=1) if len(parts) > 1 else parts[0]
                )
        return mods_ref.at[0]

    def biases():
        bias_copy.wait()
        bias_ref[...] = bias_buf[...]
        return bias_buf[0]

    def need_qkv():
        fetch(0, own_qkv, other_qkv, wqkv, w_sem.at[0]).wait()

    def need_out():
        fetch(0, own_out, other_out, wo, w_sem.at[1]).wait()

    def after_gather():
        shares[0].forward()
        shares[1].forward()
        shares[0].forward_again()
        shares[2].forward()
        shares[0].finish()
        shares[1].finish()

    def after_scatter():
        shares[2].forward_again()
        shares[3].forward()
        shares[3].forward_again()

    attend_body(
        count, None, u_ref, mods, (seg_own, seg_col, seg_row), biases, outs, scratch,
        (ag_send, ag_recv, rs_send, rs_recv), need_qkv, need_out, (after_gather, after_scatter),
    )
    shares[2].finish()
    shares[3].finish()


def attend_kernel(count, block, *refs):
    u_ref, mods_ref, bias_ref, seg_own, seg_col, seg_row = refs[:6]
    own_qkv, other_qkv, own_out, other_out = refs[6:10]
    outs, scratch, w_sem = refs[10:18], refs[18:24], refs[24]
    load_qkv = fetch(block, own_qkv, other_qkv, scratch[1], w_sem.at[0])
    load_out = fetch(block, own_out, other_out, scratch[2], w_sem.at[1])
    attend_body(
        count, z_peers(count), u_ref, lambda: mods_ref.at[block], (seg_own, seg_col, seg_row),
        lambda: bias_ref[block], outs, scratch, refs[25:29],
        load_qkv.wait, load_out.wait, (nothing, nothing),
    )


def mlp_kernel(
    count, block,
    middle_ref, mods_ref, bias_ref, seg_own, w1_own, w1_other, w2_own, w2_other,
    out_ref, branch_ref, full_ref, pre_ref, act_ref,
    full, w1, w2, send_buf, recv_buf, w_sem, *sems,
):
    me = lax.axis_index("tensor")
    rows, length, width = middle_ref.shape
    mod_ref = mods_ref.at[block]
    load_one = fetch(block, w1_own, w1_other, w1, w_sem.at[0])
    load_two = fetch(block, w2_own, w2_other, w2, w_sem.at[1])
    normed, unused = layer_norm(flat(middle_ref))
    mlp_in = normed * (1.0 + token_mod(mod_ref, seg_own, 4)) + token_mod(mod_ref, seg_own, 3)
    full[:, own_rows(me, length), :] = mlp_in.astype(BF16).reshape(rows, length, width)
    greet(z_peers(count))
    gather = start_gather(full, length, count, sems)
    load_one.wait()
    wait_all(gather)
    full_ref[...] = full[...]
    pre = dot(flat(full), w1[...]) + bias_ref[block, 3:4, : w1.shape[1]]
    pre_ref[...] = pre.reshape(pre_ref.shape)
    act_ref[...] = gelu_tanh(pre).astype(BF16).reshape(act_ref.shape)
    load_two.wait()

    def partial(which_rows):
        return dot(act_ref[:, which_rows, :].reshape(rows * length, -1), w2[...])

    buffers = (send_buf, recv_buf)
    copies, total = scatter_sum(partial, length, count, buffers, sems)
    branch = finish_sum(copies, total, buffers) + bias_ref[block, 4:5, :]
    branch_ref[...] = branch.reshape(branch_ref.shape)
    out = flat(middle_ref) + token_mod(mod_ref, seg_own, 5) * branch
    out_ref[...] = out.astype(BF16).reshape(out_ref.shape)


def mlp_back_kernel(count, block, loads, *refs):
    g_ref, middle_ref, branch_ref, mods_ref, seg_own, full_ref, pre_ref, act_ref = refs[:8]
    w1_own, w1_other, w2_own, w2_other = refs[8:12]
    grads, refs = refs[12 : 12 + loads], refs[12 + loads :]
    d_middle_ref, d_mod_ref, d_w1_ref, d_w2_ref, d_b1_ref, d_b2_ref = refs[:6]
    sums, refs = refs[6 : 6 + loads], refs[6 + loads :]
    full, d_pre, w1, w2, send_buf, recv_buf, w_sem = refs[:7]
    sems, couriers = refs[7:11], make_couriers(grads, sums, refs[11:])
    me = lax.axis_index("tensor")
    rows, length, width = middle_ref.shape
    mod_ref = mods_ref.at[block]
    load_one = fetch(block, w1_own, w1_other, w1, w_sem.at[0])
    load_two = fetch(block, w2_own, w2_other, w2, w_sem.at[1])
    g = flat(g_ref).astype(F32)
    d_branch = (g * token_mod(mod_ref, seg_own, 5)).astype(BF16)
    full[:, own_rows(me, length), :] = d_branch.reshape(rows, length, width)
    greet(z_peers(count) + courier_peers(couriers))
    gather = start_gather(full, length, count, sems)
    for courier in couriers:
        courier.begin()
    slot_sums(g * flat(branch_ref), seg_own, d_mod_ref, 2)
    for courier in couriers:
        courier.to_y()
    load_two.wait()
    wait_all(gather)
    d_act = dot(flat(full), w2[...], NT)
    d_pre[...] = (d_act * gelu_slope(flat(pre_ref))).astype(BF16).reshape(d_pre.shape)
    load_one.wait()

    def partial(which_rows):
        return dot(d_pre[:, which_rows, :].reshape(rows * length, -1), w1[...], NT)

    buffers = (send_buf, recv_buf)
    copies, total = scatter_sum(partial, length, count, buffers, sems)
    for courier in couriers:
        courier.to_x()
    d_b2_ref[...] = jnp.sum(flat(full).astype(F32), axis=0, keepdims=True)
    d_b1_ref[...] = jnp.sum(flat(d_pre).astype(F32), axis=0, keepdims=True)
    d_w2_ref[...] = dot(flat(full), flat(act_ref), TN).astype(BF16)
    d_w1_ref[...] = dot(flat(full_ref), flat(d_pre), TN).astype(BF16)
    d_in = finish_sum(copies, total, buffers)
    normed, inverse = layer_norm(flat(middle_ref))
    d_middle = flat(g_ref).astype(F32) + norm_back(
        d_in * (1.0 + token_mod(mod_ref, seg_own, 4)), normed, inverse
    )
    d_middle_ref[...] = d_middle.reshape(d_middle_ref.shape)
    slot_sums(d_in, seg_own, d_mod_ref, 0)
    slot_sums(d_in * normed, seg_own, d_mod_ref, 1)
    for courier in couriers:
        courier.finish()


def attend_back_kernel(count, block, loads, *refs):
    d_middle_ref, u_ref, branch_ref, mods_ref, seg_own, full_ref = refs[:6]
    q_ref, k_ref, v_ref, probs_ref, mixed_ref = refs[6:11]
    wqkv_own, wqkv_other, wo_own, wo_other = refs[11:15]
    grads, refs = refs[15 : 15 + loads], refs[15 + loads :]
    d_in_ref, d_mod_ref, d_wqkv_ref, d_wo_ref, d_bqv_ref, d_bo_ref = refs[:6]
    sums, refs = refs[6 : 6 + loads], refs[6 + loads :]
    full, wide, narrow, wqkv, wo, send_buf, recv_buf, w_sem = refs[:8]
    sems, couriers = refs[8:12], make_couriers(grads, sums, refs[12:])
    me = lax.axis_index("tensor")
    rows, length, width = u_ref.shape
    heads_width = wo.shape[0]
    heads = heads_width // HEAD_WIDTH
    mod_ref = mods_ref.at[block]
    load_qkv = fetch(block, wqkv_own, wqkv_other, wqkv, w_sem.at[0])
    load_out = fetch(block, wo_own, wo_other, wo, w_sem.at[1])
    d_middle = flat(d_middle_ref)
    d_branch = (d_middle * token_mod(mod_ref, seg_own, 2)).astype(BF16)
    full[:, own_rows(me, length), :] = d_branch.reshape(rows, length, width)
    greet(z_peers(count) + courier_peers(couriers))
    gather = start_gather(full, length, count, sems)
    for courier in couriers:
        courier.begin()
    slot_sums(d_middle * flat(branch_ref), seg_own, d_mod_ref, 2)
    spread = spread_matrix(heads_width)
    for courier in couriers:
        courier.to_y()
    load_out.wait()
    wait_all(gather)
    d_mixed = dot(flat(full), wo[...], NT).astype(BF16)
    wide[3] = dot(d_mixed, spread).astype(BF16).reshape(wide.shape[1:])

    def one_head(index, carry):
        row = index // heads
        head = lax.rem(index, heads)
        lanes = pl.ds(pl.multiple_of(head * HEAD_LANES, HEAD_LANES), HEAD_LANES)
        grad = wide[3, row, :, lanes]
        probs = probs_ref[index]
        d_probs = dot(grad, v_ref[row, :, lanes], NT)
        d_scores = (
            probs * (d_probs - jnp.sum(d_probs * probs, axis=-1, keepdims=True))
        ).astype(BF16)
        scale = HEAD_WIDTH ** (-0.5)
        wide[0, row, :, lanes] = (dot(d_scores, k_ref[row, :, lanes]) * scale).astype(BF16)
        wide[1, row, :, lanes] = (dot(d_scores, q_ref[row, :, lanes], TN) * scale).astype(BF16)
        wide[2, row, :, lanes] = dot(probs.astype(BF16), grad, TN).astype(BF16)
        return carry

    lax.fori_loop(0, rows * heads, one_head, 0)
    for which in range(3):
        narrow[which] = (
            dot(flat(wide.at[which]), spread, NT).astype(BF16).reshape(narrow.shape[1:])
        )
    load_qkv.wait()

    def partial(which_rows):
        total = 0.0
        for which in range(3):
            total = total + dot(
                narrow[which, :, which_rows, :].reshape(rows * length, heads_width),
                wqkv[pl.ds(which * width, width), :],
                NT,
            )
        return total

    buffers = (send_buf, recv_buf)
    copies, total = scatter_sum(partial, length, count, buffers, sems)
    for courier in couriers:
        courier.to_x()
    d_bo_ref[...] = jnp.sum(flat(full).astype(F32), axis=0, keepdims=True)
    d_bqv_ref[0:1, :] = jnp.sum(flat(narrow.at[0]).astype(F32), axis=0, keepdims=True)
    d_bqv_ref[1:2, :] = jnp.sum(flat(narrow.at[2]).astype(F32), axis=0, keepdims=True)
    d_wo_ref[...] = dot(flat(full), flat(mixed_ref), TN).astype(BF16)
    for which in range(3):
        d_wqkv_ref[which] = dot(flat(full_ref), flat(narrow.at[which]), TN).astype(BF16)
    d_attn_in = finish_sum(copies, total, buffers)
    normed, inverse = layer_norm(flat(u_ref).astype(F32))
    d_in = flat(d_middle_ref) + norm_back(
        d_attn_in * (1.0 + token_mod(mod_ref, seg_own, 1)), normed, inverse
    )
    d_in_ref[...] = d_in.reshape(d_in_ref.shape)
    slot_sums(d_attn_in, seg_own, d_mod_ref, 0)
    slot_sums(d_attn_in * normed, seg_own, d_mod_ref, 1)
    for courier in couriers:
        courier.finish()


def close_kernel(count, sections, replicas, *refs):
    outs_ref, grads_ref, mod_refs, small_refs = refs[:2], refs[2:4], refs[4:8], refs[8:17]
    cond_ref, wqkv_grad, wo_grad = refs[17:20]
    out_ref, grad_ref, ada_w_ref, ada_b_ref, small_ref, qkv_sum, wo_sum = refs[20:27]
    z_src, z_buf, mod_src, mod_buf, small_src, small_buf, cond_buf = refs[27:34]
    place_src, place_buf = refs[34:36]
    sems = refs[36:38]
    couriers = make_couriers((wqkv_grad, wo_grad), (qkv_sum, wo_sum), refs[38:])
    section, tensor, replica = (lax.axis_index(name) for name in ("section", "tensor", "dp"))
    send, recv = sems
    others = [
        {"section": lax.rem(section + a, sections), "dp": lax.rem(replica + b, replicas)}
        for a in range(sections)
        for b in range(replicas)
        if a or b
    ]
    greet(z_peers(count) + others)
    for courier in couriers:
        courier.begin()
    piece = z_src.shape[-1]
    for block in range(sections):
        attend_mod, mlp_mod = mod_refs[2 * block : 2 * block + 2]
        width = attend_mod.shape[-1]
        for part in range(count):
            at, end, cuts = part * piece, (part + 1) * piece, []
            while at < end:
                which = at // width
                stop = min((which + 1) * width, end)
                ref = attend_mod if which < 3 else mlp_mod
                cuts.append(ref[which % 3][:, at - which * width : stop - which * width])
                at = stop
            z_src[part, block] = jnp.concatenate(cuts, axis=1) if len(cuts) > 1 else cuts[0]
    z_copies = [
        remote(z_src.at[peer["tensor"]], z_buf.at[i], send.at[i], recv.at[i], peer)
        for i, peer in enumerate(z_peers(count))
    ]
    at = count - 1
    @pl.when(section == 0)
    def first_place():
        place_src[0] = outs_ref[1][...]
        place_src[1] = grads_ref[1][...].astype(BF16)

    @pl.when(section != 0)
    def second_place():
        place_src[0] = outs_ref[0][...]
        place_src[1] = grads_ref[0][...].astype(BF16)

    place_copy = remote(place_src, place_buf, send.at[at], recv.at[at], x_peer())
    at = at + 1
    heads_width = small_refs[0].shape[-1]
    small_src[...] = jnp.zeros_like(small_src)
    for block in range(sections):
        d_bqv, d_bo, d_b1, d_b2 = small_refs[4 * block : 4 * block + 4]
        small_src[block, 0:2, :heads_width] = d_bqv[...]
        small_src[block, 2:3, :] = d_bo[...]
        small_src[block, 3:4, : d_b1.shape[1]] = d_b1[...]
        small_src[block, 4:5, :] = d_b2[...]
        small_src[block, 5:8, :] = small_refs[8][...]
    small_buf[section, replica] = small_src[section]
    cond_buf[section, replica] = cond_ref[replica]
    copies = []
    for peer in others:
        copies.append(
            remote(
                small_src.at[peer["section"]], small_buf.at[section, replica],
                send.at[at], recv.at[at], peer,
            )
        )
        copies.append(
            remote(
                cond_ref.at[peer["dp"]], cond_buf.at[section, replica],
                send.at[at + 1], recv.at[at + 1], peer,
            )
        )
        at = at + 2
    for courier in couriers:
        courier.to_y()
    wait_all(z_copies)
    mine = z_src[tensor]
    for step in range(count - 1):
        mine = mine + z_buf[step]
    mod_src[...] = mine
    mod_buf[section, replica] = mod_src[section]
    for peer in others:
        copies.append(
            remote(
                mod_src.at[peer["section"]], mod_buf.at[section, replica],
                send.at[at], recv.at[at], peer,
            )
        )
        at = at + 1
    for courier in couriers:
        courier.to_x()
    place_copy.wait()
    rows = place_buf.shape[1]

    @pl.when(section == 0)
    def first_out():
        out_ref[:rows] = outs_ref[0][...]
        grad_ref[:rows] = grads_ref[0][...]
        out_ref[rows:] = place_buf[0]
        grad_ref[rows:] = place_buf[1].astype(F32)

    @pl.when(section != 0)
    def second_out():
        out_ref[rows:] = outs_ref[1][...]
        grad_ref[rows:] = grads_ref[1][...]
        out_ref[:rows] = place_buf[0]
        grad_ref[:rows] = place_buf[1].astype(F32)

    wait_all(copies)
    small = small_buf[0, 0]
    for a in range(sections):
        for b in range(replicas):
            if a or b:
                small = small + small_buf[a, b]
    small_ref[...] = small
    mod_all = flat(mod_buf)
    ada_b_ref[...] = jnp.sum(mod_all, axis=0, keepdims=True)
    ada_w_ref[...] = lax.dot_general(
        flat(cond_buf), mod_all, TN, precision=HIGHEST, preferred_element_type=F32
    )
    for courier in couriers:
        courier.finish()


VMEM = pl.BlockSpec(memory_space=pltpu.VMEM)
ANY = pl.BlockSpec(memory_space=pl.ANY)
MOD_ROWS = 8


def call(kernel, number, inputs, in_any, outs, out_any, scratch, flops):
    moved = sum(math.prod(one.shape) * one.dtype.itemsize for one in inputs)
    return pl.pallas_call(
        kernel,
        out_shape=[jax.ShapeDtypeStruct(shape, dtype) for shape, dtype in outs],
        in_specs=[VMEM] * (len(inputs) - in_any) + [ANY] * in_any,
        out_specs=[ANY if i in out_any else VMEM for i in range(len(outs))],
        scratch_shapes=scratch,
        compiler_params=pltpu.CompilerParams(
            collective_id=number, has_side_effects=True, vmem_limit_bytes=56 * 2**20
        ),
        cost_estimate=pl.CostEstimate(flops=flops, bytes_accessed=moved, transcendentals=0),
    )(*inputs)


def exchange_scratch(count, rows, length, width):
    return [
        pltpu.VMEM((count - 1, rows, length, width), BF16),
        pltpu.VMEM((count - 1, rows, length, width), BF16),
    ]


def semaphores(count):
    return [pltpu.SemaphoreType.DMA((2,))] + [pltpu.SemaphoreType.DMA((count - 1,))] * 4


class Shapes:
    def __init__(self, u, own, count):
        self.rows, self.length, self.width = u.shape
        self.count = count
        self.positions = self.length * count
        self.tokens = self.rows * self.positions
        self.heads_width = own["out"].shape[0]
        self.hidden = own["one"].shape[1]
        self.heads = self.heads_width // HEAD_WIDTH
        self.local = (self.rows, self.length, self.width)
        self.full = (self.rows, self.positions, self.width)
        self.wide = (self.rows, self.positions, self.heads * HEAD_LANES)
        self.own = own
        self.attend_outs = [
            (self.local, F32), (self.local, F32), (self.full, BF16),
            (self.wide, BF16), (self.wide, BF16), (self.wide, BF16),
            ((self.rows * self.heads, self.positions, self.positions), F32),
            ((self.rows, self.positions, self.heads_width), BF16),
        ]
        self.attend_scratch = [
            pltpu.VMEM(self.full, BF16),
            pltpu.VMEM(own["qkv"].shape, BF16),
            pltpu.VMEM(own["out"].shape, BF16),
            pltpu.VMEM(self.wide, BF16),
        ] + exchange_scratch(count, *self.local)
        self.mods = (3, MOD_ROWS, self.width)


def pairs(own, other, names):
    out = []
    for name in names:
        out += [own[name], other[name]]
    return out


def open_forward(sizes, u, cond, ada_w, ada_b, biases, segs, own, sections):
    count, width = sizes.count, sizes.width
    piece = ada_w.shape[1]
    inputs = [u, cond, ada_b, biases, *segs, ada_w] + [own[n] for n in ("qkv", "out", "one", "two")]
    plane = sections * count - 1
    results = call(
        functools.partial(open_kernel, count, sections),
        0,
        inputs,
        5,
        [((sections, 6, MOD_ROWS, width), F32), ((sections,) + biases.shape, F32)]
        + [(own[n].shape, BF16) for n in ("qkv", "out", "one", "two")]
        + sizes.attend_outs,
        (2, 3, 4, 5),
        sizes.attend_scratch
        + [
            pltpu.VMEM(ada_w.shape, BF16),
            pltpu.VMEM((sections, MOD_ROWS, piece), F32),
            pltpu.VMEM((sections, count, MOD_ROWS, piece), F32),
            pltpu.VMEM((sections,) + biases.shape, F32),
        ]
        + semaphores(count)
        + [
            pltpu.SemaphoreType.DMA((plane + 1,)),
            pltpu.SemaphoreType.DMA((plane + 1,)),
            pltpu.SemaphoreType.DMA((4, 4)),
            pltpu.SemaphoreType.DMA((4, 4)),
            pltpu.SemaphoreType.DMA,
        ],
        2 * sizes.tokens * width * sizes.heads_width * 4,
    )
    other = dict(zip(("qkv", "out", "one", "two"), results[2:6]))
    return results[0], results[1], other, results[6:]


def attend_forward(sizes, block, u, mods, biases, segs, own, other):
    inputs = [u, mods, biases, *segs] + pairs(own, other, ("qkv", "out"))
    return call(
        functools.partial(attend_kernel, sizes.count, block),
        1,
        inputs,
        4,
        sizes.attend_outs,
        (),
        sizes.attend_scratch + semaphores(sizes.count),
        2 * sizes.tokens * sizes.width * sizes.heads_width * 4,
    )


def mlp_forward(sizes, block, middle, mods, biases, segs, own, other):
    inputs = [middle, mods, biases, segs[0]] + pairs(own, other, ("one", "two"))
    hidden = (sizes.rows, sizes.positions, sizes.hidden)
    return call(
        functools.partial(mlp_kernel, sizes.count, block),
        2 + block,
        inputs,
        4,
        [
            (sizes.local, BF16), (sizes.local, F32), (sizes.full, BF16),
            (hidden, F32), (hidden, BF16),
        ],
        (),
        [
            pltpu.VMEM(sizes.full, BF16),
            pltpu.VMEM(own["one"].shape, BF16),
            pltpu.VMEM(own["two"].shape, BF16),
        ]
        + exchange_scratch(sizes.count, *sizes.local)
        + semaphores(sizes.count),
        2 * sizes.tokens * sizes.width * sizes.hidden * 2,
    )


def mlp_backward(sizes, block, g, attend, mlp, mods, segs, own, other, loads):
    out, branch, full, pre, act = mlp
    inputs = [g, attend[0], branch, mods, segs[0], full, pre, act]
    inputs += pairs(own, other, ("one", "two")) + list(loads)
    carried = [scratch for load in loads for scratch in courier_scratch(load.shape)]
    return call(
        functools.partial(mlp_back_kernel, sizes.count, block, len(loads)),
        4 + block,
        inputs,
        4 + len(loads),
        [
            (sizes.local, F32), (sizes.mods, F32),
            ((sizes.width, sizes.hidden), BF16), ((sizes.width, sizes.hidden), BF16),
            ((1, sizes.hidden), F32), ((1, sizes.width), F32),
        ]
        + [(quarter(load.shape), F32) for load in loads],
        (),
        [
            pltpu.VMEM(sizes.full, BF16),
            pltpu.VMEM((sizes.rows, sizes.positions, sizes.hidden), BF16),
            pltpu.VMEM(own["one"].shape, BF16),
            pltpu.VMEM(own["two"].shape, BF16),
        ]
        + exchange_scratch(sizes.count, *sizes.local)
        + semaphores(sizes.count)
        + carried,
        2 * sizes.tokens * sizes.width * sizes.hidden * 4,
    )


def attend_backward(sizes, block, d_middle, u, attend, mods, segs, own, other, loads):
    middle, branch, full, q, k, v, probs, mixed = attend
    inputs = [d_middle, u, branch, mods, segs[0], full, q, k, v, probs, mixed]
    inputs += pairs(own, other, ("qkv", "out")) + list(loads)
    carried = [scratch for load in loads for scratch in courier_scratch(load.shape)]
    return call(
        functools.partial(attend_back_kernel, sizes.count, block, len(loads)),
        6 + block,
        inputs,
        4 + len(loads),
        [
            (sizes.local, F32), (sizes.mods, F32),
            ((3, sizes.width, sizes.heads_width), BF16), ((sizes.width, sizes.heads_width), BF16),
            ((2, sizes.heads_width), F32), ((1, sizes.width), F32),
        ]
        + [(quarter(load.shape), F32) for load in loads],
        (),
        [
            pltpu.VMEM(sizes.full, BF16),
            pltpu.VMEM((4,) + sizes.wide, BF16),
            pltpu.VMEM((3, sizes.rows, sizes.positions, sizes.heads_width), BF16),
            pltpu.VMEM(own["qkv"].shape, BF16),
            pltpu.VMEM(own["out"].shape, BF16),
        ]
        + exchange_scratch(sizes.count, *sizes.local)
        + semaphores(sizes.count)
        + carried,
        2 * sizes.tokens * sizes.width * sizes.heads_width * 8,
    )


def close_backward(sizes, outs, grads, mod_grads, small, proj_small, cond, loads, sections, replicas):
    count, width = sizes.count, sizes.width
    piece = 6 * width // count
    share = width // replicas
    inputs = [*outs, *grads, *mod_grads, *small, proj_small, cond, *loads]
    copies = count + 3 * (sections * replicas - 1)
    carried = [scratch for load in loads for scratch in courier_scratch(load.shape)]
    both = (sections * sizes.rows,) + sizes.local[1:]
    return call(
        functools.partial(close_kernel, count, sections, replicas),
        8,
        inputs,
        len(loads),
        [
            (both, BF16), (both, F32), ((share, piece), F32), ((1, piece), F32),
            ((MOD_ROWS, width), F32),
        ]
        + [(quarter(load.shape), F32) for load in loads],
        (),
        [
            pltpu.VMEM((count, sections, MOD_ROWS, piece), F32),
            pltpu.VMEM((count - 1, sections, MOD_ROWS, piece), F32),
            pltpu.VMEM((sections, MOD_ROWS, piece), F32),
            pltpu.VMEM((sections, replicas, MOD_ROWS, piece), F32),
            pltpu.VMEM((sections, MOD_ROWS, width), F32),
            pltpu.VMEM((sections, replicas, MOD_ROWS, width), F32),
            pltpu.VMEM((sections, replicas, MOD_ROWS, share), F32),
            pltpu.VMEM((2,) + sizes.local, BF16),
            pltpu.VMEM((2,) + sizes.local, BF16),
            pltpu.SemaphoreType.DMA((copies,)),
            pltpu.SemaphoreType.DMA((copies,)),
        ]
        + carried,
        2 * sections * replicas * MOD_ROWS * share * piece,
    )


def act_grad(function, source_rows, upstream):
    unused_value, pullback = jax.vjp(function, source_rows)
    return pullback(upstream)[0]


def gather_rows(source_rows):
    return lax.all_gather(source_rows, "tensor", axis=0, tiled=True)


def scatter_rows(terms):
    return lax.psum_scatter(
        terms.astype(BF16), "tensor", scatter_dimension=0, tiled=True
    ).astype(F32)


def align_pass(sent_rows, target_cols, proj_weights, total_token_count):
    p1_w, p1_b, p2_w, p2_b, p3_w, p3_b = proj_weights
    input_full = gather_rows(sent_rows)
    first_pre = dot(input_full, p1_w) + p1_b.astype(F32)
    first_act = jax.nn.silu(first_pre).astype(BF16)
    second_pre = scatter_rows(dot(first_act, p2_w)) + p2_b.astype(F32)
    second_act = jax.nn.silu(second_pre).astype(BF16)
    second_full = gather_rows(second_act)
    predicted = dot(second_full, p3_w) + p3_b.astype(F32)
    pred_sq, cross, target_sq = lax.psum(
        jnp.stack(
            [
                jnp.sum(predicted * predicted, axis=1),
                jnp.sum(predicted * target_cols, axis=1),
                jnp.sum(target_cols * target_cols, axis=1),
            ]
        ),
        "tensor",
    )
    inv_pred = lax.rsqrt(pred_sq + COSINE_EPS)
    inv_target = lax.rsqrt(target_sq + COSINE_EPS)
    cosine = cross * inv_pred * inv_target
    loss_local = jnp.sum(cosine)
    factor = -0.5 / total_token_count
    grad_pred = (
        (factor * inv_pred * inv_target)[:, None] * target_cols
        - (factor * cosine * inv_pred * inv_pred)[:, None] * predicted
    ).astype(BF16)
    grad_p3_b = jnp.sum(grad_pred.astype(F32), axis=0)
    grad_p3_w = dot(second_full, grad_pred, TN)
    grad_second_act = scatter_rows(dot(grad_pred, p3_w, NT))
    grad_second_pre = act_grad(jax.nn.silu, second_pre, grad_second_act).astype(BF16)
    grad_second_full = gather_rows(grad_second_pre)
    grad_p2_b = jnp.sum(grad_second_full.astype(F32), axis=0)
    grad_p2_w = dot(grad_second_full, first_act, TN)
    grad_first_act = dot(grad_second_full, p2_w, NT)
    grad_first_pre = act_grad(jax.nn.silu, first_pre, grad_first_act).astype(BF16)
    grad_p1_b = jnp.sum(grad_first_pre.astype(F32), axis=0)
    grad_p1_w = dot(input_full, grad_first_pre, TN)
    grad_sent = scatter_rows(dot(grad_first_pre, p1_w, NT))
    return (
        loss_local,
        grad_sent,
        (grad_p1_w, grad_p2_w, grad_p3_w),
        (grad_p1_b, grad_p2_b, grad_p3_b),
    )


def halve(value, axis, bit, position):
    size = lax.axis_size(axis)
    mine = (lax.axis_index(axis) & bit) // bit
    keep = lax.dynamic_index_in_dim(value, mine, position, keepdims=False)
    give = lax.dynamic_index_in_dim(value, 1 - mine, position, keepdims=False)
    return keep + lax.ppermute(give, axis, [(i, i ^ bit) for i in range(size)])


def sum_beyond_quads(value):
    size = lax.axis_size("dp")
    if size == 4:
        return value
    quads = size // 4
    bits = quads.bit_length() - 1
    lead = value.ndim - 2
    shape = value.shape
    value = value.reshape(shape[:lead] + (2,) * bits + (shape[-2] // quads, shape[-1]))
    for bit in range(bits):
        value = halve(value, "dp", 4 << bit, lead + bits - 1 - bit)
    route = [(high * 4 + low, low * quads + high) for high in range(quads) for low in range(4)]
    return lax.ppermute(value, "dp", route)


def per_device(
    block_eight_input,
    cond,
    image_slot_index,
    targets,
    cot,
    ada_w,
    ada_b,
    query_key_value_weight,
    query_value_bias,
    attention_output_weight,
    attention_output_bias,
    hidden_weight,
    hidden_bias,
    output_weight_mlp,
    output_bias_mlp,
    p1_w,
    p1_b,
    p2_w,
    p2_b,
    p3_w,
    p3_b,
):
    section = lax.axis_index("section")
    tensor = lax.axis_index("tensor")
    is_first = section == 0
    count = lax.axis_size("tensor")
    sections = lax.axis_size("section")
    replicas = lax.axis_size("dp")
    length, replica_rows, width = block_eight_input.shape
    positions = length * count
    rows = replica_rows // sections
    total_token_count = positions * replica_rows * replicas
    heads_width = attention_output_weight.shape[1]
    hidden = hidden_weight.shape[2]

    def my_rows(value, axis):
        return lax.dynamic_slice_in_dim(value, section * rows, rows, axis)

    def to_rows(value):
        return jnp.transpose(my_rows(value, 1), (1, 0, 2))

    own = {
        "qkv": jnp.transpose(query_key_value_weight[0], (1, 0, 2)).reshape(3 * width, heads_width),
        "out": attention_output_weight[0],
        "one": hidden_weight[0],
        "two": output_weight_mlp[0],
    }

    def padded(value):
        return jnp.pad(value.astype(F32), ((0, 0), (0, width - value.shape[-1])))

    biases = jnp.concatenate(
        [
            padded(query_value_bias[0]), padded(attention_output_bias), padded(hidden_bias),
            padded(output_bias_mlp), jnp.zeros((MOD_ROWS - 5, width), F32),
        ],
        axis=0,
    )
    used = rows * IMAGES_PER_ROW
    cond_pad = jnp.pad(
        cond.reshape(sections, used, width), ((0, 0), (0, MOD_ROWS - used), (0, 0))
    )
    segs_full = my_rows(image_slot_index, 0)
    seg_own = lax.dynamic_slice_in_dim(segs_full, tensor * length, length, 1)
    segs = (seg_own[:, :, None], segs_full[:, :, None], segs_full[:, None, :])

    u = to_rows(block_eight_input)
    sizes = Shapes(u, own, count)
    mods, bias_all, other, attend_one = open_forward(
        sizes, u, cond_pad.reshape(-1, width), ada_w[0], ada_b, biases, segs, own, sections
    )
    mlp_one = mlp_forward(sizes, 0, attend_one[0], mods, bias_all, segs, own, other)
    first_out = mlp_one[0]
    attend_two = attend_forward(sizes, 1, first_out, mods, bias_all, segs, own, other)
    mlp_two = mlp_forward(sizes, 1, attend_two[0], mods, bias_all, segs, own, other)
    second_out = mlp_two[0]

    target_cols = my_rows(targets, 1).reshape(count, length, rows, -1)
    target_cols = jnp.transpose(target_cols, (0, 2, 1, 3)).reshape(rows * positions, -1)
    loss_local, grad_sent, proj_grads, proj_bias_grads = align_pass(
        first_out.reshape(rows * length, width),
        target_cols.astype(F32),
        (p1_w, p1_b, p2_w, p2_b, p3_w, p3_b),
        total_token_count,
    )

    back = (mods, segs, own, other)
    d_middle_two, mod_mlp_two, *mlp_grads_two = mlp_backward(
        sizes, 1, to_rows(cot), attend_two, mlp_two, *back, ()
    )
    second_grad, mod_attend_two, *attend_grads_two = attend_backward(
        sizes, 1, d_middle_two, first_out, attend_two, *back, mlp_grads_two[:2]
    )
    sums_mlp_two = attend_grads_two[4:]
    d_middle_one, mod_mlp_one, *mlp_grads_one = mlp_backward(
        sizes, 0, second_grad + grad_sent.reshape(rows, length, width), attend_one, mlp_one, *back,
        attend_grads_two[:2],
    )
    sums_attend_two = mlp_grads_one[4:]
    first_grad, mod_attend_one, *attend_grads_one = attend_backward(
        sizes, 0, d_middle_one, u, attend_one, *back, mlp_grads_one[:2]
    )
    sums_mlp_one = attend_grads_one[4:]

    p1_len, p2_len, p3_len = p1_b.shape[0], p2_b.shape[0], p3_b.shape[0]
    d_p1_b, d_p2_b, d_p3_b = proj_bias_grads
    flat_small = jnp.concatenate([d_p2_b, d_p1_b, d_p3_b, loss_local[None]])
    proj_small = jnp.pad(flat_small, (0, 3 * width - flat_small.shape[0])).reshape(3, width)
    cond_act = silu(my_rows(cond, 0).astype(F32)).astype(BF16).astype(F32)
    share = width // replicas
    cond_cols = jnp.pad(cond_act.reshape(used, width), ((0, MOD_ROWS - used), (0, 0)))
    cond_cols = jnp.transpose(cond_cols.reshape(MOD_ROWS, replicas, share), (1, 0, 2))
    small = [
        attend_grads_one[2], attend_grads_one[3], mlp_grads_one[2], mlp_grads_one[3],
        attend_grads_two[2], attend_grads_two[3], mlp_grads_two[2], mlp_grads_two[3],
    ]
    section_out, section_grad, grad_ada_w, grad_ada_b, small, *sums_attend_one = close_backward(
        sizes, (first_out, second_out), (first_grad, second_grad),
        (mod_attend_one, mod_mlp_one, mod_attend_two, mod_mlp_two),
        small, proj_small, cond_cols, attend_grads_one[:2], sections, replicas,
    )

    red_fc1, red_fc2, red_qkv, red_out = [
        sum_beyond_quads(jnp.where(is_first, one, two))
        for one, two in zip(
            list(sums_mlp_one) + list(sums_attend_one), list(sums_mlp_two) + list(sums_attend_two)
        )
    ]
    flat_small = small[5:8].reshape(-1)
    red_p2_b = flat_small[:p2_len]
    red_p1_b = flat_small[p2_len : p2_len + p1_len]
    red_p3_b = flat_small[p2_len + p1_len : p2_len + p1_len + p3_len]
    loss_total = flat_small[p2_len + p1_len + p3_len]
    align_loss = -0.5 * loss_total / total_token_count

    grad_p1_w, grad_p2_w, grad_p3_w = proj_grads
    red_p1_w, red_p2_w, red_p3_w = [
        lax.psum_scatter(value.astype(BF16), ("section", "dp"), scatter_dimension=0, tiled=True)
        for value in (grad_p1_w, grad_p2_w, grad_p3_w)
    ]
    return (
        jnp.transpose(section_out, (1, 0, 2))[None],
        jnp.transpose(section_grad, (1, 0, 2))[None],
        align_loss,
        grad_ada_w[None],
        grad_ada_b,
        jnp.transpose(red_qkv, (1, 0, 2))[None],
        small[0:2, :heads_width][None],
        red_out.T[None],
        small[2:3],
        red_fc1[None],
        small[3:4, :hidden],
        red_fc2.T[None],
        small[4:5],
        red_p1_w.astype(F32),
        red_p1_b,
        red_p2_w.T.astype(F32),
        red_p2_b,
        red_p3_w.astype(F32),
        red_p3_b,
    )


def solution(mesh):
    in_specs = (
        P("tensor", "dp", None),
        P("dp", None, None),
        P("dp", None),
        P(None, "dp", "tensor"),
        P("tensor", "dp", None),
        P("section", None, "tensor"),
        P("section", "tensor"),
        P("section", None, None, "tensor"),
        P("section", None, "tensor"),
        P("section", "tensor", None),
        P("section", None),
        P("section", None, "tensor"),
        P("section", "tensor"),
        P("section", "tensor", None),
        P("section", None),
        P(None, "tensor"),
        P("tensor"),
        P("tensor", None),
        P(),
        P(None, "tensor"),
        P("tensor"),
    )
    out_specs = (
        P("section", "tensor", "dp", None),
        P("section", "tensor", "dp", None),
        P(),
        P("section", "dp", "tensor"),
        P("section", "tensor"),
        P("section", "dp", None, "tensor"),
        P("section", None, "tensor"),
        P("section", "tensor", "dp"),
        P("section", None),
        P("section", "dp", "tensor"),
        P("section", "tensor"),
        P("section", "tensor", "dp"),
        P("section", None),
        P(("section", "dp"), "tensor"),
        P("tensor"),
        P("tensor", ("section", "dp")),
        P(),
        P(("section", "dp"), "tensor"),
        P("tensor"),
    )
    return jax.shard_map(
        per_device, mesh=mesh, in_specs=in_specs, out_specs=out_specs, check_vma=False
    )
```

time: 1060 us -> 845 us (0.80)
  local copies, waits for them, and re-layouts: 184 us -> 45.3 us
  Pallas kernels: 434 us -> 566 us
  blocking collectives: 129 us -> 33.5 us
  starting transfers between devices: 40.7 us -> 0.54 us
  waiting for transfers between devices: 170 us -> 134 us
  other arithmetic: 53.9 us -> 18.8 us
    pallas_call x8 -> x9, Pallas kernels: 434 us -> 566 us  [call(): pl.pallas_call(kernel, out_shape=[jax.ShapeDtypeStruct(shape, dtype) for...]
    ppermute x31 -> x0, waiting for transfers between devices: 106 us -> none  [the longest x23 83.6 us: swap(): return lax.ppermute(value, axis, [(i, i ^ bit) for i in range(size)])]
    all_gather x4 -> x0, blocking collectives: 70.2 us -> none  [the longest x1 34.5 us: per_device(): lax.all_gather(mod_local, ('section', 'tensor'), axis=0, tiled=False)]
    unnamed x174 -> x68, local copies, waits for them, and re-layouts: 87.9 us -> 23 us
    dynamic_slice x12 -> x0, local copies, waits for them, and re-layouts: 43.6 us -> none  [the longest x4 20.4 us: halve(): keep = lax.dynamic_index_in_dim(value, mine, position, keepdims=False)]
    ppermute x31 -> x0, starting transfers between devices: 39.6 us -> none  [the longest x23 20.4 us: swap(): return lax.ppermute(value, axis, [(i, i ^ bit) for i in range(size)])]
    all_gather x2, waiting for transfers between devices: 30.3 us -> 66.5 us  [gather_rows(): return lax.all_gather(source_rows, 'tensor', axis=0, tiled=True)]
    reduce_scatter x3, waiting for transfers between devices: 33.3 us -> 67.2 us  [scatter_rows(): lax.psum_scatter(terms.astype(BF16), 'tensor', scatter_dimension=0, tiled...]
  transfers between devices with their start and end apart: 43 -> 8, of which waited for: 14 -> 4; matrix products, arithmetic and copies ran while one was open for 21% -> 5% of each run, Pallas kernels for 37% -> 49%
where the time goes in v2:
time: 845 us; the launch traced here: 835 us
  Pallas kernels  566 us (67%)
  waiting for transfers between devices  134 us (16%)
  local copies, waits for them, and re-layouts  45.3 us (5%)
  blocking collectives  33.5 us (4%)
  matrix products  20.3 us (2%)
  other arithmetic  18.8 us (2%)
  between operations  16.8 us (2%)
    pallas_call x9, Pallas kernels, call(): pl.pallas_call(kernel, out_shape=[jax.ShapeDtypeStruct(shape, dtype) for...  566 us
    reduce_scatter x3, waiting for transfers between devices, scatter_rows(): lax.psum_scatter(terms.astype(BF16), 'tensor', scatter_dimension=0, tiled...  67.2 us
    all_gather x2, waiting for transfers between devices, gather_rows(): return lax.all_gather(source_rows, 'tensor', axis=0, tiled=True)  66.5 us
    all_gather x1, blocking collectives, gather_rows(): return lax.all_gather(source_rows, 'tensor', axis=0, tiled=True)  23.7 us
    unnamed x68, local copies, waits for them, and re-layouts  23 us
    dot_general x9, matrix products, dot(): return lax.dot_general(left, right, form, preferred_element_type=F32)  20.3 us
  transfers between devices with their start and end apart: 8, of which 4 were waited for; matrix products, arithmetic and copies ran while one was open for 5% of the time, Pallas kernels for 49%

profile of v2, /device:TPU:0, one launch (start us, length us, event | category | flops | bytes accessed | tf_op | source)
XLA Modules:
  0.0 835.5 jit_solution(14254814326794986345)
XLA Ops:
  14.5 2.3 constant_dynamic-slice_fusion
  17.5 4.2 copy.135
  21.7 6.5 copy.134
  28.8 114.3 %shard_map.348 = (f32[2,6,8,1152]{3,2,1,0:T(8,128)}, f32[2,8,1152]{2,1,0:T(8,128)}, bf16[3456,288]{1,0:T(8,128)(2,1)}, bf16[288,1152]{1,0:T(8,128)(2,1)}, bf16[1...) custom-call(bf16[2,48,1152]{2,1,0:T(8,128)(2,1)} %bitcast.98, ...), custom_call_target="tpu_custom_call" | custom-call | flops 1019215872 | bytes 12245760 | tf_op jit(solution)/shard_map/pallas_call | solution.py:791
  143.1 46.7 %shard_map.349 = (bf16[2,48,1152]{2,1,0:T(8,128)(2,1)}, f32[2,48,1152]{2,1,0:T(8,128)}, bf16[2,192,1152]{2,1,0:T(8,128)(2,1)}, f32[2,192,1152]{2,1,0:T(8,128)}, bf16[2,192,1152]{2,1,0:T(8,128)(2,1)}) custom-call(f32[2,48,1152]{2,1,0:T(8,128)} %get-tuple-element.88.middle_ref.refs_1_, f32[2,6,8,1152]{3,2,1,0:T(8,128)} %get-tuple-element.89.mods_ref.refs_1_.refs_3_, ...), custom_call_target="tpu_custom_call" | custom-call | flops 2038431744 | bytes 11575680 | tf_op jit(solution)/shard_map/pallas_call | solution.py:791
  189.9 23.7 %all_gather.9 = bf16[384,1152]{1,0:T(8,128)(2,1)S(1)} all-gather(bf16[96,1152]{1,0:T(8,128)(2,1)} %bitcast.95), channel_id=1, replica_groups=mesh['section'=2,'dp'=4,'tensor'=4] {'tensor'}, dimensions={0}, use_global_device_ids=true | all-gather | bytes 1105920 | tf_op jit(solution)/shard_map/all_gather | solution.py:1027
  213.6 0.9 copy-done.13
  215.2 0.9 copy-done.27
  216.1 2.2 convolution_convert_fusion.4
  218.9 33.4 %reduce-scatter.7.cloned.1.call-done = bf16[96,2048]{1,0:T(8,128)(2,1)} async-done(((bf16[384,2048]{1,0:T(8,128)(2,1)}), bf16[96,2048]{1,0:T(8,128)(2,1)}) %reduce-scatter.7.cloned.1.call-update) | async-done | bytes 393232 | tf_op jit(solution)/shard_map/reduce_scatter | solution.py:1031
  252.4 2.0 multiply_convert_fusion
  256.2 1.1 copy.146
  257.4 33.2 %all-gather.3.cloned.1.call-done = bf16[384,2048]{1,0:T(8,128)(2,1)} async-done(((bf16[96,2048]{1,0:T(8,128)(2,1)}), bf16[384,2048]{1,0:T(8,128)(2,1)}) %all-gather.3.cloned.1.call-update) | async-done | bytes 1572880 | tf_op jit(solution)/shard_map/all_gather | solution.py:1027
  290.6 2.8 multiply_reduce_fusion.2
  293.4 9.8 %psum.7 = f32[3,384]{1,0:T(4,128)S(1)} all-reduce(f32[3,384]{1,0:T(4,128)S(1)} %pad_maximum_fusion), channel_id=1, replica_groups=mesh['section'=2,'dp'=4,'tensor'=4] {'tensor'}, use_global_device_ids=true, to_apply=%region_4.5 | all-reduce | flops 1152 | bytes 9216 | tf_op jit(solution)/shard_map/psum | solution.py:1045
  303.9 1.1 convert_reduce_fusion.2
  305.0 1.7 convolution_convert_fusion.3
  306.8 33.7 %reduce-scatter.9.cloned.1.call-done = bf16[96,2048]{1,0:T(8,128)(2,1)} async-done(((bf16[384,2048]{1,0:T(8,128)(2,1)}), bf16[96,2048]{1,0:T(8,128)(2,1)}) %reduce-scatter.9.cloned.1.call-update) | async-done | bytes 393232 | tf_op jit(solution)/shard_map/reduce_scatter | solution.py:1031
  340.5 2.1 fusion.1
  342.7 2.9 convolution_convert_fusion.5
  345.6 33.2 %all-gather.5.cloned.1.call-done = bf16[384,2048]{1,0:T(8,128)(2,1)} async-done(((bf16[96,2048]{1,0:T(8,128)(2,1)}), bf16[384,2048]{1,0:T(8,128)(2,1)}) %all-gather.5.cloned.1.call-update) | async-done | bytes 1572880 | tf_op jit(solution)/shard_map/all_gather | solution.py:1027
  378.8 2.8 convert_reduce_fusion.1
  382.4 1.6 convolution_convert_fusion.2
  384.1 2.9 convolution_convert_fusion.1
  388.6 59.0 %shard_map.350 = (f32[2,48,1152]{2,1,0:T(8,128)}, f32[2,48,1152]{2,1,0:T(8,128)}, bf16[2,192,1152]{2,1,0:T(8,128)(2,1)}, bf16[2,192,512]{2,1,0:T(8,128)(2,1)}, b...) custom-call(bf16[2,48,1152]{2,1,0:T(8,128)(2,1)} %get-tuple-element., ...), custom_call_target="tpu_custom_call" | custom-call | flops 1019215872 | bytes 6049152 | tf_op jit(solution)/shard_map/pallas_call | solution.py:791
  447.6 50.5 %shard_map.351 = (bf16[2,48,1152]{2,1,0:T(8,128)(2,1)}, f32[2,48,1152]{2,1,0:T(8,128)}, bf16[2,192,1152]{2,1,0:T(8,128)(2,1)}, f32[2,192,1152]{2,1,0:T(8,128)}, bf16[2,192,1152]{2,1,0:T(8,128)(2,1)}) custom-call(f32[2,48,1152]{2,1,0:T(8,128)} %get-tuple-element.96.middle_ref.refs_1_, f32[2,6,8,1152]{3,2,1,0:T(8,128)} %get-tuple-element.89.mods_ref.refs_1_.refs_3_, ...), custom_call_target="tpu_custom_call" | custom-call | flops 2038431744 | bytes 11575680 | tf_op jit(solution)/shard_map/pallas_call | solution.py:791
  498.1 52.2 %shard_map.352 = (f32[2,48,1152]{2,1,0:T(8,128)}, f32[3,8,1152]{2,1,0:T(8,128)}, bf16[1152,1152]{1,0:T(8,128)(2,1)}, bf16[1152,1152]{1,0:T(8,128)(2,1)}, f32[1,1152]{1,0:T(1,128)}, /*index=5*/f32[1,1152]{1,0:T(1,128)}) custom-call(bf16[2,48,1152]{2,1,0:T(8,128)(2,1)} %bitcast.102, f32[2,48,1152]{2,1,0:T(8,128)} %get-tuple-element.96.middle_ref.refs_1_, ...), custom_call_target="tpu_custom_call" | custom-call | flops 4076863488 | bytes 15704448 | tf_op jit(solution)/shard_map/pallas_call | solution.py:791
  550.3 67.7 %shard_map.353 = (f32[2,48,1152]{2,1,0:T(8,128)}, f32[3,8,1152]{2,1,0:T(8,128)}, bf16[3,1152,288]{2,1,0:T(8,128)(2,1)}, bf16[1152,288]{1,0:T(8,128)(2,1)}, f32[2...) custom-call(f32[2,48,1152]{2,1,0:T(8,128)} %get-tuple-element.102.refs_0_, ...), custom_call_target="tpu_custom_call" | custom-call | flops 2038431744 | bytes 15630720 | tf_op jit(solution)/shard_map/pallas_call | solution.py:791
  618.1 1.6 convert_element_type.148
  621.4 2.8 convolution_convert_fusion
  624.2 1.0 copy-done.3
  625.1 1.7 convert_add_fusion.1.refs_0_
  626.9 59.5 %shard_map.354 = (f32[2,48,1152]{2,1,0:T(8,128)}, f32[3,8,1152]{2,1,0:T(8,128)}, bf16[1152,1152]{1,0:T(8,128)(2,1)}, bf16[1152,1152]{1,0:T(8,128)(2,1)}, f32[1,1...) custom-call(f32[2,48,1152]{2,1,0:T(8,128)} %convert_add_fusion.1.refs_0_, ...), custom_call_target="tpu_custom_call" | custom-call | flops 4076863488 | bytes 18579840 | tf_op jit(solution)/shard_map/pallas_call | solution.py:791
  686.4 63.2 %shard_map.355 = (f32[2,48,1152]{2,1,0:T(8,128)}, f32[3,8,1152]{2,1,0:T(8,128)}, bf16[3,1152,288]{2,1,0:T(8,128)(2,1)}, bf16[1152,288]{1,0:T(8,128)(2,1)}, f32[2...) custom-call(f32[2,48,1152]{2,1,0:T(8,128)} %get-tuple-element.119.refs_0_, ...), custom_call_target="tpu_custom_call" | custom-call | flops 2038431744 | bytes 15630720 | tf_op jit(solution)/shard_map/pallas_call | solution.py:791
  749.6 53.3 %shard_map.356 = (bf16[4,48,1152]{2,1,0:T(8,128)(2,1)}, f32[4,48,1152]{2,1,0:T(8,128)}, f32[288,1728]{1,0:T(8,128)}, f32[1,1728]{1,0:T(1,128)}, f32[8,1152]{1,0:...) custom-call(bf16[2,48,1152]{2,1,0:T(8,128)(2,1)} %get-tuple-element.93.refs_0_.refs_1_, ...), custom_call_target="tpu_custom_call" | custom-call | flops 63700992 | bytes 4506624 | tf_op jit(solution)/shard_map/pallas_call | solution.py:791
  806.1 1.1 select_bitcast_fusion.3
  807.1 1.0 copy.156
  808.1 0.9 copy.154
  809.0 2.5 copy.155
  812.2 1.7 convert_element_type.143
  813.8 1.3 slice_bitcast_fusion
  815.1 1.2 select_bitcast_fusion.2
  816.3 1.5 fusion.15
  817.8 1.2 select_bitcast_fusion
  820.0 1.2 select_bitcast_fusion.1
  821.3 1.0 convert_bitcast_fusion
  822.3 1.0 copy.157
  823.3 3.2 copy.169
  (120 shorter events, 21.5 us)
Async XLA Ops:
  7.2 208.9 %copy-start = (bf16[512,2048]{1,0:T(8,128)(2,1)S(1)}, bf16[512,2048]{1,0:T(8,128)(2,1)}, u32[]{:S(2)}) copy-start(bf16[512,2048]{1,0:T(8,128)(2,1)} %param.38) | copy-start | bytes 6291460
  7.2 245.2 %reduce-scatter.7.cloned.1.call-start = ((), (), s32[]{:S(2)}) async-start(), calls=%async_computation.6 | async-start | bytes 1966080 | tf_op jit(solution)/shard_map/reduce_scatter | solution.py:1031
  21.7 6.5 copy-start.19
  21.7 6.5 copy-start.20
  21.7 6.5 copy-start.21
  143.1 71.4 %copy-start.23 = (bf16[1152,512]{1,0:T(8,128)(2,1)S(1)}, bf16[1152,512]{1,0:T(8,128)(2,1)}, u32[]{:S(2)}) copy-start(bf16[1152,512]{1,0:T(8,128)(2,1)} %param.36) | copy-start | bytes 3538948
  213.6 0.9 copy-start.13
  215.2 0.9 copy-start.27
  218.2 0.7 copy-start.22
  218.3 36.4 %copy-start.25 = (bf16[192]{0:T(256)(128)(2,1)S(1)}, bf16[192]{0:T(256)(128)(2,1)}, u32[]{:S(2)}) copy-start(bf16[192]{0:T(256)(128)(2,1)} %param.41) | copy-start | bytes 1156
  218.3 36.4 %copy-start.17 = (bf16[192,4,192]{2,1,0:T(4,128)(2,1)S(1)}, bf16[192,4,192]{2,1,0:T(4,128)(2,1)}, u32[]{:S(2)}) copy-start(bf16[192,4,192]{2,1,0:T(4,128)(2,1)} %param.24) | copy-start | bytes 884740
  218.3 72.3 %all-gather.3.cloned.1.call-start = ((), (), s32[]{:S(2)}) async-start(), calls=%async_computation.7 | async-start | bytes 1966080 | tf_op jit(solution)/shard_map/all_gather | solution.py:1027
  254.3 36.3 %copy-start.2 = (bf16[2048,192]{0,1:T(8,128)(2,1)S(1)}, bf16[2048,192]{0,1:T(8,128)(2,1)}, u32[]{:S(2)}) copy-start(bf16[2048,192]{0,1:T(8,128)(2,1)} %param.40) | copy-start | bytes 2359300
  254.4 86.1 %reduce-scatter.9.cloned.1.call-start = ((), (), s32[]{:S(2)}) async-start(), calls=%async_computation.8 | async-start | bytes 1966080 | tf_op jit(solution)/shard_map/reduce_scatter | solution.py:1031
  305.0 35.5 %copy-start.5 = (bf16[96,2048]{1,0:T(8,128)(2,1)S(1)}, bf16[96,2048]{1,0:T(8,128)(2,1)}, u32[]{:S(2)}) copy-start(bf16[96,2048]{1,0:T(8,128)(2,1)} %reduce-scatter.7.cloned.1.call-done) | copy-start | bytes 1179652
  306.7 72.1 %all-gather.5.cloned.1.call-start = ((), (), s32[]{:S(2)}) async-start(), calls=%async_computation.9 | async-start | bytes 1966080 | tf_op jit(solution)/shard_map/all_gather | solution.py:1027
  342.6 275.5 %reduce-scatter.17.cloned.1.call-start = ((), (), s32[]{:S(2)}) async-start(), calls=%async_computation.13 | async-start | bytes 884736 | tf_op jit(solution)/shard_map/reduce_scatter | solution.py:1245
  345.6 36.8 %copy-start.24 = (bf16[1152,512]{1,0:T(8,128)(2,1)S(1)}, bf16[1152,512]{1,0:T(8,128)(2,1)}, u32[]{:S(2)}) copy-start(bf16[1152,512]{1,0:T(8,128)(2,1)} %param.36) | copy-start | bytes 3538948
  345.6 278.6 %reduce-scatter.11.cloned.1.call-start = ((), (), s32[]{:S(2)}) async-start(), calls=%async_computation.10 | async-start | bytes 1105920 | tf_op jit(solution)/shard_map/reduce_scatter | solution.py:1031
  381.6 0.7 copy-start.26
  382.4 1.7 copy-start.14
  384.0 428.1 %reduce-scatter.13.cloned.1.call-start = ((), (), s32[]{:S(2)}) async-start(), calls=%async_computation.11 | async-start | bytes 1327104 | tf_op jit(solution)/shard_map/reduce_scatter | solution.py:1245
  384.1 3.8 copy-start.12
  387.0 434.3 %reduce-scatter.15.cloned.1.call-start = ((), (), s32[]{:S(2)}) async-start(), calls=%async_computation.12 | async-start | bytes 2359296 | tf_op jit(solution)/shard_map/reduce_scatter | solution.py:1245
  550.3 69.5 %copy-start.4 = (bf16[384,2048]{1,0:T(8,128)(2,1)S(1)}, bf16[384,2048]{1,0:T(8,128)(2,1)}, u32[]{:S(2)}) copy-start(bf16[384,2048]{1,0:T(8,128)(2,1)} %all-gather.5.cloned.1.call-done) | copy-start | bytes 4718596
  618.1 3.3 copy-start.28
  624.1 1.0 copy-start.3
  749.6 56.5 %copy-start.15 = (f32[288,288]{1,0:T(8,128)S(1)}, f32[288,288]{1,0:T(8,128)}, u32[]{:S(2)}) copy-start(f32[288,288]{1,0:T(8,128)} %get-tuple-element.152) | copy-start | bytes 995332
  802.9 5.2 copy-start.16
  808.1 7.0 copy-start.8
  808.1 7.0 copy-start.11
  815.1 2.7 copy-start.7
  815.1 2.7 copy-start.10
  817.8 1.8 copy-start.6
  817.8 2.2 copy-start.9
  823.3 3.8 copy-start.1
  823.3 3.2 copy-start.18
Sparse Core Ops, SparseCore 0:
  218.4 33.9 reduce-scatter.6
  254.5 36.0 all-gather.2
  306.9 33.5 reduce-scatter.8
  342.7 36.0 all-gather.4
  382.4 33.8 reduce-scatter.16
  419.0 31.3 reduce-scatter.10
  454.2 38.7 reduce-scatter.12
  624.3 54.4 reduce-scatter.14

commit v3 on v2

--- a/solution.py
+++ b/solution.py
@@ -60,7 +60,23 @@
 
 
 def remote(source, target, send_sem, recv_sem, peer):
-    copy = pltpu.make_async_remote_copy(
+    copy = describe(source, target, send_sem, recv_sem, peer)
+    copy.start()
+    return copy
+
+
+def local(source, target, sem):
+    copy = pltpu.make_async_copy(source, target, sem)
+    copy.start()
+    return copy
+
+
+def own_rows(me, length):
+    return pl.ds(pl.multiple_of(me * length, 16), length)
+
+
+def describe(source, target, send_sem, recv_sem, peer):
+    return pltpu.make_async_remote_copy(
         src_ref=source,
         dst_ref=target,
         send_sem=send_sem,
@@ -68,26 +84,6 @@
         device_id=peer,
         device_id_type=MESH,
     )
-    copy.start()
-    return copy
-
-
-def local(source, target, sem):
-    copy = pltpu.make_async_copy(source, target, sem)
-    copy.start()
-    return copy
-
-
-def own_rows(me, length):
-    return pl.ds(pl.multiple_of(me * length, 16), length)
-
-
-def start_gather(full, length, count, sems):
-    mine = full.at[:, own_rows(lax.axis_index("tensor"), length)]
-    return [
-        remote(mine, mine, sems[0].at[step], sems[1].at[step], peer)
-        for step, peer in enumerate(z_peers(count))
-    ]
 
 
 def wait_all(copies):
@@ -95,24 +91,120 @@
         copy.wait()
 
 
-def scatter_sum(partial, length, count, buffers, sems):
-    send_buf, recv_buf = buffers
-    copies = []
-    for step, peer in enumerate(z_peers(count)):
-        term = partial(own_rows(peer["tensor"], length))
-        send_buf[step] = term.astype(BF16).reshape(send_buf.shape[1:])
-        copies.append(
-            remote(send_buf.at[step], recv_buf.at[step], sems[2].at[step], sems[3].at[step], peer)
+class Line:
+    def __init__(self, length, sems):
+        self.length, (self.ag_send, self.ag_recv, self.rs_send, self.rs_recv) = length, sems
+        self.me = lax.axis_index("tensor")
+        self.mirror = 3 - self.me
+        self.near = self.me + 1 - 2 * lax.rem(self.me, 2)
+        self.opposite = lax.rem(self.me + 2, 4)
+        self.is_end = jnp.logical_or(self.me == 0, self.me == 3)
+        self.is_middle = jnp.logical_not(self.is_end)
+
+    def block(self, full, place, which, peer):
+        part = full.at[:, own_rows(place, self.length)]
+        return describe(
+            part, part, self.ag_send.at[which], self.ag_recv.at[place], {"tensor": peer}
         )
-    return copies, partial(own_rows(lax.axis_index("tensor"), length))
-
-
-def finish_sum(copies, total, buffers):
-    wait_all(copies)
-    recv_buf = buffers[1]
-    for step in range(recv_buf.shape[0]):
-        total = total + recv_buf[step].reshape(total.shape).astype(F32)
-    return total
+
+    def start_gather(self, full):
+        self.block(full, self.me, 0, self.opposite).start()
+        self.block(full, self.me, 1, self.near).start()
+
+        @pl.when(self.is_middle)
+        def to_mirror():
+            self.block(full, self.me, 2, self.mirror).start()
+
+    def relay(self, full):
+        self.block(full, self.opposite, 2, self.mirror).wait_recv()
+
+        @pl.when(self.is_middle)
+        def pass_on():
+            self.block(full, self.opposite, 3, 3 - self.opposite).start()
+
+    def finish_gather(self, full):
+        self.block(full, self.near, 1, self.near).wait_recv()
+        self.block(full, self.mirror, 1, self.near).wait_recv()
+        self.block(full, self.me, 0, self.opposite).wait_send()
+        self.block(full, self.me, 1, self.near).wait_send()
+
+        @pl.when(self.is_middle)
+        def sent():
+            self.block(full, self.me, 2, self.mirror).wait_send()
+            self.block(full, self.opposite, 3, 3 - self.opposite).wait_send()
+
+    def scatter_sum(self, partial, buffers):
+        send_buf, recv_buf, relay_buf = buffers
+        me, relay_sem = self.me, 4
+
+        def term(peer):
+            return partial(own_rows(peer, self.length))
+
+        def keep(which, value):
+            send_buf[which] = value.astype(BF16).reshape(send_buf.shape[1:])
+
+        self.to_mirror = describe(
+            send_buf.at[0], recv_buf.at[me], self.rs_send.at[0], self.rs_recv.at[me],
+            {"tensor": self.mirror},
+        )
+        self.to_relay = describe(
+            send_buf.at[0], relay_buf, self.rs_send.at[0], self.rs_recv.at[relay_sem],
+            {"tensor": self.near},
+        )
+        self.to_near = describe(
+            send_buf.at[1], recv_buf.at[me], self.rs_send.at[1], self.rs_recv.at[me],
+            {"tensor": self.near},
+        )
+        self.to_opposite = describe(
+            send_buf.at[2], recv_buf.at[me], self.rs_send.at[2], self.rs_recv.at[me],
+            {"tensor": self.opposite},
+        )
+        keep(0, term(self.mirror))
+
+        @pl.when(self.is_end)
+        def first_end():
+            self.to_relay.start()
+            relay_buf[...] = jnp.zeros_like(relay_buf)
+            recv_buf[self.mirror] = jnp.zeros(recv_buf.shape[1:], BF16)
+
+        @pl.when(self.is_middle)
+        def first_middle():
+            self.to_mirror.start()
+
+        keep(1, term(self.near))
+        self.to_near.start()
+        last = term(self.opposite)
+
+        @pl.when(self.is_middle)
+        def relayed():
+            self.to_relay.wait_recv()
+
+        keep(2, last + relay_buf[...].reshape(last.shape).astype(F32))
+        self.to_opposite.start()
+        return term(me)
+
+    def finish_sum(self, total, buffers):
+        send_buf, recv_buf, relay_buf = buffers
+
+        def got(source):
+            describe(
+                send_buf.at[1], recv_buf.at[source], self.rs_send.at[1], self.rs_recv.at[source],
+                {"tensor": self.near},
+            ).wait_recv()
+
+        got(self.near)
+        got(self.opposite)
+
+        @pl.when(self.is_middle)
+        def third():
+            got(self.mirror)
+
+        self.to_near.wait_send()
+        self.to_opposite.wait_send()
+        self.to_mirror.wait_send()
+        for source in (self.near, self.opposite, self.mirror):
+            total = total + recv_buf[source].reshape(total.shape).astype(F32)
+        return total
 
 
 def fetch(block, own_ref, other_ref, target, sem):
@@ -218,8 +310,9 @@
             self.own.at[rows], self.other.at[rows], self.send.at[0], self.recv.at[0], x_peer()
         )
 
-    def forward(self):
-        self.first.wait()
+    def forward(self, first):
+        if first is not None:
+            first.wait()
         mine = self.other.at[self.rows(core_bit(), y_bit())]
         self.copies.append(remote(mine, mine, self.send.at[1], self.recv.at[1], core_peer()))
         if self.parts == 4:
@@ -235,79 +328,178 @@
         wait_all(self.copies)
 
 
-class Courier:
-    def __init__(self, grad, out, scratch):
-        self.grad, self.out = grad, out
-        self.keep, self.from_core, self.from_y, self.part, self.from_x, self.sems = scratch
+class Cargo:
+    inputs, outs, scratch, aliases, any_outs = (), (), (), {}, False
+
+    def bind(self, inputs, outs, scratch):
+        self.ins, self.out_refs, self.held = inputs, outs, scratch
+
+    def peers(self):
+        return []
+
+    def begin(self):
+        pass
+
+    def middle(self):
+        pass
+
+    def end(self):
+        pass
+
+
+def quarter(shape):
+    return shape[:-2] + (shape[-2] // 4, shape[-1])
+
+
+class QuadSum(Cargo):
+    def __init__(self, grad):
+        part = quarter(grad.shape)
+        self.inputs = (grad,)
+        self.outs = ((part, BF16),)
         self.size = grad.shape[-2] // 4
+        self.scratch = (
+            pltpu.VMEM((2,) + part, BF16),
+            pltpu.VMEM((2,) + part, BF16),
+            pltpu.VMEM(part, BF16),
+            pltpu.SemaphoreType.DMA((3, 3)),
+        )
+
+    def peers(self):
+        return ["core", "y"]
 
     def rows(self, core, y):
+        grad = self.ins[0]
         part = pl.ds(pl.multiple_of((core + 2 * y) * self.size, 16), self.size)
-        return self.grad.at[:, part] if len(self.grad.shape) == 3 else self.grad.at[part]
+        return grad.at[:, part] if len(grad.shape) == 3 else grad.at[part]
 
     def begin(self):
+        keep, from_core, from_y, sems = self.held
         core, self.copies = core_bit(), []
         for y in range(2):
             self.copies.append(
                 remote(
-                    self.rows(1 - core, y), self.from_core.at[y],
-                    self.sems.at[0, y], self.sems.at[1, y], core_peer(),
+                    self.rows(1 - core, y), from_core.at[y], sems.at[0, y], sems.at[1, y], core_peer()
                 )
             )
-            self.copies.append(local(self.rows(core, y), self.keep.at[y], self.sems.at[2, y]))
-
-    def to_y(self):
+            self.copies.append(local(self.rows(core, y), keep.at[y], sems.at[2, y]))
+
+    def middle(self):
+        keep, from_core, from_y, sems = self.held
         wait_all(self.copies)
         for y in range(2):
-            self.keep[y] = (self.keep[y].astype(F32) + self.from_core[y].astype(F32)).astype(BF16)
+            keep[y] = (keep[y].astype(F32) + from_core[y].astype(F32)).astype(BF16)
         self.copies = [
-            remote(
-                self.keep.at[1 - y_bit()], self.from_y,
-                self.sems.at[0, 2], self.sems.at[1, 2], y_peer(),
-            )
+            remote(keep.at[1 - y_bit()], from_y, sems.at[0, 2], sems.at[1, 2], y_peer())
         ]
 
+    def end(self):
+        keep, from_core, from_y, sems = self.held
+        wait_all(self.copies)
+        self.out_refs[0][...] = (
+            keep[y_bit()].astype(F32) + from_y[...].astype(F32)
+        ).astype(BF16)
+
+
+class SectionSum(Cargo):
+    def __init__(self, part):
+        self.inputs = (part,)
+        self.outs = ((part.shape, F32),)
+        self.scratch = (
+            pltpu.VMEM(part.shape, BF16),
+            pltpu.VMEM(part.shape, BF16),
+            pltpu.SemaphoreType.DMA((3,)),
+        )
+
+    def peers(self):
+        return ["x"]
+
+    def begin(self):
+        mine, other, sems = self.held
+        self.copies = [
+            local(self.ins[0], mine, sems.at[2]),
+            remote(self.ins[0], other, sems.at[0], sems.at[1], x_peer()),
+        ]
+
+    def end(self):
+        mine, other, sems = self.held
+        wait_all(self.copies)
+        self.out_refs[0][...] = mine[...].astype(F32) + other[...].astype(F32)
+
+
+class LastSum(QuadSum):
+    def __init__(self, grad):
+        super().__init__(grad)
+        part = quarter(grad.shape)
+        self.outs = ((part, F32),)
+        self.scratch = self.scratch + (
+            pltpu.VMEM(part, BF16),
+            pltpu.VMEM(part, BF16),
+            pltpu.SemaphoreType.DMA((2,)),
+        )
+
+    def peers(self):
+        return ["core", "y", "x"]
+
+    def begin(self):
+        self.all_held = self.held
+        self.held, self.last = self.held[:4], self.held[4:]
+        super().begin()
+
     def to_x(self):
+        keep, from_core, from_y, sems = self.held
+        mine, other, last_sems = self.last
         wait_all(self.copies)
-        mine = self.keep[y_bit()].astype(F32) + self.from_y[...].astype(F32)
-        self.part[...] = mine.astype(BF16)
-        self.copies = [
-            remote(self.part, self.from_x, self.sems.at[0, 3], self.sems.at[1, 3], x_peer())
-        ]
-
-    def finish(self):
+        mine[...] = (keep[y_bit()].astype(F32) + from_y[...].astype(F32)).astype(BF16)
+        self.copies = [remote(mine, other, last_sems.at[0], last_sems.at[1], x_peer())]
+
+    def end(self):
+        mine, other, last_sems = self.last
         wait_all(self.copies)
-        self.out[...] = self.part[...].astype(F32) + self.from_x[...].astype(F32)
-
-
-COURIER_REFS = 6
-
-
-def quarter(shape):
-    return shape[:-2] + (shape[-2] // 4, shape[-1])
-
-
-def courier_scratch(shape):
-    part = quarter(shape)
-    return [
-        pltpu.VMEM((2,) + part, BF16),
-        pltpu.VMEM((2,) + part, BF16),
-        pltpu.VMEM(part, BF16),
-        pltpu.VMEM(part, BF16),
-        pltpu.VMEM(part, BF16),
-        pltpu.SemaphoreType.DMA((3, 4)),
-    ]
-
-
-def make_couriers(grads, outs, scratch):
-    return [
-        Courier(grad, out, scratch[COURIER_REFS * i : COURIER_REFS * (i + 1)])
-        for i, (grad, out) in enumerate(zip(grads, outs))
-    ]
-
-
-def courier_peers(couriers):
-    return [core_peer(), y_peer(), x_peer()] if couriers else []
+        self.out_refs[0][...] = mine[...].astype(F32) + other[...].astype(F32)
+
+
+class LateShare(Cargo):
+    any_outs = True
+
+    def __init__(self, other):
+        self.inputs = (other,)
+        self.outs = ((other.shape, BF16),)
+        self.aliases = {0: 0}
+        self.scratch = (pltpu.SemaphoreType.DMA((4,)), pltpu.SemaphoreType.DMA((4,)))
+
+    def peers(self):
+        return ["core", "y"]
+
+    def begin(self):
+        out = self.out_refs[0]
+        self.share = Share(out, out, 4, self.held)
+        self.share.forward(None)
+
+    def middle(self):
+        self.share.forward_again()
+        self.share.finish()
+
+
+class Bundle:
+    def __init__(self, cargos):
+        self.cargos = cargos
+
+    def peers(self):
+        names = [name for cargo in self.cargos for name in cargo.peers()]
+        known = {"core": core_peer, "y": y_peer, "x": x_peer}
+        return [make() for name, make in known.items() if name in names]
+
+    def begin(self):
+        for cargo in self.cargos:
+            cargo.begin()
+
+    def middle(self):
+        for cargo in self.cargos:
+            cargo.middle()
+
+    def end(self):
+        for cargo in self.cargos:
+            cargo.end()
 
 
 def attend_body(
@@ -315,7 +507,7 @@
 ):
     middle_ref, branch_ref, full_ref, q_ref, k_ref, v_ref, probs_ref, mixed_ref = outs
     full, wqkv, wo, mixed_wide = scratch[:4]
-    buffers = scratch[4:6]
+    buffers = scratch[4:7]
     seg_own, seg_col, seg_row = segs
     mod_ref = mods()
     me = lax.axis_index("tensor")
@@ -328,11 +520,13 @@
     full[:, own_rows(me, length), :] = attn_in.astype(BF16).reshape(rows, length, width)
     if peers is not None:
         greet(peers)
-    gather = start_gather(full, length, count, sems)
+    line = Line(length, sems)
+    line.start_gather(full)
+    spread = spread_matrix(heads_width)
+    line.relay(full)
     steps[0]()
-    spread = spread_matrix(heads_width)
     need_qkv()
-    wait_all(gather)
+    line.finish_gather(full)
     full_ref[...] = full[...]
     tokens = flat(full)
     bias = biases()
@@ -361,26 +555,22 @@
     def partial(which_rows):
         return dot(mixed_ref[:, which_rows, :].reshape(rows * length, heads_width), wo[...])
 
-    copies, total = scatter_sum(partial, length, count, buffers, sems)
+    total = line.scatter_sum(partial, buffers)
     steps[1]()
-    branch = finish_sum(copies, total, buffers) + bias[2:3, :]
+    branch = line.finish_sum(total, buffers) + bias[2:3, :]
     branch_ref[...] = branch.reshape(branch_ref.shape)
     middle = flat(u_ref).astype(F32) + token_mod(mod_ref, seg_own, 2) * branch
     middle_ref[...] = middle.reshape(middle_ref.shape)
 
 
-def nothing():
-    pass
-
-
-def open_kernel(count, sections, *refs):
+def open_kernel(count, sections, *refs, cargo):
     u_ref, cond_ref, ada_b_ref, biases_ref, seg_own, seg_col, seg_row = refs[:7]
     ada_w, own_qkv, own_out, own_one, own_two = refs[7:12]
     mods_ref, bias_ref, other_qkv, other_out, other_one, other_two = refs[12:18]
     outs = refs[18:26]
-    scratch = refs[26:32]
-    ada, mod_src, mod_buf, bias_buf, w_sem, ag_send, ag_recv, rs_send, rs_recv = refs[32:41]
-    mod_send, mod_recv, share_send, share_recv, ada_sem = refs[41:]
+    scratch = refs[26:33]
+    ada, mod_src, mod_buf, bias_buf, w_sem, ag_send, ag_recv, rs_send, rs_recv = refs[33:42]
+    mod_send, mod_recv, share_send, share_recv, ada_sem = refs[42:]
     wqkv, wo = scratch[1:3]
     section, tensor = lax.axis_index("section"), lax.axis_index("tensor")
     load_ada = local(ada_w, ada, ada_sem)
@@ -400,13 +590,8 @@
         if a or b
     ]
     greet(plane + [core_peer(), y_peer()])
-    for share in shares:
-        share.begin()
-    bias_buf[section] = biases_ref[...]
-    bias_copy = remote(
-        biases_ref, bias_buf.at[section],
-        mod_send.at[len(plane)], mod_recv.at[len(plane)], x_peer(),
-    )
+    cargo.begin()
+    shares[0].begin()
     cond_act = silu(cond_ref[...].astype(F32)).astype(BF16)
     load_ada.wait()
     mod = dot(cond_act, ada[...]) + ada_b_ref[...].astype(F32)
@@ -419,6 +604,13 @@
         )
         for i, peer in enumerate(plane)
     ]
+    bias_buf[section] = biases_ref[...]
+    bias_copy = remote(
+        biases_ref, bias_buf.at[section],
+        mod_send.at[len(plane)], mod_recv.at[len(plane)], x_peer(),
+    )
+    for share in shares[1:]:
+        share.begin()
 
     def mods():
         wait_all(copies)
@@ -445,85 +637,90 @@
         fetch(0, own_qkv, other_qkv, wqkv, w_sem.at[0]).wait()
 
     def need_out():
+        shares[1].finish()
         fetch(0, own_out, other_out, wo, w_sem.at[1]).wait()
 
     def after_gather():
-        shares[0].forward()
-        shares[1].forward()
+        shares[0].forward(shares[0].first)
+        shares[1].forward(shares[1].first)
         shares[0].forward_again()
-        shares[2].forward()
         shares[0].finish()
-        shares[1].finish()
 
     def after_scatter():
+        shares[2].forward(shares[2].first)
         shares[2].forward_again()
-        shares[3].forward()
-        shares[3].forward_again()
 
     attend_body(
         count, None, u_ref, mods, (seg_own, seg_col, seg_row), biases, outs, scratch,
         (ag_send, ag_recv, rs_send, rs_recv), need_qkv, need_out, (after_gather, after_scatter),
     )
+    cargo.end()
     shares[2].finish()
-    shares[3].finish()
-
-
-def attend_kernel(count, block, *refs):
+    shares[3].first.wait()
+
+
+def attend_kernel(count, block, *refs, cargo):
     u_ref, mods_ref, bias_ref, seg_own, seg_col, seg_row = refs[:6]
     own_qkv, other_qkv, own_out, other_out = refs[6:10]
-    outs, scratch, w_sem = refs[10:18], refs[18:24], refs[24]
+    outs, scratch, w_sem = refs[10:18], refs[18:25], refs[25]
     load_qkv = fetch(block, own_qkv, other_qkv, scratch[1], w_sem.at[0])
     load_out = fetch(block, own_out, other_out, scratch[2], w_sem.at[1])
     attend_body(
-        count, z_peers(count), u_ref, lambda: mods_ref.at[block], (seg_own, seg_col, seg_row),
-        lambda: bias_ref[block], outs, scratch, refs[25:29],
-        load_qkv.wait, load_out.wait, (nothing, nothing),
-    )
+        count, z_peers(count) + cargo.peers(), u_ref, lambda: mods_ref.at[block],
+        (seg_own, seg_col, seg_row), lambda: bias_ref[block], outs, scratch, refs[26:30],
+        load_qkv.wait, load_out.wait, (cargo.begin, cargo.middle),
+    )
+    cargo.end()
 
 
 def mlp_kernel(
     count, block,
     middle_ref, mods_ref, bias_ref, seg_own, w1_own, w1_other, w2_own, w2_other,
     out_ref, branch_ref, full_ref, pre_ref, act_ref,
-    full, w1, w2, send_buf, recv_buf, w_sem, *sems,
+    full, w1, w2, send_buf, recv_buf, relay_buf, w_sem, *sems, cargo, late,
 ):
     me = lax.axis_index("tensor")
     rows, length, width = middle_ref.shape
     mod_ref = mods_ref.at[block]
     load_one = fetch(block, w1_own, w1_other, w1, w_sem.at[0])
-    load_two = fetch(block, w2_own, w2_other, w2, w_sem.at[1])
     normed, unused = layer_norm(flat(middle_ref))
     mlp_in = normed * (1.0 + token_mod(mod_ref, seg_own, 4)) + token_mod(mod_ref, seg_own, 3)
     full[:, own_rows(me, length), :] = mlp_in.astype(BF16).reshape(rows, length, width)
-    greet(z_peers(count))
-    gather = start_gather(full, length, count, sems)
+    greet(z_peers(count) + cargo.peers())
+    line = Line(length, sems)
+    line.start_gather(full)
+    cargo.begin()
+    line.relay(full)
     load_one.wait()
-    wait_all(gather)
+    line.finish_gather(full)
     full_ref[...] = full[...]
     pre = dot(flat(full), w1[...]) + bias_ref[block, 3:4, : w1.shape[1]]
     pre_ref[...] = pre.reshape(pre_ref.shape)
+    cargo.middle()
+    if late:
+        w2_other = cargo.cargos[0].out_refs[0]
+    load_two = fetch(block, w2_own, w2_other, w2, w_sem.at[1])
     act_ref[...] = gelu_tanh(pre).astype(BF16).reshape(act_ref.shape)
     load_two.wait()
 
     def partial(which_rows):
         return dot(act_ref[:, which_rows, :].reshape(rows * length, -1), w2[...])
 
-    buffers = (send_buf, recv_buf)
-    copies, total = scatter_sum(partial, length, count, buffers, sems)
-    branch = finish_sum(copies, total, buffers) + bias_ref[block, 4:5, :]
+    buffers = (send_buf, recv_buf, relay_buf)
+    total = line.scatter_sum(partial, buffers)
+    branch = line.finish_sum(total, buffers) + bias_ref[block, 4:5, :]
+    cargo.end()
     branch_ref[...] = branch.reshape(branch_ref.shape)
     out = flat(middle_ref) + token_mod(mod_ref, seg_own, 5) * branch
     out_ref[...] = out.astype(BF16).reshape(out_ref.shape)
 
 
-def mlp_back_kernel(count, block, loads, *refs):
+def mlp_back_kernel(count, block, *refs, cargo):
     g_ref, middle_ref, branch_ref, mods_ref, seg_own, full_ref, pre_ref, act_ref = refs[:8]
     w1_own, w1_other, w2_own, w2_other = refs[8:12]
-    grads, refs = refs[12 : 12 + loads], refs[12 + loads :]
-    d_middle_ref, d_mod_ref, d_w1_ref, d_w2_ref, d_b1_ref, d_b2_ref = refs[:6]
-    sums, refs = refs[6 : 6 + loads], refs[6 + loads :]
-    full, d_pre, w1, w2, send_buf, recv_buf, w_sem = refs[:7]
-    sems, couriers = refs[7:11], make_couriers(grads, sums, refs[11:])
+    d_middle_ref, d_mod_ref, d_w1_ref, d_w2_ref, d_b1_ref, d_b2_ref = refs[12:18]
+    full, d_pre, w1, w2, *buffers, w_sem = refs[18:26]
+    sems = refs[26:]
     me = lax.axis_index("tensor")
     rows, length, width = middle_ref.shape
     mod_ref = mods_ref.at[block]
@@ -532,15 +729,15 @@
     g = flat(g_ref).astype(F32)
     d_branch = (g * token_mod(mod_ref, seg_own, 5)).astype(BF16)
     full[:, own_rows(me, length), :] = d_branch.reshape(rows, length, width)
-    greet(z_peers(count) + courier_peers(couriers))
-    gather = start_gather(full, length, count, sems)
-    for courier in couriers:
-        courier.begin()
+    greet(z_peers(count) + cargo.peers())
+    line = Line(length, sems)
+    line.start_gather(full)
+    cargo.begin()
     slot_sums(g * flat(branch_ref), seg_own, d_mod_ref, 2)
-    for courier in couriers:
-        courier.to_y()
+    line.relay(full)
+    cargo.middle()
     load_two.wait()
-    wait_all(gather)
+    line.finish_gather(full)
     d_act = dot(flat(full), w2[...], NT)
     d_pre[...] = (d_act * gelu_slope(flat(pre_ref))).astype(BF16).reshape(d_pre.shape)
     load_one.wait()
@@ -548,15 +745,12 @@
     def partial(which_rows):
         return dot(d_pre[:, which_rows, :].reshape(rows * length, -1), w1[...], NT)
 
-    buffers = (send_buf, recv_buf)
-    copies, total = scatter_sum(partial, length, count, buffers, sems)
-    for courier in couriers:
-        courier.to_x()
+    total = line.scatter_sum(partial, buffers)
     d_b2_ref[...] = jnp.sum(flat(full).astype(F32), axis=0, keepdims=True)
     d_b1_ref[...] = jnp.sum(flat(d_pre).astype(F32), axis=0, keepdims=True)
     d_w2_ref[...] = dot(flat(full), flat(act_ref), TN).astype(BF16)
     d_w1_ref[...] = dot(flat(full_ref), flat(d_pre), TN).astype(BF16)
-    d_in = finish_sum(copies, total, buffers)
+    d_in = line.finish_sum(total, buffers)
     normed, inverse = layer_norm(flat(middle_ref))
     d_middle = flat(g_ref).astype(F32) + norm_back(
         d_in * (1.0 + token_mod(mod_ref, seg_own, 4)), normed, inverse
@@ -564,19 +758,16 @@
     d_middle_ref[...] = d_middle.reshape(d_middle_ref.shape)
     slot_sums(d_in, seg_own, d_mod_ref, 0)
     slot_sums(d_in * normed, seg_own, d_mod_ref, 1)
-    for courier in couriers:
-        courier.finish()
-
-
-def attend_back_kernel(count, block, loads, *refs):
+    cargo.end()
+
+
+def attend_back_kernel(count, block, *refs, cargo):
     d_middle_ref, u_ref, branch_ref, mods_ref, seg_own, full_ref = refs[:6]
     q_ref, k_ref, v_ref, probs_ref, mixed_ref = refs[6:11]
     wqkv_own, wqkv_other, wo_own, wo_other = refs[11:15]
-    grads, refs = refs[15 : 15 + loads], refs[15 + loads :]
-    d_in_ref, d_mod_ref, d_wqkv_ref, d_wo_ref, d_bqv_ref, d_bo_ref = refs[:6]
-    sums, refs = refs[6 : 6 + loads], refs[6 + loads :]
-    full, wide, narrow, wqkv, wo, send_buf, recv_buf, w_sem = refs[:8]
-    sems, couriers = refs[8:12], make_couriers(grads, sums, refs[12:])
+    d_in_ref, d_mod_ref, d_wqkv_ref, d_wo_ref, d_bqv_ref, d_bo_ref = refs[15:21]
+    full, wide, narrow, wqkv, wo, *buffers, w_sem = refs[21:30]
+    sems = refs[30:]
     me = lax.axis_index("tensor")
     rows, length, width = u_ref.shape
     heads_width = wo.shape[0]
@@ -587,16 +778,16 @@
     d_middle = flat(d_middle_ref)
     d_branch = (d_middle * token_mod(mod_ref, seg_own, 2)).astype(BF16)
     full[:, own_rows(me, length), :] = d_branch.reshape(rows, length, width)
-    greet(z_peers(count) + courier_peers(couriers))
-    gather = start_gather(full, length, count, sems)
-    for courier in couriers:
-        courier.begin()
+    greet(z_peers(count) + cargo.peers())
+    line = Line(length, sems)
+    line.start_gather(full)
+    cargo.begin()
     slot_sums(d_middle * flat(branch_ref), seg_own, d_mod_ref, 2)
     spread = spread_matrix(heads_width)
-    for courier in couriers:
-        courier.to_y()
+    line.relay(full)
+    cargo.middle()
     load_out.wait()
-    wait_all(gather)
+    line.finish_gather(full)
     d_mixed = dot(flat(full), wo[...], NT).astype(BF16)
     wide[3] = dot(d_mixed, spread).astype(BF16).reshape(wide.shape[1:])
 
@@ -633,17 +824,14 @@
             )
         return total
 
-    buffers = (send_buf, recv_buf)
-    copies, total = scatter_sum(partial, length, count, buffers, sems)
-    for courier in couriers:
-        courier.to_x()
+    total = line.scatter_sum(partial, buffers)
     d_bo_ref[...] = jnp.sum(flat(full).astype(F32), axis=0, keepdims=True)
     d_bqv_ref[0:1, :] = jnp.sum(flat(narrow.at[0]).astype(F32), axis=0, keepdims=True)
     d_bqv_ref[1:2, :] = jnp.sum(flat(narrow.at[2]).astype(F32), axis=0, keepdims=True)
     d_wo_ref[...] = dot(flat(full), flat(mixed_ref), TN).astype(BF16)
     for which in range(3):
         d_wqkv_ref[which] = dot(flat(full_ref), flat(narrow.at[which]), TN).astype(BF16)
-    d_attn_in = finish_sum(copies, total, buffers)
+    d_attn_in = line.finish_sum(total, buffers)
     normed, inverse = layer_norm(flat(u_ref).astype(F32))
     d_in = flat(d_middle_ref) + norm_back(
         d_attn_in * (1.0 + token_mod(mod_ref, seg_own, 1)), normed, inverse
@@ -651,18 +839,16 @@
     d_in_ref[...] = d_in.reshape(d_in_ref.shape)
     slot_sums(d_attn_in, seg_own, d_mod_ref, 0)
     slot_sums(d_attn_in * normed, seg_own, d_mod_ref, 1)
-    for courier in couriers:
-        courier.finish()
-
-
-def close_kernel(count, sections, replicas, *refs):
+    cargo.end()
+
+
+def close_kernel(count, sections, replicas, *refs, cargo):
     outs_ref, grads_ref, mod_refs, small_refs = refs[:2], refs[2:4], refs[4:8], refs[8:17]
-    cond_ref, wqkv_grad, wo_grad = refs[17:20]
-    out_ref, grad_ref, ada_w_ref, ada_b_ref, small_ref, qkv_sum, wo_sum = refs[20:27]
-    z_src, z_buf, mod_src, mod_buf, small_src, small_buf, cond_buf = refs[27:34]
-    place_src, place_buf = refs[34:36]
-    sems = refs[36:38]
-    couriers = make_couriers((wqkv_grad, wo_grad), (qkv_sum, wo_sum), refs[38:])
+    cond_ref = refs[17]
+    out_ref, grad_ref, ada_w_ref, ada_b_ref, small_ref = refs[18:23]
+    z_src, z_buf, mod_src, mod_buf, small_src, small_buf, cond_buf = refs[23:30]
+    place_src, place_buf = refs[30:32]
+    sems = refs[32:34]
     section, tensor, replica = (lax.axis_index(name) for name in ("section", "tensor", "dp"))
     send, recv = sems
     others = [
@@ -672,8 +858,7 @@
         if a or b
     ]
     greet(z_peers(count) + others)
-    for courier in couriers:
-        courier.begin()
+    cargo.begin()
     piece = z_src.shape[-1]
     for block in range(sections):
         attend_mod, mlp_mod = mod_refs[2 * block : 2 * block + 2]
@@ -730,8 +915,7 @@
             )
         )
         at = at + 2
-    for courier in couriers:
-        courier.to_y()
+    cargo.middle()
     wait_all(z_copies)
     mine = z_src[tensor]
     for step in range(count - 1):
@@ -746,8 +930,9 @@
             )
         )
         at = at + 1
-    for courier in couriers:
-        courier.to_x()
+    for one in cargo.cargos:
+        if isinstance(one, LastSum):
+            one.to_x()
     place_copy.wait()
     rows = place_buf.shape[1]
 
@@ -777,8 +962,7 @@
     ada_w_ref[...] = lax.dot_general(
         flat(cond_buf), mod_all, TN, precision=HIGHEST, preferred_element_type=F32
     )
-    for courier in couriers:
-        courier.finish()
+    cargo.end()
 
 
 VMEM = pl.BlockSpec(memory_space=pltpu.VMEM)
@@ -786,30 +970,66 @@
 MOD_ROWS = 8
 
 
-def call(kernel, number, inputs, in_any, outs, out_any, scratch, flops):
+def call(kernel, number, inputs, in_any, outs, out_any, scratch, flops, cargos=()):
+    own_in, own_out, own_scratch = len(inputs), len(outs), len(scratch)
+    specs = [VMEM] * (own_in - in_any) + [ANY] * in_any
+    out_specs = [ANY if i in out_any else VMEM for i in range(own_out)]
+    inputs, outs, scratch, aliases = list(inputs), list(outs), list(scratch), {}
+    for cargo in cargos:
+        for source, target in cargo.aliases.items():
+            aliases[len(inputs) + source] = len(outs) + target
+        inputs += cargo.inputs
+        outs += cargo.outs
+        scratch += cargo.scratch
+        specs += [ANY] * len(cargo.inputs)
+        out_specs += [ANY if cargo.any_outs else VMEM] * len(cargo.outs)
+
+    def body(*refs):
+        parts = [list(refs[: len(inputs)])]
+        parts.append(list(refs[len(inputs) : len(inputs) + len(outs)]))
+        parts.append(list(refs[len(inputs) + len(outs) :]))
+        base = parts[0][:own_in] + parts[1][:own_out] + parts[2][:own_scratch]
+        at = [own_in, own_out, own_scratch]
+        for cargo in cargos:
+            held = []
+            for i, items in enumerate((cargo.inputs, cargo.outs, cargo.scratch)):
+                held.append(parts[i][at[i] : at[i] + len(items)])
+                at[i] += len(items)
+            cargo.bind(*held)
+        kernel(*base, cargo=Bundle(cargos))
+
     moved = sum(math.prod(one.shape) * one.dtype.itemsize for one in inputs)
-    return pl.pallas_call(
-        kernel,
+    results = pl.pallas_call(
+        body,
         out_shape=[jax.ShapeDtypeStruct(shape, dtype) for shape, dtype in outs],
-        in_specs=[VMEM] * (len(inputs) - in_any) + [ANY] * in_any,
-        out_specs=[ANY if i in out_any else VMEM for i in range(len(outs))],
+        in_specs=specs,
+        out_specs=out_specs,
         scratch_shapes=scratch,
+        input_output_aliases=aliases,
         compiler_params=pltpu.CompilerParams(
             collective_id=number, has_side_effects=True, vmem_limit_bytes=56 * 2**20
         ),
         cost_estimate=pl.CostEstimate(flops=flops, bytes_accessed=moved, transcendentals=0),
     )(*inputs)
+    at, carried = own_out, []
+    for cargo in cargos:
+        carried.append(results[at : at + len(cargo.outs)])
+        at += len(cargo.outs)
+    return results[:own_out], carried
 
 
 def exchange_scratch(count, rows, length, width):
     return [
         pltpu.VMEM((count - 1, rows, length, width), BF16),
-        pltpu.VMEM((count - 1, rows, length, width), BF16),
+        pltpu.VMEM((count, rows, length, width), BF16),
+        pltpu.VMEM((rows, length, width), BF16),
     ]
 
 
 def semaphores(count):
-    return [pltpu.SemaphoreType.DMA((2,))] + [pltpu.SemaphoreType.DMA((count - 1,))] * 4
+    return [pltpu.SemaphoreType.DMA((2,))] + [
+        pltpu.SemaphoreType.DMA((size,)) for size in (count, count, count - 1, count + 1)
+    ]
 
 
 class Shapes:
@@ -847,12 +1067,12 @@
     return out
 
 
-def open_forward(sizes, u, cond, ada_w, ada_b, biases, segs, own, sections):
+def open_forward(sizes, u, cond, ada_w, ada_b, biases, segs, own, sections, cargos):
     count, width = sizes.count, sizes.width
     piece = ada_w.shape[1]
     inputs = [u, cond, ada_b, biases, *segs, ada_w] + [own[n] for n in ("qkv", "out", "one", "two")]
     plane = sections * count - 1
-    results = call(
+    results, carried = call(
         functools.partial(open_kernel, count, sections),
         0,
         inputs,
@@ -877,12 +1097,13 @@
             pltpu.SemaphoreType.DMA,
         ],
         2 * sizes.tokens * width * sizes.heads_width * 4,
+        cargos,
     )
     other = dict(zip(("qkv", "out", "one", "two"), results[2:6]))
-    return results[0], results[1], other, results[6:]
-
-
-def attend_forward(sizes, block, u, mods, biases, segs, own, other):
+    return results[0], results[1], other, results[6:], carried
+
+
+def attend_forward(sizes, block, u, mods, biases, segs, own, other, cargos):
     inputs = [u, mods, biases, *segs] + pairs(own, other, ("qkv", "out"))
     return call(
         functools.partial(attend_kernel, sizes.count, block),
@@ -893,14 +1114,15 @@
         (),
         sizes.attend_scratch + semaphores(sizes.count),
         2 * sizes.tokens * sizes.width * sizes.heads_width * 4,
-    )
-
-
-def mlp_forward(sizes, block, middle, mods, biases, segs, own, other):
+        cargos,
+    )
+
+
+def mlp_forward(sizes, block, middle, mods, biases, segs, own, other, late, cargos):
     inputs = [middle, mods, biases, segs[0]] + pairs(own, other, ("one", "two"))
     hidden = (sizes.rows, sizes.positions, sizes.hidden)
     return call(
-        functools.partial(mlp_kernel, sizes.count, block),
+        functools.partial(mlp_kernel, sizes.count, block, late=late),
         2 + block,
         inputs,
         4,
@@ -917,25 +1139,24 @@
         + exchange_scratch(sizes.count, *sizes.local)
         + semaphores(sizes.count),
         2 * sizes.tokens * sizes.width * sizes.hidden * 2,
-    )
-
-
-def mlp_backward(sizes, block, g, attend, mlp, mods, segs, own, other, loads):
+        cargos,
+    )
+
+
+def mlp_backward(sizes, block, g, attend, mlp, mods, segs, own, other, cargos):
     out, branch, full, pre, act = mlp
     inputs = [g, attend[0], branch, mods, segs[0], full, pre, act]
-    inputs += pairs(own, other, ("one", "two")) + list(loads)
-    carried = [scratch for load in loads for scratch in courier_scratch(load.shape)]
+    inputs += pairs(own, other, ("one", "two"))
     return call(
-        functools.partial(mlp_back_kernel, sizes.count, block, len(loads)),
+        functools.partial(mlp_back_kernel, sizes.count, block),
         4 + block,
         inputs,
-        4 + len(loads),
+        4,
         [
             (sizes.local, F32), (sizes.mods, F32),
             ((sizes.width, sizes.hidden), BF16), ((sizes.width, sizes.hidden), BF16),
             ((1, sizes.hidden), F32), ((1, sizes.width), F32),
-        ]
-        + [(quarter(load.shape), F32) for load in loads],
+        ],
         (),
         [
             pltpu.VMEM(sizes.full, BF16),
@@ -944,28 +1165,26 @@
             pltpu.VMEM(own["two"].shape, BF16),
         ]
         + exchange_scratch(sizes.count, *sizes.local)
-        + semaphores(sizes.count)
-        + carried,
+        + semaphores(sizes.count),
         2 * sizes.tokens * sizes.width * sizes.hidden * 4,
-    )
-
-
-def attend_backward(sizes, block, d_middle, u, attend, mods, segs, own, other, loads):
+        cargos,
+    )
+
+
+def attend_backward(sizes, block, d_middle, u, attend, mods, segs, own, other, cargos):
     middle, branch, full, q, k, v, probs, mixed = attend
     inputs = [d_middle, u, branch, mods, segs[0], full, q, k, v, probs, mixed]
-    inputs += pairs(own, other, ("qkv", "out")) + list(loads)
-    carried = [scratch for load in loads for scratch in courier_scratch(load.shape)]
+    inputs += pairs(own, other, ("qkv", "out"))
     return call(
-        functools.partial(attend_back_kernel, sizes.count, block, len(loads)),
+        functools.partial(attend_back_kernel, sizes.count, block),
         6 + block,
         inputs,
-        4 + len(loads),
+        4,
         [
             (sizes.local, F32), (sizes.mods, F32),
             ((3, sizes.width, sizes.heads_width), BF16), ((sizes.width, sizes.heads_width), BF16),
             ((2, sizes.heads_width), F32), ((1, sizes.width), F32),
-        ]
-        + [(quarter(load.shape), F32) for load in loads],
+        ],
         (),
         [
             pltpu.VMEM(sizes.full, BF16),
@@ -975,30 +1194,28 @@
             pltpu.VMEM(own["out"].shape, BF16),
         ]
         + exchange_scratch(sizes.count, *sizes.local)
-        + semaphores(sizes.count)
-        + carried,
+        + semaphores(sizes.count),
         2 * sizes.tokens * sizes.width * sizes.heads_width * 8,
-    )
-
-
-def close_backward(sizes, outs, grads, mod_grads, small, proj_small, cond, loads, sections, replicas):
+        cargos,
+    )
+
+
+def close_backward(sizes, outs, grads, mod_grads, small, proj_small, cond, sections, replicas, cargos):
     count, width = sizes.count, sizes.width
     piece = 6 * width // count
     share = width // replicas
-    inputs = [*outs, *grads, *mod_grads, *small, proj_small, cond, *loads]
+    inputs = [*outs, *grads, *mod_grads, *small, proj_small, cond]
     copies = count + 3 * (sections * replicas - 1)
-    carried = [scratch for load in loads for scratch in courier_scratch(load.shape)]
     both = (sections * sizes.rows,) + sizes.local[1:]
     return call(
         functools.partial(close_kernel, count, sections, replicas),
         8,
         inputs,
-        len(loads),
+        0,
         [
             (both, BF16), (both, F32), ((share, piece), F32), ((1, piece), F32),
             ((MOD_ROWS, width), F32),
-        ]
-        + [(quarter(load.shape), F32) for load in loads],
+        ],
         (),
         [
             pltpu.VMEM((count, sections, MOD_ROWS, piece), F32),
@@ -1012,9 +1229,9 @@
             pltpu.VMEM((2,) + sizes.local, BF16),
             pltpu.SemaphoreType.DMA((copies,)),
             pltpu.SemaphoreType.DMA((copies,)),
-        ]
-        + carried,
+        ],
         2 * sections * replicas * MOD_ROWS * share * piece,
+        cargos,
     )
 
 
@@ -1173,13 +1390,20 @@
 
     u = to_rows(block_eight_input)
     sizes = Shapes(u, own, count)
-    mods, bias_all, other, attend_one = open_forward(
-        sizes, u, cond_pad.reshape(-1, width), ada_w[0], ada_b, biases, segs, own, sections
-    )
-    mlp_one = mlp_forward(sizes, 0, attend_one[0], mods, bias_all, segs, own, other)
+    mods, bias_all, other, attend_one, unused = open_forward(
+        sizes, u, cond_pad.reshape(-1, width), ada_w[0], ada_b, biases, segs, own, sections, ()
+    )
+    mlp_one, carried = mlp_forward(
+        sizes, 0, attend_one[0], mods, bias_all, segs, own, other, True, (LateShare(other["two"]),)
+    )
+    other["two"] = carried[0][0]
     first_out = mlp_one[0]
-    attend_two = attend_forward(sizes, 1, first_out, mods, bias_all, segs, own, other)
-    mlp_two = mlp_forward(sizes, 1, attend_two[0], mods, bias_all, segs, own, other)
+    attend_two, carried = attend_forward(
+        sizes, 1, first_out, mods, bias_all, segs, own, other, ()
+    )
+    mlp_two, carried = mlp_forward(
+        sizes, 1, attend_two[0], mods, bias_all, segs, own, other, False, ()
+    )
     second_out = mlp_two[0]
 
     target_cols = my_rows(targets, 1).reshape(count, length, rows, -1)
@@ -1192,22 +1416,25 @@
     )
 
     back = (mods, segs, own, other)
-    d_middle_two, mod_mlp_two, *mlp_grads_two = mlp_backward(
+    (d_middle_two, mod_mlp_two, *mlp_grads_two), unused = mlp_backward(
         sizes, 1, to_rows(cot), attend_two, mlp_two, *back, ()
     )
-    second_grad, mod_attend_two, *attend_grads_two = attend_backward(
-        sizes, 1, d_middle_two, first_out, attend_two, *back, mlp_grads_two[:2]
-    )
-    sums_mlp_two = attend_grads_two[4:]
-    d_middle_one, mod_mlp_one, *mlp_grads_one = mlp_backward(
+    (second_grad, mod_attend_two, *attend_grads_two), mlp_parts_two = attend_backward(
+        sizes, 1, d_middle_two, first_out, attend_two, *back,
+        [QuadSum(grad) for grad in mlp_grads_two[:2]],
+    )
+    (d_middle_one, mod_mlp_one, *mlp_grads_one), carried = mlp_backward(
         sizes, 0, second_grad + grad_sent.reshape(rows, length, width), attend_one, mlp_one, *back,
-        attend_grads_two[:2],
-    )
-    sums_attend_two = mlp_grads_one[4:]
-    first_grad, mod_attend_one, *attend_grads_one = attend_backward(
-        sizes, 0, d_middle_one, u, attend_one, *back, mlp_grads_one[:2]
-    )
-    sums_mlp_one = attend_grads_one[4:]
+        [QuadSum(grad) for grad in attend_grads_two[:2]]
+        + [SectionSum(part) for part, in mlp_parts_two],
+    )
+    attend_parts_two, sums_mlp_two = carried[:2], carried[2:]
+    (first_grad, mod_attend_one, *attend_grads_one), carried = attend_backward(
+        sizes, 0, d_middle_one, u, attend_one, *back,
+        [QuadSum(grad) for grad in mlp_grads_one[:2]]
+        + [SectionSum(part) for part, in attend_parts_two],
+    )
+    mlp_parts_one, sums_attend_two = carried[:2], carried[2:]
 
     p1_len, p2_len, p3_len = p1_b.shape[0], p2_b.shape[0], p3_b.shape[0]
     d_p1_b, d_p2_b, d_p3_b = proj_bias_grads
@@ -1221,14 +1448,17 @@
         attend_grads_one[2], attend_grads_one[3], mlp_grads_one[2], mlp_grads_one[3],
         attend_grads_two[2], attend_grads_two[3], mlp_grads_two[2], mlp_grads_two[3],
     ]
-    section_out, section_grad, grad_ada_w, grad_ada_b, small, *sums_attend_one = close_backward(
+    (section_out, section_grad, grad_ada_w, grad_ada_b, small), carried = close_backward(
         sizes, (first_out, second_out), (first_grad, second_grad),
         (mod_attend_one, mod_mlp_one, mod_attend_two, mod_mlp_two),
-        small, proj_small, cond_cols, attend_grads_one[:2], sections, replicas,
-    )
+        small, proj_small, cond_cols, sections, replicas,
+        [LastSum(grad) for grad in attend_grads_one[:2]]
+        + [SectionSum(part) for part, in mlp_parts_one],
+    )
+    sums_attend_one, sums_mlp_one = carried[:2], carried[2:]
 
     red_fc1, red_fc2, red_qkv, red_out = [
-        sum_beyond_quads(jnp.where(is_first, one, two))
+        sum_beyond_quads(jnp.where(is_first, one[0], two[0]))
         for one, two in zip(
             list(sums_mlp_one) + list(sums_attend_one), list(sums_mlp_two) + list(sums_attend_two)
         )

time: 845 us -> 763 us (0.903)
  Pallas kernels: 566 us -> 484 us
    pallas_call x9, Pallas kernels: 566 us -> 484 us  [call(): pl.pallas_call(body, out_shape=[jax.ShapeDtypeStruct(shape, dtype) for sh...]
    unnamed x68 -> x69, local copies, waits for them, and re-layouts: 23 us -> 26.4 us
  transfers between devices with their start and end apart: 8 -> 8, of which waited for: 4 -> 4; matrix products, arithmetic and copies ran while one was open for 5% -> 5% of each run, Pallas kernels for 49% -> 45%
where the time goes in v3:
time: 763 us; the launch traced here: 753 us
  Pallas kernels  484 us (63%)
  waiting for transfers between devices  134 us (18%)
  local copies, waits for them, and re-layouts  48.7 us (6%)
  blocking collectives  30.1 us (4%)
  matrix products  20.3 us (3%)
  other arithmetic  18.8 us (2%)
  between operations  16.5 us (2%)
    pallas_call x9, Pallas kernels, call(): pl.pallas_call(body, out_shape=[jax.ShapeDtypeStruct(shape, dtype) for sh...  484 us
    reduce_scatter x3, waiting for transfers between devices, scatter_rows(): lax.psum_scatter(terms.astype(BF16), 'tensor', scatter_dimension=0, tiled...  67.3 us
    all_gather x2, waiting for transfers between devices, gather_rows(): return lax.all_gather(source_rows, 'tensor', axis=0, tiled=True)  66.7 us
    unnamed x69, local copies, waits for them, and re-layouts  26.4 us
    all_gather x1, blocking collectives, gather_rows(): return lax.all_gather(source_rows, 'tensor', axis=0, tiled=True)  20.3 us
    dot_general x9, matrix products, dot(): return lax.dot_general(left, right, form, preferred_element_type=F32)  20.3 us
  transfers between devices with their start and end apart: 8, of which 4 were waited for; matrix products, arithmetic and copies ran while one was open for 5% of the time, Pallas kernels for 45%

profile of v3, /device:TPU:0, one launch (start us, length us, event | category | flops | bytes accessed | tf_op | source)
XLA Modules:
  0.0 753.4 jit_solution(3774421904702389921)
XLA Ops:
  14.5 2.3 constant_dynamic-slice_fusion
  17.5 4.2 copy.136
  21.7 6.5 copy.135
  28.8 88.9 %shard_map.348 = (f32[2,6,8,1152]{3,2,1,0:T(8,128)}, f32[2,8,1152]{2,1,0:T(8,128)}, bf16[3456,288]{1,0:T(8,128)(2,1)}, bf16[288,1152]{1,0:T(8,128)(2,1)}, bf16[1...) custom-call(bf16[2,48,1152]{2,1,0:T(8,128)(2,1)} %bitcast.98, ...), custom_call_target="tpu_custom_call" | custom-call | flops 1019215872 | bytes 12245760 | tf_op jit(solution)/shard_map/pallas_call | solution.py:1002
  117.8 3.4 copy.168.refs_8_
  121.2 52.7 %shard_map.349 = (bf16[2,48,1152]{2,1,0:T(8,128)(2,1)}, f32[2,48,1152]{2,1,0:T(8,128)}, bf16[2,192,1152]{2,1,0:T(8,128)(2,1)}, f32[2,192,1152]{2,1,0:T(8,128)}, ...) custom-call(f32[2,48,1152]{2,1,0:T(8,128)} %get-tuple-element.95.refs_0_.refs_1_, ...), custom_call_target="tpu_custom_call", output_to_operand_aliasing={{5}: (8, {})} | custom-call | flops 2038431744 | bytes 14229888 | tf_op jit(solution)/shard_map/pallas_call | solution.py:1002
  174.0 20.3 %all_gather.9 = bf16[384,1152]{1,0:T(8,128)(2,1)S(1)} all-gather(bf16[96,1152]{1,0:T(8,128)(2,1)} %bitcast.95), channel_id=1, replica_groups=mesh['section'=2,'dp'=4,'tensor'=4] {'tensor'}, dimensions={0}, use_global_device_ids=true | all-gather | bytes 1105920 | tf_op jit(solution)/shard_map/all_gather | solution.py:1244
  194.3 0.9 copy-done.13
  196.8 2.2 convolution_convert_fusion.4
  199.7 33.6 %reduce-scatter.7.cloned.1.call-done = bf16[96,2048]{1,0:T(8,128)(2,1)} async-done(((bf16[384,2048]{1,0:T(8,128)(2,1)}), bf16[96,2048]{1,0:T(8,128)(2,1)}) %reduce-scatter.7.cloned.1.call-update) | async-done | bytes 393232 | tf_op jit(solution)/shard_map/reduce_scatter | solution.py:1248
  233.2 2.0 multiply_convert_fusion
  236.8 1.1 copy.147
  238.0 33.5 %all-gather.3.cloned.1.call-done = bf16[384,2048]{1,0:T(8,128)(2,1)} async-done(((bf16[96,2048]{1,0:T(8,128)(2,1)}), bf16[384,2048]{1,0:T(8,128)(2,1)}) %all-gather.3.cloned.1.call-update) | async-done | bytes 1572880 | tf_op jit(solution)/shard_map/all_gather | solution.py:1244
  271.5 2.8 multiply_reduce_fusion.2
  274.3 9.8 %psum.7 = f32[3,384]{1,0:T(4,128)S(1)} all-reduce(f32[3,384]{1,0:T(4,128)S(1)} %pad_maximum_fusion), channel_id=1, replica_groups=mesh['section'=2,'dp'=4,'tensor'=4] {'tensor'}, use_global_device_ids=true, to_apply=%region_4.5 | all-reduce | flops 1152 | bytes 9216 | tf_op jit(solution)/shard_map/psum | solution.py:1262
  284.7 1.1 convert_reduce_fusion.2
  285.8 1.7 convolution_convert_fusion.3
  287.6 33.7 %reduce-scatter.9.cloned.1.call-done = bf16[96,2048]{1,0:T(8,128)(2,1)} async-done(((bf16[384,2048]{1,0:T(8,128)(2,1)}), bf16[96,2048]{1,0:T(8,128)(2,1)}) %reduce-scatter.9.cloned.1.call-update) | async-done | bytes 393232 | tf_op jit(solution)/shard_map/reduce_scatter | solution.py:1248
  321.3 2.1 fusion.1
  323.5 2.9 convolution_convert_fusion.5
  326.5 33.2 %all-gather.5.cloned.1.call-done = bf16[384,2048]{1,0:T(8,128)(2,1)} async-done(((bf16[96,2048]{1,0:T(8,128)(2,1)}), bf16[384,2048]{1,0:T(8,128)(2,1)}) %all-gather.5.cloned.1.call-update) | async-done | bytes 1572880 | tf_op jit(solution)/shard_map/all_gather | solution.py:1244
  359.7 2.8 convert_reduce_fusion.1
  363.2 1.6 convolution_convert_fusion.2
  365.0 2.9 convolution_convert_fusion.1
  369.4 51.1 %shard_map.350 = (f32[2,48,1152]{2,1,0:T(8,128)}, f32[2,48,1152]{2,1,0:T(8,128)}, bf16[2,192,1152]{2,1,0:T(8,128)(2,1)}, bf16[2,192,512]{2,1,0:T(8,128)(2,1)}, b...) custom-call(bf16[2,48,1152]{2,1,0:T(8,128)(2,1)} %get-tuple-element., ...), custom_call_target="tpu_custom_call" | custom-call | flops 1019215872 | bytes 6049152 | tf_op jit(solution)/shard_map/pallas_call | solution.py:1002
  420.6 41.2 %shard_map.351 = (bf16[2,48,1152]{2,1,0:T(8,128)(2,1)}, f32[2,48,1152]{2,1,0:T(8,128)}, bf16[2,192,1152]{2,1,0:T(8,128)(2,1)}, f32[2,192,1152]{2,1,0:T(8,128)}, bf16[2,192,1152]{2,1,0:T(8,128)(2,1)}) custom-call(f32[2,48,1152]{2,1,0:T(8,128)} %get-tuple-element.103.refs_0_.refs_1_, f32[2,6,8,1152]{3,2,1,0:T(8,128)} %get-tuple-element.96.refs_1_.refs_3_, ...), custom_call_target="tpu_custom_call" | custom-call | flops 2038431744 | bytes 11575680 | tf_op jit(solution)/shard_map/pallas_call | solution.py:1002
  461.8 40.0 %shard_map.352 = (f32[2,48,1152]{2,1,0:T(8,128)}, f32[3,8,1152]{2,1,0:T(8,128)}, bf16[1152,1152]{1,0:T(8,128)(2,1)}, bf16[1152,1152]{1,0:T(8,128)(2,1)}, f32[1,1152]{1,0:T(1,128)}, /*index=5*/f32[1,1152]{1,0:T(1,128)}) custom-call(bf16[2,48,1152]{2,1,0:T(8,128)(2,1)} %bitcast.102, f32[2,48,1152]{2,1,0:T(8,128)} %get-tuple-element.103.refs_0_.refs_1_, ...), custom_call_target="tpu_custom_call" | custom-call | flops 4076863488 | bytes 15704448 | tf_op jit(solution)/shard_map/pallas_call | solution.py:1002
  501.8 44.0 %shard_map.353 = (f32[2,48,1152]{2,1,0:T(8,128)}, f32[3,8,1152]{2,1,0:T(8,128)}, bf16[3,1152,288]{2,1,0:T(8,128)(2,1)}, bf16[1152,288]{1,0:T(8,128)(2,1)}, f32[2...) custom-call(f32[2,48,1152]{2,1,0:T(8,128)} %get-tuple-element.110.refs_0_, ...), custom_call_target="tpu_custom_call" | custom-call | flops 2038431744 | bytes 15630720 | tf_op jit(solution)/shard_map/pallas_call | solution.py:1002
  545.8 1.6 convert_element_type.148
  549.1 2.8 convolution_convert_fusion
  551.9 1.0 copy-done.3
  552.9 1.7 convert_add_fusion.1.refs_0_
  554.6 44.2 %shard_map.354 = (f32[2,48,1152]{2,1,0:T(8,128)}, f32[3,8,1152]{2,1,0:T(8,128)}, bf16[1152,1152]{1,0:T(8,128)(2,1)}, bf16[1152,1152]{1,0:T(8,128)(2,1)}, f32[1,1...) custom-call(f32[2,48,1152]{2,1,0:T(8,128)} %convert_add_fusion.1.ref, ...), custom_call_target="tpu_custom_call" | custom-call | flops 4076863488 | bytes 19906944 | tf_op jit(solution)/shard_map/pallas_call | solution.py:1002
  598.8 46.0 %shard_map.355 = (f32[2,48,1152]{2,1,0:T(8,128)}, f32[3,8,1152]{2,1,0:T(8,128)}, bf16[3,1152,288]{2,1,0:T(8,128)(2,1)}, bf16[1152,288]{1,0:T(8,128)(2,1)}, f32[2...) custom-call(f32[2,48,1152]{2,1,0:T(8,128)} %get-tuple-element.129.re, ...), custom_call_target="tpu_custom_call" | custom-call | flops 2038431744 | bytes 16294272 | tf_op jit(solution)/shard_map/pallas_call | solution.py:1002
  644.8 76.2 %shard_map.356 = (bf16[4,48,1152]{2,1,0:T(8,128)(2,1)}, f32[4,48,1152]{2,1,0:T(8,128)}, f32[288,1728]{1,0:T(8,128)}, f32[1,1728]{1,0:T(1,128)}, f32[8,1152]{1,0:...) custom-call(bf16[2,48,1152]{2,1,0:T(8,128)(2,1)} %get-tuple-element.100.refs_, ...), custom_call_target="tpu_custom_call" | custom-call | flops 63700992 | bytes 5833728 | tf_op jit(solution)/shard_map/pallas_call | solution.py:1002
  724.2 1.1 select_bitcast_fusion.3
  725.3 1.0 copy.157
  726.3 0.9 copy.155
  727.2 2.5 copy.156
  730.3 1.7 convert_element_type.143
  732.0 1.3 slice_bitcast_fusion
  733.3 1.2 select_bitcast_fusion.2
  734.5 1.5 fusion.15
  736.0 1.2 select_bitcast_fusion
  738.2 1.2 select_bitcast_fusion.1
  739.4 1.0 convert_bitcast_fusion
  740.4 1.0 copy.158
  741.4 3.2 copy.171
  (121 shorter events, 22.2 us)
Async XLA Ops:
  7.2 189.6 %copy-start = (bf16[512,2048]{1,0:T(8,128)(2,1)S(1)}, bf16[512,2048]{1,0:T(8,128)(2,1)}, u32[]{:S(2)}) copy-start(bf16[512,2048]{1,0:T(8,128)(2,1)} %param.38) | copy-start | bytes 6291460
  7.2 226.0 %reduce-scatter.7.cloned.1.call-start = ((), (), s32[]{:S(2)}) async-start(), calls=%async_computation.6 | async-start | bytes 1966080 | tf_op jit(solution)/shard_map/reduce_scatter | solution.py:1248
  21.7 6.5 copy-start.19
  21.7 6.5 copy-start.20
  21.7 6.5 copy-start.21
  121.2 74.0 %copy-start.23 = (bf16[1152,512]{1,0:T(8,128)(2,1)S(1)}, bf16[1152,512]{1,0:T(8,128)(2,1)}, u32[]{:S(2)}) copy-start(bf16[1152,512]{1,0:T(8,128)(2,1)} %param.36) | copy-start | bytes 3538948
  194.3 0.9 copy-start.13
  195.9 0.9 copy-start.27
  199.0 0.7 copy-start.22
  199.0 36.3 %copy-start.25 = (bf16[192]{0:T(256)(128)(2,1)S(1)}, bf16[192]{0:T(256)(128)(2,1)}, u32[]{:S(2)}) copy-start(bf16[192]{0:T(256)(128)(2,1)} %param.41) | copy-start | bytes 1156
  199.0 36.3 %copy-start.17 = (bf16[192,4,192]{2,1,0:T(4,128)(2,1)S(1)}, bf16[192,4,192]{2,1,0:T(4,128)(2,1)}, u32[]{:S(2)}) copy-start(bf16[192,4,192]{2,1,0:T(4,128)(2,1)} %param.24) | copy-start | bytes 884740
  199.0 72.5 %all-gather.3.cloned.1.call-start = ((), (), s32[]{:S(2)}) async-start(), calls=%async_computation.7 | async-start | bytes 1966080 | tf_op jit(solution)/shard_map/all_gather | solution.py:1244
  235.2 36.3 %copy-start.2 = (bf16[2048,192]{0,1:T(8,128)(2,1)S(1)}, bf16[2048,192]{0,1:T(8,128)(2,1)}, u32[]{:S(2)}) copy-start(bf16[2048,192]{0,1:T(8,128)(2,1)} %param.40) | copy-start | bytes 2359300
  235.2 86.2 %reduce-scatter.9.cloned.1.call-start = ((), (), s32[]{:S(2)}) async-start(), calls=%async_computation.8 | async-start | bytes 1966080 | tf_op jit(solution)/shard_map/reduce_scatter | solution.py:1248
  285.8 35.5 %copy-start.5 = (bf16[96,2048]{1,0:T(8,128)(2,1)S(1)}, bf16[96,2048]{1,0:T(8,128)(2,1)}, u32[]{:S(2)}) copy-start(bf16[96,2048]{1,0:T(8,128)(2,1)} %reduce-scatter.7.cloned.1.call-done) | copy-start | bytes 1179652
  287.6 72.1 %all-gather.5.cloned.1.call-start = ((), (), s32[]{:S(2)}) async-start(), calls=%async_computation.9 | async-start | bytes 1966080 | tf_op jit(solution)/shard_map/all_gather | solution.py:1244
  323.5 222.3 %reduce-scatter.17.cloned.1.call-start = ((), (), s32[]{:S(2)}) async-start(), calls=%async_computation.13 | async-start | bytes 884736 | tf_op jit(solution)/shard_map/reduce_scatter | solution.py:1475
  326.4 36.8 %copy-start.24 = (bf16[1152,512]{1,0:T(8,128)(2,1)S(1)}, bf16[1152,512]{1,0:T(8,128)(2,1)}, u32[]{:S(2)}) copy-start(bf16[1152,512]{1,0:T(8,128)(2,1)} %param.36) | copy-start | bytes 3538948
  326.4 225.5 %reduce-scatter.11.cloned.1.call-start = ((), (), s32[]{:S(2)}) async-start(), calls=%async_computation.10 | async-start | bytes 1105920 | tf_op jit(solution)/shard_map/reduce_scatter | solution.py:1248
  362.5 0.7 copy-start.26
  363.2 1.7 copy-start.14
  364.9 365.5 %reduce-scatter.13.cloned.1.call-start = ((), (), s32[]{:S(2)}) async-start(), calls=%async_computation.11 | async-start | bytes 1327104 | tf_op jit(solution)/shard_map/reduce_scatter | solution.py:1475
  364.9 3.8 copy-start.12
  367.8 371.6 %reduce-scatter.15.cloned.1.call-start = ((), (), s32[]{:S(2)}) async-start(), calls=%async_computation.12 | async-start | bytes 2359296 | tf_op jit(solution)/shard_map/reduce_scatter | solution.py:1475
  501.8 45.7 %copy-start.4 = (bf16[384,2048]{1,0:T(8,128)(2,1)S(1)}, bf16[384,2048]{1,0:T(8,128)(2,1)}, u32[]{:S(2)}) copy-start(bf16[384,2048]{1,0:T(8,128)(2,1)} %all-gather.5.cloned.1.call-done) | copy-start | bytes 4718596
  545.8 3.3 copy-start.28
  551.8 1.0 copy-start.3
  644.8 79.4 %copy-start.15 = (f32[288,288]{1,0:T(8,128)S(1)}, f32[288,288]{1,0:T(8,128)}, u32[]{:S(2)}) copy-start(f32[288,288]{1,0:T(8,128)} %get-tuple-element.166) | copy-start | bytes 995332
  721.1 5.2 copy-start.16
  726.3 7.0 copy-start.8
  726.3 7.0 copy-start.11
  733.3 2.7 copy-start.7
  733.3 2.7 copy-start.10
  736.0 1.8 copy-start.6
  736.0 2.2 copy-start.9
  741.4 3.8 copy-start.1
  741.4 3.2 copy-start.18
Sparse Core Ops, SparseCore 0:
  199.1 34.0 reduce-scatter.6
  235.3 36.0 all-gather.2
  287.7 33.5 reduce-scatter.8
  323.6 36.0 all-gather.4
  363.3 33.8 reduce-scatter.16
  399.9 33.7 reduce-scatter.10
  437.5 38.0 reduce-scatter.12
  552.0 48.2 reduce-scatter.14

commit v4 on v3

--- a/solution.py
+++ b/solution.py
@@ -480,6 +480,340 @@
         self.share.finish()
 
 
+class QuadSumX(Cargo):
+    def __init__(self, grad):
+        part = (2,) + quarter(grad.shape)
+        self.inputs = (grad,)
+        self.outs = ((part, BF16),)
+        self.size = grad.shape[-2] // 4
+        self.scratch = (
+            pltpu.VMEM(part, BF16),
+            pltpu.VMEM(part, BF16),
+            pltpu.VMEM(part, BF16),
+            pltpu.SemaphoreType.DMA((3, 3)),
+        )
+
+    def peers(self):
+        return ["core", "x"]
+
+    rows = QuadSum.rows
+
+    def begin(self):
+        QuadSum.begin(self)
+
+    def middle(self):
+        keep, from_core, from_x, sems = self.held
+        wait_all(self.copies)
+        for y in range(2):
+            keep[y] = (keep[y].astype(F32) + from_core[y].astype(F32)).astype(BF16)
+        self.copies = [remote(keep, from_x, sems.at[0, 2], sems.at[1, 2], x_peer())]
+
+    def end(self):
+        keep, from_core, from_x, sems = self.held
+        wait_all(self.copies)
+        self.out_refs[0][...] = (keep[...].astype(F32) + from_x[...].astype(F32)).astype(BF16)
+
+
+class LastY(Cargo):
+    def __init__(self, parts):
+        part = parts.shape[1:]
+        self.inputs = (parts,)
+        self.outs = ((part, F32),)
+        self.scratch = (
+            pltpu.VMEM(part, BF16),
+            pltpu.VMEM(part, BF16),
+            pltpu.SemaphoreType.DMA((3,)),
+        )
+
+    def peers(self):
+        return ["y"]
+
+    def begin(self):
+        mine, other, sems = self.held
+        self.copies = [
+            local(self.ins[0].at[y_bit()], mine, sems.at[2]),
+            remote(self.ins[0].at[1 - y_bit()], other, sems.at[0], sems.at[1], y_peer()),
+        ]
+
+    end = SectionSum.end
+
+
+class Swap(Cargo):
+    def __init__(self, one, two):
+        self.inputs = (one, two)
+        self.outs = ((one.shape, one.dtype),)
+        self.scratch = (pltpu.VMEM(one.shape, one.dtype), pltpu.SemaphoreType.DMA((2,)))
+
+    def peers(self):
+        return ["x"]
+
+    def begin(self):
+        got, sems = self.held
+        one, two = self.ins
+        self.copy = describe(two, got, sems.at[0], sems.at[1], x_peer())
+        is_first = lax.axis_index("section") == 0
+
+        @pl.when(is_first)
+        def give_two():
+            self.copy.start()
+
+        @pl.when(jnp.logical_not(is_first))
+        def give_one():
+            describe(one, got, sems.at[0], sems.at[1], x_peer()).start()
+
+    def end(self):
+        self.copy.wait()
+        self.out_refs[0][...] = self.held[0][...]
+
+
+def span(ref, axis, start, size):
+    part = pl.ds(pl.multiple_of(start, 128 if axis == 1 else 16), size)
+    lead = (slice(None),) * (len(ref.shape) - 2)
+    return ref.at[lead + ((slice(None), part) if axis == 1 else (part, slice(None)))]
+
+
+def cut(shape, axis, by):
+    shape = list(shape)
+    shape[axis - 2] //= by
+    return tuple(shape)
+
+
+class HalfSum(Cargo):
+    def __init__(self, grad, axis, name):
+        part = cut(grad.shape, axis, 2)
+        self.axis, self.name, self.size = axis, name, part[axis - 2]
+        self.inputs = (grad,)
+        self.outs = ((part, BF16),)
+        self.scratch = (
+            pltpu.VMEM(part, BF16),
+            pltpu.VMEM(part, BF16),
+            pltpu.SemaphoreType.DMA((3,)),
+        )
+
+    def peers(self):
+        return [self.name]
+
+    def begin(self):
+        mine, other, sems = self.held
+        if self.name == "x":
+            bit, peer = lax.axis_index("section"), x_peer()
+        else:
+            bit, peer = y_bit(), y_peer()
+        grad = self.ins[0]
+        self.copies = [
+            remote(
+                span(grad, self.axis, (1 - bit) * self.size, self.size), other,
+                sems.at[0], sems.at[1], peer,
+            ),
+            local(span(grad, self.axis, bit * self.size, self.size), mine, sems.at[2]),
+        ]
+
+    def end(self):
+        mine, other, sems = self.held
+        wait_all(self.copies)
+        self.out_refs[0][...] = (mine[...].astype(F32) + other[...].astype(F32)).astype(BF16)
+
+
+class ColumnGather(Cargo):
+    any_outs = True
+
+    def __init__(self, weights, targets, biases, sections):
+        self.inputs = (*weights, targets, biases)
+        self.outs = tuple(((2,) + one.shape, BF16) for one in weights) + (
+            ((2, 2) + targets.shape[1:], BF16),
+            ((2, 2) + biases.shape, F32),
+        )
+        self.scratch = (
+            pltpu.SemaphoreType.DMA((5, 4)),
+            pltpu.SemaphoreType.DMA((5, 2, 2)),
+            pltpu.SemaphoreType.DMA((5,)),
+        )
+
+    def peers(self):
+        return ["core", "cross"]
+
+    def pieces(self, target):
+        tensor, core = lax.axis_index("tensor"), core_bit()
+        eighth = lax.axis_index("section") * 4 + y_bit() * 2 + core
+        slot, out = lax.rem(tensor, 2), []
+        for source, place in zip(self.ins[:3], self.out_refs[:3]):
+            size = source.shape[0] // 8
+            rows = pl.ds(pl.multiple_of(eighth * size, 16), size)
+            out.append((source.at[rows], place.at[slot, rows]))
+        out.append((self.ins[3].at[target], self.out_refs[3].at[slot, core]))
+        out.append((self.ins[4], self.out_refs[4].at[slot, core]))
+        return out
+
+    def copies(self, step):
+        tensor, core = lax.axis_index("tensor"), core_bit()
+        send, recv, own = self.held
+        target = lax.rem(tensor + step, 4)
+        peer = {"tensor": target, "dp": lax.axis_index("dp") - core + tensor // 2}
+        return [
+            describe(source, place, send.at[i, step], recv.at[i, lax.rem(tensor, 2), core], peer)
+            for i, (source, place) in enumerate(self.pieces(target))
+        ]
+
+    def stays(self):
+        return core_bit() == lax.axis_index("tensor") // 2
+
+    def own_copies(self):
+        own = self.held[2]
+        return [
+            pltpu.make_async_copy(source, place, own.at[i])
+            for i, (source, place) in enumerate(self.pieces(lax.axis_index("tensor")))
+        ]
+
+    def begin(self):
+        for step in range(1, 4):
+            for copy in self.copies(step):
+                copy.start()
+
+        @pl.when(self.stays())
+        def keep():
+            for copy in self.own_copies():
+                copy.start()
+
+        @pl.when(jnp.logical_not(self.stays()))
+        def give():
+            for copy in self.copies(0):
+                copy.start()
+
+    def end(self):
+        send, recv, own = self.held
+        tensor, core = lax.axis_index("tensor"), core_bit()
+        for step in range(1, 4):
+            for copy in self.copies(step):
+                copy.wait_send()
+
+        @pl.when(self.stays())
+        def kept():
+            for copy in self.own_copies():
+                copy.wait()
+
+        @pl.when(jnp.logical_not(self.stays()))
+        def given():
+            for copy in self.copies(0):
+                copy.wait_send()
+
+        for slot in range(2):
+            for other in range(2):
+                mine = jnp.logical_and(2 * core + slot == tensor, core == other)
+
+                @pl.when(jnp.logical_not(mine))
+                def arrived(slot=slot, other=other):
+                    peer = {"tensor": lax.rem(tensor + 1, 4)}
+                    for i, (source, place) in enumerate(self.pieces(tensor)):
+                        describe(
+                            source, place, send.at[i, 1], recv.at[i, slot, other], peer
+                        ).wait_recv()
+
+
+class ShareAlong(Cargo):
+    any_outs = True
+
+    def __init__(self, weights, second):
+        self.inputs = tuple(weights)
+        self.outs = tuple((one.shape, BF16) for one in weights)
+        self.aliases = {0: 0, 1: 1, 2: 2}
+        self.second = second
+        self.scratch = (pltpu.SemaphoreType.DMA((4,)), pltpu.SemaphoreType.DMA((4,)))
+
+    def peers(self):
+        return ["x", "y"]
+
+    def begin(self):
+        send, recv = self.held
+        section, y, self.copies = lax.axis_index("section"), y_bit(), []
+
+        def give(which, start, parts, peer):
+            ref = self.out_refs[which]
+            size = ref.shape[1] // 4
+            part = ref.at[:, pl.ds(pl.multiple_of(start * size, 16), parts * size)]
+            i = len(self.copies)
+            self.copies.append(remote(part, part, send.at[i], recv.at[i], peer))
+
+        if not self.second:
+            give(1, 2 * section + y, 1, x_peer())
+            give(0, 2 * section + y, 1, y_peer())
+            give(2, 2 * section + y, 1, y_peer())
+        else:
+            give(0, 2 * section, 2, x_peer())
+            give(2, 2 * section, 2, x_peer())
+            give(1, y, 1, y_peer())
+            give(1, 2 + y, 1, y_peer())
+
+    def end(self):
+        wait_all(self.copies)
+
+
+class ColumnSum(Cargo):
+    def __init__(self, grad, axis):
+        self.axis = axis
+        self.part = cut(grad.shape[1:], axis, 2)
+        self.inputs = (grad,)
+        self.outs = ((self.part, F32),)
+        self.scratch = (
+            pltpu.VMEM((4,) + self.part, BF16),
+            pltpu.SemaphoreType.DMA((4,)),
+            pltpu.SemaphoreType.DMA((4,)),
+            pltpu.SemaphoreType.DMA,
+        )
+
+    def peers(self):
+        return ["core", "cross"]
+
+    def copy(self, slot, other):
+        got, send, recv, own = self.held
+        tensor, core = lax.axis_index("tensor"), core_bit()
+        size = self.part[self.axis]
+        source = span(self.ins[0].at[slot], self.axis, other * size, size)
+        peer = {"tensor": 2 * core + slot, "dp": lax.axis_index("dp") - core + other}
+        mine = jnp.logical_and(2 * core + slot == tensor, core == other)
+        away = describe(source, got.at[tensor], send.at[2 * slot + other], recv.at[tensor], peer)
+        return mine, away, pltpu.make_async_copy(source, got.at[tensor], own)
+
+    def each(self, act_away, act_own):
+        for slot in range(2):
+            for other in range(2):
+                mine, away, own = self.copy(slot, other)
+
+                @pl.when(mine)
+                def stay(own=own):
+                    act_own(own)
+
+                @pl.when(jnp.logical_not(mine))
+                def leave(away=away):
+                    act_away(away)
+
+    def begin(self):
+        self.each(lambda copy: copy.start(), lambda copy: copy.start())
+
+    def end(self):
+        got, send, recv, own = self.held
+        tensor, core = lax.axis_index("tensor"), core_bit()
+        self.each(lambda copy: copy.wait_send(), lambda copy: copy.wait())
+        for source in range(4):
+            mine = jnp.logical_and(tensor == source, core == tensor // 2)
+
+            @pl.when(jnp.logical_not(mine))
+            def arrived(source=source):
+                describe(
+                    got.at[source], got.at[source], send.at[0], recv.at[source],
+                    {"tensor": lax.rem(tensor + 1, 4)},
+                ).wait_recv()
+
+        total = got[0].astype(F32)
+        for source in range(1, 4):
+            total = total + got[source].astype(F32)
+        self.out_refs[0][...] = total
+
+
+def cross_peers():
+    tensor, dp = lax.axis_index("tensor"), core_peer()["dp"]
+    return [{"tensor": lax.rem(tensor + step, 4), "dp": dp} for step in range(1, 4)]
+
+
 class Bundle:
     def __init__(self, cargos):
         self.cargos = cargos
@@ -487,7 +821,8 @@
     def peers(self):
         names = [name for cargo in self.cargos for name in cargo.peers()]
         known = {"core": core_peer, "y": y_peer, "x": x_peer}
-        return [make() for name, make in known.items() if name in names]
+        cross = cross_peers() if "cross" in names else []
+        return [make() for name, make in known.items() if name in names] + cross
 
     def begin(self):
         for cargo in self.cargos:
@@ -589,8 +924,7 @@
         for b in range(count)
         if a or b
     ]
-    greet(plane + [core_peer(), y_peer()])
-    cargo.begin()
+    greet(plane + [core_peer(), y_peer()] + cross_peers())
     shares[0].begin()
     cond_act = silu(cond_ref[...].astype(F32)).astype(BF16)
     load_ada.wait()
@@ -611,6 +945,7 @@
     )
     for share in shares[1:]:
         share.begin()
+    cargo.begin()
 
     def mods():
         wait_all(copies)
@@ -842,13 +1177,148 @@
     cargo.end()
 
 
+def silu_slope(value):
+    gate = 1.0 / (1.0 + jnp.exp(-value))
+    return gate * (1.0 + value * (1.0 - gate))
+
+
+def project_kernel(token_count, *refs, cargo):
+    sent_ref, targets_ref, biases_ref, p2_b_ref, p1_any, p2_any, p3_any = refs[:7]
+    d_sent_ref, d_p1_ref, d_p2_ref, d_p3_ref, small_ref = refs[7:12]
+    p1, p2, p3, tokens, first_pre, first, second_pre, second, d_second, norms = refs[12:22]
+    buf_a, buf_b, buf_c, d_first, load_sem, send, recv = refs[22:]
+    core, peer = core_bit(), core_peer()
+    loads = [
+        local(source, place, load_sem.at[i])
+        for i, (source, place) in enumerate(((p1_any, p1), (p2_any, p2), (p3_any, p3)))
+    ]
+    count = tokens.shape[1]
+    tokens[core] = flat(sent_ref)
+    greet([peer])
+
+    def trade(ref, which):
+        return remote(ref.at[core], ref.at[core], send.at[which], recv.at[which], peer)
+
+    def give(buffer, value, which):
+        buffer[0] = value.astype(BF16)
+        return remote(buffer.at[0], buffer.at[1], send.at[which], recv.at[which], peer)
+
+    def block(ref, side):
+        return ref[side]
+
+    copy = trade(tokens, 0)
+    target = [
+        targets_ref[slot].reshape(2 * count, targets_ref.shape[-1]).astype(F32) for slot in range(2)
+    ]
+    target_sq = sum(jnp.sum(one * one, axis=1, keepdims=True) for one in target)
+    loads[0].wait()
+    copy.wait()
+    all_tokens = flat(tokens)
+    for slot in range(2):
+        pre = dot(all_tokens, p1[slot]) + biases_ref[slot, 0, 0:1, :]
+        first_pre[slot] = pre
+        first[slot] = silu(pre).astype(BF16)
+    loads[1].wait()
+
+    def second_term(side):
+        rows = pl.ds(pl.multiple_of(side * count, 16), count)
+        return dot(first[0, rows, :], p2[0]) + dot(first[1, rows, :], p2[1])
+
+    copy = give(buf_a, second_term(1 - core), 1)
+    pre = second_term(core)
+    copy.wait()
+    pre = pre + buf_a[1].astype(F32) + p2_b_ref[...].astype(F32)
+    second_pre[...] = pre
+    second[core] = silu(pre).astype(BF16)
+    copy = trade(second, 2)
+    loads[2].wait()
+    copy.wait()
+    all_second = flat(second)
+    width = target[0].shape[1]
+    predicted = [
+        dot(all_second, p3[slot]) + biases_ref[slot, 0, 1:2, :width] for slot in range(2)
+    ]
+    pred_sq = sum(jnp.sum(one * one, axis=1, keepdims=True) for one in predicted)
+    cross = sum(
+        jnp.sum(one * two, axis=1, keepdims=True) for one, two in zip(predicted, target)
+    )
+    lanes = lax.broadcasted_iota(jnp.int32, norms.shape[1:], 1)
+    norms[core] = jnp.where(lanes == 0, pred_sq, jnp.where(lanes == 1, cross, target_sq))
+    copy = trade(norms, 3)
+    copy.wait()
+    total = norms[0] + norms[1]
+    inv_pred = lax.rsqrt(total[:, 0:1] + COSINE_EPS)
+    inv_target = lax.rsqrt(total[:, 2:3] + COSINE_EPS)
+    cosine = total[:, 1:2] * inv_pred * inv_target
+    side = lax.broadcasted_iota(jnp.int32, cosine.shape, 0)
+    own = jnp.logical_and(side >= core * count, side < (core + 1) * count)
+    loss = jnp.sum(jnp.where(own, cosine, 0.0), axis=0, keepdims=True)
+    factor = -0.5 / token_count
+    one_scale = factor * inv_pred * inv_target
+    two_scale = factor * cosine * inv_pred * inv_pred
+    d_pred = [
+        (one_scale * two - two_scale * one).astype(BF16) for one, two in zip(predicted, target)
+    ]
+    small_ref[...] = jnp.zeros_like(small_ref)
+    for slot in range(2):
+        small_ref[2 * core + slot, 1:2, :width] = jnp.sum(
+            d_pred[slot].astype(F32), axis=0, keepdims=True
+        )
+
+    def d_second_term(side):
+        terms = 0.0
+        for slot in range(2):
+            mine = jnp.where(
+                side == 0, d_pred[slot][:count].astype(F32), d_pred[slot][count:].astype(F32)
+            )
+            terms = terms + dot(mine.astype(BF16), p3[slot], NT)
+        return terms
+
+    copy = give(buf_b, d_second_term(1 - core), 4)
+    grad = d_second_term(core)
+    for slot in range(2):
+        d_p3_ref[slot] = dot(all_second, d_pred[slot], TN).astype(BF16)
+    copy.wait()
+    grad = ((grad + buf_b[1].astype(F32)) * silu_slope(second_pre[...])).astype(BF16)
+    d_second[core] = grad
+    copy = trade(d_second, 5)
+    d_p2_b = jnp.sum(grad.astype(F32), axis=0, keepdims=True)
+    lane = small_ref.shape[2]
+    loss_row = jnp.where(lax.broadcasted_iota(jnp.int32, (1, lane), 1) == 0, loss, 0.0)
+    for part in range(4):
+        for row in range(d_p2_b.shape[1] // lane):
+            small_ref[part, 2 + row : 3 + row, :] = d_p2_b[:, row * lane : (row + 1) * lane]
+        small_ref[part, 6:7, :] = loss_row
+    copy.wait()
+    all_d_second = flat(d_second)
+    for slot in range(2):
+        back = dot(all_d_second, p2[slot], NT) * silu_slope(first_pre[slot])
+        d_first[slot] = back.astype(BF16)
+        small_ref[2 * core + slot, 0:1, :] = jnp.sum(
+            d_first[slot].astype(F32), axis=0, keepdims=True
+        )
+
+    def d_sent_term(side):
+        rows = pl.ds(pl.multiple_of(side * count, 16), count)
+        return dot(d_first[0, rows, :], p1[0], NT) + dot(d_first[1, rows, :], p1[1], NT)
+
+    copy = give(buf_c, d_sent_term(1 - core), 6)
+    grad = d_sent_term(core)
+    for slot in range(2):
+        d_p2_ref[slot] = dot(first[slot], all_d_second, TN).astype(BF16)
+        d_p1_ref[slot] = dot(all_tokens, d_first[slot], TN).astype(BF16)
+    copy.wait()
+    d_sent_ref[...] = (grad + buf_c[1].astype(F32)).reshape(d_sent_ref.shape)
+
+
 def close_kernel(count, sections, replicas, *refs, cargo):
-    outs_ref, grads_ref, mod_refs, small_refs = refs[:2], refs[2:4], refs[4:8], refs[8:17]
-    cond_ref = refs[17]
-    out_ref, grad_ref, ada_w_ref, ada_b_ref, small_ref = refs[18:23]
-    z_src, z_buf, mod_src, mod_buf, small_src, small_buf, cond_buf = refs[23:30]
-    place_src, place_buf = refs[30:32]
-    sems = refs[32:34]
+    grads_ref, mod_refs, small_refs, proj_ref, cond_ref = (
+        refs[:2], refs[2:6], refs[6:14], refs[14], refs[15]
+    )
+    grad_ref, ada_w_ref, ada_b_ref, small_ref, proj_sum_ref = refs[16:21]
+    z_src, z_buf, mod_src, mod_buf, small_src, small_buf, cond_buf = refs[21:28]
+    place_src, place_buf, proj_got, proj_src, proj_buf = refs[28:33]
+    sems = refs[33:35]
     section, tensor, replica = (lax.axis_index(name) for name in ("section", "tensor", "dp"))
     send, recv = sems
     others = [
@@ -857,8 +1327,10 @@
         for b in range(replicas)
         if a or b
     ]
-    greet(z_peers(count) + others)
-    cargo.begin()
+    greet(z_peers(count) + others + cross_peers())
+    for one in cargo.cargos:
+        if isinstance(one, LastSum):
+            one.begin()
     piece = z_src.shape[-1]
     for block in range(sections):
         attend_mod, mlp_mod = mod_refs[2 * block : 2 * block + 2]
@@ -877,15 +1349,19 @@
         for i, peer in enumerate(z_peers(count))
     ]
     at = count - 1
+    z_copies += [
+        remote(proj_ref.at[peer["tensor"]], proj_got.at[i], send.at[at + i], recv.at[at + i], peer)
+        for i, peer in enumerate(z_peers(count))
+    ]
+    at = at + count - 1
+
     @pl.when(section == 0)
     def first_place():
-        place_src[0] = outs_ref[1][...]
-        place_src[1] = grads_ref[1][...].astype(BF16)
+        place_src[...] = grads_ref[1][...].astype(BF16)
 
     @pl.when(section != 0)
     def second_place():
-        place_src[0] = outs_ref[0][...]
-        place_src[1] = grads_ref[0][...].astype(BF16)
+        place_src[...] = grads_ref[0][...].astype(BF16)
 
     place_copy = remote(place_src, place_buf, send.at[at], recv.at[at], x_peer())
     at = at + 1
@@ -897,7 +1373,6 @@
         small_src[block, 2:3, :] = d_bo[...]
         small_src[block, 3:4, : d_b1.shape[1]] = d_b1[...]
         small_src[block, 4:5, :] = d_b2[...]
-        small_src[block, 5:8, :] = small_refs[8][...]
     small_buf[section, replica] = small_src[section]
     cond_buf[section, replica] = cond_ref[replica]
     copies = []
@@ -917,11 +1392,14 @@
         at = at + 2
     cargo.middle()
     wait_all(z_copies)
-    mine = z_src[tensor]
+    mine, mine_proj = z_src[tensor], proj_ref[tensor]
     for step in range(count - 1):
         mine = mine + z_buf[step]
+        mine_proj = mine_proj + proj_got[step]
     mod_src[...] = mine
     mod_buf[section, replica] = mod_src[section]
+    proj_src[...] = mine_proj
+    proj_buf[section, replica] = mine_proj
     for peer in others:
         copies.append(
             remote(
@@ -929,34 +1407,40 @@
                 send.at[at], recv.at[at], peer,
             )
         )
-        at = at + 1
+        copies.append(
+            remote(
+                proj_src, proj_buf.at[section, replica], send.at[at + 1], recv.at[at + 1], peer
+            )
+        )
+        at = at + 2
+    for one in cargo.cargos:
+        if not isinstance(one, LastSum):
+            one.begin()
     for one in cargo.cargos:
         if isinstance(one, LastSum):
             one.to_x()
     place_copy.wait()
-    rows = place_buf.shape[1]
+    rows = place_buf.shape[0]
 
     @pl.when(section == 0)
     def first_out():
-        out_ref[:rows] = outs_ref[0][...]
         grad_ref[:rows] = grads_ref[0][...]
-        out_ref[rows:] = place_buf[0]
-        grad_ref[rows:] = place_buf[1].astype(F32)
+        grad_ref[rows:] = place_buf[...].astype(F32)
 
     @pl.when(section != 0)
     def second_out():
-        out_ref[rows:] = outs_ref[1][...]
         grad_ref[rows:] = grads_ref[1][...]
-        out_ref[:rows] = place_buf[0]
-        grad_ref[:rows] = place_buf[1].astype(F32)
+        grad_ref[:rows] = place_buf[...].astype(F32)
 
     wait_all(copies)
-    small = small_buf[0, 0]
+    small, proj_sum = small_buf[0, 0], proj_buf[0, 0]
     for a in range(sections):
         for b in range(replicas):
             if a or b:
                 small = small + small_buf[a, b]
+                proj_sum = proj_sum + proj_buf[a, b]
     small_ref[...] = small
+    proj_sum_ref[...] = proj_sum
     mod_all = flat(mod_buf)
     ada_b_ref[...] = jnp.sum(mod_all, axis=0, keepdims=True)
     ada_w_ref[...] = lax.dot_general(
@@ -1200,12 +1684,51 @@
     )
 
 
-def close_backward(sizes, outs, grads, mod_grads, small, proj_small, cond, sections, replicas, cargos):
+def project(sizes, sent, weights, targets, biases, p2_b, token_count):
+    tokens = sizes.rows * sizes.length
+    p1, p2, p3 = weights
+    lane, hidden = p1.shape[2], p2.shape[2]
+    inputs = [sent, targets, biases, p2_b, p1, p2, p3]
+    results, unused = call(
+        functools.partial(project_kernel, token_count),
+        9,
+        inputs,
+        3,
+        [
+            (sizes.local, F32), (p1.shape, BF16), (p2.shape, BF16), (p3.shape, BF16),
+            ((sizes.count, MOD_ROWS, lane), F32),
+        ],
+        (),
+        [
+            pltpu.VMEM(p1.shape, BF16),
+            pltpu.VMEM(p2.shape, BF16),
+            pltpu.VMEM(p3.shape, BF16),
+            pltpu.VMEM((2, tokens, sizes.width), BF16),
+            pltpu.VMEM((2, 2 * tokens, lane), F32),
+            pltpu.VMEM((2, 2 * tokens, lane), BF16),
+            pltpu.VMEM((tokens, hidden), F32),
+            pltpu.VMEM((2, tokens, hidden), BF16),
+            pltpu.VMEM((2, tokens, hidden), BF16),
+            pltpu.VMEM((2, 2 * tokens, HEAD_LANES), F32),
+            pltpu.VMEM((2, tokens, hidden), BF16),
+            pltpu.VMEM((2, tokens, hidden), BF16),
+            pltpu.VMEM((2, tokens, sizes.width), BF16),
+            pltpu.VMEM((2, 2 * tokens, lane), BF16),
+            pltpu.SemaphoreType.DMA((3,)),
+            pltpu.SemaphoreType.DMA((7,)),
+            pltpu.SemaphoreType.DMA((7,)),
+        ],
+        12 * tokens * sum(math.prod(one.shape) for one in weights),
+    )
+    return results
+
+
+def close_backward(sizes, grads, mod_grads, small, proj_small, cond, sections, replicas, cargos):
     count, width = sizes.count, sizes.width
     piece = 6 * width // count
     share = width // replicas
-    inputs = [*outs, *grads, *mod_grads, *small, proj_small, cond]
-    copies = count + 3 * (sections * replicas - 1)
+    inputs = [*grads, *mod_grads, *small, proj_small, cond]
+    copies = 2 * count + 4 * (sections * replicas - 1)
     both = (sections * sizes.rows,) + sizes.local[1:]
     return call(
         functools.partial(close_kernel, count, sections, replicas),
@@ -1213,8 +1736,8 @@
         inputs,
         0,
         [
-            (both, BF16), (both, F32), ((share, piece), F32), ((1, piece), F32),
-            ((MOD_ROWS, width), F32),
+            (both, F32), ((share, piece), F32), ((1, piece), F32),
+            ((MOD_ROWS, width), F32), (proj_small.shape[1:], F32),
         ],
         (),
         [
@@ -1225,76 +1748,16 @@
             pltpu.VMEM((sections, MOD_ROWS, width), F32),
             pltpu.VMEM((sections, replicas, MOD_ROWS, width), F32),
             pltpu.VMEM((sections, replicas, MOD_ROWS, share), F32),
-            pltpu.VMEM((2,) + sizes.local, BF16),
-            pltpu.VMEM((2,) + sizes.local, BF16),
+            pltpu.VMEM(sizes.local, BF16),
+            pltpu.VMEM(sizes.local, BF16),
+            pltpu.VMEM((count - 1,) + proj_small.shape[1:], F32),
+            pltpu.VMEM(proj_small.shape[1:], F32),
+            pltpu.VMEM((sections, replicas) + proj_small.shape[1:], F32),
             pltpu.SemaphoreType.DMA((copies,)),
             pltpu.SemaphoreType.DMA((copies,)),
         ],
         2 * sections * replicas * MOD_ROWS * share * piece,
         cargos,
-    )
-
-
-def act_grad(function, source_rows, upstream):
-    unused_value, pullback = jax.vjp(function, source_rows)
-    return pullback(upstream)[0]
-
-
-def gather_rows(source_rows):
-    return lax.all_gather(source_rows, "tensor", axis=0, tiled=True)
-
-
-def scatter_rows(terms):
-    return lax.psum_scatter(
-        terms.astype(BF16), "tensor", scatter_dimension=0, tiled=True
-    ).astype(F32)
-
-
-def align_pass(sent_rows, target_cols, proj_weights, total_token_count):
-    p1_w, p1_b, p2_w, p2_b, p3_w, p3_b = proj_weights
-    input_full = gather_rows(sent_rows)
-    first_pre = dot(input_full, p1_w) + p1_b.astype(F32)
-    first_act = jax.nn.silu(first_pre).astype(BF16)
-    second_pre = scatter_rows(dot(first_act, p2_w)) + p2_b.astype(F32)
-    second_act = jax.nn.silu(second_pre).astype(BF16)
-    second_full = gather_rows(second_act)
-    predicted = dot(second_full, p3_w) + p3_b.astype(F32)
-    pred_sq, cross, target_sq = lax.psum(
-        jnp.stack(
-            [
-                jnp.sum(predicted * predicted, axis=1),
-                jnp.sum(predicted * target_cols, axis=1),
-                jnp.sum(target_cols * target_cols, axis=1),
-            ]
-        ),
-        "tensor",
-    )
-    inv_pred = lax.rsqrt(pred_sq + COSINE_EPS)
-    inv_target = lax.rsqrt(target_sq + COSINE_EPS)
-    cosine = cross * inv_pred * inv_target
-    loss_local = jnp.sum(cosine)
-    factor = -0.5 / total_token_count
-    grad_pred = (
-        (factor * inv_pred * inv_target)[:, None] * target_cols
-        - (factor * cosine * inv_pred * inv_pred)[:, None] * predicted
-    ).astype(BF16)
-    grad_p3_b = jnp.sum(grad_pred.astype(F32), axis=0)
-    grad_p3_w = dot(second_full, grad_pred, TN)
-    grad_second_act = scatter_rows(dot(grad_pred, p3_w, NT))
-    grad_second_pre = act_grad(jax.nn.silu, second_pre, grad_second_act).astype(BF16)
-    grad_second_full = gather_rows(grad_second_pre)
-    grad_p2_b = jnp.sum(grad_second_full.astype(F32), axis=0)
-    grad_p2_w = dot(grad_second_full, first_act, TN)
-    grad_first_act = dot(grad_second_full, p2_w, NT)
-    grad_first_pre = act_grad(jax.nn.silu, first_pre, grad_first_act).astype(BF16)
-    grad_p1_b = jnp.sum(grad_first_pre.astype(F32), axis=0)
-    grad_p1_w = dot(input_full, grad_first_pre, TN)
-    grad_sent = scatter_rows(dot(grad_first_pre, p1_w, NT))
-    return (
-        loss_local,
-        grad_sent,
-        (grad_p1_w, grad_p2_w, grad_p3_w),
-        (grad_p1_b, grad_p2_b, grad_p3_b),
     )
 
 
@@ -1388,58 +1851,74 @@
     seg_own = lax.dynamic_slice_in_dim(segs_full, tensor * length, length, 1)
     segs = (seg_own[:, :, None], segs_full[:, :, None], segs_full[:, None, :])
 
+    target_parts = my_rows(targets, 1).reshape(count, length, rows, targets.shape[2])
+    target_parts = jnp.transpose(target_parts, (0, 2, 1, 3))
+    lane = p1_b.shape[0]
+    proj_biases = jnp.concatenate(
+        [
+            p1_b.astype(F32)[None],
+            jnp.pad(p3_b.astype(F32), (0, lane - p3_b.shape[0]))[None],
+            jnp.zeros((MOD_ROWS - 2, lane), F32),
+        ],
+        axis=0,
+    )
+    gather = ColumnGather((p1_w, p2_w, p3_w), target_parts, proj_biases, sections)
+
     u = to_rows(block_eight_input)
     sizes = Shapes(u, own, count)
-    mods, bias_all, other, attend_one, unused = open_forward(
-        sizes, u, cond_pad.reshape(-1, width), ada_w[0], ada_b, biases, segs, own, sections, ()
-    )
+    mods, bias_all, other, attend_one, carried = open_forward(
+        sizes, u, cond_pad.reshape(-1, width), ada_w[0], ada_b, biases, segs, own, sections,
+        (gather,),
+    )
+    *proj_weights, target_all, proj_bias_all = carried[0]
     mlp_one, carried = mlp_forward(
-        sizes, 0, attend_one[0], mods, bias_all, segs, own, other, True, (LateShare(other["two"]),)
+        sizes, 0, attend_one[0], mods, bias_all, segs, own, other, True,
+        (LateShare(other["two"]), ShareAlong(proj_weights, False)),
     )
     other["two"] = carried[0][0]
+    proj_weights = carried[1]
     first_out = mlp_one[0]
     attend_two, carried = attend_forward(
-        sizes, 1, first_out, mods, bias_all, segs, own, other, ()
-    )
+        sizes, 1, first_out, mods, bias_all, segs, own, other, (ShareAlong(proj_weights, True),)
+    )
+    proj_weights = carried[0]
     mlp_two, carried = mlp_forward(
         sizes, 1, attend_two[0], mods, bias_all, segs, own, other, False, ()
     )
     second_out = mlp_two[0]
 
-    target_cols = my_rows(targets, 1).reshape(count, length, rows, -1)
-    target_cols = jnp.transpose(target_cols, (0, 2, 1, 3)).reshape(rows * positions, -1)
-    loss_local, grad_sent, proj_grads, proj_bias_grads = align_pass(
-        first_out.reshape(rows * length, width),
-        target_cols.astype(F32),
-        (p1_w, p1_b, p2_w, p2_b, p3_w, p3_b),
-        total_token_count,
+    grad_sent, grad_p1, grad_p2, grad_p3, proj_small = project(
+        sizes, first_out, proj_weights, target_all, proj_bias_all, p2_b[None], total_token_count
     )
 
     back = (mods, segs, own, other)
-    (d_middle_two, mod_mlp_two, *mlp_grads_two), unused = mlp_backward(
-        sizes, 1, to_rows(cot), attend_two, mlp_two, *back, ()
-    )
-    (second_grad, mod_attend_two, *attend_grads_two), mlp_parts_two = attend_backward(
+    (d_middle_two, mod_mlp_two, *mlp_grads_two), carried = mlp_backward(
+        sizes, 1, to_rows(cot), attend_two, mlp_two, *back,
+        [HalfSum(grad_p2, 1, "x"), Swap(first_out, second_out)],
+    )
+    (grad_p2,), (other_out,) = carried
+    (second_grad, mod_attend_two, *attend_grads_two), carried = attend_backward(
         sizes, 1, d_middle_two, first_out, attend_two, *back,
-        [QuadSum(grad) for grad in mlp_grads_two[:2]],
-    )
+        [QuadSum(grad) for grad in mlp_grads_two[:2]]
+        + [HalfSum(grad_p1, 0, "x"), HalfSum(grad_p3, 0, "x")],
+    )
+    mlp_parts_two, ((grad_p1,), (grad_p3,)) = carried[:2], carried[2:]
     (d_middle_one, mod_mlp_one, *mlp_grads_one), carried = mlp_backward(
-        sizes, 0, second_grad + grad_sent.reshape(rows, length, width), attend_one, mlp_one, *back,
+        sizes, 0, second_grad + grad_sent, attend_one, mlp_one, *back,
         [QuadSum(grad) for grad in attend_grads_two[:2]]
-        + [SectionSum(part) for part, in mlp_parts_two],
-    )
-    attend_parts_two, sums_mlp_two = carried[:2], carried[2:]
+        + [SectionSum(part) for part, in mlp_parts_two]
+        + [HalfSum(grad_p2, 1, "y")],
+    )
+    attend_parts_two, sums_mlp_two, ((grad_p2,),) = carried[:2], carried[2:4], carried[4:]
     (first_grad, mod_attend_one, *attend_grads_one), carried = attend_backward(
         sizes, 0, d_middle_one, u, attend_one, *back,
-        [QuadSum(grad) for grad in mlp_grads_one[:2]]
-        + [SectionSum(part) for part, in attend_parts_two],
-    )
-    mlp_parts_one, sums_attend_two = carried[:2], carried[2:]
-
-    p1_len, p2_len, p3_len = p1_b.shape[0], p2_b.shape[0], p3_b.shape[0]
-    d_p1_b, d_p2_b, d_p3_b = proj_bias_grads
-    flat_small = jnp.concatenate([d_p2_b, d_p1_b, d_p3_b, loss_local[None]])
-    proj_small = jnp.pad(flat_small, (0, 3 * width - flat_small.shape[0])).reshape(3, width)
+        [QuadSum(mlp_grads_one[0]), QuadSumX(mlp_grads_one[1])]
+        + [SectionSum(part) for part, in attend_parts_two]
+        + [HalfSum(grad_p1, 0, "y"), HalfSum(grad_p3, 0, "y"), ColumnSum(grad_p2, 1)],
+    )
+    ((mlp_part_one,), (mlp_part_two,)), sums_attend_two = carried[:2], carried[2:4]
+    (grad_p1,), (grad_p3,), (red_p2_w,) = carried[4:]
+
     cond_act = silu(my_rows(cond, 0).astype(F32)).astype(BF16).astype(F32)
     share = width // replicas
     cond_cols = jnp.pad(cond_act.reshape(used, width), ((0, MOD_ROWS - used), (0, 0)))
@@ -1448,14 +1927,15 @@
         attend_grads_one[2], attend_grads_one[3], mlp_grads_one[2], mlp_grads_one[3],
         attend_grads_two[2], attend_grads_two[3], mlp_grads_two[2], mlp_grads_two[3],
     ]
-    (section_out, section_grad, grad_ada_w, grad_ada_b, small), carried = close_backward(
-        sizes, (first_out, second_out), (first_grad, second_grad),
+    (section_grad, grad_ada_w, grad_ada_b, small, proj_small), carried = close_backward(
+        sizes, (first_grad, second_grad),
         (mod_attend_one, mod_mlp_one, mod_attend_two, mod_mlp_two),
         small, proj_small, cond_cols, sections, replicas,
         [LastSum(grad) for grad in attend_grads_one[:2]]
-        + [SectionSum(part) for part, in mlp_parts_one],
-    )
-    sums_attend_one, sums_mlp_one = carried[:2], carried[2:]
+        + [SectionSum(mlp_part_one), LastY(mlp_part_two)]
+        + [ColumnSum(grad_p1, 0), ColumnSum(grad_p3, 0)],
+    )
+    sums_attend_one, sums_mlp_one, ((red_p1_w,), (red_p3_w,)) = carried[:2], carried[2:4], carried[4:]
 
     red_fc1, red_fc2, red_qkv, red_out = [
         sum_beyond_quads(jnp.where(is_first, one[0], two[0]))
@@ -1463,18 +1943,16 @@
             list(sums_mlp_one) + list(sums_attend_one), list(sums_mlp_two) + list(sums_attend_two)
         )
     ]
-    flat_small = small[5:8].reshape(-1)
-    red_p2_b = flat_small[:p2_len]
-    red_p1_b = flat_small[p2_len : p2_len + p1_len]
-    red_p3_b = flat_small[p2_len + p1_len : p2_len + p1_len + p3_len]
-    loss_total = flat_small[p2_len + p1_len + p3_len]
-    align_loss = -0.5 * loss_total / total_token_count
-
-    grad_p1_w, grad_p2_w, grad_p3_w = proj_grads
-    red_p1_w, red_p2_w, red_p3_w = [
-        lax.psum_scatter(value.astype(BF16), ("section", "dp"), scatter_dimension=0, tiled=True)
-        for value in (grad_p1_w, grad_p2_w, grad_p3_w)
-    ]
+    red_p1_w, red_p3_w = sum_beyond_quads(red_p1_w), sum_beyond_quads(red_p3_w)
+    if replicas > 4:
+        red_p2_w = sum_beyond_quads(red_p2_w.T).T
+    align_loss = -0.5 * proj_small[6, 0] / total_token_count
+    own_out = jnp.where(is_first, first_out, second_out)
+    section_out = jnp.where(
+        is_first,
+        jnp.concatenate([own_out, other_out], axis=0),
+        jnp.concatenate([other_out, own_out], axis=0),
+    )
     return (
         jnp.transpose(section_out, (1, 0, 2))[None],
         jnp.transpose(section_grad, (1, 0, 2))[None],
@@ -1489,12 +1967,12 @@
         small[3:4, :hidden],
         red_fc2.T[None],
         small[4:5],
-        red_p1_w.astype(F32),
-        red_p1_b,
-        red_p2_w.T.astype(F32),
-        red_p2_b,
-        red_p3_w.astype(F32),
-        red_p3_b,
+        red_p1_w,
+        proj_small[0],
+        red_p2_w,
+        proj_small[2:6].reshape(-1)[: p2_b.shape[0]],
+        red_p3_w,
+        proj_small[1, : p3_b.shape[0]],
     )
 
 

time: 763 us -> 673 us (0.88)
  waiting for transfers between devices: 134 us -> 0 us
  Pallas kernels: 484 us -> 615 us
  blocking collectives: 30.1 us -> 0 us
  matrix products: 20.3 us -> 0 us
  between operations: 16.5 us -> 3.01 us
  other arithmetic: 18.8 us -> 7.84 us
  local copies, waits for them, and re-layouts: 48.7 us -> 38.1 us
    pallas_call x9 -> x10, Pallas kernels: 484 us -> 615 us  [call(): pl.pallas_call(body, out_shape=[jax.ShapeDtypeStruct(shape, dtype) for sh...]
    reduce_scatter x6 -> x0, waiting for transfers between devices: 67.3 us -> none  [the longest x3 67.3 us: scatter_rows(): lax.psum_scatter(terms.astype(BF16), 'tensor', scatter_dimension=0, tiled...]
    all_gather x2 -> x0, waiting for transfers between devices: 66.7 us -> none  [gather_rows(): return lax.all_gather(source_rows, 'tensor', axis=0, tiled=True)]
    all_gather x1 -> x0, blocking collectives: 20.3 us -> none  [gather_rows(): return lax.all_gather(source_rows, 'tensor', axis=0, tiled=True)]
    dot_general x9 -> x0, matrix products: 20.3 us -> none  [dot(): return lax.dot_general(left, right, form, preferred_element_type=F32)]
    psum x1 -> x0, blocking collectives: 9.79 us -> none  [align_pass(): lax.psum(jnp.stack([jnp.sum(predicted * predicted, axis=1), jnp.sum(predi...]
    convert_element_type x9 -> x0, other arithmetic: 9.22 us -> none  [the longest x1 2.09 us: align_pass(): act_grad(jax.nn.silu, second_pre, grad_second_act).astype(BF16)]
    unnamed x69 -> x77, local copies, waits for them, and re-layouts: 26.4 us -> 21.4 us
  transfers between devices with their start and end apart: 8 -> 0, of which waited for: 4 -> 0; matrix products, arithmetic and copies ran while one was open for 5% -> 0% of each run, Pallas kernels for 45% -> 0%
where the time goes in v4:
time: 673 us; the launch traced here: 664 us
  Pallas kernels  615 us (91%)
  local copies, waits for them, and re-layouts  38.1 us (6%)
  other arithmetic  7.84 us (1%)
    pallas_call x10, Pallas kernels, call(): pl.pallas_call(body, out_shape=[jax.ShapeDtypeStruct(shape, dtype) for sh...  615 us
    unnamed x77, local copies, waits for them, and re-layouts  21.4 us

profile of v4, /device:TPU:0, one launch (start us, length us, event | category | flops | bytes accessed | tf_op | source)
XLA Modules:
  0.0 664.3 jit_solution(4165485813137598035)
XLA Ops:
  0.7 0.9 dynamic-slice_bitcast_fusion
  1.6 0.7 copy.94.refs_4_.refs_3_
  2.3 1.6 constant_dynamic-slice_fusion
  3.9 0.7 copy.121
  4.7 0.7 fusion.5
  5.3 0.8 copy.95.refs_5_.refs_4_
  6.2 0.7 constant_dynamic-slice_fusion.2
  6.9 0.6 broadcast_in_dim.57.refs_6_.refs_5_
  7.7 0.7 copy.122
  8.4 2.6 copy.91
  11.1 0.6 pad_bitcast_fusion.refs_1_
  11.7 6.6 copy.90
  18.3 1.3 copy.96.refs_14_
  19.6 0.7 concatenate.12.refs_3_
  20.4 0.7 maximum_maximum_fusion.refs_16_
  21.1 131.6 %shard_map.348 = (f32[2,6,8,1152]{3,2,1,0:T(8,128)}, f32[2,8,1152]{2,1,0:T(8,128)}, bf16[3456,288]{1,0:T(8,128)(2,1)}, bf16[288,1152]{1,0:T(8,128)(2,1)}, bf16[1...) custom-call(bf16[2,48,1152]{2,1,0:T(8,128)(2,1)} %bitcast.81, ...), custom_call_target="tpu_custom_call" | custom-call | flops 1019215872 | bytes 16472832 | tf_op jit(solution)/shard_map/pallas_call | solution.py:1486
  152.7 3.4 copy.124.refs_8_
  156.1 53.6 %shard_map.349 = (bf16[2,48,1152]{2,1,0:T(8,128)(2,1)}, f32[2,48,1152]{2,1,0:T(8,128)}, bf16[2,192,1152]{2,1,0:T(8,128)(2,1)}, f32[2,192,1152]{2,1,0:T(8,128)}, ...) custom-call(f32[2,48,1152]{2,1,0:T(8,128)} %get-tuple-element.121.re, ...), custom_call_target="tpu_custom_call", output_to_operand_aliasing={{5}: (8, {}), {6}: (9, {}), {7}: (10, {}), {8}: (11, {})} | custom-call | flops 2038431744 | bytes 22356352 | tf_op jit(solution)/shard_map/pallas_call | solution.py:1486
  209.7 65.5 %shard_map.350 = (f32[2,48,1152]{2,1,0:T(8,128)}, f32[2,48,1152]{2,1,0:T(8,128)}, bf16[2,192,1152]{2,1,0:T(8,128)(2,1)}, bf16[2,192,512]{2,1,0:T(8,128)(2,1)}, b...) custom-call(bf16[2,48,1152]{2,1,0:T(8,128)(2,1)} %get-tuple-element., ...), custom_call_target="tpu_custom_call", output_to_operand_aliasing={{8}: (10, {}), {9}: (11, {}), {10}: (12, {})} | custom-call | flops 1019215872 | bytes 14175616 | tf_op jit(solution)/shard_map/pallas_call | solution.py:1486
  275.2 0.6 broadcast_in_dim.63.refs_3_
  275.8 22.6 %shard_map.352 = (f32[2,48,1152]{2,1,0:T(8,128)}, bf16[2,1152,512]{2,1,0:T(8,128)(2,1)}, bf16[2,512,2048]{2,1,0:T(8,128)(2,1)}, bf16[2,2048,192]{2,1,0:T(8,128)(2,1)}, f32[4,8,512]{2,1,0:T(8,128)}) custom-call(bf16[2,48,1152]{2,1,0:T(8,128)(2,1)} %get-tuple-element.129.refs_0_.refs_13_.refs_1_, bf16[2,2,2,48,192]{4,3,2,1,0:T(8,128)(2,1)} %get-tuple-element.142.refs_1_, ...), custom_call_target="tpu_custom_call" | custom-call | flops 4680843264 | bytes 8564736 | tf_op jit(solution)/shard_map/pallas_call | solution.py:1486
  298.4 50.4 %shard_map.351 = (bf16[2,48,1152]{2,1,0:T(8,128)(2,1)}, f32[2,48,1152]{2,1,0:T(8,128)}, bf16[2,192,1152]{2,1,0:T(8,128)(2,1)}, f32[2,192,1152]{2,1,0:T(8,128)}, bf16[2,192,1152]{2,1,0:T(8,128)(2,1)}) custom-call(f32[2,48,1152]{2,1,0:T(8,128)} %get-tuple-element.135.refs_0_.refs_1_, f32[2,6,8,1152]{3,2,1,0:T(8,128)} %get-tuple-element.122.refs_1_.refs_3_, ...), custom_call_target="tpu_custom_call" | custom-call | flops 2038431744 | bytes 11575680 | tf_op jit(solution)/shard_map/pallas_call | solution.py:1486
  348.8 0.7 copy.120
  349.6 57.7 %shard_map.353 = (f32[2,48,1152]{2,1,0:T(8,128)}, f32[3,8,1152]{2,1,0:T(8,128)}, bf16[1152,1152]{1,0:T(8,128)(2,1)}, bf16[1152,1152]{1,0:T(8,128)(2,1)}, f32[1,1...) custom-call(bf16[2,48,1152]{2,1,0:T(8,128)(2,1)} %bitcast.83, ...), custom_call_target="tpu_custom_call" | custom-call | flops 4076863488 | bytes 20341120 | tf_op jit(solution)/shard_map/pallas_call | solution.py:1486
  407.3 57.1 %shard_map.354 = (f32[2,48,1152]{2,1,0:T(8,128)}, f32[3,8,1152]{2,1,0:T(8,128)}, bf16[3,1152,288]{2,1,0:T(8,128)(2,1)}, bf16[1152,288]{1,0:T(8,128)(2,1)}, f32[2...) custom-call(f32[2,48,1152]{2,1,0:T(8,128)} %get-tuple-element.149.re, ...), custom_call_target="tpu_custom_call" | custom-call | flops 2038431744 | bytes 19562880 | tf_op jit(solution)/shard_map/pallas_call | solution.py:1486
  464.4 1.8 add.31.refs_0_
  466.2 51.9 %shard_map.355 = (f32[2,48,1152]{2,1,0:T(8,128)}, f32[3,8,1152]{2,1,0:T(8,128)}, bf16[1152,1152]{1,0:T(8,128)(2,1)}, bf16[1152,1152]{1,0:T(8,128)(2,1)}, f32[1,1...) custom-call(f32[2,48,1152]{2,1,0:T(8,128)} %add.31.refs_0_, ...), custom_call_target="tpu_custom_call" | custom-call | flops 4076863488 | bytes 22004096 | tf_op jit(solution)/shard_map/pallas_call | solution.py:1486
  518.0 63.6 %shard_map.356 = (f32[2,48,1152]{2,1,0:T(8,128)}, f32[3,8,1152]{2,1,0:T(8,128)}, bf16[3,1152,288]{2,1,0:T(8,128)(2,1)}, bf16[1152,288]{1,0:T(8,128)(2,1)}, f32[2...) custom-call(f32[2,48,1152]{2,1,0:T(8,128)} %get-tuple-element.172.re, ...), custom_call_target="tpu_custom_call" | custom-call | flops 2038431744 | bytes 19308928 | tf_op jit(solution)/shard_map/pallas_call | solution.py:1486
  581.9 0.6 copy.123
  582.5 61.4 %shard_map.357 = (f32[4,48,1152]{2,1,0:T(8,128)}, f32[288,1728]{1,0:T(8,128)}, f32[1,1728]{1,0:T(1,128)}, f32[8,1152]{1,0:T(8,128)}, f32[8,512]{1,0:T(8,128)}, /...) custom-call(f32[2,48,1152]{2,1,0:T(8,128)} %get-tuple-element.187.re, ...), custom_call_target="tpu_custom_call" | custom-call | flops 63700992 | bytes 7089664 | tf_op jit(solution)/shard_map/pallas_call | solution.py:1486
  643.9 2.7 select_bitcast_fusion
  646.6 1.2 select_bitcast_fusion.1
  647.9 1.0 copy.110
  648.9 0.5 copy-done.7
  649.5 1.2 select_bitcast_fusion.2
  650.7 1.3 copy.109
  651.9 0.8 copy.111
  652.7 0.6 copy.115
  653.3 1.5 fusion.4
  654.8 1.3 slice_bitcast_fusion.1
  656.1 0.6 slice.29
  656.7 0.5 slice.24
  657.9 0.6 slice.31
  658.6 0.9 copy.108
  659.5 1.3 copy.135
  660.8 0.6 copy.136
  661.4 0.7 copy.137
  662.2 0.8 copy.138
  (77 shorter events, 0.8 us)
Async XLA Ops:
  0.7 6.8 %copy-start = (bf16[192,4,192]{2,1,0:T(4,128)(2,1)S(1)}, bf16[192,4,192]{2,1,0:T(4,128)(2,1)}, u32[]{:S(2)}) copy-start(bf16[192,4,192]{2,1,0:T(4,128)(2,1)} %param.24) | copy-start | bytes 884740
  0.7 7.7 %copy-start.4 = (bf16[1,1152,3,288]{1,3,2,0:T(8,128)(2,1)S(1)}, bf16[1,1152,3,288]{1,3,2,0:T(8,128)(2,1)}, u32[]{:S(2)}) copy-start(bf16[1,1152,3,288]{1,3,2,0:T(8,128)(2,1)} %param.28) | copy-start | bytes 5971972
  8.4 2.6 copy-start.20
  11.7 6.6 copy-start.12
  11.7 7.9 %copy-start.27 = (bf16[1,2,288]{2,1,0:T(2,128)(2,1)S(1)}, bf16[1,2,288]{2,1,0:T(2,128)(2,1)}, u32[]{:S(2)}) copy-start(bf16[1,2,288]{2,1,0:T(2,128)(2,1)} %param.29) | copy-start | bytes 3460
  11.7 7.9 %copy-start.23 = (bf16[1,1152]{1,0:T(2,128)(2,1)S(1)}, bf16[1,1152]{1,0:T(2,128)(2,1)}, u32[]{:S(2)}) copy-start(bf16[1,1152]{1,0:T(2,128)(2,1)} %param.31) | copy-start | bytes 6916
  11.7 7.9 %copy-start.24 = (bf16[1,1152]{1,0:T(2,128)(2,1)S(1)}, bf16[1,1152]{1,0:T(2,128)(2,1)}, u32[]{:S(2)}) copy-start(bf16[1,1152]{1,0:T(2,128)(2,1)} %param.33) | copy-start | bytes 6916
  11.7 7.9 %copy-start.25 = (bf16[1,1152]{1,0:T(2,128)(2,1)S(1)}, bf16[1,1152]{1,0:T(2,128)(2,1)}, u32[]{:S(2)}) copy-start(bf16[1,1152]{1,0:T(2,128)(2,1)} %param.35) | copy-start | bytes 6916
  11.7 8.6 %copy-start.28 = (bf16[512]{0:T(512)(128)(2,1)S(1)}, bf16[512]{0:T(512)(128)(2,1)}, u32[]{:S(2)}) copy-start(bf16[512]{0:T(512)(128)(2,1)} %param.37) | copy-start | bytes 3076
  11.7 8.6 %copy-start.29 = (bf16[192]{0:T(256)(128)(2,1)S(1)}, bf16[192]{0:T(256)(128)(2,1)}, u32[]{:S(2)}) copy-start(bf16[192]{0:T(256)(128)(2,1)} %param.41) | copy-start | bytes 1156
  209.7 65.5 %copy-start.26 = (bf16[2048]{0:T(1024)(128)(2,1)S(1)}, bf16[2048]{0:T(1024)(128)(2,1)}, u32[]{:S(2)}) copy-start(bf16[2048]{0:T(1024)(128)(2,1)} %param.39) | copy-start | bytes 12292
  407.3 57.1 %copy-start.16 = (f32[2,48,1152]{2,1,0:T(8,128)S(1)}, f32[2,48,1152]{2,1,0:T(8,128)}, u32[]{:S(2)}) copy-start(f32[2,48,1152]{2,1,0:T(8,128)} %get-tuple-element.162) | copy-start | bytes 1327108
  582.5 61.4 %copy-start.6 = (f32[288,1152]{1,0:T(8,128)S(1)}, f32[288,1152]{1,0:T(8,128)}, u32[]{:S(2)}) copy-start(f32[288,1152]{1,0:T(8,128)} %get-tuple-element.219) | copy-start | bytes 3981316
  643.9 2.7 copy-start.5
  643.9 2.7 copy-start.9
  646.6 1.3 copy-start.14
  646.6 1.3 copy-start.15
  646.6 2.3 copy-start.8
  647.9 1.6 copy-start.7
  648.9 1.8 copy-start.11
  649.5 2.5 copy-start.18
  650.7 2.1 copy-start.21
  650.7 7.8 %copy-start.2 = (bf16[2,48,1152]{2,1,0:T(8,128)(2,1)S(1)}, bf16[2,48,1152]{2,1,0:T(8,128)(2,1)}, u32[]{:S(2)}) copy-start(bf16[2,48,1152]{2,1,0:T(8,128)(2,1)} %get-tuple-element.129.refs_0_.refs_13_.refs_1_) | copy-start | bytes 663556
  650.7 7.8 %copy-start.10 = (bf16[2,48,1152]{2,1,0:T(8,128)(2,1)S(1)}, bf16[2,48,1152]{2,1,0:T(8,128)(2,1)}, u32[]{:S(2)}) copy-start(bf16[2,48,1152]{2,1,0:T(8,128)(2,1)} %get-tuple-element.137.refs_14_) | copy-start | bytes 663556
  650.7 7.8 %copy-start.19 = (bf16[2,48,1152]{2,1,0:T(8,128)(2,1)S(1)}, bf16[2,48,1152]{2,1,0:T(8,128)(2,1)}, u32[]{:S(2)}) copy-start(bf16[2,48,1152]{2,1,0:T(8,128)(2,1)} %get-tuple-element.148) | copy-start | bytes 663556
  650.7 8.8 %copy-start.3 = (f32[288,1728]{1,0:T(8,128)S(1)}, f32[288,1728]{1,0:T(8,128)}, u32[]{:S(2)}) copy-start(f32[288,1728]{1,0:T(8,128)} %get-tuple-element.209) | copy-start | bytes 5971972
  658.6 4.4 copy-start.1
  659.5 1.3 copy-start.22
  659.5 1.9 copy-start.17
  659.5 2.6 copy-start.13

commit v5 on v4

--- a/solution.py
+++ b/solution.py
@@ -343,6 +343,9 @@
     def middle(self):
         pass
 
+    def late(self):
+        pass
+
     def end(self):
         pass
 
@@ -351,59 +354,73 @@
     return shape[:-2] + (shape[-2] // 4, shape[-1])
 
 
-class QuadSum(Cargo):
-    def __init__(self, grad):
-        part = quarter(grad.shape)
-        self.inputs = (grad,)
-        self.outs = ((part, BF16),)
-        self.size = grad.shape[-2] // 4
-        self.scratch = (
-            pltpu.VMEM((2,) + part, BF16),
-            pltpu.VMEM((2,) + part, BF16),
-            pltpu.VMEM(part, BF16),
-            pltpu.SemaphoreType.DMA((3, 3)),
-        )
-
-    def peers(self):
-        return ["core", "y"]
+class CoreSum:
+    def __init__(self, whole, got, out, sems):
+        self.whole, self.got, self.out, self.sems = whole, got, out, sems
+        self.size = whole.shape[-2] // 4
 
     def rows(self, core, y):
-        grad = self.ins[0]
         part = pl.ds(pl.multiple_of((core + 2 * y) * self.size, 16), self.size)
-        return grad.at[:, part] if len(grad.shape) == 3 else grad.at[part]
+        whole = self.whole
+        return whole.at[:, part] if len(whole.shape) == 3 else whole.at[part]
 
     def begin(self):
-        keep, from_core, from_y, sems = self.held
-        core, self.copies = core_bit(), []
-        for y in range(2):
-            self.copies.append(
-                remote(
-                    self.rows(1 - core, y), from_core.at[y], sems.at[0, y], sems.at[1, y], core_peer()
-                )
+        self.copies = [
+            remote(
+                self.rows(1 - core_bit(), y), self.got.at[y],
+                self.sems.at[0, y], self.sems.at[1, y], core_peer(),
             )
-            self.copies.append(local(self.rows(core, y), keep.at[y], sems.at[2, y]))
-
-    def middle(self):
-        keep, from_core, from_y, sems = self.held
+            for y in range(2)
+        ]
+
+    def end(self):
         wait_all(self.copies)
         for y in range(2):
-            keep[y] = (keep[y].astype(F32) + from_core[y].astype(F32)).astype(BF16)
+            mine = self.rows(core_bit(), y)[...]
+            self.out[y] = (mine.astype(F32) + self.got[y].astype(F32)).astype(BF16)
+
+
+def core_sum_scratch(shape):
+    return [
+        pltpu.VMEM(shape, BF16),
+        pltpu.VMEM((2,) + quarter(shape), BF16),
+        pltpu.SemaphoreType.DMA((2, 2)),
+    ]
+
+
+class YSum(Cargo):
+    def __init__(self, parts, dtype):
+        part = parts.shape[1:]
+        self.inputs = (parts,)
+        self.outs = ((part, dtype),)
+        self.scratch = (
+            pltpu.VMEM(part, BF16),
+            pltpu.VMEM(part, BF16),
+            pltpu.SemaphoreType.DMA((3,)),
+        )
+
+    def peers(self):
+        return ["y"]
+
+    def begin(self):
+        mine, other, sems = self.held
         self.copies = [
-            remote(keep.at[1 - y_bit()], from_y, sems.at[0, 2], sems.at[1, 2], y_peer())
+            remote(self.ins[0].at[1 - y_bit()], other, sems.at[0], sems.at[1], y_peer()),
+            local(self.ins[0].at[y_bit()], mine, sems.at[2]),
         ]
 
     def end(self):
-        keep, from_core, from_y, sems = self.held
+        mine, other, sems = self.held
+        out = self.out_refs[0]
         wait_all(self.copies)
-        self.out_refs[0][...] = (
-            keep[y_bit()].astype(F32) + from_y[...].astype(F32)
-        ).astype(BF16)
+        out[...] = (mine[...].astype(F32) + other[...].astype(F32)).astype(out.dtype)
 
 
 class SectionSum(Cargo):
-    def __init__(self, part):
+    def __init__(self, part, owner, dtype=F32):
+        self.owner = owner
         self.inputs = (part,)
-        self.outs = ((part.shape, F32),)
+        self.outs = ((part.shape, dtype),)
         self.scratch = (
             pltpu.VMEM(part.shape, BF16),
             pltpu.VMEM(part.shape, BF16),
@@ -413,24 +430,45 @@
     def peers(self):
         return ["x"]
 
+    def source(self):
+        return self.ins[0]
+
     def begin(self):
         mine, other, sems = self.held
-        self.copies = [
-            local(self.ins[0], mine, sems.at[2]),
-            remote(self.ins[0], other, sems.at[0], sems.at[1], x_peer()),
-        ]
+        self.copy = describe(self.source(), other, sems.at[0], sems.at[1], x_peer())
+        self.load = pltpu.make_async_copy(self.source(), mine, sems.at[2])
+        is_owner = lax.axis_index("section") == self.owner
+
+        @pl.when(is_owner)
+        def take():
+            self.load.start()
+
+        @pl.when(jnp.logical_not(is_owner))
+        def give():
+            self.copy.start()
 
     def end(self):
         mine, other, sems = self.held
-        wait_all(self.copies)
-        self.out_refs[0][...] = mine[...].astype(F32) + other[...].astype(F32)
-
-
-class LastSum(QuadSum):
-    def __init__(self, grad):
-        super().__init__(grad)
-        part = quarter(grad.shape)
-        self.outs = ((part, F32),)
+        is_owner = lax.axis_index("section") == self.owner
+
+        @pl.when(is_owner)
+        def add():
+            self.load.wait()
+            self.copy.wait_recv()
+            out = self.out_refs[0]
+            out[...] = (mine[...].astype(F32) + other[...].astype(F32)).astype(out.dtype)
+
+        @pl.when(jnp.logical_not(is_owner))
+        def given():
+            self.copy.wait_send()
+            self.out_refs[0][...] = jnp.zeros_like(self.out_refs[0])
+
+
+class LastSum(YSum):
+    def __init__(self, parts, owner):
+        super().__init__(parts, F32)
+        part = parts.shape[1:]
+        self.owner = owner
         self.scratch = self.scratch + (
             pltpu.VMEM(part, BF16),
             pltpu.VMEM(part, BF16),
@@ -438,24 +476,36 @@
         )
 
     def peers(self):
-        return ["core", "y", "x"]
+        return ["y", "x"]
 
     def begin(self):
-        self.all_held = self.held
-        self.held, self.last = self.held[:4], self.held[4:]
+        self.held, self.last = self.held[:3], self.held[3:]
         super().begin()
 
     def to_x(self):
-        keep, from_core, from_y, sems = self.held
-        mine, other, last_sems = self.last
+        mine, other, sems = self.held
+        total, got, last_sems = self.last
         wait_all(self.copies)
-        mine[...] = (keep[y_bit()].astype(F32) + from_y[...].astype(F32)).astype(BF16)
-        self.copies = [remote(mine, other, last_sems.at[0], last_sems.at[1], x_peer())]
+        total[...] = (mine[...].astype(F32) + other[...].astype(F32)).astype(BF16)
+        self.copy = describe(total, got, last_sems.at[0], last_sems.at[1], x_peer())
+
+        @pl.when(lax.axis_index("section") != self.owner)
+        def give():
+            self.copy.start()
 
     def end(self):
-        mine, other, last_sems = self.last
-        wait_all(self.copies)
-        self.out_refs[0][...] = mine[...].astype(F32) + other[...].astype(F32)
+        total, got, last_sems = self.last
+        is_owner = lax.axis_index("section") == self.owner
+
+        @pl.when(is_owner)
+        def add():
+            self.copy.wait_recv()
+            self.out_refs[0][...] = total[...].astype(F32) + got[...].astype(F32)
+
+        @pl.when(jnp.logical_not(is_owner))
+        def given():
+            self.copy.wait_send()
+            self.out_refs[0][...] = jnp.zeros_like(self.out_refs[0])
 
 
 class LateShare(Cargo):
@@ -477,65 +527,9 @@
 
     def middle(self):
         self.share.forward_again()
+
+    def late(self):
         self.share.finish()
-
-
-class QuadSumX(Cargo):
-    def __init__(self, grad):
-        part = (2,) + quarter(grad.shape)
-        self.inputs = (grad,)
-        self.outs = ((part, BF16),)
-        self.size = grad.shape[-2] // 4
-        self.scratch = (
-            pltpu.VMEM(part, BF16),
-            pltpu.VMEM(part, BF16),
-            pltpu.VMEM(part, BF16),
-            pltpu.SemaphoreType.DMA((3, 3)),
-        )
-
-    def peers(self):
-        return ["core", "x"]
-
-    rows = QuadSum.rows
-
-    def begin(self):
-        QuadSum.begin(self)
-
-    def middle(self):
-        keep, from_core, from_x, sems = self.held
-        wait_all(self.copies)
-        for y in range(2):
-            keep[y] = (keep[y].astype(F32) + from_core[y].astype(F32)).astype(BF16)
-        self.copies = [remote(keep, from_x, sems.at[0, 2], sems.at[1, 2], x_peer())]
-
-    def end(self):
-        keep, from_core, from_x, sems = self.held
-        wait_all(self.copies)
-        self.out_refs[0][...] = (keep[...].astype(F32) + from_x[...].astype(F32)).astype(BF16)
-
-
-class LastY(Cargo):
-    def __init__(self, parts):
-        part = parts.shape[1:]
-        self.inputs = (parts,)
-        self.outs = ((part, F32),)
-        self.scratch = (
-            pltpu.VMEM(part, BF16),
-            pltpu.VMEM(part, BF16),
-            pltpu.SemaphoreType.DMA((3,)),
-        )
-
-    def peers(self):
-        return ["y"]
-
-    def begin(self):
-        mine, other, sems = self.held
-        self.copies = [
-            local(self.ins[0].at[y_bit()], mine, sems.at[2]),
-            remote(self.ins[0].at[1 - y_bit()], other, sems.at[0], sems.at[1], y_peer()),
-        ]
-
-    end = SectionSum.end
 
 
 class Swap(Cargo):
@@ -579,8 +573,9 @@
 
 
 class HalfSum(Cargo):
-    def __init__(self, grad, axis, name):
-        part = cut(grad.shape, axis, 2)
+    def __init__(self, grad, axis, name, slots=None):
+        self.slots = slots if slots is not None else (0, grad.shape[0])
+        part = cut((self.slots[1],) + grad.shape[1:], axis, 2)
         self.axis, self.name, self.size = axis, name, part[axis - 2]
         self.inputs = (grad,)
         self.outs = ((part, BF16),)
@@ -599,7 +594,7 @@
             bit, peer = lax.axis_index("section"), x_peer()
         else:
             bit, peer = y_bit(), y_peer()
-        grad = self.ins[0]
+        grad = self.ins[0].at[pl.ds(*self.slots)]
         self.copies = [
             remote(
                 span(grad, self.axis, (1 - bit) * self.size, self.size), other,
@@ -624,7 +619,7 @@
             ((2, 2) + biases.shape, F32),
         )
         self.scratch = (
-            pltpu.SemaphoreType.DMA((5, 4)),
+            pltpu.SemaphoreType.DMA((5, 6)),
             pltpu.SemaphoreType.DMA((5, 2, 2)),
             pltpu.SemaphoreType.DMA((5,)),
         )
@@ -664,27 +659,81 @@
             for i, (source, place) in enumerate(self.pieces(lax.axis_index("tensor")))
         ]
 
-    def begin(self):
+    def direct(self, step, i):
+        if step == 2 or i > 2:
+            return None
+        return lax.axis_index("tensor") != (3 if step == 1 else 0)
+
+    def each(self, which, act):
         for step in range(1, 4):
-            for copy in self.copies(step):
-                copy.start()
+            for i, copy in enumerate(self.copies(step)):
+                if i in which:
+                    allowed = self.direct(step, i)
+                    if allowed is None:
+                        act(copy)
+                    else:
+
+                        @pl.when(allowed)
+                        def go(copy=copy):
+                            act(copy)
+
+    def start(self, which):
+        self.each(which, lambda copy: copy.start())
 
         @pl.when(self.stays())
         def keep():
-            for copy in self.own_copies():
-                copy.start()
+            for i, copy in enumerate(self.own_copies()):
+                if i in which:
+                    copy.start()
 
         @pl.when(jnp.logical_not(self.stays()))
         def give():
-            for copy in self.copies(0):
-                copy.start()
+            for i, copy in enumerate(self.copies(0)):
+                if i in which:
+                    copy.start()
+
+    def passes_on(self):
+        tensor, core = lax.axis_index("tensor"), core_bit()
+        return jnp.logical_or(
+            jnp.logical_and(tensor == 2, core == 0), jnp.logical_and(tensor == 1, core == 1)
+        )
+
+    def passed(self, i, other):
+        send, recv, own = self.held
+        tensor, slot = lax.axis_index("tensor"), core_bit()
+        place = self.out_refs[i]
+        size = self.ins[i].shape[0] // 8
+        eighth = lax.axis_index("section") * 4 + y_bit() * 2 + other
+        part = place.at[slot, pl.ds(pl.multiple_of(eighth * size, 16), size)]
+        return describe(
+            part, part, send.at[i, 4 + other], recv.at[i, slot, other], {"tensor": 3 * (tensor - 1)}
+        )
+
+    def relay(self, which):
+        @pl.when(self.passes_on())
+        def pass_on():
+            for i in which:
+                for other in range(2):
+                    copy = self.passed(i, other)
+                    copy.wait_recv()
+                    copy.start()
+
+    def begin(self):
+        self.start((2, 3, 4))
+
+    def middle(self):
+        self.relay((2,))
+        self.start((0,))
+
+    def late(self):
+        self.relay((0,))
+        self.start((1,))
 
     def end(self):
         send, recv, own = self.held
         tensor, core = lax.axis_index("tensor"), core_bit()
-        for step in range(1, 4):
-            for copy in self.copies(step):
-                copy.wait_send()
+        self.relay((1,))
+        self.each(range(5), lambda copy: copy.wait_send())
 
         @pl.when(self.stays())
         def kept():
@@ -696,27 +745,41 @@
             for copy in self.copies(0):
                 copy.wait_send()
 
+        @pl.when(self.passes_on())
+        def passed_on():
+            for i in range(3):
+                for other in range(2):
+                    self.passed(i, other).wait_send()
+
         for slot in range(2):
             for other in range(2):
                 mine = jnp.logical_and(2 * core + slot == tensor, core == other)
+                relayed = jnp.logical_and(self.passes_on(), core == slot)
+                peer = {"tensor": lax.rem(tensor + 1, 4)}
+                waits = [
+                    describe(source, place, send.at[i, 1], recv.at[i, slot, other], peer)
+                    for i, (source, place) in enumerate(self.pieces(tensor))
+                ]
 
                 @pl.when(jnp.logical_not(mine))
-                def arrived(slot=slot, other=other):
-                    peer = {"tensor": lax.rem(tensor + 1, 4)}
-                    for i, (source, place) in enumerate(self.pieces(tensor)):
-                        describe(
-                            source, place, send.at[i, 1], recv.at[i, slot, other], peer
-                        ).wait_recv()
+                def arrived(waits=waits):
+                    for copy in waits[3:]:
+                        copy.wait_recv()
+
+                @pl.when(jnp.logical_not(jnp.logical_or(mine, relayed)))
+                def weights_arrived(waits=waits):
+                    for copy in waits[:3]:
+                        copy.wait_recv()
 
 
 class ShareAlong(Cargo):
     any_outs = True
 
-    def __init__(self, weights, second):
+    def __init__(self, weights, stage):
         self.inputs = tuple(weights)
         self.outs = tuple((one.shape, BF16) for one in weights)
         self.aliases = {0: 0, 1: 1, 2: 2}
-        self.second = second
+        self.stage = stage
         self.scratch = (pltpu.SemaphoreType.DMA((4,)), pltpu.SemaphoreType.DMA((4,)))
 
     def peers(self):
@@ -733,14 +796,15 @@
             i = len(self.copies)
             self.copies.append(remote(part, part, send.at[i], recv.at[i], peer))
 
-        if not self.second:
+        if self.stage == 0:
             give(1, 2 * section + y, 1, x_peer())
             give(0, 2 * section + y, 1, y_peer())
             give(2, 2 * section + y, 1, y_peer())
+        elif self.stage == 1:
+            give(0, 2 * section, 2, x_peer())
+            give(1, y, 1, y_peer())
         else:
-            give(0, 2 * section, 2, x_peer())
             give(2, 2 * section, 2, x_peer())
-            give(1, y, 1, y_peer())
             give(1, 2 + y, 1, y_peer())
 
     def end(self):
@@ -748,10 +812,10 @@
 
 
 class ColumnSum(Cargo):
-    def __init__(self, grad, axis):
+    def __init__(self, grads, axis):
         self.axis = axis
-        self.part = cut(grad.shape[1:], axis, 2)
-        self.inputs = (grad,)
+        self.part = cut(grads[0].shape[1:], axis, 2)
+        self.inputs = tuple(grads)
         self.outs = ((self.part, F32),)
         self.scratch = (
             pltpu.VMEM((4,) + self.part, BF16),
@@ -767,7 +831,8 @@
         got, send, recv, own = self.held
         tensor, core = lax.axis_index("tensor"), core_bit()
         size = self.part[self.axis]
-        source = span(self.ins[0].at[slot], self.axis, other * size, size)
+        ref = self.ins[0].at[slot] if len(self.ins) == 1 else self.ins[slot].at[0]
+        source = span(ref, self.axis, other * size, size)
         peer = {"tensor": 2 * core + slot, "dp": lax.axis_index("dp") - core + other}
         mine = jnp.logical_and(2 * core + slot == tensor, core == other)
         away = describe(source, got.at[tensor], send.at[2 * slot + other], recv.at[tensor], peer)
@@ -818,8 +883,8 @@
     def __init__(self, cargos):
         self.cargos = cargos
 
-    def peers(self):
-        names = [name for cargo in self.cargos for name in cargo.peers()]
+    def peers(self, names=()):
+        names = list(names) + [name for cargo in self.cargos for name in cargo.peers()]
         known = {"core": core_peer, "y": y_peer, "x": x_peer}
         cross = cross_peers() if "cross" in names else []
         return [make() for name, make in known.items() if name in names] + cross
@@ -831,6 +896,10 @@
     def middle(self):
         for cargo in self.cargos:
             cargo.middle()
+
+    def late(self):
+        for cargo in self.cargos:
+            cargo.late()
 
     def end(self):
         for cargo in self.cargos:
@@ -883,6 +952,7 @@
         mixed_wide[row, :, lanes] = dot(probs.astype(BF16), v_ref[row, :, lanes]).astype(BF16)
         return carry
 
+    steps[1]()
     lax.fori_loop(0, rows * heads, one_head, 0)
     mixed_ref[...] = dot(flat(mixed_wide), spread, NT).astype(BF16).reshape(mixed_ref.shape)
     need_out()
@@ -891,7 +961,7 @@
         return dot(mixed_ref[:, which_rows, :].reshape(rows * length, heads_width), wo[...])
 
     total = line.scatter_sum(partial, buffers)
-    steps[1]()
+    steps[2]()
     branch = line.finish_sum(total, buffers) + bias[2:3, :]
     branch_ref[...] = branch.reshape(branch_ref.shape)
     middle = flat(u_ref).astype(F32) + token_mod(mod_ref, seg_own, 2) * branch
@@ -926,6 +996,7 @@
     ]
     greet(plane + [core_peer(), y_peer()] + cross_peers())
     shares[0].begin()
+    cargo.begin()
     cond_act = silu(cond_ref[...].astype(F32)).astype(BF16)
     load_ada.wait()
     mod = dot(cond_act, ada[...]) + ada_b_ref[...].astype(F32)
@@ -945,7 +1016,6 @@
     )
     for share in shares[1:]:
         share.begin()
-    cargo.begin()
 
     def mods():
         wait_all(copies)
@@ -977,21 +1047,26 @@
 
     def after_gather():
         shares[0].forward(shares[0].first)
+        cargo.middle()
         shares[1].forward(shares[1].first)
         shares[0].forward_again()
         shares[0].finish()
 
+    def before_heads():
+        shares[2].forward(shares[2].first)
+
     def after_scatter():
-        shares[2].forward(shares[2].first)
+        cargo.late()
         shares[2].forward_again()
+        shares[2].finish()
 
     attend_body(
         count, None, u_ref, mods, (seg_own, seg_col, seg_row), biases, outs, scratch,
-        (ag_send, ag_recv, rs_send, rs_recv), need_qkv, need_out, (after_gather, after_scatter),
-    )
+        (ag_send, ag_recv, rs_send, rs_recv), need_qkv, need_out,
+        (after_gather, before_heads, after_scatter),
+    )
+    shares[3].first.wait()
     cargo.end()
-    shares[2].finish()
-    shares[3].first.wait()
 
 
 def attend_kernel(count, block, *refs, cargo):
@@ -1003,7 +1078,7 @@
     attend_body(
         count, z_peers(count) + cargo.peers(), u_ref, lambda: mods_ref.at[block],
         (seg_own, seg_col, seg_row), lambda: bias_ref[block], outs, scratch, refs[26:30],
-        load_qkv.wait, load_out.wait, (cargo.begin, cargo.middle),
+        load_qkv.wait, load_out.wait, (cargo.begin, cargo.middle, cargo.late),
     )
     cargo.end()
 
@@ -1012,12 +1087,15 @@
     count, block,
     middle_ref, mods_ref, bias_ref, seg_own, w1_own, w1_other, w2_own, w2_other,
     out_ref, branch_ref, full_ref, pre_ref, act_ref,
-    full, w1, w2, send_buf, recv_buf, relay_buf, w_sem, *sems, cargo, late,
+    full, w1, w2, send_buf, recv_buf, relay_buf, w_sem, *sems, cargo,
 ):
     me = lax.axis_index("tensor")
     rows, length, width = middle_ref.shape
     mod_ref = mods_ref.at[block]
     load_one = fetch(block, w1_own, w1_other, w1, w_sem.at[0])
+    late = [one for one in cargo.cargos if isinstance(one, LateShare)]
+    if not late:
+        load_two = fetch(block, w2_own, w2_other, w2, w_sem.at[1])
     normed, unused = layer_norm(flat(middle_ref))
     mlp_in = normed * (1.0 + token_mod(mod_ref, seg_own, 4)) + token_mod(mod_ref, seg_own, 3)
     full[:, own_rows(me, length), :] = mlp_in.astype(BF16).reshape(rows, length, width)
@@ -1032,10 +1110,10 @@
     pre = dot(flat(full), w1[...]) + bias_ref[block, 3:4, : w1.shape[1]]
     pre_ref[...] = pre.reshape(pre_ref.shape)
     cargo.middle()
+    act_ref[...] = gelu_tanh(pre).astype(BF16).reshape(act_ref.shape)
+    cargo.late()
     if late:
-        w2_other = cargo.cargos[0].out_refs[0]
-    load_two = fetch(block, w2_own, w2_other, w2, w_sem.at[1])
-    act_ref[...] = gelu_tanh(pre).astype(BF16).reshape(act_ref.shape)
+        load_two = fetch(block, w2_own, late[0].out_refs[0], w2, w_sem.at[1])
     load_two.wait()
 
     def partial(which_rows):
@@ -1055,7 +1133,10 @@
     w1_own, w1_other, w2_own, w2_other = refs[8:12]
     d_middle_ref, d_mod_ref, d_w1_ref, d_w2_ref, d_b1_ref, d_b2_ref = refs[12:18]
     full, d_pre, w1, w2, *buffers, w_sem = refs[18:26]
-    sems = refs[26:]
+    sems = refs[26:30]
+    w1_whole, w1_got, w1_sems, w2_whole, w2_got, w2_sems = refs[30:]
+    w1_sum = CoreSum(w1_whole, w1_got, d_w1_ref, w1_sems)
+    w2_sum = CoreSum(w2_whole, w2_got, d_w2_ref, w2_sems)
     me = lax.axis_index("tensor")
     rows, length, width = middle_ref.shape
     mod_ref = mods_ref.at[block]
@@ -1064,7 +1145,7 @@
     g = flat(g_ref).astype(F32)
     d_branch = (g * token_mod(mod_ref, seg_own, 5)).astype(BF16)
     full[:, own_rows(me, length), :] = d_branch.reshape(rows, length, width)
-    greet(z_peers(count) + cargo.peers())
+    greet(z_peers(count) + cargo.peers(["core"]))
     line = Line(length, sems)
     line.start_gather(full)
     cargo.begin()
@@ -1081,10 +1162,12 @@
         return dot(d_pre[:, which_rows, :].reshape(rows * length, -1), w1[...], NT)
 
     total = line.scatter_sum(partial, buffers)
+    w2_whole[...] = dot(flat(full), flat(act_ref), TN).astype(BF16)
+    w2_sum.begin()
+    w1_whole[...] = dot(flat(full_ref), flat(d_pre), TN).astype(BF16)
+    w1_sum.begin()
     d_b2_ref[...] = jnp.sum(flat(full).astype(F32), axis=0, keepdims=True)
     d_b1_ref[...] = jnp.sum(flat(d_pre).astype(F32), axis=0, keepdims=True)
-    d_w2_ref[...] = dot(flat(full), flat(act_ref), TN).astype(BF16)
-    d_w1_ref[...] = dot(flat(full_ref), flat(d_pre), TN).astype(BF16)
     d_in = line.finish_sum(total, buffers)
     normed, inverse = layer_norm(flat(middle_ref))
     d_middle = flat(g_ref).astype(F32) + norm_back(
@@ -1093,6 +1176,8 @@
     d_middle_ref[...] = d_middle.reshape(d_middle_ref.shape)
     slot_sums(d_in, seg_own, d_mod_ref, 0)
     slot_sums(d_in * normed, seg_own, d_mod_ref, 1)
+    w2_sum.end()
+    w1_sum.end()
     cargo.end()
 
 
@@ -1102,7 +1187,10 @@
     wqkv_own, wqkv_other, wo_own, wo_other = refs[11:15]
     d_in_ref, d_mod_ref, d_wqkv_ref, d_wo_ref, d_bqv_ref, d_bo_ref = refs[15:21]
     full, wide, narrow, wqkv, wo, *buffers, w_sem = refs[21:30]
-    sems = refs[30:]
+    sems = refs[30:34]
+    qkv_whole, qkv_got, qkv_sems, wo_whole, wo_got, wo_sems = refs[34:]
+    qkv_sum = CoreSum(qkv_whole, qkv_got, d_wqkv_ref, qkv_sems)
+    wo_sum = CoreSum(wo_whole, wo_got, d_wo_ref, wo_sems)
     me = lax.axis_index("tensor")
     rows, length, width = u_ref.shape
     heads_width = wo.shape[0]
@@ -1113,7 +1201,7 @@
     d_middle = flat(d_middle_ref)
     d_branch = (d_middle * token_mod(mod_ref, seg_own, 2)).astype(BF16)
     full[:, own_rows(me, length), :] = d_branch.reshape(rows, length, width)
-    greet(z_peers(count) + cargo.peers())
+    greet(z_peers(count) + cargo.peers(["core"]))
     line = Line(length, sems)
     line.start_gather(full)
     cargo.begin()
@@ -1163,9 +1251,11 @@
     d_bo_ref[...] = jnp.sum(flat(full).astype(F32), axis=0, keepdims=True)
     d_bqv_ref[0:1, :] = jnp.sum(flat(narrow.at[0]).astype(F32), axis=0, keepdims=True)
     d_bqv_ref[1:2, :] = jnp.sum(flat(narrow.at[2]).astype(F32), axis=0, keepdims=True)
-    d_wo_ref[...] = dot(flat(full), flat(mixed_ref), TN).astype(BF16)
+    wo_whole[...] = dot(flat(full), flat(mixed_ref), TN).astype(BF16)
+    wo_sum.begin()
     for which in range(3):
-        d_wqkv_ref[which] = dot(flat(full_ref), flat(narrow.at[which]), TN).astype(BF16)
+        qkv_whole[which] = dot(flat(full_ref), flat(narrow.at[which]), TN).astype(BF16)
+    qkv_sum.begin()
     d_attn_in = line.finish_sum(total, buffers)
     normed, inverse = layer_norm(flat(u_ref).astype(F32))
     d_in = flat(d_middle_ref) + norm_back(
@@ -1174,6 +1264,8 @@
     d_in_ref[...] = d_in.reshape(d_in_ref.shape)
     slot_sums(d_attn_in, seg_own, d_mod_ref, 0)
     slot_sums(d_attn_in * normed, seg_own, d_mod_ref, 1)
+    wo_sum.end()
+    qkv_sum.end()
     cargo.end()
 
 
@@ -1329,7 +1421,7 @@
     ]
     greet(z_peers(count) + others + cross_peers())
     for one in cargo.cargos:
-        if isinstance(one, LastSum):
+        if isinstance(one, YSum):
             one.begin()
     piece = z_src.shape[-1]
     for block in range(sections):
@@ -1390,7 +1482,9 @@
             )
         )
         at = at + 2
-    cargo.middle()
+    for one in cargo.cargos:
+        if not isinstance(one, YSum):
+            one.begin()
     wait_all(z_copies)
     mine, mine_proj = z_src[tensor], proj_ref[tensor]
     for step in range(count - 1):
@@ -1413,9 +1507,6 @@
             )
         )
         at = at + 2
-    for one in cargo.cargos:
-        if not isinstance(one, LastSum):
-            one.begin()
     for one in cargo.cargos:
         if isinstance(one, LastSum):
             one.to_x()
@@ -1602,11 +1693,11 @@
     )
 
 
-def mlp_forward(sizes, block, middle, mods, biases, segs, own, other, late, cargos):
+def mlp_forward(sizes, block, middle, mods, biases, segs, own, other, cargos):
     inputs = [middle, mods, biases, segs[0]] + pairs(own, other, ("one", "two"))
     hidden = (sizes.rows, sizes.positions, sizes.hidden)
     return call(
-        functools.partial(mlp_kernel, sizes.count, block, late=late),
+        functools.partial(mlp_kernel, sizes.count, block),
         2 + block,
         inputs,
         4,
@@ -1638,7 +1729,8 @@
         4,
         [
             (sizes.local, F32), (sizes.mods, F32),
-            ((sizes.width, sizes.hidden), BF16), ((sizes.width, sizes.hidden), BF16),
+            ((2,) + quarter((sizes.width, sizes.hidden)), BF16),
+            ((2,) + quarter((sizes.width, sizes.hidden)), BF16),
             ((1, sizes.hidden), F32), ((1, sizes.width), F32),
         ],
         (),
@@ -1649,7 +1741,8 @@
             pltpu.VMEM(own["two"].shape, BF16),
         ]
         + exchange_scratch(sizes.count, *sizes.local)
-        + semaphores(sizes.count),
+        + semaphores(sizes.count)
+        + core_sum_scratch((sizes.width, sizes.hidden)) * 2,
         2 * sizes.tokens * sizes.width * sizes.hidden * 4,
         cargos,
     )
@@ -1666,7 +1759,8 @@
         4,
         [
             (sizes.local, F32), (sizes.mods, F32),
-            ((3, sizes.width, sizes.heads_width), BF16), ((sizes.width, sizes.heads_width), BF16),
+            ((2,) + quarter((3, sizes.width, sizes.heads_width)), BF16),
+            ((2,) + quarter((sizes.width, sizes.heads_width)), BF16),
             ((2, sizes.heads_width), F32), ((1, sizes.width), F32),
         ],
         (),
@@ -1678,7 +1772,9 @@
             pltpu.VMEM(own["out"].shape, BF16),
         ]
         + exchange_scratch(sizes.count, *sizes.local)
-        + semaphores(sizes.count),
+        + semaphores(sizes.count)
+        + core_sum_scratch((3, sizes.width, sizes.heads_width))
+        + core_sum_scratch((sizes.width, sizes.heads_width)),
         2 * sizes.tokens * sizes.width * sizes.heads_width * 8,
         cargos,
     )
@@ -1872,19 +1968,19 @@
     )
     *proj_weights, target_all, proj_bias_all = carried[0]
     mlp_one, carried = mlp_forward(
-        sizes, 0, attend_one[0], mods, bias_all, segs, own, other, True,
-        (LateShare(other["two"]), ShareAlong(proj_weights, False)),
-    )
-    other["two"] = carried[0][0]
-    proj_weights = carried[1]
+        sizes, 0, attend_one[0], mods, bias_all, segs, own, other,
+        (LateShare(other["two"]), ShareAlong(proj_weights, 0)),
+    )
+    (other["two"],), proj_weights = carried
     first_out = mlp_one[0]
     attend_two, carried = attend_forward(
-        sizes, 1, first_out, mods, bias_all, segs, own, other, (ShareAlong(proj_weights, True),)
+        sizes, 1, first_out, mods, bias_all, segs, own, other, (ShareAlong(proj_weights, 1),)
     )
     proj_weights = carried[0]
     mlp_two, carried = mlp_forward(
-        sizes, 1, attend_two[0], mods, bias_all, segs, own, other, False, ()
-    )
+        sizes, 1, attend_two[0], mods, bias_all, segs, own, other, (ShareAlong(proj_weights, 2),)
+    )
+    proj_weights = carried[0]
     second_out = mlp_two[0]
 
     grad_sent, grad_p1, grad_p2, grad_p3, proj_small = project(
@@ -1894,30 +1990,33 @@
     back = (mods, segs, own, other)
     (d_middle_two, mod_mlp_two, *mlp_grads_two), carried = mlp_backward(
         sizes, 1, to_rows(cot), attend_two, mlp_two, *back,
-        [HalfSum(grad_p2, 1, "x"), Swap(first_out, second_out)],
-    )
-    (grad_p2,), (other_out,) = carried
+        [Swap(first_out, second_out), HalfSum(grad_p1, 0, "x")],
+    )
+    (other_out,), (grad_p1,) = carried
     (second_grad, mod_attend_two, *attend_grads_two), carried = attend_backward(
         sizes, 1, d_middle_two, first_out, attend_two, *back,
-        [QuadSum(grad) for grad in mlp_grads_two[:2]]
-        + [HalfSum(grad_p1, 0, "x"), HalfSum(grad_p3, 0, "x")],
-    )
-    mlp_parts_two, ((grad_p1,), (grad_p3,)) = carried[:2], carried[2:]
+        [YSum(grad, BF16) for grad in mlp_grads_two[:2]]
+        + [HalfSum(grad_p2, 1, "x", (0, 1)), HalfSum(grad_p3, 0, "x"), HalfSum(grad_p1, 0, "y")],
+    )
+    ((mlp_part_a,), (mlp_part_b,)), ((grad_p2_a,), (grad_p3,), (grad_p1,)) = (
+        carried[:2], carried[2:]
+    )
     (d_middle_one, mod_mlp_one, *mlp_grads_one), carried = mlp_backward(
         sizes, 0, second_grad + grad_sent, attend_one, mlp_one, *back,
-        [QuadSum(grad) for grad in attend_grads_two[:2]]
-        + [SectionSum(part) for part, in mlp_parts_two]
-        + [HalfSum(grad_p2, 1, "y")],
-    )
-    attend_parts_two, sums_mlp_two, ((grad_p2,),) = carried[:2], carried[2:4], carried[4:]
+        [YSum(grad, BF16) for grad in attend_grads_two[:2]]
+        + [SectionSum(mlp_part_a, 1), HalfSum(grad_p2, 1, "x", (1, 1))]
+        + [HalfSum(grad_p3, 0, "y"), HalfSum(grad_p2_a, 1, "y"), ColumnSum((grad_p1,), 0)],
+    )
+    attend_parts_two, sum_mlp_a = carried[:2], carried[2]
+    (grad_p2_b,), (grad_p3,), (grad_p2_a,), (red_p1_w,) = carried[3:]
     (first_grad, mod_attend_one, *attend_grads_one), carried = attend_backward(
         sizes, 0, d_middle_one, u, attend_one, *back,
-        [QuadSum(mlp_grads_one[0]), QuadSumX(mlp_grads_one[1])]
-        + [SectionSum(part) for part, in attend_parts_two]
-        + [HalfSum(grad_p1, 0, "y"), HalfSum(grad_p3, 0, "y"), ColumnSum(grad_p2, 1)],
+        [YSum(mlp_grads_one[0], BF16), SectionSum(mlp_grads_one[1], 0, BF16)]
+        + [SectionSum(part, 1) for part, in attend_parts_two]
+        + [SectionSum(mlp_part_b, 1), HalfSum(grad_p2_b, 1, "y"), ColumnSum((grad_p3,), 0)],
     )
     ((mlp_part_one,), (mlp_part_two,)), sums_attend_two = carried[:2], carried[2:4]
-    (grad_p1,), (grad_p3,), (red_p2_w,) = carried[4:]
+    sums_mlp_two, ((grad_p2_b,), (red_p3_w,)) = (sum_mlp_a, carried[4]), carried[5:]
 
     cond_act = silu(my_rows(cond, 0).astype(F32)).astype(BF16).astype(F32)
     share = width // replicas
@@ -1931,11 +2030,12 @@
         sizes, (first_grad, second_grad),
         (mod_attend_one, mod_mlp_one, mod_attend_two, mod_mlp_two),
         small, proj_small, cond_cols, sections, replicas,
-        [LastSum(grad) for grad in attend_grads_one[:2]]
-        + [SectionSum(mlp_part_one), LastY(mlp_part_two)]
-        + [ColumnSum(grad_p1, 0), ColumnSum(grad_p3, 0)],
-    )
-    sums_attend_one, sums_mlp_one, ((red_p1_w,), (red_p3_w,)) = carried[:2], carried[2:4], carried[4:]
+        [LastSum(grad, 0) for grad in attend_grads_one[:2]]
+        + [YSum(mlp_part_two, F32), SectionSum(mlp_part_one, 0)]
+        + [ColumnSum((grad_p2_a, grad_p2_b), 1)],
+    )
+    sums_attend_one, sums_mlp_one = carried[:2], (carried[3], carried[2])
+    (red_p2_w,) = carried[4]
 
     red_fc1, red_fc2, red_qkv, red_out = [
         sum_beyond_quads(jnp.where(is_first, one[0], two[0]))

time: 673 us -> 596 us (0.89)
  Pallas kernels: 615 us -> 538 us
    pallas_call x10, Pallas kernels: 615 us -> 538 us  [call(): pl.pallas_call(body, out_shape=[jax.ShapeDtypeStruct(shape, dtype) for sh...]
    unnamed x77 -> x75, local copies, waits for them, and re-layouts: 21.4 us -> 23.1 us
where the time goes in v5:
time: 596 us; the launch traced here: 588 us
  Pallas kernels  538 us (90%)
  local copies, waits for them, and re-layouts  37.8 us (6%)
  other arithmetic  8.9 us (1%)
    pallas_call x10, Pallas kernels, call(): pl.pallas_call(body, out_shape=[jax.ShapeDtypeStruct(shape, dtype) for sh...  538 us
    unnamed x75, local copies, waits for them, and re-layouts  23.1 us

profile of v5, /device:TPU:0, one launch (start us, length us, event | category | flops | bytes accessed | tf_op | source)
XLA Modules:
  0.0 587.8 jit_solution(11733286034366059003)
XLA Ops:
  0.7 1.7 constant_dynamic-slice_fusion
  2.4 0.7 copy.123
  3.1 0.7 copy.124
  3.9 0.6 pad_bitcast_fusion.refs_1_
  4.6 0.7 concatenate.12.refs_3_
  5.3 0.7 copy.97.refs_4_.refs_3_
  6.1 0.8 copy.98.refs_5_.refs_4_
  6.9 0.6 broadcast_in_dim.57.refs_6_.refs_5_
  7.5 6.6 %copy.93 = bf16[1,1152,1728]{2,1,0:T(8,128)(2,1)} copy(bf16[1,1152,1728]{1,2,0:T(8,128)(2,1)} %param.26) | data formatting | bytes 7962624 | tf_op args[5]
  14.1 2.6 copy.94
  16.6 1.3 copy.99.refs_14_
  17.9 0.2 constant_dynamic-slice_fusion.1
  18.2 0.7 copy.125
  19.0 0.7 maximum_maximum_fusion.refs_16_
  19.7 103.4 %shard_map.348 = (f32[2,6,8,1152]{3,2,1,0:T(8,128)}, f32[2,8,1152]{2,1,0:T(8,128)}, bf16[3456,288]{1,0:T(8,128)(2,1)}, bf16[288,1152]{1,0:T(8,128)(2,1)}, bf16[1...) custom-call(bf16[2,48,1152]{2,1,0:T(8,128)(2,1)} %bitcast.81, ...), custom_call_target="tpu_custom_call" | custom-call | flops 1019215872 | bytes 16472832 | tf_op jit(solution)/shard_map/pallas_call | solution.py:1577
  123.1 3.4 copy.127.refs_8_
  126.5 59.1 %shard_map.349 = (bf16[2,48,1152]{2,1,0:T(8,128)(2,1)}, f32[2,48,1152]{2,1,0:T(8,128)}, bf16[2,192,1152]{2,1,0:T(8,128)(2,1)}, f32[2,192,1152]{2,1,0:T(8,128)}, ...) custom-call(f32[2,48,1152]{2,1,0:T(8,128)} %get-tuple-element.126.re, ...), custom_call_target="tpu_custom_call", output_to_operand_aliasing={{5}: (8, {}), {6}: (9, {}), {7}: (10, {}), {8}: (11, {})} | custom-call | flops 2038431744 | bytes 22356352 | tf_op jit(solution)/shard_map/pallas_call | solution.py:1577
  185.6 45.0 %shard_map.350 = (f32[2,48,1152]{2,1,0:T(8,128)}, f32[2,48,1152]{2,1,0:T(8,128)}, bf16[2,192,1152]{2,1,0:T(8,128)(2,1)}, bf16[2,192,512]{2,1,0:T(8,128)(2,1)}, b...) custom-call(bf16[2,48,1152]{2,1,0:T(8,128)(2,1)} %get-tuple-element., ...), custom_call_target="tpu_custom_call", output_to_operand_aliasing={{8}: (10, {}), {9}: (11, {}), {10}: (12, {})} | custom-call | flops 1019215872 | bytes 14175616 | tf_op jit(solution)/shard_map/pallas_call | solution.py:1577
  230.7 38.4 %shard_map.351 = (bf16[2,48,1152]{2,1,0:T(8,128)(2,1)}, f32[2,48,1152]{2,1,0:T(8,128)}, bf16[2,192,1152]{2,1,0:T(8,128)(2,1)}, f32[2,192,1152]{2,1,0:T(8,128)}, ...) custom-call(f32[2,48,1152]{2,1,0:T(8,128)} %get-tuple-element.140.re, ...), custom_call_target="tpu_custom_call", output_to_operand_aliasing={{5}: (8, {}), {6}: (9, {}), {7}: (10, {})} | custom-call | flops 2038431744 | bytes 19702144 | tf_op jit(solution)/shard_map/pallas_call | solution.py:1577
  269.0 0.6 broadcast_in_dim.63.refs_3_
  269.6 22.6 %shard_map.352 = (f32[2,48,1152]{2,1,0:T(8,128)}, bf16[2,1152,512]{2,1,0:T(8,128)(2,1)}, bf16[2,512,2048]{2,1,0:T(8,128)(2,1)}, bf16[2,2048,192]{2,1,0:T(8,128)(2,1)}, f32[4,8,512]{2,1,0:T(8,128)}) custom-call(bf16[2,48,1152]{2,1,0:T(8,128)(2,1)} %get-tuple-element.134.refs_0_.refs_12_.refs_1_, bf16[2,2,2,48,192]{4,3,2,1,0:T(8,128)(2,1)} %get-tuple-element.150.refs_1_, ...), custom_call_target="tpu_custom_call" | custom-call | flops 4680843264 | bytes 8564736 | tf_op jit(solution)/shard_map/pallas_call | solution.py:1577
  292.3 47.8 %shard_map.353 = (f32[2,48,1152]{2,1,0:T(8,128)}, f32[3,8,1152]{2,1,0:T(8,128)}, bf16[2,288,1152]{2,1,0:T(8,128)(2,1)}, bf16[2,288,1152]{2,1,0:T(8,128)(2,1)}, f...) custom-call(bf16[2,48,1152]{2,1,0:T(8,128)(2,1)} %bitcast.83, ...), custom_call_target="tpu_custom_call" | custom-call | flops 4076863488 | bytes 18506112 | tf_op jit(solution)/shard_map/pallas_call | solution.py:1577
  340.2 1.1 fusion
  341.3 0.9 copy.111
  342.3 53.5 %shard_map.354 = (f32[2,48,1152]{2,1,0:T(8,128)}, f32[3,8,1152]{2,1,0:T(8,128)}, bf16[2,3,288,288]{3,2,1,0:T(8,128)(2,1)}, bf16[2,288,288]{2,1,0:T(8,128)(2,1)},...) custom-call(f32[2,48,1152]{2,1,0:T(8,128)} %get-tuple-element.157.re, ...), custom_call_target="tpu_custom_call" | custom-call | flops 2038431744 | bytes 19923328 | tf_op jit(solution)/shard_map/pallas_call | solution.py:1577
  395.8 1.8 add.31.refs_0_
  397.6 54.2 %shard_map.355 = (f32[2,48,1152]{2,1,0:T(8,128)}, f32[3,8,1152]{2,1,0:T(8,128)}, bf16[2,288,1152]{2,1,0:T(8,128)(2,1)}, bf16[2,288,1152]{2,1,0:T(8,128)(2,1)}, f...) custom-call(f32[2,48,1152]{2,1,0:T(8,128)} %add.31.refs_0_, ...), custom_call_target="tpu_custom_call" | custom-call | flops 4076863488 | bytes 24535424 | tf_op jit(solution)/shard_map/pallas_call | solution.py:1577
  451.8 54.8 %shard_map.356 = (f32[2,48,1152]{2,1,0:T(8,128)}, f32[3,8,1152]{2,1,0:T(8,128)}, bf16[2,3,288,288]{3,2,1,0:T(8,128)(2,1)}, bf16[2,288,288]{2,1,0:T(8,128)(2,1)},...) custom-call(f32[2,48,1152]{2,1,0:T(8,128)} %get-tuple-element.182.re, ...), custom_call_target="tpu_custom_call" | custom-call | flops 2038431744 | bytes 15745408 | tf_op jit(solution)/shard_map/pallas_call | solution.py:1577
  506.8 0.6 copy.126
  507.4 59.0 %shard_map.357 = (f32[4,48,1152]{2,1,0:T(8,128)}, f32[288,1728]{1,0:T(8,128)}, f32[1,1728]{1,0:T(1,128)}, f32[8,1152]{1,0:T(8,128)}, f32[8,512]{1,0:T(8,128)}, /...) custom-call(f32[2,48,1152]{2,1,0:T(8,128)} %get-tuple-element.197.re, ...), custom_call_target="tpu_custom_call" | custom-call | flops 63700992 | bytes 5828096 | tf_op jit(solution)/shard_map/pallas_call | solution.py:1577
  566.5 2.5 copy.112
  569.0 0.5 slice.24
  570.2 2.7 select_bitcast_fusion.2
  573.0 1.4 slice_bitcast_fusion.1
  574.4 1.0 copy.113
  575.4 1.5 fusion.4
  576.9 1.2 select_bitcast_fusion.1
  578.1 0.6 copy-done.6
  578.7 0.4 copy-done.8
  579.1 1.2 select_bitcast_fusion
  580.3 0.6 slice.29
  580.9 0.6 copy.118
  581.5 0.8 copy.114
  582.3 0.6 slice.31
  582.8 1.3 copy.141
  584.2 0.6 copy.142
  584.8 0.7 copy.143
  585.5 0.8 copy.144
  (75 shorter events, 0.6 us)
Async XLA Ops:
  0.7 17.3 %copy-start = (bf16[192,4,192]{2,1,0:T(4,128)(2,1)S(1)}, bf16[192,4,192]{2,1,0:T(4,128)(2,1)}, u32[]{:S(2)}) copy-start(bf16[192,4,192]{2,1,0:T(4,128)(2,1)} %param.24) | copy-start | bytes 884740
  0.7 3.2 copy-start.18
  0.7 3.8 copy-start.26
  0.7 3.9 copy-start.22
  0.7 3.9 copy-start.23
  0.7 3.9 copy-start.24
  0.7 4.5 copy-start.21
  7.5 6.6 %copy-start.4 = (bf16[1,1152,3,288]{1,3,2,0:T(8,128)(2,1)S(1)}, bf16[1,1152,3,288]{1,3,2,0:T(8,128)(2,1)}, u32[]{:S(2)}) copy-start(bf16[1,1152,3,288]{1,3,2,0:T(8,128)(2,1)} %param.28) | copy-start | bytes 5971972
  14.1 2.6 copy-start.11
  16.6 2.2 copy-start.28
  16.6 2.2 copy-start.27
  230.6 38.4 %copy-start.25 = (bf16[2048]{0:T(1024)(128)(2,1)S(1)}, bf16[2048]{0:T(1024)(128)(2,1)}, u32[]{:S(2)}) copy-start(bf16[2048]{0:T(1024)(128)(2,1)} %param.39) | copy-start | bytes 12292
  292.3 47.9 %copy-start.2 = (bf16[2,48,1152]{2,1,0:T(8,128)(2,1)S(1)}, bf16[2,48,1152]{2,1,0:T(8,128)(2,1)}, u32[]{:S(2)}) copy-start(bf16[2,48,1152]{2,1,0:T(8,128)(2,1)} %get-tuple-element.134.refs_0_.refs_12_.refs_1_) | copy-start | bytes 663556
  292.3 47.9 %copy-start.10 = (bf16[2,48,1152]{2,1,0:T(8,128)(2,1)S(1)}, bf16[2,48,1152]{2,1,0:T(8,128)(2,1)}, u32[]{:S(2)}) copy-start(bf16[2,48,1152]{2,1,0:T(8,128)(2,1)} %get-tuple-element.145.refs_13_) | copy-start | bytes 663556
  342.3 53.5 %copy-start.15 = (f32[2,48,1152]{2,1,0:T(8,128)S(1)}, f32[2,48,1152]{2,1,0:T(8,128)}, u32[]{:S(2)}) copy-start(f32[2,48,1152]{2,1,0:T(8,128)} %get-tuple-element.171) | copy-start | bytes 1327108
  566.5 2.5 copy-start.19
  566.5 3.7 copy-start.7
  570.2 4.2 copy-start.13
  570.2 4.2 copy-start.14
  570.2 6.7 %copy-start.9 = (f32[288,1152]{1,0:T(8,128)S(1)}, f32[288,1152]{1,0:T(8,128)}, u32[]{:S(2)}) copy-start(f32[288,1152]{1,0:T(8,128)} %get-tuple-element.226) | copy-start | bytes 3981316
  572.9 3.9 copy-start.5
  576.9 1.8 copy-start.6
  576.9 2.2 copy-start.8
  579.1 2.4 copy-start.17
  579.1 3.8 copy-start.3
  582.8 1.3 copy-start.20
  582.8 1.9 copy-start.16
  582.8 2.6 copy-start.12
  582.8 3.4 copy-start.1

commit v6 on v5

--- a/solution.py
+++ b/solution.py
@@ -265,13 +265,14 @@
     return ref[...].reshape(-1, ref.shape[-1])
 
 
-def spread_matrix(width):
+def spread_matrix(width, which=0, total=None):
     lanes = width // HEAD_WIDTH * HEAD_LANES
-    source = lax.broadcasted_iota(jnp.int32, (width, lanes), 0)
-    target = lax.broadcasted_iota(jnp.int32, (width, lanes), 1)
+    shape = (total or width, lanes)
+    source = lax.broadcasted_iota(jnp.int32, shape, 0)
+    target = lax.broadcasted_iota(jnp.int32, shape, 1)
     within = target & (HEAD_LANES - 1)
     head = target >> (HEAD_LANES.bit_length() - 1)
-    hit = (within < HEAD_WIDTH) & (source == head * HEAD_WIDTH + within)
+    hit = (within < HEAD_WIDTH) & (source == which * width + head * HEAD_WIDTH + within)
     return jnp.where(hit, 1.0, 0.0).astype(BF16)
 
 
@@ -482,7 +483,7 @@
         self.held, self.last = self.held[:3], self.held[3:]
         super().begin()
 
-    def to_x(self):
+    def middle(self):
         mine, other, sems = self.held
         total, got, last_sems = self.last
         wait_all(self.copies)
@@ -506,30 +507,6 @@
         def given():
             self.copy.wait_send()
             self.out_refs[0][...] = jnp.zeros_like(self.out_refs[0])
-
-
-class LateShare(Cargo):
-    any_outs = True
-
-    def __init__(self, other):
-        self.inputs = (other,)
-        self.outs = ((other.shape, BF16),)
-        self.aliases = {0: 0}
-        self.scratch = (pltpu.SemaphoreType.DMA((4,)), pltpu.SemaphoreType.DMA((4,)))
-
-    def peers(self):
-        return ["core", "y"]
-
-    def begin(self):
-        out = self.out_refs[0]
-        self.share = Share(out, out, 4, self.held)
-        self.share.forward(None)
-
-    def middle(self):
-        self.share.forward_again()
-
-    def late(self):
-        self.share.finish()
 
 
 class Swap(Cargo):
@@ -612,7 +589,8 @@
 class ColumnGather(Cargo):
     any_outs = True
 
-    def __init__(self, weights, targets, biases, sections):
+    def __init__(self, weights, axes, targets, biases):
+        self.axes = axes
         self.inputs = (*weights, targets, biases)
         self.outs = tuple(((2,) + one.shape, BF16) for one in weights) + (
             ((2, 2) + targets.shape[1:], BF16),
@@ -631,10 +609,14 @@
         tensor, core = lax.axis_index("tensor"), core_bit()
         eighth = lax.axis_index("section") * 4 + y_bit() * 2 + core
         slot, out = lax.rem(tensor, 2), []
-        for source, place in zip(self.ins[:3], self.out_refs[:3]):
-            size = source.shape[0] // 8
-            rows = pl.ds(pl.multiple_of(eighth * size, 16), size)
-            out.append((source.at[rows], place.at[slot, rows]))
+        for source, place, axis in zip(self.ins[:3], self.out_refs[:3], self.axes):
+            size = source.shape[axis] // 8
+            out.append(
+                (
+                    span(source, axis, eighth * size, size),
+                    span(place.at[slot], axis, eighth * size, size),
+                )
+            )
         out.append((self.ins[3].at[target], self.out_refs[3].at[slot, core]))
         out.append((self.ins[4], self.out_refs[4].at[slot, core]))
         return out
@@ -701,10 +683,9 @@
     def passed(self, i, other):
         send, recv, own = self.held
         tensor, slot = lax.axis_index("tensor"), core_bit()
-        place = self.out_refs[i]
-        size = self.ins[i].shape[0] // 8
+        size = self.ins[i].shape[self.axes[i]] // 8
         eighth = lax.axis_index("section") * 4 + y_bit() * 2 + other
-        part = place.at[slot, pl.ds(pl.multiple_of(eighth * size, 16), size)]
+        part = span(self.out_refs[i].at[slot], self.axes[i], eighth * size, size)
         return describe(
             part, part, send.at[i, 4 + other], recv.at[i, slot, other], {"tensor": 3 * (tensor - 1)}
         )
@@ -726,13 +707,11 @@
         self.start((0,))
 
     def late(self):
-        self.relay((0,))
         self.start((1,))
 
     def end(self):
         send, recv, own = self.held
         tensor, core = lax.axis_index("tensor"), core_bit()
-        self.relay((1,))
         self.each(range(5), lambda copy: copy.wait_send())
 
         @pl.when(self.stays())
@@ -775,7 +754,8 @@
 class ShareAlong(Cargo):
     any_outs = True
 
-    def __init__(self, weights, stage):
+    def __init__(self, weights, axes, stage):
+        self.axes = axes
         self.inputs = tuple(weights)
         self.outs = tuple((one.shape, BF16) for one in weights)
         self.aliases = {0: 0, 1: 1, 2: 2}
@@ -790,9 +770,9 @@
         section, y, self.copies = lax.axis_index("section"), y_bit(), []
 
         def give(which, start, parts, peer):
-            ref = self.out_refs[which]
-            size = ref.shape[1] // 4
-            part = ref.at[:, pl.ds(pl.multiple_of(start * size, 16), parts * size)]
+            ref, axis = self.out_refs[which], self.axes[which]
+            size = ref.shape[axis + 1] // 4
+            part = span(ref, axis, start * size, parts * size)
             i = len(self.copies)
             self.copies.append(remote(part, part, send.at[i], recv.at[i], peer))
 
@@ -934,11 +914,11 @@
     full_ref[...] = full[...]
     tokens = flat(full)
     bias = biases()
-    for which, target in ((0, q_ref), (1, k_ref), (2, v_ref)):
-        projected = dot(tokens, wqkv[pl.ds(which * width, width), :])
-        if which != 1:
-            projected = projected + bias[which // 2 : which // 2 + 1, :heads_width]
-        target[...] = dot(projected.astype(BF16), spread).astype(BF16).reshape(target.shape)
+    both = 3 * heads_width
+    projected = (dot(tokens, wqkv[...]) + bias[0:1, :both]).astype(BF16)
+    for which, target in enumerate((q_ref, k_ref, v_ref)):
+        parts = dot(projected, spread_matrix(heads_width, which, both))
+        target[...] = parts.astype(BF16).reshape(target.shape)
 
     def one_head(index, carry):
         row = index // heads
@@ -999,7 +979,7 @@
     cargo.begin()
     cond_act = silu(cond_ref[...].astype(F32)).astype(BF16)
     load_ada.wait()
-    mod = dot(cond_act, ada[...]) + ada_b_ref[...].astype(F32)
+    mod = dot(cond_act, ada[...], NT) + ada_b_ref[...].astype(F32)
     mod_src[...] = mod.reshape(mod_src.shape)
     mod_buf[section, tensor] = mod_src[section]
     copies = [
@@ -1053,11 +1033,15 @@
         shares[0].finish()
 
     def before_heads():
+        cargo.late()
         shares[2].forward(shares[2].first)
 
     def after_scatter():
-        cargo.late()
+        gather = cargo.cargos[0]
+        gather.relay((0,))
         shares[2].forward_again()
+        shares[3].forward(shares[3].first)
+        gather.relay((1,))
         shares[2].finish()
 
     attend_body(
@@ -1065,8 +1049,9 @@
         (ag_send, ag_recv, rs_send, rs_recv), need_qkv, need_out,
         (after_gather, before_heads, after_scatter),
     )
-    shares[3].first.wait()
+    shares[3].forward_again()
     cargo.end()
+    shares[3].finish()
 
 
 def attend_kernel(count, block, *refs, cargo):
@@ -1093,9 +1078,7 @@
     rows, length, width = middle_ref.shape
     mod_ref = mods_ref.at[block]
     load_one = fetch(block, w1_own, w1_other, w1, w_sem.at[0])
-    late = [one for one in cargo.cargos if isinstance(one, LateShare)]
-    if not late:
-        load_two = fetch(block, w2_own, w2_other, w2, w_sem.at[1])
+    load_two = fetch(block, w2_own, w2_other, w2, w_sem.at[1])
     normed, unused = layer_norm(flat(middle_ref))
     mlp_in = normed * (1.0 + token_mod(mod_ref, seg_own, 4)) + token_mod(mod_ref, seg_own, 3)
     full[:, own_rows(me, length), :] = mlp_in.astype(BF16).reshape(rows, length, width)
@@ -1111,9 +1094,6 @@
     pre_ref[...] = pre.reshape(pre_ref.shape)
     cargo.middle()
     act_ref[...] = gelu_tanh(pre).astype(BF16).reshape(act_ref.shape)
-    cargo.late()
-    if late:
-        load_two = fetch(block, w2_own, late[0].out_refs[0], w2, w_sem.at[1])
     load_two.wait()
 
     def partial(which_rows):
@@ -1231,30 +1211,24 @@
         return carry
 
     lax.fori_loop(0, rows * heads, one_head, 0)
+    both = 3 * heads_width
+    gathered = 0.0
     for which in range(3):
-        narrow[which] = (
-            dot(flat(wide.at[which]), spread, NT).astype(BF16).reshape(narrow.shape[1:])
-        )
+        gathered = gathered + dot(
+            flat(wide.at[which]), spread_matrix(heads_width, which, both), NT
+        )
+    narrow[...] = gathered.astype(BF16).reshape(narrow.shape)
     load_qkv.wait()
 
     def partial(which_rows):
-        total = 0.0
-        for which in range(3):
-            total = total + dot(
-                narrow[which, :, which_rows, :].reshape(rows * length, heads_width),
-                wqkv[pl.ds(which * width, width), :],
-                NT,
-            )
-        return total
+        return dot(narrow[:, which_rows, :].reshape(rows * length, both), wqkv[...], NT)
 
     total = line.scatter_sum(partial, buffers)
     d_bo_ref[...] = jnp.sum(flat(full).astype(F32), axis=0, keepdims=True)
-    d_bqv_ref[0:1, :] = jnp.sum(flat(narrow.at[0]).astype(F32), axis=0, keepdims=True)
-    d_bqv_ref[1:2, :] = jnp.sum(flat(narrow.at[2]).astype(F32), axis=0, keepdims=True)
+    d_bqv_ref[...] = jnp.sum(flat(narrow).astype(F32), axis=0, keepdims=True)
     wo_whole[...] = dot(flat(full), flat(mixed_ref), TN).astype(BF16)
     wo_sum.begin()
-    for which in range(3):
-        qkv_whole[which] = dot(flat(full_ref), flat(narrow.at[which]), TN).astype(BF16)
+    qkv_whole[...] = dot(flat(full_ref), flat(narrow), TN).astype(BF16)
     qkv_sum.begin()
     d_attn_in = line.finish_sum(total, buffers)
     normed, inverse = layer_norm(flat(u_ref).astype(F32))
@@ -1328,7 +1302,7 @@
     all_second = flat(second)
     width = target[0].shape[1]
     predicted = [
-        dot(all_second, p3[slot]) + biases_ref[slot, 0, 1:2, :width] for slot in range(2)
+        dot(all_second, p3[slot], NT) + biases_ref[slot, 0, 1:2, :width] for slot in range(2)
     ]
     pred_sq = sum(jnp.sum(one * one, axis=1, keepdims=True) for one in predicted)
     cross = sum(
@@ -1363,13 +1337,13 @@
             mine = jnp.where(
                 side == 0, d_pred[slot][:count].astype(F32), d_pred[slot][count:].astype(F32)
             )
-            terms = terms + dot(mine.astype(BF16), p3[slot], NT)
+            terms = terms + dot(mine.astype(BF16), p3[slot])
         return terms
 
     copy = give(buf_b, d_second_term(1 - core), 4)
     grad = d_second_term(core)
     for slot in range(2):
-        d_p3_ref[slot] = dot(all_second, d_pred[slot], TN).astype(BF16)
+        d_p3_ref[slot] = dot(d_pred[slot], all_second, TN).astype(BF16)
     copy.wait()
     grad = ((grad + buf_b[1].astype(F32)) * silu_slope(second_pre[...])).astype(BF16)
     d_second[core] = grad
@@ -1457,11 +1431,11 @@
 
     place_copy = remote(place_src, place_buf, send.at[at], recv.at[at], x_peer())
     at = at + 1
-    heads_width = small_refs[0].shape[-1]
+    both = small_refs[0].shape[-1]
     small_src[...] = jnp.zeros_like(small_src)
     for block in range(sections):
         d_bqv, d_bo, d_b1, d_b2 = small_refs[4 * block : 4 * block + 4]
-        small_src[block, 0:2, :heads_width] = d_bqv[...]
+        small_src[block, 0:1, :both] = d_bqv[...]
         small_src[block, 2:3, :] = d_bo[...]
         small_src[block, 3:4, : d_b1.shape[1]] = d_b1[...]
         small_src[block, 4:5, :] = d_b2[...]
@@ -1509,7 +1483,7 @@
         at = at + 2
     for one in cargo.cargos:
         if isinstance(one, LastSum):
-            one.to_x()
+            one.middle()
     place_copy.wait()
     rows = place_buf.shape[0]
 
@@ -1543,6 +1517,7 @@
 VMEM = pl.BlockSpec(memory_space=pltpu.VMEM)
 ANY = pl.BlockSpec(memory_space=pl.ANY)
 MOD_ROWS = 8
+PROJECTOR_AXES = (0, 0, 1)
 
 
 def call(kernel, number, inputs, in_any, outs, out_any, scratch, flops, cargos=()):
@@ -1644,7 +1619,7 @@
 
 def open_forward(sizes, u, cond, ada_w, ada_b, biases, segs, own, sections, cargos):
     count, width = sizes.count, sizes.width
-    piece = ada_w.shape[1]
+    piece = ada_w.shape[0]
     inputs = [u, cond, ada_b, biases, *segs, ada_w] + [own[n] for n in ("qkv", "out", "one", "two")]
     plane = sections * count - 1
     results, carried = call(
@@ -1759,21 +1734,21 @@
         4,
         [
             (sizes.local, F32), (sizes.mods, F32),
-            ((2,) + quarter((3, sizes.width, sizes.heads_width)), BF16),
+            ((2,) + quarter((sizes.width, 3 * sizes.heads_width)), BF16),
             ((2,) + quarter((sizes.width, sizes.heads_width)), BF16),
-            ((2, sizes.heads_width), F32), ((1, sizes.width), F32),
+            ((1, 3 * sizes.heads_width), F32), ((1, sizes.width), F32),
         ],
         (),
         [
             pltpu.VMEM(sizes.full, BF16),
             pltpu.VMEM((4,) + sizes.wide, BF16),
-            pltpu.VMEM((3, sizes.rows, sizes.positions, sizes.heads_width), BF16),
+            pltpu.VMEM((sizes.rows, sizes.positions, 3 * sizes.heads_width), BF16),
             pltpu.VMEM(own["qkv"].shape, BF16),
             pltpu.VMEM(own["out"].shape, BF16),
         ]
         + exchange_scratch(sizes.count, *sizes.local)
         + semaphores(sizes.count)
-        + core_sum_scratch((3, sizes.width, sizes.heads_width))
+        + core_sum_scratch((sizes.width, 3 * sizes.heads_width))
         + core_sum_scratch((sizes.width, sizes.heads_width)),
         2 * sizes.tokens * sizes.width * sizes.heads_width * 8,
         cargos,
@@ -1857,6 +1832,66 @@
     )
 
 
+def assemble_kernel(heads_width, *refs):
+    fc1, fc2 = refs[0:2], refs[2:4]
+    alone, (qkv, wo) = refs[4:9], (refs[9:11], refs[11:13])
+    grad_ref, small, proj = refs[13:16]
+    outs, sems = refs[16:-1], refs[-1]
+    is_first = lax.axis_index("section") == 0
+    waits = []
+    for i, pair in enumerate((fc1, fc2)):
+        waits.append(pltpu.make_async_copy(pair[0], outs[i], sems.at[i]))
+
+        @pl.when(is_first)
+        def take_one(pair=pair, i=i):
+            pltpu.make_async_copy(pair[0], outs[i], sems.at[i]).start()
+
+        @pl.when(jnp.logical_not(is_first))
+        def take_two(pair=pair, i=i):
+            pltpu.make_async_copy(pair[1], outs[i], sems.at[i]).start()
+
+    for i, one in enumerate(alone):
+        waits.append(local(one, outs[2 + i], sems.at[2 + i]))
+    grad_out, qkv_out, wo_out, qv_b, out_b, fc1_b, fc2_b, p1_b, p2_b, p3_b, loss = outs[7:]
+    for row in range(grad_ref.shape[0]):
+        grad_out[:, row, :] = grad_ref[row]
+    qkv_own = jnp.where(is_first, qkv[0][...], qkv[1][...])
+    for which in range(3):
+        qkv_out[which] = qkv_own[:, which * heads_width : (which + 1) * heads_width]
+    wo_out[...] = jnp.where(is_first, wo[0][...], wo[1][...]).T
+    qv_b[0:1, :] = small[0:1, :heads_width]
+    qv_b[1:2, :] = small[0:1, 2 * heads_width : 3 * heads_width]
+    out_b[...] = small[2:3, :]
+    fc1_b[...] = small[3:4, :]
+    fc2_b[...] = small[4:5, :]
+    p1_b[...] = proj[0:1, :]
+    p2_b[...] = jnp.concatenate([proj[2 + row : 3 + row, :] for row in range(4)], axis=1)
+    p3_b[...] = proj[1:2, : p3_b.shape[1]]
+    loss[...] = proj[6:7, :HEAD_LANES]
+    wait_all(waits)
+
+
+def assemble(choices, alone, section_grad, small, proj_small, heads_width):
+    (fc1, fc2, qkv, wo) = choices
+    inputs = [*fc1, *fc2, *alone, *qkv, *wo, section_grad, small, proj_small]
+    both, length, width = section_grad.shape
+    share, lane = fc1[0].shape[0], proj_small.shape[1]
+    third = alone[4].shape[0]
+    shapes = [fc1[0].shape, fc2[0].shape] + [one.shape for one in alone] + [
+        (length, both, width), (3, share, heads_width), wo[0].shape[::-1], (2, heads_width),
+        (1, width), (1, width), (1, width), (1, lane), (1, 4 * lane), (1, third), (1, HEAD_LANES),
+    ]
+    return pl.pallas_call(
+        functools.partial(assemble_kernel, heads_width),
+        out_shape=[jax.ShapeDtypeStruct(shape, F32) for shape in shapes],
+        in_specs=[ANY] * 9 + [VMEM] * 7,
+        out_specs=[ANY] * 7 + [VMEM] * 11,
+        scratch_shapes=[pltpu.SemaphoreType.DMA((7,))],
+        compiler_params=pltpu.CompilerParams(vmem_limit_bytes=40 * 2**20),
+        cost_estimate=pl.CostEstimate(flops=1000, bytes_accessed=2**24, transcendentals=0),
+    )(*inputs)
+
+
 def halve(value, axis, bit, position):
     size = lax.axis_size(axis)
     mine = (lax.axis_index(axis) & bit) // bit
@@ -1923,7 +1958,7 @@
         return jnp.transpose(my_rows(value, 1), (1, 0, 2))
 
     own = {
-        "qkv": jnp.transpose(query_key_value_weight[0], (1, 0, 2)).reshape(3 * width, heads_width),
+        "qkv": query_key_value_weight[0].reshape(width, 3 * heads_width),
         "out": attention_output_weight[0],
         "one": hidden_weight[0],
         "two": output_weight_mlp[0],
@@ -1934,7 +1969,16 @@
 
     biases = jnp.concatenate(
         [
-            padded(query_value_bias[0]), padded(attention_output_bias), padded(hidden_bias),
+            padded(
+                jnp.concatenate(
+                    [
+                        query_value_bias[0, 0:1], jnp.zeros((1, heads_width), BF16),
+                        query_value_bias[0, 1:2],
+                    ],
+                    axis=1,
+                )
+            ),
+            jnp.zeros((1, width), F32), padded(attention_output_bias), padded(hidden_bias),
             padded(output_bias_mlp), jnp.zeros((MOD_ROWS - 5, width), F32),
         ],
         axis=0,
@@ -1958,27 +2002,27 @@
         ],
         axis=0,
     )
-    gather = ColumnGather((p1_w, p2_w, p3_w), target_parts, proj_biases, sections)
+    gather = ColumnGather((p1_w, p2_w, p3_w.T), PROJECTOR_AXES, target_parts, proj_biases)
 
     u = to_rows(block_eight_input)
     sizes = Shapes(u, own, count)
     mods, bias_all, other, attend_one, carried = open_forward(
-        sizes, u, cond_pad.reshape(-1, width), ada_w[0], ada_b, biases, segs, own, sections,
+        sizes, u, cond_pad.reshape(-1, width), ada_w[0].T, ada_b, biases, segs, own, sections,
         (gather,),
     )
     *proj_weights, target_all, proj_bias_all = carried[0]
     mlp_one, carried = mlp_forward(
         sizes, 0, attend_one[0], mods, bias_all, segs, own, other,
-        (LateShare(other["two"]), ShareAlong(proj_weights, 0)),
-    )
-    (other["two"],), proj_weights = carried
+        (ShareAlong(proj_weights, PROJECTOR_AXES, 0),),
+    )
+    proj_weights = carried[0]
     first_out = mlp_one[0]
     attend_two, carried = attend_forward(
-        sizes, 1, first_out, mods, bias_all, segs, own, other, (ShareAlong(proj_weights, 1),)
+        sizes, 1, first_out, mods, bias_all, segs, own, other, (ShareAlong(proj_weights, PROJECTOR_AXES, 1),)
     )
     proj_weights = carried[0]
     mlp_two, carried = mlp_forward(
-        sizes, 1, attend_two[0], mods, bias_all, segs, own, other, (ShareAlong(proj_weights, 2),)
+        sizes, 1, attend_two[0], mods, bias_all, segs, own, other, (ShareAlong(proj_weights, PROJECTOR_AXES, 2),)
     )
     proj_weights = carried[0]
     second_out = mlp_two[0]
@@ -1996,27 +2040,26 @@
     (second_grad, mod_attend_two, *attend_grads_two), carried = attend_backward(
         sizes, 1, d_middle_two, first_out, attend_two, *back,
         [YSum(grad, BF16) for grad in mlp_grads_two[:2]]
-        + [HalfSum(grad_p2, 1, "x", (0, 1)), HalfSum(grad_p3, 0, "x"), HalfSum(grad_p1, 0, "y")],
-    )
-    ((mlp_part_a,), (mlp_part_b,)), ((grad_p2_a,), (grad_p3,), (grad_p1,)) = (
-        carried[:2], carried[2:]
-    )
+        + [HalfSum(grad_p2, 1, "x", (0, 1)), HalfSum(grad_p3, 1, "x")],
+    )
+    ((mlp_part_a,), (mlp_part_b,)), ((grad_p2_a,), (grad_p3,)) = carried[:2], carried[2:]
     (d_middle_one, mod_mlp_one, *mlp_grads_one), carried = mlp_backward(
         sizes, 0, second_grad + grad_sent, attend_one, mlp_one, *back,
         [YSum(grad, BF16) for grad in attend_grads_two[:2]]
         + [SectionSum(mlp_part_a, 1), HalfSum(grad_p2, 1, "x", (1, 1))]
-        + [HalfSum(grad_p3, 0, "y"), HalfSum(grad_p2_a, 1, "y"), ColumnSum((grad_p1,), 0)],
+        + [HalfSum(grad_p1, 0, "y"), HalfSum(grad_p2_a, 1, "y")],
     )
     attend_parts_two, sum_mlp_a = carried[:2], carried[2]
-    (grad_p2_b,), (grad_p3,), (grad_p2_a,), (red_p1_w,) = carried[3:]
+    (grad_p2_b,), (grad_p1,), (grad_p2_a,) = carried[3:]
     (first_grad, mod_attend_one, *attend_grads_one), carried = attend_backward(
         sizes, 0, d_middle_one, u, attend_one, *back,
-        [YSum(mlp_grads_one[0], BF16), SectionSum(mlp_grads_one[1], 0, BF16)]
+        [LastSum(mlp_grads_one[0], 0), SectionSum(mlp_grads_one[1], 0, BF16)]
         + [SectionSum(part, 1) for part, in attend_parts_two]
-        + [SectionSum(mlp_part_b, 1), HalfSum(grad_p2_b, 1, "y"), ColumnSum((grad_p3,), 0)],
-    )
-    ((mlp_part_one,), (mlp_part_two,)), sums_attend_two = carried[:2], carried[2:4]
-    sums_mlp_two, ((grad_p2_b,), (red_p3_w,)) = (sum_mlp_a, carried[4]), carried[5:]
+        + [SectionSum(mlp_part_b, 1), HalfSum(grad_p2_b, 1, "y"), HalfSum(grad_p3, 1, "y")]
+        + [ColumnSum((grad_p1,), 0)],
+    )
+    sum_mlp_c, (mlp_part_two,), sums_attend_two = carried[0], carried[1], carried[2:4]
+    sums_mlp_two, ((grad_p2_b,), (grad_p3,), (red_p1_w,)) = (sum_mlp_a, carried[4]), carried[5:]
 
     cond_act = silu(my_rows(cond, 0).astype(F32)).astype(BF16).astype(F32)
     share = width // replicas
@@ -2031,48 +2074,68 @@
         (mod_attend_one, mod_mlp_one, mod_attend_two, mod_mlp_two),
         small, proj_small, cond_cols, sections, replicas,
         [LastSum(grad, 0) for grad in attend_grads_one[:2]]
-        + [YSum(mlp_part_two, F32), SectionSum(mlp_part_one, 0)]
-        + [ColumnSum((grad_p2_a, grad_p2_b), 1)],
-    )
-    sums_attend_one, sums_mlp_one = carried[:2], (carried[3], carried[2])
-    (red_p2_w,) = carried[4]
-
-    red_fc1, red_fc2, red_qkv, red_out = [
-        sum_beyond_quads(jnp.where(is_first, one[0], two[0]))
-        for one, two in zip(
-            list(sums_mlp_one) + list(sums_attend_one), list(sums_mlp_two) + list(sums_attend_two)
-        )
-    ]
-    red_p1_w, red_p3_w = sum_beyond_quads(red_p1_w), sum_beyond_quads(red_p3_w)
-    if replicas > 4:
-        red_p2_w = sum_beyond_quads(red_p2_w.T).T
-    align_loss = -0.5 * proj_small[6, 0] / total_token_count
+        + [YSum(mlp_part_two, F32)]
+        + [ColumnSum((grad_p2_a, grad_p2_b), 1), ColumnSum((grad_p3,), 1)],
+    )
+    sums_attend_one, sums_mlp_one = carried[:2], (sum_mlp_c, carried[2])
+    (red_p2_w,), (red_p3_w,) = carried[3:]
+
     own_out = jnp.where(is_first, first_out, second_out)
     section_out = jnp.where(
         is_first,
         jnp.concatenate([own_out, other_out], axis=0),
         jnp.concatenate([other_out, own_out], axis=0),
     )
+    section_out = jnp.transpose(section_out, (1, 0, 2))[None]
+    choices = [
+        (one[0], two[0])
+        for one, two in zip(
+            list(sums_mlp_one) + list(sums_attend_one), list(sums_mlp_two) + list(sums_attend_two)
+        )
+    ]
+    if replicas == 4:
+        alone = [grad_ada_w, grad_ada_b, red_p1_w, red_p2_w, red_p3_w]
+        final = assemble(choices, alone, section_grad, small, proj_small, heads_width)
+        red_fc1, red_fc2, grad_ada_w, grad_ada_b, red_p1_w, red_p2_w, red_p3_w = final[:7]
+        section_grad, red_qkv, red_out, qv_b, out_b, fc1_b, fc2_b, p1_sum, p2_sum, p3_sum, loss = (
+            final[7:]
+        )
+        red_p1_b, red_p2_b, red_p3_b = p1_sum[0], p2_sum[0], p3_sum[0]
+        loss_total = loss[0, 0]
+    else:
+        red_fc1, red_fc2, red_qkv, red_out = [
+            sum_beyond_quads(jnp.where(is_first, one, two)) for one, two in choices
+        ]
+        red_qkv = jnp.transpose(red_qkv.reshape(-1, 3, heads_width), (1, 0, 2))
+        red_out = red_out.T
+        red_p1_w = sum_beyond_quads(red_p1_w)
+        red_p2_w, red_p3_w = sum_beyond_quads(red_p2_w.T).T, sum_beyond_quads(red_p3_w.T).T
+        section_grad = jnp.transpose(section_grad, (1, 0, 2))
+        qv_b = jnp.stack([small[0, :heads_width], small[0, 2 * heads_width : 3 * heads_width]])
+        out_b, fc1_b, fc2_b = small[2:3], small[3:4], small[4:5]
+        red_p1_b, red_p2_b = proj_small[0], proj_small[2:6].reshape(-1)
+        red_p3_b, loss_total = proj_small[1, : p3_b.shape[0]], proj_small[6, 0]
+    align_loss = -0.5 * loss_total / total_token_count
     return (
-        jnp.transpose(section_out, (1, 0, 2))[None],
-        jnp.transpose(section_grad, (1, 0, 2))[None],
+        section_out,
+        section_grad[None],
         align_loss,
         grad_ada_w[None],
         grad_ada_b,
         jnp.transpose(red_qkv, (1, 0, 2))[None],
-        small[0:2, :heads_width][None],
-        red_out.T[None],
-        small[2:3],
+        qv_b[None],
+        red_out[None],
+        out_b,
         red_fc1[None],
-        small[3:4, :hidden],
+        fc1_b[:, :hidden],
         red_fc2.T[None],
-        small[4:5],
+        fc2_b,
         red_p1_w,
-        proj_small[0],
+        red_p1_b,
         red_p2_w,
-        proj_small[2:6].reshape(-1)[: p2_b.shape[0]],
-        red_p3_w,
-        proj_small[1, : p3_b.shape[0]],
+        red_p2_b[: p2_b.shape[0]],
+        red_p3_w.T,
+        red_p3_b,
     )
 
 

time: 596 us -> 541 us (0.908)
  Pallas kernels: 538 us -> 503 us
  local copies, waits for them, and re-layouts: 37.8 us -> 23 us
    pallas_call x10, Pallas kernels: 538 us -> 499 us  [call(): pl.pallas_call(body, out_shape=[jax.ShapeDtypeStruct(shape, dtype) for sh...]
    unnamed x75 -> x67, local copies, waits for them, and re-layouts: 23.1 us -> 12.9 us
where the time goes in v6:
time: 541 us; the launch traced here: 533 us
  Pallas kernels  503 us (93%)
  local copies, waits for them, and re-layouts  23 us (4%)
    pallas_call x10, Pallas kernels, call(): pl.pallas_call(body, out_shape=[jax.ShapeDtypeStruct(shape, dtype) for sh...  499 us
    unnamed x67, local copies, waits for them, and re-layouts  12.9 us

profile of v6, /device:TPU:0, one launch (start us, length us, event | category | flops | bytes accessed | tf_op | source)
XLA Modules:
  0.0 532.8 jit_solution(1626822309654813487)
XLA Ops:
  0.7 0.0 copy-start
  0.7 0.0 copy-start.22
  0.7 0.0 copy-start.24
  0.7 0.0 copy-start.25
  0.8 1.8 constant_dynamic-slice_fusion
  2.5 0.7 copy.112
  3.2 0.7 copy.113
  4.0 0.6 pad_bitcast_fusion.refs_1_
  4.6 0.1 pad.34.clone
  4.7 0.1 fusion.4
  4.9 0.7 concatenate.30.refs_3_
  5.5 0.1 dynamic-slice_bitcast_fusion
  5.6 0.7 copy.87.refs_4_.refs_3_
  6.3 0.8 copy.88.refs_5_.refs_4_
  7.2 0.6 broadcast_in_dim.65.refs_6_.refs_5_
  7.8 2.4 copy.89.refs_8_.refs_6_.refs_11_
  10.1 0.2 constant_dynamic-slice_fusion.1
  10.4 0.7 copy.114
  11.1 0.1 pad.32.clone
  11.2 0.7 maximum_maximum_fusion.refs_16_
  11.9 98.3 %shard_map.348 = (f32[2,6,8,1152]{3,2,1,0:T(8,128)}, f32[2,8,1152]{2,1,0:T(8,128)}, bf16[1152,864]{1,0:T(8,128)(2,1)}, bf16[288,1152]{1,0:T(8,128)(2,1)}, bf16[1...) custom-call(bf16[2,48,1152]{2,1,0:T(8,128)(2,1)} %bitcast.70, ...), custom_call_target="tpu_custom_call" | custom-call | flops 1019215872 | bytes 16472832 | tf_op jit(solution)/shard_map/pallas_call | solution.py:1552
  110.2 46.8 %shard_map.349 = (bf16[2,48,1152]{2,1,0:T(8,128)(2,1)}, f32[2,48,1152]{2,1,0:T(8,128)}, bf16[2,192,1152]{2,1,0:T(8,128)(2,1)}, f32[2,192,1152]{2,1,0:T(8,128)}, ...) custom-call(f32[2,48,1152]{2,1,0:T(8,128)} %get-tuple-element.142.re, ...), custom_call_target="tpu_custom_call", output_to_operand_aliasing={{5}: (8, {}), {6}: (9, {}), {7}: (10, {})} | custom-call | flops 2038431744 | bytes 19702144 | tf_op jit(solution)/shard_map/pallas_call | solution.py:1552
  157.0 43.6 %shard_map.350 = (f32[2,48,1152]{2,1,0:T(8,128)}, f32[2,48,1152]{2,1,0:T(8,128)}, bf16[2,192,1152]{2,1,0:T(8,128)(2,1)}, bf16[2,192,512]{2,1,0:T(8,128)(2,1)}, b...) custom-call(bf16[2,48,1152]{2,1,0:T(8,128)(2,1)} %get-tuple-element., ...), custom_call_target="tpu_custom_call", output_to_operand_aliasing={{8}: (10, {}), {9}: (11, {}), {10}: (12, {})} | custom-call | flops 1019215872 | bytes 14175616 | tf_op jit(solution)/shard_map/pallas_call | solution.py:1552
  200.6 0.0 copy-start.28
  200.6 34.8 %shard_map.351 = (bf16[2,48,1152]{2,1,0:T(8,128)(2,1)}, f32[2,48,1152]{2,1,0:T(8,128)}, bf16[2,192,1152]{2,1,0:T(8,128)(2,1)}, f32[2,192,1152]{2,1,0:T(8,128)}, ...) custom-call(f32[2,48,1152]{2,1,0:T(8,128)} %get-tuple-element.156.re, ...), custom_call_target="tpu_custom_call", output_to_operand_aliasing={{5}: (8, {}), {6}: (9, {}), {7}: (10, {})} | custom-call | flops 2038431744 | bytes 19702144 | tf_op jit(solution)/shard_map/pallas_call | solution.py:1552
  235.4 0.6 broadcast_in_dim.71.refs_3_
  236.0 22.1 %shard_map.352 = (f32[2,48,1152]{2,1,0:T(8,128)}, bf16[2,1152,512]{2,1,0:T(8,128)(2,1)}, bf16[2,512,2048]{2,1,0:T(8,128)(2,1)}, bf16[2,192,2048]{2,1,0:T(8,128)(2,1)}, f32[4,8,512]{2,1,0:T(8,128)}) custom-call(bf16[2,48,1152]{2,1,0:T(8,128)(2,1)} %get-tuple-element.150.refs_0_.refs_12_.refs_1_, bf16[2,2,2,48,192]{4,3,2,1,0:T(8,128)(2,1)} %get-tuple-element.165.refs_1_, ...), custom_call_target="tpu_custom_call" | custom-call | flops 4680843264 | bytes 8564736 | tf_op jit(solution)/shard_map/pallas_call | solution.py:1552
  258.2 48.9 %shard_map.353 = (f32[2,48,1152]{2,1,0:T(8,128)}, f32[3,8,1152]{2,1,0:T(8,128)}, bf16[2,288,1152]{2,1,0:T(8,128)(2,1)}, bf16[2,288,1152]{2,1,0:T(8,128)(2,1)}, f...) custom-call(bf16[2,48,1152]{2,1,0:T(8,128)(2,1)} %bitcast.73, ...), custom_call_target="tpu_custom_call" | custom-call | flops 4076863488 | bytes 18506112 | tf_op jit(solution)/shard_map/pallas_call | solution.py:1552
  307.2 1.1 fusion
  308.3 0.9 copy.104
  309.3 47.4 %shard_map.354 = (f32[2,48,1152]{2,1,0:T(8,128)}, f32[3,8,1152]{2,1,0:T(8,128)}, bf16[2,288,864]{2,1,0:T(8,128)(2,1)}, bf16[2,288,288]{2,1,0:T(8,128)(2,1)}, f32...) custom-call(f32[2,48,1152]{2,1,0:T(8,128)} %get-tuple-element.172.re, ...), custom_call_target="tpu_custom_call" | custom-call | flops 2038431744 | bytes 18743680 | tf_op jit(solution)/shard_map/pallas_call | solution.py:1552
  356.6 1.8 add.31.refs_0_
  358.5 48.6 %shard_map.355 = (f32[2,48,1152]{2,1,0:T(8,128)}, f32[3,8,1152]{2,1,0:T(8,128)}, bf16[2,288,1152]{2,1,0:T(8,128)(2,1)}, bf16[2,288,1152]{2,1,0:T(8,128)(2,1)}, f...) custom-call(f32[2,48,1152]{2,1,0:T(8,128)} %add.31.refs_0_, ...), custom_call_target="tpu_custom_call" | custom-call | flops 4076863488 | bytes 24338816 | tf_op jit(solution)/shard_map/pallas_call | solution.py:1552
  407.0 55.9 %shard_map.356 = (f32[2,48,1152]{2,1,0:T(8,128)}, f32[3,8,1152]{2,1,0:T(8,128)}, bf16[2,288,864]{2,1,0:T(8,128)(2,1)}, bf16[2,288,288]{2,1,0:T(8,128)(2,1)}, f32...) custom-call(f32[2,48,1152]{2,1,0:T(8,128)} %get-tuple-element.195.re, ...), custom_call_target="tpu_custom_call" | custom-call | flops 2038431744 | bytes 16728448 | tf_op jit(solution)/shard_map/pallas_call | solution.py:1552
  463.1 0.1 reshape.108
  463.2 0.6 copy.115
  463.8 52.3 %shard_map.357 = (f32[4,48,1152]{2,1,0:T(8,128)}, f32[288,1728]{1,0:T(8,128)}, f32[1,1728]{1,0:T(1,128)}, f32[8,1152]{1,0:T(8,128)}, f32[8,512]{1,0:T(8,128)}, /...) custom-call(f32[2,48,1152]{2,1,0:T(8,128)} %get-tuple-element.213.re, ...), custom_call_target="tpu_custom_call" | custom-call | flops 63700992 | bytes 5560064 | tf_op jit(solution)/shard_map/pallas_call | solution.py:1552
  516.2 1.6 copy-done.2
  517.8 1.3 copy-done.6
  519.1 1.2 copy-done.8
  520.4 1.2 copy-done.9
  521.5 1.0 copy-done.10
  522.6 1.0 copy-done.12
  523.6 0.9 copy-done.14
  524.5 0.8 copy-done.15
  525.3 0.7 copy-done.16
  526.0 0.7 copy-done.17
  526.7 4.4 shard_map.358
  (64 shorter events, 0.3 us)
Async XLA Ops:
  0.7 9.5 %copy-start = (bf16[192,4,192]{2,1,0:T(4,128)(2,1)S(1)}, bf16[192,4,192]{2,1,0:T(4,128)(2,1)}, u32[]{:S(2)}) copy-start(bf16[192,4,192]{2,1,0:T(4,128)(2,1)} %param.24) | copy-start | bytes 884740
  0.7 3.3 copy-start.22
  0.7 4.0 copy-start.24
  0.7 4.1 copy-start.25
  0.7 4.1 copy-start.26
  0.7 4.1 copy-start.27
  0.7 4.8 copy-start.23
  0.7 7.0 %copy-start.19 = (bf16[1,1152,3,288]{1,3,2,0:T(8,128)(2,1)S(1)}, bf16[1,1152,3,288]{1,3,2,0:T(8,128)(2,1)}, u32[]{:S(2)}) copy-start(bf16[1,1152,3,288]{1,3,2,0:T(8,128)(2,1)} %param.28) | copy-start | bytes 5971972
  7.7 3.3 copy-start.30
  7.7 3.3 copy-start.29
  200.6 34.8 %copy-start.28 = (bf16[2048]{0:T(1024)(128)(2,1)S(1)}, bf16[2048]{0:T(1024)(128)(2,1)}, u32[]{:S(2)}) copy-start(bf16[2048]{0:T(1024)(128)(2,1)} %param.39) | copy-start | bytes 12292
  258.2 48.9 %copy-start.18 = (bf16[2,48,1152]{2,1,0:T(8,128)(2,1)S(1)}, bf16[2,48,1152]{2,1,0:T(8,128)(2,1)}, u32[]{:S(2)}) copy-start(bf16[2,48,1152]{2,1,0:T(8,128)(2,1)} %get-tuple-element.150.refs_0_.refs_12_.refs_1_) | copy-start | bytes 663556
  258.2 48.9 %copy-start.20 = (bf16[2,48,1152]{2,1,0:T(8,128)(2,1)S(1)}, bf16[2,48,1152]{2,1,0:T(8,128)(2,1)}, u32[]{:S(2)}) copy-start(bf16[2,48,1152]{2,1,0:T(8,128)(2,1)} %get-tuple-element.160.refs_13_) | copy-start | bytes 663556
  309.3 47.4 %copy-start.21 = (f32[2,48,1152]{2,1,0:T(8,128)S(1)}, f32[2,48,1152]{2,1,0:T(8,128)}, u32[]{:S(2)}) copy-start(f32[2,48,1152]{2,1,0:T(8,128)} %get-tuple-element.185) | copy-start | bytes 1327108
  463.2 53.0 %copy-start.13 = (f32[144,512]{1,0:T(8,128)S(1)}, f32[144,512]{1,0:T(8,128)}, u32[]{:S(2)}) copy-start(f32[144,512]{1,0:T(8,128)} %get-tuple-element.237.refs_6_) | copy-start | bytes 884740
  463.8 52.4 %copy-start.3 = (f32[288,1152]{1,0:T(8,128)S(1)}, f32[288,1152]{1,0:T(8,128)}, u32[]{:S(2)}) copy-start(f32[288,1152]{1,0:T(8,128)} %get-tuple-element.212.refs_1_) | copy-start | bytes 3981316
  463.8 52.4 %copy-start.4 = (f32[288,1152]{1,0:T(8,128)S(1)}, f32[288,1152]{1,0:T(8,128)}, u32[]{:S(2)}) copy-start(f32[288,1152]{1,0:T(8,128)} %get-tuple-element.211.refs_0_) | copy-start | bytes 3981316
  463.8 52.4 %copy-start.5 = (f32[288,1152]{1,0:T(8,128)S(1)}, f32[288,1152]{1,0:T(8,128)}, u32[]{:S(2)}) copy-start(f32[288,1152]{1,0:T(8,128)} %get-tuple-element.234.refs_3_) | copy-start | bytes 3981316
  463.8 52.4 %copy-start.7 = (f32[288,864]{1,0:T(8,128)S(1)}, f32[288,864]{1,0:T(8,128)}, u32[]{:S(2)}) copy-start(f32[288,864]{1,0:T(8,128)} %get-tuple-element.241.refs_10_) | copy-start | bytes 2985988
  463.8 52.4 %copy-start.11 = (f32[288,288]{1,0:T(8,128)S(1)}, f32[288,288]{1,0:T(8,128)}, u32[]{:S(2)}) copy-start(f32[288,288]{1,0:T(8,128)} %get-tuple-element.243.refs_12_) | copy-start | bytes 995332
  516.2 1.6 copy-start.2
  517.8 1.3 copy-start.6
  519.1 1.2 copy-start.8
  520.4 1.2 copy-start.9
  521.5 1.0 copy-start.10
  522.6 1.0 copy-start.12
  523.6 0.9 copy-start.14
  524.5 0.8 copy-start.15
  525.3 0.7 copy-start.16
  526.0 0.7 copy-start.17
  526.7 4.5 copy-start.1

commit v7 on v6

--- a/solution.py
+++ b/solution.py
@@ -122,18 +122,24 @@
         def pass_on():
             self.block(full, self.opposite, 3, 3 - self.opposite).start()
 
+    def arrived(self, full, place):
+        self.block(full, place, 1, self.near).wait_recv()
+
     def finish_gather(self, full):
-        self.block(full, self.near, 1, self.near).wait_recv()
-        self.block(full, self.mirror, 1, self.near).wait_recv()
+        self.arrived(full, self.near)
+        self.arrived(full, self.mirror)
+        self.sent(full)
+
+    def sent(self, full):
         self.block(full, self.me, 0, self.opposite).wait_send()
         self.block(full, self.me, 1, self.near).wait_send()
 
         @pl.when(self.is_middle)
-        def sent():
+        def more_sent():
             self.block(full, self.me, 2, self.mirror).wait_send()
             self.block(full, self.opposite, 3, 3 - self.opposite).wait_send()
 
-    def scatter_sum(self, partial, buffers):
+    def scatter_sum(self, partial, buffers, prepare=lambda place: None):
         send_buf, recv_buf, relay_buf = buffers
         me, relay_sem = self.me, 4
 
@@ -159,6 +165,7 @@
             send_buf.at[2], recv_buf.at[me], self.rs_send.at[2], self.rs_recv.at[me],
             {"tensor": self.opposite},
         )
+        prepare(self.mirror)
         keep(0, term(self.mirror))
 
         @pl.when(self.is_end)
@@ -171,6 +178,7 @@
         def first_middle():
             self.to_mirror.start()
 
+        prepare(self.near)
         keep(1, term(self.near))
         self.to_near.start()
         last = term(self.opposite)
@@ -700,14 +708,10 @@
                     copy.start()
 
     def begin(self):
-        self.start((2, 3, 4))
+        self.start((3, 4))
 
     def middle(self):
-        self.relay((2,))
-        self.start((0,))
-
-    def late(self):
-        self.start((1,))
+        self.start((0, 2))
 
     def end(self):
         send, recv, own = self.held
@@ -862,6 +866,21 @@
 class Bundle:
     def __init__(self, cargos):
         self.cargos = cargos
+        self.loads, self.stores = {}, {}
+
+    def load(self):
+        for copy in self.loads.values():
+            copy.start()
+
+    def need(self, *which):
+        for i in which:
+            if i in self.loads:
+                self.loads[i].wait()
+
+    def flush(self, *which):
+        for i in which:
+            if i in self.stores:
+                self.stores[i].start()
 
     def peers(self, names=()):
         names = list(names) + [name for cargo in self.cargos for name in cargo.peers()]
@@ -882,16 +901,18 @@
             cargo.late()
 
     def end(self):
+        for copy in self.stores.values():
+            copy.wait()
         for cargo in self.cargos:
             cargo.end()
 
 
 def attend_body(
-    count, peers, u_ref, mods, segs, biases, outs, scratch, sems, need_qkv, need_out, steps
+    count, peers, u_ref, mods, segs, biases, outs, scratch, sems, need_qkv, need_out, steps, flush
 ):
     middle_ref, branch_ref, full_ref, q_ref, k_ref, v_ref, probs_ref, mixed_ref = outs
-    full, wqkv, wo, mixed_wide = scratch[:4]
-    buffers = scratch[4:7]
+    full, wqkv, wo, mixed_wide = (full_ref, *scratch[:3])
+    buffers, spreads = scratch[3:6], scratch[6]
     seg_own, seg_col, seg_row = segs
     mod_ref = mods()
     me = lax.axis_index("tensor")
@@ -909,15 +930,17 @@
     spread = spread_matrix(heads_width)
     line.relay(full)
     steps[0]()
+    both = 3 * heads_width
+    for which in range(3):
+        spreads[which] = spread_matrix(heads_width, which, both)
     need_qkv()
     line.finish_gather(full)
-    full_ref[...] = full[...]
+    flush(2)
     tokens = flat(full)
     bias = biases()
-    both = 3 * heads_width
     projected = (dot(tokens, wqkv[...]) + bias[0:1, :both]).astype(BF16)
     for which, target in enumerate((q_ref, k_ref, v_ref)):
-        parts = dot(projected, spread_matrix(heads_width, which, both))
+        parts = dot(projected, spreads[which])
         target[...] = parts.astype(BF16).reshape(target.shape)
 
     def one_head(index, carry):
@@ -935,6 +958,7 @@
     steps[1]()
     lax.fori_loop(0, rows * heads, one_head, 0)
     mixed_ref[...] = dot(flat(mixed_wide), spread, NT).astype(BF16).reshape(mixed_ref.shape)
+    flush(3, 4, 5, 6, 7)
     need_out()
 
     def partial(which_rows):
@@ -956,7 +980,7 @@
     scratch = refs[26:33]
     ada, mod_src, mod_buf, bias_buf, w_sem, ag_send, ag_recv, rs_send, rs_recv = refs[33:42]
     mod_send, mod_recv, share_send, share_recv, ada_sem = refs[42:]
-    wqkv, wo = scratch[1:3]
+    wqkv, wo = scratch[:2]
     section, tensor = lax.axis_index("section"), lax.axis_index("tensor")
     load_ada = local(ada_w, ada, ada_sem)
     shares = [
@@ -975,8 +999,6 @@
         if a or b
     ]
     greet(plane + [core_peer(), y_peer()] + cross_peers())
-    shares[0].begin()
-    cargo.begin()
     cond_act = silu(cond_ref[...].astype(F32)).astype(BF16)
     load_ada.wait()
     mod = dot(cond_act, ada[...], NT) + ada_b_ref[...].astype(F32)
@@ -994,8 +1016,9 @@
         biases_ref, bias_buf.at[section],
         mod_send.at[len(plane)], mod_recv.at[len(plane)], x_peer(),
     )
-    for share in shares[1:]:
+    for share in shares:
         share.begin()
+    cargo.begin()
 
     def mods():
         wait_all(copies)
@@ -1037,19 +1060,20 @@
         shares[2].forward(shares[2].first)
 
     def after_scatter():
-        gather = cargo.cargos[0]
-        gather.relay((0,))
+        cargo.cargos[0].start((1,))
+        cargo.cargos[0].relay((0, 2))
         shares[2].forward_again()
         shares[3].forward(shares[3].first)
-        gather.relay((1,))
         shares[2].finish()
 
     attend_body(
         count, None, u_ref, mods, (seg_own, seg_col, seg_row), biases, outs, scratch,
         (ag_send, ag_recv, rs_send, rs_recv), need_qkv, need_out,
         (after_gather, before_heads, after_scatter),
+        lambda *which: cargo.flush(*(6 + i for i in which)),
     )
     shares[3].forward_again()
+    cargo.cargos[0].relay((1,))
     cargo.end()
     shares[3].finish()
 
@@ -1058,12 +1082,12 @@
     u_ref, mods_ref, bias_ref, seg_own, seg_col, seg_row = refs[:6]
     own_qkv, other_qkv, own_out, other_out = refs[6:10]
     outs, scratch, w_sem = refs[10:18], refs[18:25], refs[25]
-    load_qkv = fetch(block, own_qkv, other_qkv, scratch[1], w_sem.at[0])
-    load_out = fetch(block, own_out, other_out, scratch[2], w_sem.at[1])
+    load_qkv = fetch(block, own_qkv, other_qkv, scratch[0], w_sem.at[0])
+    load_out = fetch(block, own_out, other_out, scratch[1], w_sem.at[1])
     attend_body(
         count, z_peers(count) + cargo.peers(), u_ref, lambda: mods_ref.at[block],
         (seg_own, seg_col, seg_row), lambda: bias_ref[block], outs, scratch, refs[26:30],
-        load_qkv.wait, load_out.wait, (cargo.begin, cargo.middle, cargo.late),
+        load_qkv.wait, load_out.wait, (cargo.begin, cargo.middle, cargo.late), cargo.flush,
     )
     cargo.end()
 
@@ -1072,8 +1096,9 @@
     count, block,
     middle_ref, mods_ref, bias_ref, seg_own, w1_own, w1_other, w2_own, w2_other,
     out_ref, branch_ref, full_ref, pre_ref, act_ref,
-    full, w1, w2, send_buf, recv_buf, relay_buf, w_sem, *sems, cargo,
+    w1, w2, send_buf, recv_buf, relay_buf, w_sem, *sems, cargo,
 ):
+    full = full_ref
     me = lax.axis_index("tensor")
     rows, length, width = middle_ref.shape
     mod_ref = mods_ref.at[block]
@@ -1088,19 +1113,29 @@
     cargo.begin()
     line.relay(full)
     load_one.wait()
-    line.finish_gather(full)
-    full_ref[...] = full[...]
-    pre = dot(flat(full), w1[...]) + bias_ref[block, 3:4, : w1.shape[1]]
-    pre_ref[...] = pre.reshape(pre_ref.shape)
-    cargo.middle()
-    act_ref[...] = gelu_tanh(pre).astype(BF16).reshape(act_ref.shape)
     load_two.wait()
+
+    def hidden(place):
+        which_rows = own_rows(place, length)
+        pre = dot(full[:, which_rows, :].reshape(rows * length, width), w1[...])
+        pre = pre + bias_ref[block, 3:4, : w1.shape[1]]
+        pre_ref[:, which_rows, :] = pre.reshape(rows, length, -1)
+        act_ref[:, which_rows, :] = gelu_tanh(pre).astype(BF16).reshape(rows, length, -1)
+
+    def prepare(place):
+        line.arrived(full, place)
+        hidden(place)
 
     def partial(which_rows):
         return dot(act_ref[:, which_rows, :].reshape(rows * length, -1), w2[...])
 
+    hidden(me)
+    hidden(line.opposite)
     buffers = (send_buf, recv_buf, relay_buf)
-    total = line.scatter_sum(partial, buffers)
+    total = line.scatter_sum(partial, buffers, prepare)
+    cargo.flush(2, 3, 4)
+    line.sent(full)
+    cargo.middle()
     branch = line.finish_sum(total, buffers) + bias_ref[block, 4:5, :]
     cargo.end()
     branch_ref[...] = branch.reshape(branch_ref.shape)
@@ -1114,7 +1149,7 @@
     d_middle_ref, d_mod_ref, d_w1_ref, d_w2_ref, d_b1_ref, d_b2_ref = refs[12:18]
     full, d_pre, w1, w2, *buffers, w_sem = refs[18:26]
     sems = refs[26:30]
-    w1_whole, w1_got, w1_sems, w2_whole, w2_got, w2_sems = refs[30:]
+    w1_whole, w1_got, w1_sems, w2_whole, w2_got, w2_sems, normed_buf = refs[30:]
     w1_sum = CoreSum(w1_whole, w1_got, d_w1_ref, w1_sems)
     w2_sum = CoreSum(w2_whole, w2_got, d_w2_ref, w2_sems)
     me = lax.axis_index("tensor")
@@ -1122,6 +1157,7 @@
     mod_ref = mods_ref.at[block]
     load_one = fetch(block, w1_own, w1_other, w1, w_sem.at[0])
     load_two = fetch(block, w2_own, w2_other, w2, w_sem.at[1])
+    cargo.load()
     g = flat(g_ref).astype(F32)
     d_branch = (g * token_mod(mod_ref, seg_own, 5)).astype(BF16)
     full[:, own_rows(me, length), :] = d_branch.reshape(rows, length, width)
@@ -1132,16 +1168,31 @@
     slot_sums(g * flat(branch_ref), seg_own, d_mod_ref, 2)
     line.relay(full)
     cargo.middle()
+    normed, inverse = layer_norm(flat(middle_ref))
+    normed_buf[...] = normed
     load_two.wait()
-    line.finish_gather(full)
-    d_act = dot(flat(full), w2[...], NT)
-    d_pre[...] = (d_act * gelu_slope(flat(pre_ref))).astype(BF16).reshape(d_pre.shape)
+    cargo.need(6)
+
+    def d_hidden(place):
+        which_rows = own_rows(place, length)
+        d_act = dot(full[:, which_rows, :].reshape(rows * length, width), w2[...], NT)
+        slope = gelu_slope(pre_ref[:, which_rows, :].reshape(rows * length, -1))
+        d_pre[:, which_rows, :] = (d_act * slope).astype(BF16).reshape(rows, length, -1)
+
+    def prepare(place):
+        line.arrived(full, place)
+        d_hidden(place)
+
+    d_hidden(me)
+    d_hidden(line.opposite)
     load_one.wait()
 
     def partial(which_rows):
         return dot(d_pre[:, which_rows, :].reshape(rows * length, -1), w1[...], NT)
 
-    total = line.scatter_sum(partial, buffers)
+    total = line.scatter_sum(partial, buffers, prepare)
+    line.sent(full)
+    cargo.need(5, 7)
     w2_whole[...] = dot(flat(full), flat(act_ref), TN).astype(BF16)
     w2_sum.begin()
     w1_whole[...] = dot(flat(full_ref), flat(d_pre), TN).astype(BF16)
@@ -1149,7 +1200,7 @@
     d_b2_ref[...] = jnp.sum(flat(full).astype(F32), axis=0, keepdims=True)
     d_b1_ref[...] = jnp.sum(flat(d_pre).astype(F32), axis=0, keepdims=True)
     d_in = line.finish_sum(total, buffers)
-    normed, inverse = layer_norm(flat(middle_ref))
+    normed = normed_buf[...]
     d_middle = flat(g_ref).astype(F32) + norm_back(
         d_in * (1.0 + token_mod(mod_ref, seg_own, 4)), normed, inverse
     )
@@ -1168,7 +1219,7 @@
     d_in_ref, d_mod_ref, d_wqkv_ref, d_wo_ref, d_bqv_ref, d_bo_ref = refs[15:21]
     full, wide, narrow, wqkv, wo, *buffers, w_sem = refs[21:30]
     sems = refs[30:34]
-    qkv_whole, qkv_got, qkv_sems, wo_whole, wo_got, wo_sems = refs[34:]
+    qkv_whole, qkv_got, qkv_sems, wo_whole, wo_got, wo_sems, spreads, normed_buf = refs[34:]
     qkv_sum = CoreSum(qkv_whole, qkv_got, d_wqkv_ref, qkv_sems)
     wo_sum = CoreSum(wo_whole, wo_got, d_wo_ref, wo_sems)
     me = lax.axis_index("tensor")
@@ -1178,6 +1229,7 @@
     mod_ref = mods_ref.at[block]
     load_qkv = fetch(block, wqkv_own, wqkv_other, wqkv, w_sem.at[0])
     load_out = fetch(block, wo_own, wo_other, wo, w_sem.at[1])
+    cargo.load()
     d_middle = flat(d_middle_ref)
     d_branch = (d_middle * token_mod(mod_ref, seg_own, 2)).astype(BF16)
     full[:, own_rows(me, length), :] = d_branch.reshape(rows, length, width)
@@ -1186,13 +1238,19 @@
     line.start_gather(full)
     cargo.begin()
     slot_sums(d_middle * flat(branch_ref), seg_own, d_mod_ref, 2)
-    spread = spread_matrix(heads_width)
     line.relay(full)
     cargo.middle()
+    spread = spread_matrix(heads_width)
+    both = 3 * heads_width
+    for which in range(3):
+        spreads[which] = spread_matrix(heads_width, which, both)
+    normed, inverse = layer_norm(flat(u_ref).astype(F32))
+    normed_buf[...] = normed
     load_out.wait()
     line.finish_gather(full)
     d_mixed = dot(flat(full), wo[...], NT).astype(BF16)
     wide[3] = dot(d_mixed, spread).astype(BF16).reshape(wide.shape[1:])
+    cargo.need(6, 7, 8, 9)
 
     def one_head(index, carry):
         row = index // heads
@@ -1211,12 +1269,9 @@
         return carry
 
     lax.fori_loop(0, rows * heads, one_head, 0)
-    both = 3 * heads_width
     gathered = 0.0
     for which in range(3):
-        gathered = gathered + dot(
-            flat(wide.at[which]), spread_matrix(heads_width, which, both), NT
-        )
+        gathered = gathered + dot(flat(wide.at[which]), spreads[which], NT)
     narrow[...] = gathered.astype(BF16).reshape(narrow.shape)
     load_qkv.wait()
 
@@ -1226,12 +1281,13 @@
     total = line.scatter_sum(partial, buffers)
     d_bo_ref[...] = jnp.sum(flat(full).astype(F32), axis=0, keepdims=True)
     d_bqv_ref[...] = jnp.sum(flat(narrow).astype(F32), axis=0, keepdims=True)
+    cargo.need(5, 10)
     wo_whole[...] = dot(flat(full), flat(mixed_ref), TN).astype(BF16)
     wo_sum.begin()
     qkv_whole[...] = dot(flat(full_ref), flat(narrow), TN).astype(BF16)
     qkv_sum.begin()
     d_attn_in = line.finish_sum(total, buffers)
-    normed, inverse = layer_norm(flat(u_ref).astype(F32))
+    normed = normed_buf[...]
     d_in = flat(d_middle_ref) + norm_back(
         d_attn_in * (1.0 + token_mod(mod_ref, seg_own, 1)), normed, inverse
     )
@@ -1394,9 +1450,10 @@
         if a or b
     ]
     greet(z_peers(count) + others + cross_peers())
-    for one in cargo.cargos:
-        if isinstance(one, YSum):
-            one.begin()
+    last_sums = [one for one in cargo.cargos if isinstance(one, LastSum)]
+    y_sums = [one for one in cargo.cargos if type(one) is YSum]
+    for one in last_sums:
+        one.begin()
     piece = z_src.shape[-1]
     for block in range(sections):
         attend_mod, mlp_mod = mod_refs[2 * block : 2 * block + 2]
@@ -1481,9 +1538,10 @@
             )
         )
         at = at + 2
-    for one in cargo.cargos:
-        if isinstance(one, LastSum):
-            one.middle()
+    for one in last_sums:
+        one.middle()
+    for one in y_sums:
+        one.begin()
     place_copy.wait()
     rows = place_buf.shape[0]
 
@@ -1520,11 +1578,20 @@
 PROJECTOR_AXES = (0, 0, 1)
 
 
-def call(kernel, number, inputs, in_any, outs, out_any, scratch, flops, cargos=()):
+def call(
+    kernel, number, inputs, in_any, outs, out_any, scratch, flops, cargos=(), lazy=(), streamed=()
+):
     own_in, own_out, own_scratch = len(inputs), len(outs), len(scratch)
     specs = [VMEM] * (own_in - in_any) + [ANY] * in_any
-    out_specs = [ANY if i in out_any else VMEM for i in range(own_out)]
+    specs = [ANY if i in lazy else spec for i, spec in enumerate(specs)]
+    out_specs = [ANY if i in out_any or i in streamed else VMEM for i in range(own_out)]
     inputs, outs, scratch, aliases = list(inputs), list(outs), list(scratch), {}
+    moved_refs = len(lazy) + len(streamed)
+    scratch += [pltpu.VMEM(inputs[i].shape, inputs[i].dtype) for i in lazy]
+    scratch += [pltpu.VMEM(*outs[i]) for i in streamed]
+    if moved_refs:
+        scratch.append(pltpu.SemaphoreType.DMA((moved_refs,)))
+        moved_refs += 1
     for cargo in cargos:
         for source, target in cargo.aliases.items():
             aliases[len(inputs) + source] = len(outs) + target
@@ -1539,14 +1606,22 @@
         parts.append(list(refs[len(inputs) : len(inputs) + len(outs)]))
         parts.append(list(refs[len(inputs) + len(outs) :]))
         base = parts[0][:own_in] + parts[1][:own_out] + parts[2][:own_scratch]
-        at = [own_in, own_out, own_scratch]
+        held = parts[2][own_scratch : own_scratch + moved_refs]
+        bundle = Bundle(cargos)
+        for k, i in enumerate(lazy):
+            bundle.loads[i] = pltpu.make_async_copy(base[i], held[k], held[-1].at[k])
+            base[i] = held[k]
+        for k, i in enumerate(streamed, len(lazy)):
+            bundle.stores[i] = pltpu.make_async_copy(held[k], base[own_in + i], held[-1].at[k])
+            base[own_in + i] = held[k]
+        at = [own_in, own_out, own_scratch + moved_refs]
         for cargo in cargos:
             held = []
             for i, items in enumerate((cargo.inputs, cargo.outs, cargo.scratch)):
                 held.append(parts[i][at[i] : at[i] + len(items)])
                 at[i] += len(items)
             cargo.bind(*held)
-        kernel(*base, cargo=Bundle(cargos))
+        kernel(*base, cargo=bundle)
 
     moved = sum(math.prod(one.shape) * one.dtype.itemsize for one in inputs)
     results = pl.pallas_call(
@@ -1602,11 +1677,12 @@
             ((self.rows, self.positions, self.heads_width), BF16),
         ]
         self.attend_scratch = [
-            pltpu.VMEM(self.full, BF16),
             pltpu.VMEM(own["qkv"].shape, BF16),
             pltpu.VMEM(own["out"].shape, BF16),
             pltpu.VMEM(self.wide, BF16),
         ] + exchange_scratch(count, *self.local)
+        self.spreads = pltpu.VMEM((3, 3 * self.heads_width, self.heads * HEAD_LANES), BF16)
+        self.attend_scratch.append(self.spreads)
         self.mods = (3, MOD_ROWS, self.width)
 
 
@@ -1648,6 +1724,7 @@
         ],
         2 * sizes.tokens * width * sizes.heads_width * 4,
         cargos,
+        streamed=tuple(range(8, 14)),
     )
     other = dict(zip(("qkv", "out", "one", "two"), results[2:6]))
     return results[0], results[1], other, results[6:], carried
@@ -1665,6 +1742,7 @@
         sizes.attend_scratch + semaphores(sizes.count),
         2 * sizes.tokens * sizes.width * sizes.heads_width * 4,
         cargos,
+        streamed=tuple(range(2, 8)),
     )
 
 
@@ -1682,7 +1760,6 @@
         ],
         (),
         [
-            pltpu.VMEM(sizes.full, BF16),
             pltpu.VMEM(own["one"].shape, BF16),
             pltpu.VMEM(own["two"].shape, BF16),
         ]
@@ -1690,6 +1767,7 @@
         + semaphores(sizes.count),
         2 * sizes.tokens * sizes.width * sizes.hidden * 2,
         cargos,
+        streamed=(2, 3, 4),
     )
 
 
@@ -1717,9 +1795,13 @@
         ]
         + exchange_scratch(sizes.count, *sizes.local)
         + semaphores(sizes.count)
-        + core_sum_scratch((sizes.width, sizes.hidden)) * 2,
+        + core_sum_scratch((sizes.width, sizes.hidden)) * 2
+        + [
+            pltpu.VMEM((sizes.rows * sizes.length, sizes.width), F32),
+        ],
         2 * sizes.tokens * sizes.width * sizes.hidden * 4,
         cargos,
+        lazy=(5, 6, 7),
     )
 
 
@@ -1749,9 +1831,14 @@
         + exchange_scratch(sizes.count, *sizes.local)
         + semaphores(sizes.count)
         + core_sum_scratch((sizes.width, 3 * sizes.heads_width))
-        + core_sum_scratch((sizes.width, sizes.heads_width)),
+        + core_sum_scratch((sizes.width, sizes.heads_width))
+        + [
+            sizes.spreads,
+            pltpu.VMEM((sizes.rows * sizes.length, sizes.width), F32),
+        ],
         2 * sizes.tokens * sizes.width * sizes.heads_width * 8,
         cargos,
+        lazy=(5, 6, 7, 8, 9, 10),
     )
 
 
@@ -1885,9 +1972,9 @@
         functools.partial(assemble_kernel, heads_width),
         out_shape=[jax.ShapeDtypeStruct(shape, F32) for shape in shapes],
         in_specs=[ANY] * 9 + [VMEM] * 7,
-        out_specs=[ANY] * 7 + [VMEM] * 11,
+        out_specs=[VMEM] * 18,
         scratch_shapes=[pltpu.SemaphoreType.DMA((7,))],
-        compiler_params=pltpu.CompilerParams(vmem_limit_bytes=40 * 2**20),
+        compiler_params=pltpu.CompilerParams(vmem_limit_bytes=62 * 2**20),
         cost_estimate=pl.CostEstimate(flops=1000, bytes_accessed=2**24, transcendentals=0),
     )(*inputs)
 

time: 541 us -> 506 us (0.935)
  Pallas kernels: 503 us -> 479 us
  local copies, waits for them, and re-layouts: 23 us -> 12.6 us
    pallas_call x10, Pallas kernels: 499 us -> 471 us  [call(): pl.pallas_call(body, out_shape=[jax.ShapeDtypeStruct(shape, dtype) for sh...]
    unnamed x67 -> x35, local copies, waits for them, and re-layouts: 12.9 us -> 2.46 us
where the time goes in v7:
time: 506 us; the launch traced here: 498 us
  Pallas kernels  479 us (95%)
  local copies, waits for them, and re-layouts  12.6 us (2%)
    pallas_call x10, Pallas kernels, call(): pl.pallas_call(body, out_shape=[jax.ShapeDtypeStruct(shape, dtype) for sh...  471 us

profile of v7, /device:TPU:0, one launch (start us, length us, event | category | flops | bytes accessed | tf_op | source)
XLA Modules:
  0.0 498.4 jit_solution(11415699638933998365)
XLA Ops:
  0.7 0.0 copy-start
  0.7 0.0 copy-start.6
  0.7 0.0 copy-start.8
  0.7 0.0 copy-start.9
  0.7 0.0 copy-start.10
  0.7 0.0 copy-start.11
  0.8 1.8 constant_dynamic-slice_fusion
  2.5 0.7 copy.112
  3.2 0.7 copy.113
  3.9 0.0 copy-done.6
  4.0 0.6 pad_bitcast_fusion.refs_1_
  4.6 0.1 pad.34.clone
  4.7 0.0 copy-done.8
  4.7 0.1 fusion.4
  4.8 0.0 copy-done.9
  4.8 0.0 copy-done.10
  4.8 0.0 copy-done.11
  4.9 0.7 concatenate.30.refs_3_
  5.5 0.1 dynamic-slice_bitcast_fusion
  5.6 0.7 copy.87.refs_4_.refs_3_
  6.3 0.8 copy.88.refs_5_.refs_4_
  7.2 0.6 broadcast_in_dim.65.refs_6_.refs_5_
  7.8 2.4 copy.89.refs_8_.refs_6_.refs_11_
  10.1 0.2 constant_dynamic-slice_fusion.1
  10.4 0.7 copy.114
  11.1 0.1 pad.32.clone
  11.2 0.7 maximum_maximum_fusion.refs_16_
  11.9 90.5 %shard_map.348 = (f32[2,6,8,1152]{3,2,1,0:T(8,128)}, f32[2,8,1152]{2,1,0:T(8,128)}, bf16[1152,864]{1,0:T(8,128)(2,1)}, bf16[288,1152]{1,0:T(8,128)(2,1)}, bf16[1...) custom-call(bf16[2,48,1152]{2,1,0:T(8,128)(2,1)} %bitcast.69, ...), custom_call_target="tpu_custom_call" | custom-call | flops 1019215872 | bytes 16472832 | tf_op jit(solution)/shard_map/pallas_call | solution.py:1627
  102.4 43.9 %shard_map.349 = (bf16[2,48,1152]{2,1,0:T(8,128)(2,1)}, f32[2,48,1152]{2,1,0:T(8,128)}, bf16[2,192,1152]{2,1,0:T(8,128)(2,1)}, f32[2,192,1152]{2,1,0:T(8,128)}, ...) custom-call(f32[2,48,1152]{2,1,0:T(8,128)} %get-tuple-element.142.re, ...), custom_call_target="tpu_custom_call", output_to_operand_aliasing={{5}: (8, {}), {6}: (9, {}), {7}: (10, {})} | custom-call | flops 2038431744 | bytes 19702144 | tf_op jit(solution)/shard_map/pallas_call | solution.py:1627
  146.2 36.5 %shard_map.350 = (f32[2,48,1152]{2,1,0:T(8,128)}, f32[2,48,1152]{2,1,0:T(8,128)}, bf16[2,192,1152]{2,1,0:T(8,128)(2,1)}, bf16[2,192,512]{2,1,0:T(8,128)(2,1)}, b...) custom-call(bf16[2,48,1152]{2,1,0:T(8,128)(2,1)} %get-tuple-element., ...), custom_call_target="tpu_custom_call", output_to_operand_aliasing={{8}: (10, {}), {9}: (11, {}), {10}: (12, {})} | custom-call | flops 1019215872 | bytes 14175616 | tf_op jit(solution)/shard_map/pallas_call | solution.py:1627
  182.8 0.0 copy-start.12
  182.8 32.5 %shard_map.351 = (bf16[2,48,1152]{2,1,0:T(8,128)(2,1)}, f32[2,48,1152]{2,1,0:T(8,128)}, bf16[2,192,1152]{2,1,0:T(8,128)(2,1)}, f32[2,192,1152]{2,1,0:T(8,128)}, ...) custom-call(f32[2,48,1152]{2,1,0:T(8,128)} %get-tuple-element.156.re, ...), custom_call_target="tpu_custom_call", output_to_operand_aliasing={{5}: (8, {}), {6}: (9, {}), {7}: (10, {})} | custom-call | flops 2038431744 | bytes 19702144 | tf_op jit(solution)/shard_map/pallas_call | solution.py:1627
  215.3 0.6 broadcast_in_dim.71.refs_3_
  215.9 22.2 %shard_map.352 = (f32[2,48,1152]{2,1,0:T(8,128)}, bf16[2,1152,512]{2,1,0:T(8,128)(2,1)}, bf16[2,512,2048]{2,1,0:T(8,128)(2,1)}, bf16[2,192,2048]{2,1,0:T(8,128)(2,1)}, f32[4,8,512]{2,1,0:T(8,128)}) custom-call(bf16[2,48,1152]{2,1,0:T(8,128)(2,1)} %get-tuple-element.150.refs_0_.refs_12_.refs_1_, bf16[2,2,2,48,192]{4,3,2,1,0:T(8,128)(2,1)} %get-tuple-element.165.refs_1_, ...), custom_call_target="tpu_custom_call" | custom-call | flops 4680843264 | bytes 8564736 | tf_op jit(solution)/shard_map/pallas_call | solution.py:1627
  238.1 44.6 %shard_map.353 = (f32[2,48,1152]{2,1,0:T(8,128)}, f32[3,8,1152]{2,1,0:T(8,128)}, bf16[2,288,1152]{2,1,0:T(8,128)(2,1)}, bf16[2,288,1152]{2,1,0:T(8,128)(2,1)}, f...) custom-call(bf16[2,48,1152]{2,1,0:T(8,128)(2,1)} %bitcast.72, ...), custom_call_target="tpu_custom_call" | custom-call | flops 4076863488 | bytes 18506112 | tf_op jit(solution)/shard_map/pallas_call | solution.py:1627
  282.7 0.0 copy-done.2
  282.7 0.0 copy-done.4
  282.7 1.1 fusion
  283.9 0.9 copy.104
  284.8 47.0 %shard_map.354 = (f32[2,48,1152]{2,1,0:T(8,128)}, f32[3,8,1152]{2,1,0:T(8,128)}, bf16[2,288,864]{2,1,0:T(8,128)(2,1)}, bf16[2,288,288]{2,1,0:T(8,128)(2,1)}, f32...) custom-call(f32[2,48,1152]{2,1,0:T(8,128)} %get-tuple-element.172.re, ...), custom_call_target="tpu_custom_call" | custom-call | flops 2038431744 | bytes 18743680 | tf_op jit(solution)/shard_map/pallas_call | solution.py:1627
  331.9 1.8 add.31.refs_0_
  333.7 47.3 %shard_map.355 = (f32[2,48,1152]{2,1,0:T(8,128)}, f32[3,8,1152]{2,1,0:T(8,128)}, bf16[2,288,1152]{2,1,0:T(8,128)(2,1)}, bf16[2,288,1152]{2,1,0:T(8,128)(2,1)}, f...) custom-call(f32[2,48,1152]{2,1,0:T(8,128)} %add.31.refs_0_, ...), custom_call_target="tpu_custom_call" | custom-call | flops 4076863488 | bytes 24338816 | tf_op jit(solution)/shard_map/pallas_call | solution.py:1627
  381.0 54.1 %shard_map.356 = (f32[2,48,1152]{2,1,0:T(8,128)}, f32[3,8,1152]{2,1,0:T(8,128)}, bf16[2,288,864]{2,1,0:T(8,128)(2,1)}, bf16[2,288,288]{2,1,0:T(8,128)(2,1)}, f32...) custom-call(f32[2,48,1152]{2,1,0:T(8,128)} %get-tuple-element.195.re, ...), custom_call_target="tpu_custom_call" | custom-call | flops 2038431744 | bytes 16728448 | tf_op jit(solution)/shard_map/pallas_call | solution.py:1627
  435.2 0.1 reshape.108
  435.3 0.6 copy.115
  435.9 52.3 %shard_map.357 = (f32[4,48,1152]{2,1,0:T(8,128)}, f32[288,1728]{1,0:T(8,128)}, f32[1,1728]{1,0:T(1,128)}, f32[8,1152]{1,0:T(8,128)}, f32[8,512]{1,0:T(8,128)}, /...) custom-call(f32[2,48,1152]{2,1,0:T(8,128)} %get-tuple-element.213.re, ...), custom_call_target="tpu_custom_call" | custom-call | flops 63700992 | bytes 5560064 | tf_op jit(solution)/shard_map/pallas_call | solution.py:1627
  488.2 0.0 copy-start.1
  488.2 8.2 %shard_map.358 = (f32[288,1152]{1,0:T(8,128)}, f32[288,1152]{1,0:T(8,128)}, f32[288,1728]{1,0:T(8,128)}, f32[1,1728]{1,0:T(1,128)}, f32[144,512]{1,0:T(8,128)}, ...) custom-call(f32[288,1152]{1,0:T(8,128)} %get-tuple-element.211.refs_, ...), custom_call_target="tpu_custom_call" | custom-call | flops 1000 | bytes 16777216 | tf_op jit(solution)/shard_map/pallas_call | solution.py:1971
  (32 shorter events, 0.2 us)
Async XLA Ops:
  0.7 9.5 %copy-start = (bf16[192,4,192]{2,1,0:T(4,128)(2,1)S(1)}, bf16[192,4,192]{2,1,0:T(4,128)(2,1)}, u32[]{:S(2)}) copy-start(bf16[192,4,192]{2,1,0:T(4,128)(2,1)} %param.24) | copy-start | bytes 884740
  0.7 3.3 copy-start.6
  0.7 4.0 copy-start.8
  0.7 4.1 copy-start.9
  0.7 4.1 copy-start.10
  0.7 4.1 copy-start.11
  0.7 4.8 copy-start.7
  0.7 7.0 %copy-start.3 = (bf16[1,1152,3,288]{1,3,2,0:T(8,128)(2,1)S(1)}, bf16[1,1152,3,288]{1,3,2,0:T(8,128)(2,1)}, u32[]{:S(2)}) copy-start(bf16[1,1152,3,288]{1,3,2,0:T(8,128)(2,1)} %param.28) | copy-start | bytes 5971972
  7.7 3.3 copy-start.14
  7.8 3.3 copy-start.13
  182.8 32.5 %copy-start.12 = (bf16[2048]{0:T(1024)(128)(2,1)S(1)}, bf16[2048]{0:T(1024)(128)(2,1)}, u32[]{:S(2)}) copy-start(bf16[2048]{0:T(1024)(128)(2,1)} %param.39) | copy-start | bytes 12292
  238.1 44.6 %copy-start.2 = (bf16[2,48,1152]{2,1,0:T(8,128)(2,1)S(1)}, bf16[2,48,1152]{2,1,0:T(8,128)(2,1)}, u32[]{:S(2)}) copy-start(bf16[2,48,1152]{2,1,0:T(8,128)(2,1)} %get-tuple-element.150.refs_0_.refs_12_.refs_1_) | copy-start | bytes 663556
  238.1 44.6 %copy-start.4 = (bf16[2,48,1152]{2,1,0:T(8,128)(2,1)S(1)}, bf16[2,48,1152]{2,1,0:T(8,128)(2,1)}, u32[]{:S(2)}) copy-start(bf16[2,48,1152]{2,1,0:T(8,128)(2,1)} %get-tuple-element.160.refs_13_) | copy-start | bytes 663556
  284.8 47.1 %copy-start.5 = (f32[2,48,1152]{2,1,0:T(8,128)S(1)}, f32[2,48,1152]{2,1,0:T(8,128)}, u32[]{:S(2)}) copy-start(f32[2,48,1152]{2,1,0:T(8,128)} %get-tuple-element.185) | copy-start | bytes 1327108
  488.2 8.8 %copy-start.1 = (bf16[192,4,192]{2,1,0:T(4,128)(2,1)S(1)}, bf16[192,4,192]{2,1,0:T(4,128)(2,1)}, u32[]{:S(2)}) copy-start(bf16[192,4,192]{2,1,0:T(4,128)(2,1)} %param.24) | copy-start | bytes 884740

commit v8 on v7

--- a/solution.py
+++ b/solution.py
@@ -956,7 +956,7 @@
         return carry
 
     steps[1]()
-    lax.fori_loop(0, rows * heads, one_head, 0)
+    lax.fori_loop(0, rows * heads, one_head, 0, unroll=4)
     mixed_ref[...] = dot(flat(mixed_wide), spread, NT).astype(BF16).reshape(mixed_ref.shape)
     flush(3, 4, 5, 6, 7)
     need_out()
@@ -1143,13 +1143,15 @@
     out_ref[...] = out.astype(BF16).reshape(out_ref.shape)
 
 
-def mlp_back_kernel(count, block, *refs, cargo):
-    g_ref, middle_ref, branch_ref, mods_ref, seg_own, full_ref, pre_ref, act_ref = refs[:8]
-    w1_own, w1_other, w2_own, w2_other = refs[8:12]
-    d_middle_ref, d_mod_ref, d_w1_ref, d_w2_ref, d_b1_ref, d_b2_ref = refs[12:18]
-    full, d_pre, w1, w2, *buffers, w_sem = refs[18:26]
-    sems = refs[26:30]
-    w1_whole, w1_got, w1_sems, w2_whole, w2_got, w2_sems, normed_buf = refs[30:]
+def mlp_back_kernel(count, block, given, *refs, cargo):
+    g_refs, refs = refs[:given], refs[given:]
+    g_ref = g_refs[0]
+    middle_ref, branch_ref, mods_ref, seg_own, full_ref, pre_ref, act_ref = refs[:7]
+    w1_own, w1_other, w2_own, w2_other = refs[7:11]
+    d_middle_ref, d_mod_ref, d_w1_ref, d_w2_ref, d_b1_ref, d_b2_ref = refs[11:17]
+    full, d_pre, w1, w2, *buffers, w_sem = refs[17:25]
+    sems = refs[25:29]
+    w1_whole, w1_got, w1_sems, w2_whole, w2_got, w2_sems, normed_buf, g_buf = refs[29:]
     w1_sum = CoreSum(w1_whole, w1_got, d_w1_ref, w1_sems)
     w2_sum = CoreSum(w2_whole, w2_got, d_w2_ref, w2_sems)
     me = lax.axis_index("tensor")
@@ -1159,6 +1161,9 @@
     load_two = fetch(block, w2_own, w2_other, w2, w_sem.at[1])
     cargo.load()
     g = flat(g_ref).astype(F32)
+    if len(g_refs) > 1:
+        g = g + flat(g_refs[1])
+    g_buf[...] = g
     d_branch = (g * token_mod(mod_ref, seg_own, 5)).astype(BF16)
     full[:, own_rows(me, length), :] = d_branch.reshape(rows, length, width)
     greet(z_peers(count) + cargo.peers(["core"]))
@@ -1171,7 +1176,7 @@
     normed, inverse = layer_norm(flat(middle_ref))
     normed_buf[...] = normed
     load_two.wait()
-    cargo.need(6)
+    cargo.need(given + 5)
 
     def d_hidden(place):
         which_rows = own_rows(place, length)
@@ -1192,7 +1197,7 @@
 
     total = line.scatter_sum(partial, buffers, prepare)
     line.sent(full)
-    cargo.need(5, 7)
+    cargo.need(given + 4, given + 6)
     w2_whole[...] = dot(flat(full), flat(act_ref), TN).astype(BF16)
     w2_sum.begin()
     w1_whole[...] = dot(flat(full_ref), flat(d_pre), TN).astype(BF16)
@@ -1201,7 +1206,7 @@
     d_b1_ref[...] = jnp.sum(flat(d_pre).astype(F32), axis=0, keepdims=True)
     d_in = line.finish_sum(total, buffers)
     normed = normed_buf[...]
-    d_middle = flat(g_ref).astype(F32) + norm_back(
+    d_middle = g_buf[...] + norm_back(
         d_in * (1.0 + token_mod(mod_ref, seg_own, 4)), normed, inverse
     )
     d_middle_ref[...] = d_middle.reshape(d_middle_ref.shape)
@@ -1268,7 +1273,7 @@
         wide[2, row, :, lanes] = dot(probs.astype(BF16), grad, TN).astype(BF16)
         return carry
 
-    lax.fori_loop(0, rows * heads, one_head, 0)
+    lax.fori_loop(0, rows * heads, one_head, 0, unroll=8)
     gathered = 0.0
     for which in range(3):
         gathered = gathered + dot(flat(wide.at[which]), spreads[which], NT)
@@ -1771,12 +1776,13 @@
     )
 
 
-def mlp_backward(sizes, block, g, attend, mlp, mods, segs, own, other, cargos):
+def mlp_backward(sizes, block, grads, attend, mlp, mods, segs, own, other, cargos):
     out, branch, full, pre, act = mlp
-    inputs = [g, attend[0], branch, mods, segs[0], full, pre, act]
+    inputs = [*grads, attend[0], branch, mods, segs[0], full, pre, act]
+    given = len(grads)
     inputs += pairs(own, other, ("one", "two"))
     return call(
-        functools.partial(mlp_back_kernel, sizes.count, block),
+        functools.partial(mlp_back_kernel, sizes.count, block, given),
         4 + block,
         inputs,
         4,
@@ -1798,10 +1804,11 @@
         + core_sum_scratch((sizes.width, sizes.hidden)) * 2
         + [
             pltpu.VMEM((sizes.rows * sizes.length, sizes.width), F32),
+            pltpu.VMEM((sizes.rows * sizes.length, sizes.width), F32),
         ],
         2 * sizes.tokens * sizes.width * sizes.hidden * 4,
         cargos,
-        lazy=(5, 6, 7),
+        lazy=(given + 4, given + 5, given + 6),
     )
 
 
@@ -2120,33 +2127,39 @@
 
     back = (mods, segs, own, other)
     (d_middle_two, mod_mlp_two, *mlp_grads_two), carried = mlp_backward(
-        sizes, 1, to_rows(cot), attend_two, mlp_two, *back,
-        [Swap(first_out, second_out), HalfSum(grad_p1, 0, "x")],
-    )
-    (other_out,), (grad_p1,) = carried
+        sizes, 1, [to_rows(cot)], attend_two, mlp_two, *back,
+        [
+            Swap(first_out, second_out), HalfSum(grad_p1, 0, "x"),
+            HalfSum(grad_p3, 1, "x", (0, 1)),
+        ],
+    )
+    (other_out,), (grad_p1,), (grad_p3_a,) = carried
     (second_grad, mod_attend_two, *attend_grads_two), carried = attend_backward(
         sizes, 1, d_middle_two, first_out, attend_two, *back,
         [YSum(grad, BF16) for grad in mlp_grads_two[:2]]
-        + [HalfSum(grad_p2, 1, "x", (0, 1)), HalfSum(grad_p3, 1, "x")],
-    )
-    ((mlp_part_a,), (mlp_part_b,)), ((grad_p2_a,), (grad_p3,)) = carried[:2], carried[2:]
+        + [HalfSum(grad_p2, 1, "x", (0, 1)), HalfSum(grad_p3, 1, "x", (1, 1))]
+        + [HalfSum(grad_p1, 0, "y", (0, 1))],
+    )
+    (mlp_part_a,), (mlp_part_b,), (grad_p2_a,), (grad_p3_b,), (grad_p1_a,) = carried
     (d_middle_one, mod_mlp_one, *mlp_grads_one), carried = mlp_backward(
-        sizes, 0, second_grad + grad_sent, attend_one, mlp_one, *back,
+        sizes, 0, [second_grad, grad_sent], attend_one, mlp_one, *back,
         [YSum(grad, BF16) for grad in attend_grads_two[:2]]
         + [SectionSum(mlp_part_a, 1), HalfSum(grad_p2, 1, "x", (1, 1))]
-        + [HalfSum(grad_p1, 0, "y"), HalfSum(grad_p2_a, 1, "y")],
+        + [HalfSum(grad_p1, 0, "y", (1, 1)), HalfSum(grad_p2_a, 1, "y")],
     )
     attend_parts_two, sum_mlp_a = carried[:2], carried[2]
-    (grad_p2_b,), (grad_p1,), (grad_p2_a,) = carried[3:]
+    (grad_p2_b,), (grad_p1_b,), (grad_p2_a,) = carried[3:]
     (first_grad, mod_attend_one, *attend_grads_one), carried = attend_backward(
         sizes, 0, d_middle_one, u, attend_one, *back,
         [LastSum(mlp_grads_one[0], 0), SectionSum(mlp_grads_one[1], 0, BF16)]
         + [SectionSum(part, 1) for part, in attend_parts_two]
-        + [SectionSum(mlp_part_b, 1), HalfSum(grad_p2_b, 1, "y"), HalfSum(grad_p3, 1, "y")]
-        + [ColumnSum((grad_p1,), 0)],
+        + [SectionSum(mlp_part_b, 1), HalfSum(grad_p2_b, 1, "y")]
+        + [HalfSum(grad_p3_a, 1, "y"), HalfSum(grad_p3_b, 1, "y")]
+        + [ColumnSum((grad_p1_a, grad_p1_b), 0)],
     )
     sum_mlp_c, (mlp_part_two,), sums_attend_two = carried[0], carried[1], carried[2:4]
-    sums_mlp_two, ((grad_p2_b,), (grad_p3,), (red_p1_w,)) = (sum_mlp_a, carried[4]), carried[5:]
+    sums_mlp_two = (sum_mlp_a, carried[4])
+    (grad_p2_b,), (grad_p3_a,), (grad_p3_b,), (red_p1_w,) = carried[5:]
 
     cond_act = silu(my_rows(cond, 0).astype(F32)).astype(BF16).astype(F32)
     share = width // replicas
@@ -2162,7 +2175,7 @@
         small, proj_small, cond_cols, sections, replicas,
         [LastSum(grad, 0) for grad in attend_grads_one[:2]]
         + [YSum(mlp_part_two, F32)]
-        + [ColumnSum((grad_p2_a, grad_p2_b), 1), ColumnSum((grad_p3,), 1)],
+        + [ColumnSum((grad_p2_a, grad_p2_b), 1), ColumnSum((grad_p3_a, grad_p3_b), 1)],
     )
     sums_attend_one, sums_mlp_one = carried[:2], (sum_mlp_c, carried[2])
     (red_p2_w,), (red_p3_w,) = carried[3:]

time: 506 us -> 499 us (0.986)
  Pallas kernels: 479 us -> 473 us
    pallas_call x10, Pallas kernels: 471 us -> 465 us  [call(): pl.pallas_call(body, out_shape=[jax.ShapeDtypeStruct(shape, dtype) for sh...]
where the time goes in v8:
time: 499 us; the launch traced here: 491 us
  Pallas kernels  473 us (95%)
  local copies, waits for them, and re-layouts  12.6 us (3%)
    pallas_call x10, Pallas kernels, call(): pl.pallas_call(body, out_shape=[jax.ShapeDtypeStruct(shape, dtype) for sh...  465 us

profile of v8, /device:TPU:0, one launch (start us, length us, event | category | flops | bytes accessed | tf_op | source)
XLA Modules:
  0.0 490.7 jit_solution(11081684584764423374)
XLA Ops:
  0.7 0.0 copy-start
  0.7 0.0 copy-start.5
  0.7 0.0 copy-start.7
  0.7 0.0 copy-start.8
  0.7 0.0 copy-start.9
  0.7 0.0 copy-start.10
  0.7 0.0 copy-start.6
  0.7 0.0 copy-start.3
  0.8 1.8 constant_dynamic-slice_fusion
  2.5 0.7 copy.112
  3.2 0.7 copy.113
  3.9 0.0 copy-done.5
  4.0 0.6 pad_bitcast_fusion.refs_1_
  4.6 0.1 pad.34.clone
  4.7 0.0 copy-done.7
  4.7 0.1 fusion.4
  4.8 0.0 copy-done.8
  4.8 0.0 copy-done.9
  4.9 0.7 concatenate.30.refs_3_
  5.5 0.1 dynamic-slice_bitcast_fusion
  5.6 0.7 copy.87.refs_4_.refs_3_.refs_5_
  6.3 0.8 copy.88.refs_5_.refs_4_
  7.2 0.6 broadcast_in_dim.65.refs_6_.refs_5_
  7.8 2.4 copy.89.refs_8_.refs_6_.refs_11_
  10.1 0.2 constant_dynamic-slice_fusion.1
  10.4 0.7 copy.114
  11.1 0.1 pad.32.clone
  11.2 0.7 maximum_maximum_fusion.refs_16_
  11.9 90.5 %shard_map.348 = (f32[2,6,8,1152]{3,2,1,0:T(8,128)}, f32[2,8,1152]{2,1,0:T(8,128)}, bf16[1152,864]{1,0:T(8,128)(2,1)}, bf16[288,1152]{1,0:T(8,128)(2,1)}, bf16[1...) custom-call(bf16[2,48,1152]{2,1,0:T(8,128)(2,1)} %bitcast.69, ...), custom_call_target="tpu_custom_call" | custom-call | flops 1019215872 | bytes 16472832 | tf_op jit(solution)/shard_map/pallas_call | solution.py:1632
  102.4 41.7 %shard_map.349 = (bf16[2,48,1152]{2,1,0:T(8,128)(2,1)}, f32[2,48,1152]{2,1,0:T(8,128)}, bf16[2,192,1152]{2,1,0:T(8,128)(2,1)}, f32[2,192,1152]{2,1,0:T(8,128)}, ...) custom-call(f32[2,48,1152]{2,1,0:T(8,128)} %get-tuple-element.145.re, ...), custom_call_target="tpu_custom_call", output_to_operand_aliasing={{5}: (8, {}), {6}: (9, {}), {7}: (10, {})} | custom-call | flops 2038431744 | bytes 19702144 | tf_op jit(solution)/shard_map/pallas_call | solution.py:1632
  144.1 34.6 %shard_map.350 = (f32[2,48,1152]{2,1,0:T(8,128)}, f32[2,48,1152]{2,1,0:T(8,128)}, bf16[2,192,1152]{2,1,0:T(8,128)(2,1)}, bf16[2,192,512]{2,1,0:T(8,128)(2,1)}, b...) custom-call(bf16[2,48,1152]{2,1,0:T(8,128)(2,1)} %get-tuple-element., ...), custom_call_target="tpu_custom_call", output_to_operand_aliasing={{8}: (10, {}), {9}: (11, {}), {10}: (12, {})} | custom-call | flops 1019215872 | bytes 14175616 | tf_op jit(solution)/shard_map/pallas_call | solution.py:1632
  178.7 0.0 copy-start.11
  178.7 32.7 %shard_map.351 = (bf16[2,48,1152]{2,1,0:T(8,128)(2,1)}, f32[2,48,1152]{2,1,0:T(8,128)}, bf16[2,192,1152]{2,1,0:T(8,128)(2,1)}, f32[2,192,1152]{2,1,0:T(8,128)}, ...) custom-call(f32[2,48,1152]{2,1,0:T(8,128)} %get-tuple-element.159.re, ...), custom_call_target="tpu_custom_call", output_to_operand_aliasing={{5}: (8, {}), {6}: (9, {}), {7}: (10, {})} | custom-call | flops 2038431744 | bytes 19702144 | tf_op jit(solution)/shard_map/pallas_call | solution.py:1632
  211.4 0.6 broadcast_in_dim.71.refs_3_
  212.0 22.1 %shard_map.352 = (f32[2,48,1152]{2,1,0:T(8,128)}, bf16[2,1152,512]{2,1,0:T(8,128)(2,1)}, bf16[2,512,2048]{2,1,0:T(8,128)(2,1)}, bf16[2,192,2048]{2,1,0:T(8,128)(2,1)}, f32[4,8,512]{2,1,0:T(8,128)}) custom-call(bf16[2,48,1152]{2,1,0:T(8,128)(2,1)} %get-tuple-element.153.refs_0_.refs_12_.refs_1_, bf16[2,2,2,48,192]{4,3,2,1,0:T(8,128)(2,1)} %get-tuple-element.168.refs_1_, ...), custom_call_target="tpu_custom_call" | custom-call | flops 4680843264 | bytes 8564736 | tf_op jit(solution)/shard_map/pallas_call | solution.py:1632
  234.2 0.0 copy-start.2
  234.2 0.0 copy-start.4
  234.2 47.2 %shard_map.353 = (f32[2,48,1152]{2,1,0:T(8,128)}, f32[3,8,1152]{2,1,0:T(8,128)}, bf16[2,288,1152]{2,1,0:T(8,128)(2,1)}, bf16[2,288,1152]{2,1,0:T(8,128)(2,1)}, f...) custom-call(bf16[2,48,1152]{2,1,0:T(8,128)(2,1)} %bitcast.72, ...), custom_call_target="tpu_custom_call" | custom-call | flops 4076863488 | bytes 20078976 | tf_op jit(solution)/shard_map/pallas_call | solution.py:1632
  281.4 1.1 fusion
  282.5 0.9 copy.104
  283.5 48.0 %shard_map.354 = (f32[2,48,1152]{2,1,0:T(8,128)}, f32[3,8,1152]{2,1,0:T(8,128)}, bf16[2,288,864]{2,1,0:T(8,128)(2,1)}, bf16[2,288,288]{2,1,0:T(8,128)(2,1)}, f32...) custom-call(f32[2,48,1152]{2,1,0:T(8,128)} %get-tuple-element.176.re, ...), custom_call_target="tpu_custom_call" | custom-call | flops 2038431744 | bytes 19923328 | tf_op jit(solution)/shard_map/pallas_call | solution.py:1632
  331.5 43.4 %shard_map.355 = (f32[2,48,1152]{2,1,0:T(8,128)}, f32[3,8,1152]{2,1,0:T(8,128)}, bf16[2,288,1152]{2,1,0:T(8,128)(2,1)}, bf16[2,288,1152]{2,1,0:T(8,128)(2,1)}, f...) custom-call(f32[2,48,1152]{2,1,0:T(8,128)} %get-tuple-element.188.re, ...), custom_call_target="tpu_custom_call" | custom-call | flops 4076863488 | bytes 24781184 | tf_op jit(solution)/shard_map/pallas_call | solution.py:1632
  375.0 53.8 %shard_map.356 = (f32[2,48,1152]{2,1,0:T(8,128)}, f32[3,8,1152]{2,1,0:T(8,128)}, bf16[2,288,864]{2,1,0:T(8,128)(2,1)}, bf16[2,288,288]{2,1,0:T(8,128)(2,1)}, f32...) custom-call(f32[2,48,1152]{2,1,0:T(8,128)} %get-tuple-element.198.re, ...), custom_call_target="tpu_custom_call" | custom-call | flops 2038431744 | bytes 16728448 | tf_op jit(solution)/shard_map/pallas_call | solution.py:1632
  428.9 0.1 reshape.108
  429.0 0.6 copy.115
  429.6 50.9 %shard_map.357 = (f32[4,48,1152]{2,1,0:T(8,128)}, f32[288,1728]{1,0:T(8,128)}, f32[1,1728]{1,0:T(1,128)}, f32[8,1152]{1,0:T(8,128)}, f32[8,512]{1,0:T(8,128)}, /...) custom-call(f32[2,48,1152]{2,1,0:T(8,128)} %get-tuple-element.218.re, ...), custom_call_target="tpu_custom_call" | custom-call | flops 63700992 | bytes 5560064 | tf_op jit(solution)/shard_map/pallas_call | solution.py:1632
  480.5 0.0 copy-start.1
  480.5 8.2 %shard_map.358 = (f32[288,1152]{1,0:T(8,128)}, f32[288,1152]{1,0:T(8,128)}, f32[288,1728]{1,0:T(8,128)}, f32[1,1728]{1,0:T(1,128)}, f32[144,512]{1,0:T(8,128)}, ...) custom-call(f32[288,1152]{1,0:T(8,128)} %get-tuple-element.216.refs_, ...), custom_call_target="tpu_custom_call" | custom-call | flops 1000 | bytes 16777216 | tf_op jit(solution)/shard_map/pallas_call | solution.py:1978
  (29 shorter events, 0.2 us)
Async XLA Ops:
  0.7 9.5 %copy-start = (bf16[192,4,192]{2,1,0:T(4,128)(2,1)S(1)}, bf16[192,4,192]{2,1,0:T(4,128)(2,1)}, u32[]{:S(2)}) copy-start(bf16[192,4,192]{2,1,0:T(4,128)(2,1)} %param.24) | copy-start | bytes 884740
  0.7 3.3 copy-start.5
  0.7 4.0 copy-start.7
  0.7 4.1 copy-start.8
  0.7 4.1 copy-start.9
  0.7 4.1 copy-start.10
  0.7 4.8 copy-start.6
  0.7 7.0 %copy-start.3 = (bf16[1,1152,3,288]{1,3,2,0:T(8,128)(2,1)S(1)}, bf16[1,1152,3,288]{1,3,2,0:T(8,128)(2,1)}, u32[]{:S(2)}) copy-start(bf16[1,1152,3,288]{1,3,2,0:T(8,128)(2,1)} %param.28) | copy-start | bytes 5971972
  7.7 3.3 copy-start.13
  7.8 3.3 copy-start.12
  178.7 32.7 %copy-start.11 = (bf16[2048]{0:T(1024)(128)(2,1)S(1)}, bf16[2048]{0:T(1024)(128)(2,1)}, u32[]{:S(2)}) copy-start(bf16[2048]{0:T(1024)(128)(2,1)} %param.39) | copy-start | bytes 12292
  234.2 47.2 %copy-start.2 = (bf16[2,48,1152]{2,1,0:T(8,128)(2,1)S(1)}, bf16[2,48,1152]{2,1,0:T(8,128)(2,1)}, u32[]{:S(2)}) copy-start(bf16[2,48,1152]{2,1,0:T(8,128)(2,1)} %get-tuple-element.153.refs_0_.refs_12_.refs_1_) | copy-start | bytes 663556
  234.2 47.2 %copy-start.4 = (bf16[2,48,1152]{2,1,0:T(8,128)(2,1)S(1)}, bf16[2,48,1152]{2,1,0:T(8,128)(2,1)}, u32[]{:S(2)}) copy-start(bf16[2,48,1152]{2,1,0:T(8,128)(2,1)} %get-tuple-element.163.refs_13_) | copy-start | bytes 663556
  480.5 8.8 %copy-start.1 = (bf16[192,4,192]{2,1,0:T(4,128)(2,1)S(1)}, bf16[192,4,192]{2,1,0:T(4,128)(2,1)}, u32[]{:S(2)}) copy-start(bf16[192,4,192]{2,1,0:T(4,128)(2,1)} %param.24) | copy-start | bytes 884740

commit v9 on v8

--- a/solution.py
+++ b/solution.py
@@ -52,11 +52,15 @@
     return {"dp": lax.axis_index("dp") + 2 - 4 * y_bit()}
 
 
-def greet(peers):
+def call_peers(peers):
     barrier = pltpu.get_barrier_semaphore()
     for peer in peers:
         pl.semaphore_signal(barrier, inc=1, device_id=peer, device_id_type=MESH)
-    pl.semaphore_wait(barrier, len(peers))
+    return lambda: pl.semaphore_wait(barrier, len(peers))
+
+
+def greet(peers):
+    call_peers(peers)()
 
 
 def remote(source, target, send_sem, recv_sem, peer):
@@ -914,6 +918,7 @@
     full, wqkv, wo, mixed_wide = (full_ref, *scratch[:3])
     buffers, spreads = scratch[3:6], scratch[6]
     seg_own, seg_col, seg_row = segs
+    await_peers = call_peers(peers) if peers is not None else None
     mod_ref = mods()
     me = lax.axis_index("tensor")
     rows, length, width = u_ref.shape
@@ -924,7 +929,7 @@
     attn_in = normed * (1.0 + token_mod(mod_ref, seg_own, 1)) + token_mod(mod_ref, seg_own, 0)
     full[:, own_rows(me, length), :] = attn_in.astype(BF16).reshape(rows, length, width)
     if peers is not None:
-        greet(peers)
+        await_peers()
     line = Line(length, sems)
     line.start_gather(full)
     spread = spread_matrix(heads_width)
@@ -1099,6 +1104,7 @@
     w1, w2, send_buf, recv_buf, relay_buf, w_sem, *sems, cargo,
 ):
     full = full_ref
+    await_peers = call_peers(z_peers(count) + cargo.peers())
     me = lax.axis_index("tensor")
     rows, length, width = middle_ref.shape
     mod_ref = mods_ref.at[block]
@@ -1107,7 +1113,7 @@
     normed, unused = layer_norm(flat(middle_ref))
     mlp_in = normed * (1.0 + token_mod(mod_ref, seg_own, 4)) + token_mod(mod_ref, seg_own, 3)
     full[:, own_rows(me, length), :] = mlp_in.astype(BF16).reshape(rows, length, width)
-    greet(z_peers(count) + cargo.peers())
+    await_peers()
     line = Line(length, sems)
     line.start_gather(full)
     cargo.begin()
@@ -1159,6 +1165,7 @@
     mod_ref = mods_ref.at[block]
     load_one = fetch(block, w1_own, w1_other, w1, w_sem.at[0])
     load_two = fetch(block, w2_own, w2_other, w2, w_sem.at[1])
+    await_peers = call_peers(z_peers(count) + cargo.peers(["core"]))
     cargo.load()
     g = flat(g_ref).astype(F32)
     if len(g_refs) > 1:
@@ -1166,7 +1173,7 @@
     g_buf[...] = g
     d_branch = (g * token_mod(mod_ref, seg_own, 5)).astype(BF16)
     full[:, own_rows(me, length), :] = d_branch.reshape(rows, length, width)
-    greet(z_peers(count) + cargo.peers(["core"]))
+    await_peers()
     line = Line(length, sems)
     line.start_gather(full)
     cargo.begin()
@@ -1234,11 +1241,12 @@
     mod_ref = mods_ref.at[block]
     load_qkv = fetch(block, wqkv_own, wqkv_other, wqkv, w_sem.at[0])
     load_out = fetch(block, wo_own, wo_other, wo, w_sem.at[1])
+    await_peers = call_peers(z_peers(count) + cargo.peers(["core"]))
     cargo.load()
     d_middle = flat(d_middle_ref)
     d_branch = (d_middle * token_mod(mod_ref, seg_own, 2)).astype(BF16)
     full[:, own_rows(me, length), :] = d_branch.reshape(rows, length, width)
-    greet(z_peers(count) + cargo.peers(["core"]))
+    await_peers()
     line = Line(length, sems)
     line.start_gather(full)
     cargo.begin()

time: 499 us -> 497 us (level)
  no operation moved by 1% of the time
where the time goes in v9:
time: 497 us; the launch traced here: 489 us
  Pallas kernels  472 us (95%)
  local copies, waits for them, and re-layouts  12.6 us (3%)
    pallas_call x10, Pallas kernels, call(): pl.pallas_call(body, out_shape=[jax.ShapeDtypeStruct(shape, dtype) for sh...  463 us

profile of v9, /device:TPU:0, one launch (start us, length us, event | category | flops | bytes accessed | tf_op | source)
XLA Modules:
  0.0 489.2 jit_solution(17515662525960930328)
XLA Ops:
  0.7 0.0 copy-start
  0.7 0.0 copy-start.5
  0.7 0.0 copy-start.7
  0.7 0.0 copy-start.8
  0.7 0.0 copy-start.9
  0.7 0.0 copy-start.10
  0.7 0.0 copy-start.6
  0.7 0.0 copy-start.3
  0.8 1.8 constant_dynamic-slice_fusion
  2.5 0.7 copy.112
  3.2 0.7 copy.113
  3.9 0.0 copy-done.5
  4.0 0.6 pad_bitcast_fusion.refs_1_
  4.6 0.1 pad.34.clone
  4.7 0.0 copy-done.7
  4.7 0.1 fusion.4
  4.8 0.0 copy-done.8
  4.9 0.7 concatenate.30.refs_3_
  5.5 0.1 dynamic-slice_bitcast_fusion
  5.6 0.7 copy.87.refs_4_.refs_3_.refs_5_
  6.3 0.8 copy.88.refs_5_.refs_4_
  7.2 0.6 broadcast_in_dim.65.refs_6_.refs_5_
  7.8 2.4 copy.89.refs_8_.refs_6_.refs_11_
  10.1 0.0 copy-done
  10.1 0.2 constant_dynamic-slice_fusion.1
  10.4 0.7 copy.114
  11.1 0.1 pad.32.clone
  11.2 0.7 maximum_maximum_fusion.refs_16_
  11.9 90.5 %shard_map.348 = (f32[2,6,8,1152]{3,2,1,0:T(8,128)}, f32[2,8,1152]{2,1,0:T(8,128)}, bf16[1152,864]{1,0:T(8,128)(2,1)}, bf16[288,1152]{1,0:T(8,128)(2,1)}, bf16[1...) custom-call(bf16[2,48,1152]{2,1,0:T(8,128)(2,1)} %bitcast.69, ...), custom_call_target="tpu_custom_call" | custom-call | flops 1019215872 | bytes 16472832 | tf_op jit(solution)/shard_map/pallas_call | solution.py:1640
  102.4 41.4 %shard_map.349 = (bf16[2,48,1152]{2,1,0:T(8,128)(2,1)}, f32[2,48,1152]{2,1,0:T(8,128)}, bf16[2,192,1152]{2,1,0:T(8,128)(2,1)}, f32[2,192,1152]{2,1,0:T(8,128)}, ...) custom-call(f32[2,48,1152]{2,1,0:T(8,128)} %get-tuple-element.145.re, ...), custom_call_target="tpu_custom_call", output_to_operand_aliasing={{5}: (8, {}), {6}: (9, {}), {7}: (10, {})} | custom-call | flops 2038431744 | bytes 19702144 | tf_op jit(solution)/shard_map/pallas_call | solution.py:1640
  143.8 34.3 %shard_map.350 = (f32[2,48,1152]{2,1,0:T(8,128)}, f32[2,48,1152]{2,1,0:T(8,128)}, bf16[2,192,1152]{2,1,0:T(8,128)(2,1)}, bf16[2,192,512]{2,1,0:T(8,128)(2,1)}, b...) custom-call(bf16[2,48,1152]{2,1,0:T(8,128)(2,1)} %get-tuple-element., ...), custom_call_target="tpu_custom_call", output_to_operand_aliasing={{8}: (10, {}), {9}: (11, {}), {10}: (12, {})} | custom-call | flops 1019215872 | bytes 14175616 | tf_op jit(solution)/shard_map/pallas_call | solution.py:1640
  178.1 0.0 copy-start.11
  178.1 32.1 %shard_map.351 = (bf16[2,48,1152]{2,1,0:T(8,128)(2,1)}, f32[2,48,1152]{2,1,0:T(8,128)}, bf16[2,192,1152]{2,1,0:T(8,128)(2,1)}, f32[2,192,1152]{2,1,0:T(8,128)}, ...) custom-call(f32[2,48,1152]{2,1,0:T(8,128)} %get-tuple-element.159.re, ...), custom_call_target="tpu_custom_call", output_to_operand_aliasing={{5}: (8, {}), {6}: (9, {}), {7}: (10, {})} | custom-call | flops 2038431744 | bytes 19702144 | tf_op jit(solution)/shard_map/pallas_call | solution.py:1640
  210.2 0.6 broadcast_in_dim.71.refs_3_
  210.8 22.1 %shard_map.352 = (f32[2,48,1152]{2,1,0:T(8,128)}, bf16[2,1152,512]{2,1,0:T(8,128)(2,1)}, bf16[2,512,2048]{2,1,0:T(8,128)(2,1)}, bf16[2,192,2048]{2,1,0:T(8,128)(2,1)}, f32[4,8,512]{2,1,0:T(8,128)}) custom-call(bf16[2,48,1152]{2,1,0:T(8,128)(2,1)} %get-tuple-element.153.refs_0_.refs_12_.refs_1_, bf16[2,2,2,48,192]{4,3,2,1,0:T(8,128)(2,1)} %get-tuple-element.168.refs_1_, ...), custom_call_target="tpu_custom_call" | custom-call | flops 4680843264 | bytes 8564736 | tf_op jit(solution)/shard_map/pallas_call | solution.py:1640
  233.0 47.3 %shard_map.353 = (f32[2,48,1152]{2,1,0:T(8,128)}, f32[3,8,1152]{2,1,0:T(8,128)}, bf16[2,288,1152]{2,1,0:T(8,128)(2,1)}, bf16[2,288,1152]{2,1,0:T(8,128)(2,1)}, f...) custom-call(bf16[2,48,1152]{2,1,0:T(8,128)(2,1)} %bitcast.72, ...), custom_call_target="tpu_custom_call" | custom-call | flops 4076863488 | bytes 20078976 | tf_op jit(solution)/shard_map/pallas_call | solution.py:1640
  280.3 0.0 copy-done.2
  280.3 0.0 copy-done.4
  280.3 1.1 fusion
  281.5 0.9 copy.104
  282.4 48.0 %shard_map.354 = (f32[2,48,1152]{2,1,0:T(8,128)}, f32[3,8,1152]{2,1,0:T(8,128)}, bf16[2,288,864]{2,1,0:T(8,128)(2,1)}, bf16[2,288,288]{2,1,0:T(8,128)(2,1)}, f32...) custom-call(f32[2,48,1152]{2,1,0:T(8,128)} %get-tuple-element.176.re, ...), custom_call_target="tpu_custom_call" | custom-call | flops 2038431744 | bytes 19923328 | tf_op jit(solution)/shard_map/pallas_call | solution.py:1640
  330.4 43.3 %shard_map.355 = (f32[2,48,1152]{2,1,0:T(8,128)}, f32[3,8,1152]{2,1,0:T(8,128)}, bf16[2,288,1152]{2,1,0:T(8,128)(2,1)}, bf16[2,288,1152]{2,1,0:T(8,128)(2,1)}, f...) custom-call(f32[2,48,1152]{2,1,0:T(8,128)} %get-tuple-element.188.re, ...), custom_call_target="tpu_custom_call" | custom-call | flops 4076863488 | bytes 24781184 | tf_op jit(solution)/shard_map/pallas_call | solution.py:1640
  373.7 53.6 %shard_map.356 = (f32[2,48,1152]{2,1,0:T(8,128)}, f32[3,8,1152]{2,1,0:T(8,128)}, bf16[2,288,864]{2,1,0:T(8,128)(2,1)}, bf16[2,288,288]{2,1,0:T(8,128)(2,1)}, f32...) custom-call(f32[2,48,1152]{2,1,0:T(8,128)} %get-tuple-element.198.re, ...), custom_call_target="tpu_custom_call" | custom-call | flops 2038431744 | bytes 16728448 | tf_op jit(solution)/shard_map/pallas_call | solution.py:1640
  427.4 0.1 reshape.108
  427.5 0.6 copy.115
  428.1 50.9 %shard_map.357 = (f32[4,48,1152]{2,1,0:T(8,128)}, f32[288,1728]{1,0:T(8,128)}, f32[1,1728]{1,0:T(1,128)}, f32[8,1152]{1,0:T(8,128)}, f32[8,512]{1,0:T(8,128)}, /...) custom-call(f32[2,48,1152]{2,1,0:T(8,128)} %get-tuple-element.218.re, ...), custom_call_target="tpu_custom_call" | custom-call | flops 63700992 | bytes 5560064 | tf_op jit(solution)/shard_map/pallas_call | solution.py:1640
  479.0 0.0 copy-start.1
  479.0 8.2 %shard_map.358 = (f32[288,1152]{1,0:T(8,128)}, f32[288,1152]{1,0:T(8,128)}, f32[288,1728]{1,0:T(8,128)}, f32[1,1728]{1,0:T(1,128)}, f32[144,512]{1,0:T(8,128)}, ...) custom-call(f32[288,1152]{1,0:T(8,128)} %get-tuple-element.216.refs_, ...), custom_call_target="tpu_custom_call" | custom-call | flops 1000 | bytes 16777216 | tf_op jit(solution)/shard_map/pallas_call | solution.py:1986
  (29 shorter events, 0.2 us)
Async XLA Ops:
  0.7 9.5 %copy-start = (bf16[192,4,192]{2,1,0:T(4,128)(2,1)S(1)}, bf16[192,4,192]{2,1,0:T(4,128)(2,1)}, u32[]{:S(2)}) copy-start(bf16[192,4,192]{2,1,0:T(4,128)(2,1)} %param.24) | copy-start | bytes 884740
  0.7 3.3 copy-start.5
  0.7 4.0 copy-start.7
  0.7 4.1 copy-start.8
  0.7 4.1 copy-start.9
  0.7 4.1 copy-start.10
  0.7 4.8 copy-start.6
  0.7 7.0 %copy-start.3 = (bf16[1,1152,3,288]{1,3,2,0:T(8,128)(2,1)S(1)}, bf16[1,1152,3,288]{1,3,2,0:T(8,128)(2,1)}, u32[]{:S(2)}) copy-start(bf16[1,1152,3,288]{1,3,2,0:T(8,128)(2,1)} %param.28) | copy-start | bytes 5971972
  7.7 3.3 copy-start.13
  7.8 3.3 copy-start.12
  178.1 32.2 %copy-start.11 = (bf16[2048]{0:T(1024)(128)(2,1)S(1)}, bf16[2048]{0:T(1024)(128)(2,1)}, u32[]{:S(2)}) copy-start(bf16[2048]{0:T(1024)(128)(2,1)} %param.39) | copy-start | bytes 12292
  233.0 47.3 %copy-start.2 = (bf16[2,48,1152]{2,1,0:T(8,128)(2,1)S(1)}, bf16[2,48,1152]{2,1,0:T(8,128)(2,1)}, u32[]{:S(2)}) copy-start(bf16[2,48,1152]{2,1,0:T(8,128)(2,1)} %get-tuple-element.153.refs_0_.refs_12_.refs_1_) | copy-start | bytes 663556
  233.0 47.3 %copy-start.4 = (bf16[2,48,1152]{2,1,0:T(8,128)(2,1)S(1)}, bf16[2,48,1152]{2,1,0:T(8,128)(2,1)}, u32[]{:S(2)}) copy-start(bf16[2,48,1152]{2,1,0:T(8,128)(2,1)} %get-tuple-element.163.refs_13_) | copy-start | bytes 663556
  479.0 8.8 %copy-start.1 = (bf16[192,4,192]{2,1,0:T(4,128)(2,1)S(1)}, bf16[192,4,192]{2,1,0:T(4,128)(2,1)}, u32[]{:S(2)}) copy-start(bf16[192,4,192]{2,1,0:T(4,128)(2,1)} %param.24) | copy-start | bytes 884740

commit v10 on v9

--- a/solution.py
+++ b/solution.py
@@ -961,7 +961,7 @@
         return carry
 
     steps[1]()
-    lax.fori_loop(0, rows * heads, one_head, 0, unroll=4)
+    lax.fori_loop(0, rows * heads, one_head, 0, unroll=8)
     mixed_ref[...] = dot(flat(mixed_wide), spread, NT).astype(BF16).reshape(mixed_ref.shape)
     flush(3, 4, 5, 6, 7)
     need_out()

time: 497 us -> 498 us (level)
  no operation moved by 1% of the time
where the time goes in v10:
time: 498 us; the launch traced here: 493 us
  Pallas kernels  475 us (95%)
  local copies, waits for them, and re-layouts  12.6 us (3%)
    pallas_call x10, Pallas kernels, call(): pl.pallas_call(body, out_shape=[jax.ShapeDtypeStruct(shape, dtype) for sh...  467 us

profile of v10, /device:TPU:0, one launch (start us, length us, event | category | flops | bytes accessed | tf_op | source)
XLA Modules:
  0.0 492.6 jit_solution(5953868286941687775)
XLA Ops:
  0.7 0.0 copy-start
  0.7 0.0 copy-start.5
  0.7 0.0 copy-start.7
  0.7 0.0 copy-start.8
  0.7 0.0 copy-start.9
  0.7 0.0 copy-start.10
  0.7 0.0 copy-start.6
  0.7 0.0 copy-start.3
  0.8 1.8 constant_dynamic-slice_fusion
  2.5 0.7 copy.112
  3.2 0.7 copy.113
  3.9 0.0 copy-done.5
  4.0 0.6 pad_bitcast_fusion.refs_1_
  4.6 0.1 pad.34.clone
  4.7 0.0 copy-done.7
  4.7 0.1 fusion.4
  4.8 0.0 copy-done.8
  4.9 0.7 concatenate.30.refs_3_
  5.5 0.1 dynamic-slice_bitcast_fusion
  5.6 0.7 copy.87.refs_4_.refs_3_.refs_5_
  6.3 0.8 copy.88.refs_5_.refs_4_
  7.2 0.6 broadcast_in_dim.65.refs_6_.refs_5_
  7.8 2.4 copy.89.refs_8_.refs_6_.refs_11_
  10.1 0.2 constant_dynamic-slice_fusion.1
  10.4 0.7 copy.114
  11.1 0.1 pad.32.clone
  11.2 0.7 maximum_maximum_fusion.refs_16_
  11.9 90.6 %shard_map.348 = (f32[2,6,8,1152]{3,2,1,0:T(8,128)}, f32[2,8,1152]{2,1,0:T(8,128)}, bf16[1152,864]{1,0:T(8,128)(2,1)}, bf16[288,1152]{1,0:T(8,128)(2,1)}, bf16[1...) custom-call(bf16[2,48,1152]{2,1,0:T(8,128)(2,1)} %bitcast.69, ...), custom_call_target="tpu_custom_call" | custom-call | flops 1019215872 | bytes 16472832 | tf_op jit(solution)/shard_map/pallas_call | solution.py:1640
  102.4 41.5 %shard_map.349 = (bf16[2,48,1152]{2,1,0:T(8,128)(2,1)}, f32[2,48,1152]{2,1,0:T(8,128)}, bf16[2,192,1152]{2,1,0:T(8,128)(2,1)}, f32[2,192,1152]{2,1,0:T(8,128)}, ...) custom-call(f32[2,48,1152]{2,1,0:T(8,128)} %get-tuple-element.145.re, ...), custom_call_target="tpu_custom_call", output_to_operand_aliasing={{5}: (8, {}), {6}: (9, {}), {7}: (10, {})} | custom-call | flops 2038431744 | bytes 19702144 | tf_op jit(solution)/shard_map/pallas_call | solution.py:1640
  144.0 36.6 %shard_map.350 = (f32[2,48,1152]{2,1,0:T(8,128)}, f32[2,48,1152]{2,1,0:T(8,128)}, bf16[2,192,1152]{2,1,0:T(8,128)(2,1)}, bf16[2,192,512]{2,1,0:T(8,128)(2,1)}, b...) custom-call(bf16[2,48,1152]{2,1,0:T(8,128)(2,1)} %get-tuple-element., ...), custom_call_target="tpu_custom_call", output_to_operand_aliasing={{8}: (10, {}), {9}: (11, {}), {10}: (12, {})} | custom-call | flops 1019215872 | bytes 14175616 | tf_op jit(solution)/shard_map/pallas_call | solution.py:1640
  180.6 0.0 copy-start.11
  180.6 34.8 %shard_map.351 = (bf16[2,48,1152]{2,1,0:T(8,128)(2,1)}, f32[2,48,1152]{2,1,0:T(8,128)}, bf16[2,192,1152]{2,1,0:T(8,128)(2,1)}, f32[2,192,1152]{2,1,0:T(8,128)}, ...) custom-call(f32[2,48,1152]{2,1,0:T(8,128)} %get-tuple-element.159.re, ...), custom_call_target="tpu_custom_call", output_to_operand_aliasing={{5}: (8, {}), {6}: (9, {}), {7}: (10, {})} | custom-call | flops 2038431744 | bytes 19702144 | tf_op jit(solution)/shard_map/pallas_call | solution.py:1640
  215.4 0.0 copy-done.11
  215.4 0.6 broadcast_in_dim.71.refs_3_
  216.0 22.1 %shard_map.352 = (f32[2,48,1152]{2,1,0:T(8,128)}, bf16[2,1152,512]{2,1,0:T(8,128)(2,1)}, bf16[2,512,2048]{2,1,0:T(8,128)(2,1)}, bf16[2,192,2048]{2,1,0:T(8,128)(2,1)}, f32[4,8,512]{2,1,0:T(8,128)}) custom-call(bf16[2,48,1152]{2,1,0:T(8,128)(2,1)} %get-tuple-element.153.refs_0_.refs_12_.refs_1_, bf16[2,2,2,48,192]{4,3,2,1,0:T(8,128)(2,1)} %get-tuple-element.168.refs_1_, ...), custom_call_target="tpu_custom_call" | custom-call | flops 4680843264 | bytes 8564736 | tf_op jit(solution)/shard_map/pallas_call | solution.py:1640
  238.1 45.7 %shard_map.353 = (f32[2,48,1152]{2,1,0:T(8,128)}, f32[3,8,1152]{2,1,0:T(8,128)}, bf16[2,288,1152]{2,1,0:T(8,128)(2,1)}, bf16[2,288,1152]{2,1,0:T(8,128)(2,1)}, f...) custom-call(bf16[2,48,1152]{2,1,0:T(8,128)(2,1)} %bitcast.72, ...), custom_call_target="tpu_custom_call" | custom-call | flops 4076863488 | bytes 20078976 | tf_op jit(solution)/shard_map/pallas_call | solution.py:1640
  283.8 0.0 copy-done.2
  283.8 0.0 copy-done.4
  283.9 1.1 fusion
  285.0 0.9 copy.104
  286.0 47.7 %shard_map.354 = (f32[2,48,1152]{2,1,0:T(8,128)}, f32[3,8,1152]{2,1,0:T(8,128)}, bf16[2,288,864]{2,1,0:T(8,128)(2,1)}, bf16[2,288,288]{2,1,0:T(8,128)(2,1)}, f32...) custom-call(f32[2,48,1152]{2,1,0:T(8,128)} %get-tuple-element.176.re, ...), custom_call_target="tpu_custom_call" | custom-call | flops 2038431744 | bytes 19923328 | tf_op jit(solution)/shard_map/pallas_call | solution.py:1640
  333.6 43.3 %shard_map.355 = (f32[2,48,1152]{2,1,0:T(8,128)}, f32[3,8,1152]{2,1,0:T(8,128)}, bf16[2,288,1152]{2,1,0:T(8,128)(2,1)}, bf16[2,288,1152]{2,1,0:T(8,128)(2,1)}, f...) custom-call(f32[2,48,1152]{2,1,0:T(8,128)} %get-tuple-element.188.re, ...), custom_call_target="tpu_custom_call" | custom-call | flops 4076863488 | bytes 24781184 | tf_op jit(solution)/shard_map/pallas_call | solution.py:1640
  376.9 54.9 %shard_map.356 = (f32[2,48,1152]{2,1,0:T(8,128)}, f32[3,8,1152]{2,1,0:T(8,128)}, bf16[2,288,864]{2,1,0:T(8,128)(2,1)}, bf16[2,288,288]{2,1,0:T(8,128)(2,1)}, f32...) custom-call(f32[2,48,1152]{2,1,0:T(8,128)} %get-tuple-element.198.re, ...), custom_call_target="tpu_custom_call" | custom-call | flops 2038431744 | bytes 16728448 | tf_op jit(solution)/shard_map/pallas_call | solution.py:1640
  431.9 0.1 reshape.108
  432.0 0.6 copy.115
  432.6 49.8 %shard_map.357 = (f32[4,48,1152]{2,1,0:T(8,128)}, f32[288,1728]{1,0:T(8,128)}, f32[1,1728]{1,0:T(1,128)}, f32[8,1152]{1,0:T(8,128)}, f32[8,512]{1,0:T(8,128)}, /...) custom-call(f32[2,48,1152]{2,1,0:T(8,128)} %get-tuple-element.218.re, ...), custom_call_target="tpu_custom_call" | custom-call | flops 63700992 | bytes 5560064 | tf_op jit(solution)/shard_map/pallas_call | solution.py:1640
  482.4 0.0 copy-start.1
  482.4 8.2 %shard_map.358 = (f32[288,1152]{1,0:T(8,128)}, f32[288,1152]{1,0:T(8,128)}, f32[288,1728]{1,0:T(8,128)}, f32[1,1728]{1,0:T(1,128)}, f32[144,512]{1,0:T(8,128)}, ...) custom-call(f32[288,1152]{1,0:T(8,128)} %get-tuple-element.216.refs_, ...), custom_call_target="tpu_custom_call" | custom-call | flops 1000 | bytes 16777216 | tf_op jit(solution)/shard_map/pallas_call | solution.py:1986
  (29 shorter events, 0.2 us)
Async XLA Ops:
  0.7 9.5 %copy-start = (bf16[192,4,192]{2,1,0:T(4,128)(2,1)S(1)}, bf16[192,4,192]{2,1,0:T(4,128)(2,1)}, u32[]{:S(2)}) copy-start(bf16[192,4,192]{2,1,0:T(4,128)(2,1)} %param.24) | copy-start | bytes 884740
  0.7 3.3 copy-start.5
  0.7 4.0 copy-start.7
  0.7 4.1 copy-start.8
  0.7 4.1 copy-start.9
  0.7 4.1 copy-start.10
  0.7 4.8 copy-start.6
  0.7 7.0 %copy-start.3 = (bf16[1,1152,3,288]{1,3,2,0:T(8,128)(2,1)S(1)}, bf16[1,1152,3,288]{1,3,2,0:T(8,128)(2,1)}, u32[]{:S(2)}) copy-start(bf16[1,1152,3,288]{1,3,2,0:T(8,128)(2,1)} %param.28) | copy-start | bytes 5971972
  7.7 3.3 copy-start.13
  7.8 3.3 copy-start.12
  180.6 34.8 %copy-start.11 = (bf16[2048]{0:T(1024)(128)(2,1)S(1)}, bf16[2048]{0:T(1024)(128)(2,1)}, u32[]{:S(2)}) copy-start(bf16[2048]{0:T(1024)(128)(2,1)} %param.39) | copy-start | bytes 12292
  238.1 45.7 %copy-start.2 = (bf16[2,48,1152]{2,1,0:T(8,128)(2,1)S(1)}, bf16[2,48,1152]{2,1,0:T(8,128)(2,1)}, u32[]{:S(2)}) copy-start(bf16[2,48,1152]{2,1,0:T(8,128)(2,1)} %get-tuple-element.153.refs_0_.refs_12_.refs_1_) | copy-start | bytes 663556
  238.1 45.7 %copy-start.4 = (bf16[2,48,1152]{2,1,0:T(8,128)(2,1)S(1)}, bf16[2,48,1152]{2,1,0:T(8,128)(2,1)}, u32[]{:S(2)}) copy-start(bf16[2,48,1152]{2,1,0:T(8,128)(2,1)} %get-tuple-element.163.refs_13_) | copy-start | bytes 663556
  482.4 8.8 %copy-start.1 = (bf16[192,4,192]{2,1,0:T(4,128)(2,1)S(1)}, bf16[192,4,192]{2,1,0:T(4,128)(2,1)}, u32[]{:S(2)}) copy-start(bf16[192,4,192]{2,1,0:T(4,128)(2,1)} %param.24) | copy-start | bytes 884740
